TPU v7x, 128 devices: a whole 4x4x4 slice. The times are simulated.
128 devices in a mesh: group: 32 (over y, x, core), blk: 4 (over z).
Axes of the slice: x: 4, y: 4, z: 4, core: 2. Of those that a mesh axis runs over, the one named last changes fastest.
Arguments:
- inverses: bfloat16 [8, 1536, 1536], P('blk', 'group'), may hold values from -0.5 to 2
- lower: bfloat16 [8, 1536, 1536], P('blk', 'group'), may hold values from -0.5 to 0.5
- forcing: bfloat16 [8, 1536, 32], P('blk', 'group'), may hold values from -1.796875 to 1.796875
- inflow: float32 [1536, 32], P('group'), may hold values from -6 to 6
Outputs:
- states: float32 [8, 1536, 32], P('blk', 'group')
All inputs are finite; a program needn't handle non-finite values.
Results may differ from a plain program's by a relative error of at most 0.0057.
Values may be sent and summed in bfloat16 or wider, within the bound.
No kernel may reach another device: no remote copies, remote signals or barrier semaphores. Data moves between devices by JAX's collectives and lax.ppermute only.
A program may use at most 64 MiB of HBM per device.

v0:
```python
import jax
import jax.numpy as jnp
from jax import lax
from jax.sharding import PartitionSpec as P


def passed_along(value, axis, steps):
    count = lax.axis_size(axis)
    initial, last = (max(0, -steps), min(count, count - steps))
    return lax.ppermute(value, axis, [(source, source + steps) for source in range(initial, last)])


def apply_block(matrix, vector):
    return jnp.dot(
        matrix, vector, preferred_element_type=jnp.float32, precision=lax.Precision.HIGHEST
    )


def split_chain(local_rows, coupling, entry):
    results = []
    previous = None
    for step in range(coupling.shape[0]):
        if step == 0:
            if entry is None:
                state = local_rows[0]
            else:
                state = local_rows[0] - apply_block(coupling[0], entry)
        else:
            gathered = lax.all_gather(previous, "group", axis=0, tiled=True)
            state = local_rows[step] - apply_block(coupling[step], gathered)
        results.append(state)
        previous = state
    return results


def local(inverses, lower, forcing, inflow):
    stations = inverses.shape[0]
    lower_piece = lax.all_gather(lower, "group", axis=1, tiled=True)
    forcing_piece = lax.all_gather(forcing, "group", axis=1, tiled=True)
    acc_coupling = jnp.einsum(
        "kri,kic->krc", inverses, lower_piece, preferred_element_type=jnp.float32
    )
    acc_local = jnp.einsum(
        "kri,kic->krc", inverses, forcing_piece, preferred_element_type=jnp.float32
    )
    coupling = acc_coupling.astype(jnp.bfloat16)
    parity = 1.0 - 2.0 * (stations % 2)
    product_rows = coupling[0].astype(jnp.float32)
    step = 1
    product_full = lax.all_gather(
        product_rows.astype(jnp.bfloat16), "group", axis=0, tiled=True
    ).astype(product_rows.dtype)
    product_rows = apply_block(coupling[step], product_full)
    partial_value = split_chain(acc_local, coupling, None)
    last_rows = partial_value[-1]
    is_first = lax.axis_index("blk") == 0

    def hop(step, carry):
        out_rows, entry = carry
        incoming = passed_along(out_rows, "blk", 1)
        incoming = jnp.where(is_first, inflow, incoming)
        entry = lax.all_gather(incoming, "group", axis=0, tiled=True)
        out_rows = last_rows + parity * apply_block(product_rows, entry)
        return (out_rows, entry)

    entry_start = jnp.zeros((inverses.shape[2], forcing.shape[2]), jnp.float32)
    final_rows, entry = lax.fori_loop(0, lax.axis_size("blk"), hop, (last_rows, entry_start))
    results = split_chain(acc_local, coupling, entry)
    return jnp.stack(results, axis=0)


def solution(mesh):
    placed = (
        P("blk", "group", None),
        P("blk", "group", None),
        P("blk", "group", None),
        P("group", None),
    )
    return jax.shard_map(
        local, mesh=mesh, in_specs=placed, out_specs=P("blk", "group", None), check_vma=False
    )
```

profile of v0, /device:TPU:96, one launch (start us, length us, event | category | flops | bytes accessed | tf_op | source)
XLA Modules:
  0.0 279.0 jit_solution(11514653514317567171)
XLA Ops:
  6.5 0.7 all-gather.9.cloned.1.call-update
  7.3 59.0 %all-gather.9.cloned.1.call-done = bf16[2,1536,1536]{2,1,0:T(8,128)(2,1)} async-done(((bf16[2,48,1536]{2,1,0:T(8,128)(2,1)}), bf16[2,1536,1536]{2,1,0:T(8,128)(2,1)}) %all-gather.9.cloned.1.call-update) | async-done | bytes 9437200 | tf_op jit(solution)/shard_map/all_gather | solution.py:38
  66.3 5.4 %convolution_convert_fusion = bf16[2,48,1536]{2,1,0:T(8,128)(2,1)S(1)} fusion(bf16[2,48,1536]{2,1,0:T(8,128)(2,1)S(1)} %copy-done, bf16[2,1536,1536]{2,1,0:T(8,128)(2,1)} %all-gather.9.cloned.1.call-done), kind=kOutput, calls=%fused_computation.5 | convolution fusion | flops 453132288 | bytes 10027008 | tf_op jit(solution)/shard_map/kri,kic->krc/dot_general | solution.py:40
  71.7 0.7 slice.22
  72.5 24.8 %all_gather.18 = bf16[2,1536,32]{2,0,1:T(2,128)(2,1)S(1)} all-gather(bf16[2,48,32]{2,0,1:T(2,128)(2,1)S(1)} %copy.13), channel_id=1, replica_groups=mesh['group'=32,'blk'=4] {'group'}, dimensions={1}, use_global_device_ids=true | all-gather | bytes 202752 | tf_op jit(solution)/shard_map/all_gather | solution.py:39
  97.3 0.4 fusion.5
  97.8 22.9 %all-gather = f32[1,1536,32]{2,0,1:T(1,128)S(1)} all-gather(f32[1,48,32]{2,0,1:T(1,128)S(1)} %copy.15), channel_id=2, replica_groups=mesh['group'=32,'blk'=4] {'group'}, dimensions={1}, use_global_device_ids=true | all-gather | bytes 202752 | tf_op jit(solution)/shard_map/all_gather | solution.py:29
  120.6 0.8 convolution_subtract_fusion.2
  121.4 3.2 %fusion.1 = f32[48,1536]{1,0:T(8,128)S(1)} fusion(bf16[1,1536,1536]{2,1,0:T(8,128)(2,1)} %all-gather.11.cloned.1.call-done, bf16[2,48,1536]{2,1,0:T(8,128)(2,1)S(1)} %convolution_convert_fusion), kind=kOutput, calls=%fused_computation.3 | convolution fusion | flops 226492416 | bytes 5160960 | tf_op jit(solution)/shard_map/dot_general | solution.py:14
  124.7 120.8 %while.12 = (s32[]{:T(128)}, f32[48,32]{0,1:T(8,128)S(1)}, f32[1536,32]{0,1:T(8,128)}, pred[]{:T(512)}, f32[48,32]{0,1:T(8,128)S(1)}, /*index=5*/f32[48,1536]{1,0:T(8,128)S(1)}, f32[48,32]{0,1:T(8,128)S(1)}, s32[]{:T(128)}) while((s32[]{:T(128)}, f32[48,32]{0,1:T(8,128)S(1)}, f32[1536,32]{0,1:T(8,128)}, pred[]{:T(512)}, ...), condition=%wide.region_1.2_spmd, body=%wide.region_0.1_spmd.sunk | while | flops 28314624 | bytes 2322586 | solution.py:67
  124.7 1.3 collective-permute-start
  126.0 4.3 %collective-permute-done = f32[48,32]{0,1:T(8,128)S(1)} collective-permute-done((f32[48,32]{0,1:T(8,128)S(1)}, f32[48,32]{0,1:T(8,128)S(1)}, u32[]{:S(2)}, u32[]{:S(2)}) %collective-permute-start) | collective-permute-done | bytes 6176 | tf_op jit(solution)/shard_map/while/body/eval_jaxpr/ppermute | solution.py:10
  130.3 24.0 %all-gather.5 = f32[32,48,32]{1,2,0:T(8,128)S(1)} all-gather(f32[1,48,32]{1,2,0:T(8,128)S(1)} %select_bitcast_fusion.2), channel_id=1, replica_groups=mesh['group'=32,'blk'=4] {'group'}, dimensions={0}, use_global_device_ids=true | all-gather | bytes 202752 | tf_op jit(solution)/shard_map/while/body/eval_jaxpr/all_gather | solution.py:62
  154.4 0.3 copy.20
  154.9 0.4 fusion.22
  155.6 1.3 collective-permute-start
  156.9 4.3 %collective-permute-done = f32[48,32]{0,1:T(8,128)S(1)} collective-permute-done((f32[48,32]{0,1:T(8,128)S(1)}, f32[48,32]{0,1:T(8,128)S(1)}, u32[]{:S(2)}, u32[]{:S(2)}) %collective-permute-start) | collective-permute-done | bytes 6176 | tf_op jit(solution)/shard_map/while/body/eval_jaxpr/ppermute | solution.py:10
  161.2 22.6 %all-gather.5 = f32[32,48,32]{1,2,0:T(8,128)S(1)} all-gather(f32[1,48,32]{1,2,0:T(8,128)S(1)} %select_bitcast_fusion.2), channel_id=1, replica_groups=mesh['group'=32,'blk'=4] {'group'}, dimensions={0}, use_global_device_ids=true | all-gather | bytes 202752 | tf_op jit(solution)/shard_map/while/body/eval_jaxpr/all_gather | solution.py:62
  183.9 0.3 copy.20
  184.4 0.4 fusion.22
  185.1 1.3 collective-permute-start
  186.4 4.3 %collective-permute-done = f32[48,32]{0,1:T(8,128)S(1)} collective-permute-done((f32[48,32]{0,1:T(8,128)S(1)}, f32[48,32]{0,1:T(8,128)S(1)}, u32[]{:S(2)}, u32[]{:S(2)}) %collective-permute-start) | collective-permute-done | bytes 6176 | tf_op jit(solution)/shard_map/while/body/eval_jaxpr/ppermute | solution.py:10
  190.8 24.0 %all-gather.5 = f32[32,48,32]{1,2,0:T(8,128)S(1)} all-gather(f32[1,48,32]{1,2,0:T(8,128)S(1)} %select_bitcast_fusion.2), channel_id=1, replica_groups=mesh['group'=32,'blk'=4] {'group'}, dimensions={0}, use_global_device_ids=true | all-gather | bytes 202752 | tf_op jit(solution)/shard_map/while/body/eval_jaxpr/all_gather | solution.py:62
  214.8 0.3 copy.20
  215.3 0.4 fusion.22
  216.0 1.3 collective-permute-start
  217.3 4.3 %collective-permute-done = f32[48,32]{0,1:T(8,128)S(1)} collective-permute-done((f32[48,32]{0,1:T(8,128)S(1)}, f32[48,32]{0,1:T(8,128)S(1)}, u32[]{:S(2)}, u32[]{:S(2)}) %collective-permute-start) | collective-permute-done | bytes 6176 | tf_op jit(solution)/shard_map/while/body/eval_jaxpr/ppermute | solution.py:10
  221.7 22.6 %all-gather.5 = f32[32,48,32]{1,2,0:T(8,128)S(1)} all-gather(f32[1,48,32]{1,2,0:T(8,128)S(1)} %select_bitcast_fusion.2), channel_id=1, replica_groups=mesh['group'=32,'blk'=4] {'group'}, dimensions={0}, use_global_device_ids=true | all-gather | bytes 202752 | tf_op jit(solution)/shard_map/while/body/eval_jaxpr/all_gather | solution.py:62
  244.9 0.4 fusion.22
  245.5 1.2 fusion.4
  246.7 24.0 %all-gather.3 = f32[32,48,32]{1,2,0:T(8,128)S(1)} all-gather(f32[1,48,32]{1,2,0:T(8,128)S(1)} %fusion.4), channel_id=1, replica_groups=mesh['group'=32,'blk'=4] {'group'}, dimensions={0}, use_global_device_ids=true | all-gather | bytes 202752 | tf_op jit(solution)/shard_map/all_gather | solution.py:29
  271.6 0.6 pad_maximum_fusion
  (35 shorter events, 3.7 us)
Async XLA Ops:
  6.5 59.7 %copy-start = (bf16[2,48,1536]{2,1,0:T(8,128)(2,1)S(1)}, bf16[2,48,1536]{2,1,0:T(8,128)(2,1)}, u32[]{:S(2)}) copy-start(bf16[2,48,1536]{2,1,0:T(8,128)(2,1)} %param.6) | copy-start | bytes 884740
  6.5 65.8 %copy-start.3 = (bf16[2,48,32]{1,2,0:T(8,128)(2,1)S(1)}, bf16[2,48,32]{1,2,0:T(8,128)(2,1)}, u32[]{:S(2)}) copy-start(bf16[2,48,32]{1,2,0:T(8,128)(2,1)} %param.8) | copy-start | bytes 18436
  6.5 59.7 %all-gather.9.cloned.1.call-start = ((), (), s32[]{:S(2)}) async-start(), calls=%async_computation | async-start | bytes 9732096 | tf_op jit(solution)/shard_map/all_gather | solution.py:38
  7.3 117.4 %copy-start.2 = (f32[48,32]{0,1:T(8,128)S(1)}, f32[48,32]{0,1:T(8,128)}, u32[]{:S(2)}) copy-start(f32[48,32]{0,1:T(8,128)} %param.9) | copy-start | bytes 18436
  7.3 114.2 %all-gather.11.cloned.1.call-start = ((), (), s32[]{:S(2)}) async-start(), calls=%async_computation.1 | async-start | bytes 4866048 | tf_op jit(solution)/shard_map/all_gather | solution.py:50
  124.7 5.6 %collective-permute-start = (f32[48,32]{0,1:T(8,128)S(1)}, f32[48,32]{0,1:T(8,128)S(1)}, u32[]{:S(2)}, u32[]{:S(2)}) collective-permute-start(f32[48,32]{0,1:T(8,128)S(1)} %get-tuple-element.106), channel_id=1, source_target_pairs={{0,1},{1,2},{2,3},{4,5},{5,6},{6,7},{8,9},{9,10},{10,11},{12,13},{... | collective-permute-start | bytes 18440 | tf_op jit(solution)/shard_map/while/body/eval_jaxpr/ppermute | solution.py:10
  154.9 0.7 copy-start.1
  155.6 5.6 %collective-permute-start = (f32[48,32]{0,1:T(8,128)S(1)}, f32[48,32]{0,1:T(8,128)S(1)}, u32[]{:S(2)}, u32[]{:S(2)}) collective-permute-start(f32[48,32]{0,1:T(8,128)S(1)} %get-tuple-element.106), channel_id=1, source_target_pairs={{0,1},{1,2},{2,3},{4,5},{5,6},{6,7},{8,9},{9,10},{10,11},{12,13},{... | collective-permute-start | bytes 18440 | tf_op jit(solution)/shard_map/while/body/eval_jaxpr/ppermute | solution.py:10
  184.4 0.7 copy-start.1
  185.1 5.6 %collective-permute-start = (f32[48,32]{0,1:T(8,128)S(1)}, f32[48,32]{0,1:T(8,128)S(1)}, u32[]{:S(2)}, u32[]{:S(2)}) collective-permute-start(f32[48,32]{0,1:T(8,128)S(1)} %get-tuple-element.106), channel_id=1, source_target_pairs={{0,1},{1,2},{2,3},{4,5},{5,6},{6,7},{8,9},{9,10},{10,11},{12,13},{... | collective-permute-start | bytes 18440 | tf_op jit(solution)/shard_map/while/body/eval_jaxpr/ppermute | solution.py:10
  215.3 0.7 copy-start.1
  216.0 5.6 %collective-permute-start = (f32[48,32]{0,1:T(8,128)S(1)}, f32[48,32]{0,1:T(8,128)S(1)}, u32[]{:S(2)}, u32[]{:S(2)}) collective-permute-start(f32[48,32]{0,1:T(8,128)S(1)} %get-tuple-element.106), channel_id=1, source_target_pairs={{0,1},{1,2},{2,3},{4,5},{5,6},{6,7},{8,9},{9,10},{10,11},{12,13},{... | collective-permute-start | bytes 18440 | tf_op jit(solution)/shard_map/while/body/eval_jaxpr/ppermute | solution.py:10
  244.8 0.7 copy-start.1
Sparse Core Ops, SparseCore 0:
  9.7 56.5 all-gather.8
  72.5 47.0 all-gather.10
where the time goes:
time: 281 us; the launch traced here: 279 us
  blocking collectives  165 us (59%)
  waiting for transfers between devices  77 us (27%)
  between operations  13.5 us (5%)
  matrix products  12.6 us (4%)
  starting transfers between devices  5.17 us (2%)
  local copies, waits for them, and re-layouts  4.95 us (2%)
    all_gather x4, blocking collectives, hop(): entry = lax.all_gather(incoming, 'group', axis=0, tiled=True)  93.3 us
    all_gather x1, waiting for transfers between devices, local(): lower_piece = lax.all_gather(lower, 'group', axis=1, tiled=True)  59 us
    all_gather x2, blocking collectives, split_chain(): gathered = lax.all_gather(previous, 'group', axis=0, tiled=True)  46.9 us
    all_gather x1, blocking collectives, local(): forcing_piece = lax.all_gather(forcing, 'group', axis=1, tiled=True)  24.8 us
    ppermute x4, waiting for transfers between devices, passed_along(): lax.ppermute(value, axis, [(source, source + steps) for source in range(i...  17.3 us
    dot_general x8, matrix products, apply_block(): jnp.dot(matrix, vector, preferred_element_type=jnp.float32, precision=lax...  6.9 us
  transfers between devices with their start and end apart: 6, of which 5 were waited for; matrix products, arithmetic and copies ran while one was open for 0% of the time, Pallas kernels for 0%

commit v1 on v0

v1 whole, which is shorter than its diff:
```python
import jax
import jax.numpy as jnp
from jax import lax
from jax.sharding import PartitionSpec as P

Y, X, CORES, Z = 4, 4, 2, 4
AXES = ("group", "blk")
HIGHEST = lax.Precision.HIGHEST


def send(value, target):
    pairs = []
    for y in range(Y):
        for x in range(X):
            for c in range(CORES):
                for z in range(Z):
                    to = target(y, x, c, z)
                    if to is not None:
                        ty, tx, tc, tz = to
                        pairs.append((
                            ((y * X + x) * CORES + c) * Z + z,
                            ((ty * X + tx) * CORES + tc) * Z + tz,
                        ))
    return lax.ppermute(value, AXES, pairs)


def to_peer(value):
    return send(value, lambda y, x, c, z: (y, x, 1 - c, z))


def along_x(d):
    return lambda y, x, c, z: (y, (x + d) % X, c, z)


def along_y(d):
    return lambda y, x, c, z: ((y + d) % Y, x, c, z)


def in_order(parts, me, axis):
    n = len(parts)
    ordered = []
    for j in range(n):
        pick = parts[0]
        for d in range(1, n):
            pick = jnp.where(lax.rem(me - j + n, n) == d, parts[d], pick)
        ordered.append(pick)
    return jnp.concatenate(ordered, axis=axis)


def times_t(vector_t, matrix):
    return lax.dot_general(
        vector_t, matrix.astype(jnp.float32), (((1,), (1,)), ((), ())),
        preferred_element_type=jnp.float32, precision=HIGHEST,
    )


def local(inverses, lower, forcing, inflow):
    group = lax.axis_index("group")
    z = lax.axis_index("blk")
    y, x, c = group // (X * CORES), (group // CORES) % X, group % CORES
    rows = inverses.shape[1]
    chip = rows * CORES
    block = chip * X

    def pick(array, k):
        return lax.dynamic_index_in_dim(array, k, 0, keepdims=False)

    def both(own, axis):
        def join(mine, theirs):
            return jnp.where(
                c == 0,
                jnp.concatenate([mine, theirs], axis=axis),
                jnp.concatenate([theirs, mine], axis=axis),
            )
        return join

    def station(array, axis):
        theirs = to_peer(pick(array, 1 - c))
        return both(None, axis)(pick(array, c), theirs)

    low = station(lower, 0)
    inv = station(inverses, 0)
    forcing_t = jnp.swapaxes(forcing, 1, 2).astype(jnp.float32)
    inflow_t = inflow.T
    small = jnp.stack([
        jnp.concatenate([forcing_t[0], inflow_t], axis=0),
        jnp.concatenate([forcing_t[1], inflow_t], axis=0),
    ])
    small = station(small, 1)

    def columns(xx):
        return lax.dynamic_slice_in_dim(low, lax.rem(xx, X) * block, block, 1)

    low_parts = [columns(x)] + [send(columns(x + d), along_x(d)) for d in range(1, X)]
    small_parts = [small] + [send(small, along_x(d)) for d in range(1, X)]
    inv_parts = [inv] + [send(inv, along_x(d)) for d in range(1, X)]
    low_block = in_order(low_parts, x, 0)
    small_block = in_order(small_parts, x, 1)
    low_panel = in_order([low_block] + [send(low_block, along_y(d)) for d in range(1, Y)], y, 0)
    small_all = in_order([small_block] + [send(small_block, along_y(d)) for d in range(1, Y)], y, 1)
    inv_panel = in_order(inv_parts, x, 0)

    forcing_all = small_all[:32].astype(jnp.bfloat16)
    entry_x = lax.dynamic_slice_in_dim(small_all[32:], x * block, block, 1)
    coupling = jnp.dot(inv_panel, low_panel, preferred_element_type=jnp.float32).astype(jnp.bfloat16)
    local_t = lax.dot_general(
        forcing_all, inv_panel, (((1,), (1,)), ((), ())), preferred_element_type=jnp.float32
    )
    local_t = jnp.where(x == 0, local_t, 0.0)
    entry_x = jnp.where(z == 0, entry_x, 0.0)
    share = local_t - jnp.where(c == 0, times_t(entry_x, coupling), 0.0)

    def across(d):
        def target(y, x, c, z):
            return ((y + d) % Y, x, c, z) if c == 0 else (y, (x + d) % X, c, z)
        return target

    turn = jnp.where(c == 0, y, x)
    panel = in_order([coupling] + [send(coupling, across(d)) for d in range(1, X)], turn, 0)
    shares = in_order([share] + [send(share, across(d)) for d in range(1, X)], turn, 1)
    panel_peer = to_peer(panel)
    shares_peer = to_peer(shares)
    share_peer = to_peer(share)
    first = jnp.where(c == 0, panel, panel_peer)
    second = jnp.where(c == 0, panel_peer, panel)
    first_shares = jnp.where(c == 0, shares, shares_peer)
    first_share = jnp.where(c == 0, share, share_peer)
    second_share = jnp.where(c == 0, share_peer, share)
    second = second.reshape(X, block, block).swapaxes(0, 1).reshape(block, X * block)

    product = jnp.dot(second, first, preferred_element_type=jnp.float32)
    base = second_share - times_t(first_shares, second)

    entry = jnp.zeros((32, block), jnp.float32)
    for _ in range(Z - 1):
        out = base + times_t(entry, product)
        arrived = [
            send(out, lambda y, x, c, z, d=d: ((x + d) % Y, y, c, z + 1) if z + 1 < Z else None)
            for d in range(X)
        ]
        entry = (arrived[0] + arrived[1]) + (arrived[2] + arrived[3])

    own_first = lax.dynamic_slice_in_dim(first, y * block, block, 0)
    finals = jnp.stack([
        first_share - times_t(entry, own_first),
        base + times_t(entry, product),
    ])
    finals = jnp.swapaxes(finals, 1, 2)

    def piece(xx):
        return lax.dynamic_slice_in_dim(finals, lax.rem(xx, X) * chip + c * rows, rows, 1)

    total = piece(x)
    for d in range(1, X):
        total = total + send(piece(x + d), along_x(d))
    return total


def solution(mesh):
    placed = (
        P("blk", "group", None),
        P("blk", "group", None),
        P("blk", "group", None),
        P("group", None),
    )
    return jax.shard_map(
        local, mesh=mesh, in_specs=placed, out_specs=P("blk", "group", None), check_vma=False
    )
```

time: 281 us -> 148 us (0.53)
  the two profiles are of different devices: /device:TPU:96 before, /device:TPU:40 now
where the time goes in v1:
time: 148 us; the launch traced here: 147 us
  starting transfers between devices  74.1 us (50%)
  waiting for transfers between devices  56.4 us (38%)
  matrix products  8.45 us (6%)
  other arithmetic  5.85 us (4%)
  local copies, waits for them, and re-layouts  1.91 us (1%)
    ppermute x42, starting transfers between devices, send(): return lax.ppermute(value, AXES, pairs)  74.1 us
    ppermute x42, waiting for transfers between devices, send(): return lax.ppermute(value, AXES, pairs)  56.4 us
    dot_general x7, matrix products, times_t(): lax.dot_general(vector_t, matrix.astype(jnp.float32), (((1,), (1,)), ((),...  5.77 us
  transfers between devices with their start and end apart: 42, of which 23 were waited for; matrix products, arithmetic and copies ran while one was open for 6% of the time, Pallas kernels for 0%

profile of v1, /device:TPU:40, one launch (start us, length us, event | category | flops | bytes accessed | tf_op | source)
XLA Modules:
  0.0 147.4 jit_solution(3462438850664754152)
XLA Ops:
  3.3 2.8 %collective-permute-start.1 = (f32[64,96]{1,0:T(8,128)S(1)}, f32[64,96]{1,0:T(8,128)S(1)}, u32[]{:S(2)}, u32[]{:S(2)}) collective-permute-start(f32[64,96]{1,0:T(8,128)S(1)} %maximum_select_fusion.2), channel_id=1, source_target_pairs={{0,24},{1,25},{2,26},{3,27},{4,28},{5,29},{6,30},{7,31},{8,0},{9,1... | collective-permute-start | bytes 73736 | tf_op jit(solution)/shard_map/ppermute | solution.py:24
  8.1 3.4 %collective-permute-done.2 = f32[64,96]{1,0:T(8,128)S(1)} collective-permute-done((f32[64,96]{1,0:T(8,128)S(1)}, f32[64,96]{1,0:T(8,128)S(1)}, u32[]{:S(2)}, u32[]{:S(2)}) %collective-permute-start.2) | collective-permute-done | bytes 24608 | tf_op jit(solution)/shard_map/ppermute | solution.py:24
  12.7 2.6 %collective-permute-start.5 = (f32[64,384]{1,0:T(8,128)S(1)}, f32[64,384]{1,0:T(8,128)S(1)}, u32[]{:S(2)}, u32[]{:S(2)}) collective-permute-start(f32[64,384]{1,0:T(8,128)S(1)} %pad_maximum_fusion.7), channel_id=1, source_target_pairs={{0,64},{1,65},{2,66},{3,67},{4,68},{5,69},{6,70},{7,71},{8,72},{9,... | collective-permute-start | bytes 294920 | tf_op jit(solution)/shard_map/ppermute | solution.py:24
  23.1 2.3 %collective-permute-start.10 = (bf16[96,1536]{1,0:T(8,128)(2,1)S(1)}, bf16[96,1536]{1,0:T(8,128)(2,1)S(1)}, u32[]{:S(2)}, u32[]{:S(2)}) collective-permute-start(bf16[96,1536]{1,0:T(8,128)(2,1)S(1)} %maximum_select_fusion), channel_id=1, source_target_pairs={{0,8},{1,9},{2,10},{3,11},{4,12},{5,13},{6,14},{7,15},{8,16},{9,17... | collective-permute-start | bytes 884744 | tf_op jit(solution)/shard_map/ppermute | solution.py:24
  25.5 4.5 %collective-permute-done.8 = bf16[96,1536]{1,0:T(8,128)(2,1)S(1)} collective-permute-done((bf16[96,1536]{1,0:T(8,128)(2,1)S(1)}, bf16[96,1536]{1,0:T(8,128)(2,1)S(1)}, u32[]{:S(2)}, u32[]{:S(2)}) %collective-permute-start.8) | collective-permute-done | bytes 294944 | tf_op jit(solution)/shard_map/ppermute | solution.py:24
  35.7 1.9 %collective-permute-start.17 = (bf16[384,384]{1,0:T(8,128)(2,1)S(1)}, bf16[384,384]{1,0:T(8,128)(2,1)S(1)}, u32[]{:S(2)}, u32[]{:S(2)}) collective-permute-start(bf16[384,384]{1,0:T(8,128)(2,1)S(1)} %pad_maximum_fusion.3), channel_id=1, source_target_pairs={{0,32},{1,33},{2,34},{3,35},{4,36},{5,37},{6,38},{7,39},{8,40},{9,... | collective-permute-start | bytes 884744 | tf_op jit(solution)/shard_map/ppermute | solution.py:24
  38.7 2.6 %collective-permute-done.16 = bf16[384,384]{1,0:T(8,128)(2,1)S(1)} collective-permute-done((bf16[384,384]{1,0:T(8,128)(2,1)S(1)}, bf16[384,384]{1,0:T(8,128)(2,1)S(1)}, u32[]{:S(2)}, u32[]{:S(2)}) %collective-permute-start.16) | collective-permute-done | bytes 294944 | tf_op jit(solution)/shard_map/ppermute | solution.py:24
  41.3 6.1 %collective-permute-done.17 = bf16[384,384]{1,0:T(8,128)(2,1)S(1)} collective-permute-done((bf16[384,384]{1,0:T(8,128)(2,1)S(1)}, bf16[384,384]{1,0:T(8,128)(2,1)S(1)}, u32[]{:S(2)}, u32[]{:S(2)}) %collective-permute-start.17) | collective-permute-done | bytes 294944 | tf_op jit(solution)/shard_map/ppermute | solution.py:24
  48.6 2.1 %collective-permute-start.23 = (bf16[384,384]{1,0:T(8,128)(2,1)S(1)}, bf16[384,384]{1,0:T(8,128)(2,1)S(1)}, u32[]{:S(2)}, u32[]{:S(2)}) collective-permute-start(bf16[384,384]{1,0:T(8,128)(2,1)S(1)} %convolution_convert_fusion), channel_id=1, source_target_pairs={{0,96},{1,97},{2,98},{3,99},{4,28},{5,29},{6,30},{7,31},{8,104},{9... | collective-permute-start | bytes 884744 | tf_op jit(solution)/shard_map/ppermute | solution.py:24
  53.1 2.3 %collective-permute-done.23 = bf16[384,384]{1,0:T(8,128)(2,1)S(1)} collective-permute-done((bf16[384,384]{1,0:T(8,128)(2,1)S(1)}, bf16[384,384]{1,0:T(8,128)(2,1)S(1)}, u32[]{:S(2)}, u32[]{:S(2)}) %collective-permute-start.23) | collective-permute-done | bytes 294944 | tf_op jit(solution)/shard_map/ppermute | solution.py:24
  55.4 4.5 %collective-permute-done.24 = bf16[384,384]{1,0:T(8,128)(2,1)S(1)} collective-permute-done((bf16[384,384]{1,0:T(8,128)(2,1)S(1)}, bf16[384,384]{1,0:T(8,128)(2,1)S(1)}, u32[]{:S(2)}, u32[]{:S(2)}) %collective-permute-start.24) | collective-permute-done | bytes 294944 | tf_op jit(solution)/shard_map/ppermute | solution.py:24
  62.7 2.2 %collective-permute-start.19 = (f32[32,384]{1,0:T(8,128)}, f32[32,384]{1,0:T(8,128)S(1)}, u32[]{:S(2)}, u32[]{:S(2)}) collective-permute-start(f32[32,384]{1,0:T(8,128)} %fusion.8), channel_id=1, source_target_pairs={{0,96},{1,97},{2,98},{3,99},{4,28},{5,29},{6,30},{7,31},{8,104},{9... | collective-permute-start | bytes 147464 | tf_op jit(solution)/shard_map/ppermute | solution.py:24
  67.0 3.7 %collective-permute-done.20 = f32[32,384]{1,0:T(8,128)S(1)} collective-permute-done((f32[32,384]{1,0:T(8,128)}, f32[32,384]{1,0:T(8,128)S(1)}, u32[]{:S(2)}, u32[]{:S(2)}) %collective-permute-start.20) | collective-permute-done | bytes 49184 | tf_op jit(solution)/shard_map/ppermute | solution.py:24
  77.2 3.7 %collective-permute-start.29 = (f32[32,384]{1,0:T(8,128)S(1)}, f32[32,384]{1,0:T(8,128)S(1)}, u32[]{:S(2)}, u32[]{:S(2)}) collective-permute-start(f32[32,384]{1,0:T(8,128)S(1)} %convolution_add_fusion.3), channel_id=1, source_target_pairs={{0,65},{1,66},{2,67},{4,69},{5,70},{6,71},{8,97},{9,98},{10,99},{1... | collective-permute-start | bytes 147464 | tf_op jit(solution)/shard_map/ppermute | solution.py:24
  80.9 6.0 %collective-permute-start.30 = (f32[32,384]{1,0:T(8,128)S(1)}, f32[32,384]{1,0:T(8,128)S(1)}, u32[]{:S(2)}, u32[]{:S(2)}) collective-permute-start(f32[32,384]{1,0:T(8,128)S(1)} %convolution_add_fusion.3), channel_id=1, source_target_pairs={{0,97},{1,98},{2,99},{4,101},{5,102},{6,103},{8,1},{9,2},{10,3},{1... | collective-permute-start | bytes 147464 | tf_op jit(solution)/shard_map/ppermute | solution.py:24
  86.9 2.0 %collective-permute-start.27 = (f32[32,384]{1,0:T(8,128)S(1)}, f32[32,384]{1,0:T(8,128)S(1)}, u32[]{:S(2)}, u32[]{:S(2)}) collective-permute-start(f32[32,384]{1,0:T(8,128)S(1)} %convolution_add_fusion.3), channel_id=1, source_target_pairs={{0,1},{1,2},{2,3},{4,5},{5,6},{6,7},{8,33},{9,34},{10,35},{12,37},... | collective-permute-start | bytes 147464 | tf_op jit(solution)/shard_map/ppermute | solution.py:24
  88.9 1.9 %collective-permute-start.28 = (f32[32,384]{1,0:T(8,128)S(1)}, f32[32,384]{1,0:T(8,128)S(1)}, u32[]{:S(2)}, u32[]{:S(2)}) collective-permute-start(f32[32,384]{1,0:T(8,128)S(1)} %convolution_add_fusion.3), channel_id=1, source_target_pairs={{0,33},{1,34},{2,35},{4,37},{5,38},{6,39},{8,65},{9,66},{10,67},{1... | collective-permute-start | bytes 147464 | tf_op jit(solution)/shard_map/ppermute | solution.py:24
  90.8 3.9 %collective-permute-done.27 = f32[32,384]{1,0:T(8,128)S(1)} collective-permute-done((f32[32,384]{1,0:T(8,128)S(1)}, f32[32,384]{1,0:T(8,128)S(1)}, u32[]{:S(2)}, u32[]{:S(2)}) %collective-permute-start.27) | collective-permute-done | bytes 49184 | tf_op jit(solution)/shard_map/ppermute | solution.py:24
  96.5 1.9 %collective-permute-start.33 = (f32[32,384]{1,0:T(8,128)S(1)}, f32[32,384]{1,0:T(8,128)S(1)}, u32[]{:S(2)}, u32[]{:S(2)}) collective-permute-start(f32[32,384]{1,0:T(8,128)S(1)} %convolution_add_fusion.2), channel_id=1, source_target_pairs={{0,65},{1,66},{2,67},{4,69},{5,70},{6,71},{8,97},{9,98},{10,99},{1... | collective-permute-start | bytes 147464 | tf_op jit(solution)/shard_map/ppermute | solution.py:24
  98.4 7.8 %collective-permute-start.34 = (f32[32,384]{1,0:T(8,128)S(1)}, f32[32,384]{1,0:T(8,128)S(1)}, u32[]{:S(2)}, u32[]{:S(2)}) collective-permute-start(f32[32,384]{1,0:T(8,128)S(1)} %convolution_add_fusion.2), channel_id=1, source_target_pairs={{0,97},{1,98},{2,99},{4,101},{5,102},{6,103},{8,1},{9,2},{10,3},{1... | collective-permute-start | bytes 147464 | tf_op jit(solution)/shard_map/ppermute | solution.py:24
  106.2 1.9 %collective-permute-start.31 = (f32[32,384]{1,0:T(8,128)S(1)}, f32[32,384]{1,0:T(8,128)S(1)}, u32[]{:S(2)}, u32[]{:S(2)}) collective-permute-start(f32[32,384]{1,0:T(8,128)S(1)} %convolution_add_fusion.2), channel_id=1, source_target_pairs={{0,1},{1,2},{2,3},{4,5},{5,6},{6,7},{8,33},{9,34},{10,35},{12,37},... | collective-permute-start | bytes 147464 | tf_op jit(solution)/shard_map/ppermute | solution.py:24
  108.2 1.9 %collective-permute-start.32 = (f32[32,384]{1,0:T(8,128)S(1)}, f32[32,384]{1,0:T(8,128)S(1)}, u32[]{:S(2)}, u32[]{:S(2)}) collective-permute-start(f32[32,384]{1,0:T(8,128)S(1)} %convolution_add_fusion.2), channel_id=1, source_target_pairs={{0,33},{1,34},{2,35},{4,37},{5,38},{6,39},{8,65},{9,66},{10,67},{1... | collective-permute-start | bytes 147464 | tf_op jit(solution)/shard_map/ppermute | solution.py:24
  110.1 4.2 %collective-permute-done.31 = f32[32,384]{1,0:T(8,128)S(1)} collective-permute-done((f32[32,384]{1,0:T(8,128)S(1)}, f32[32,384]{1,0:T(8,128)S(1)}, u32[]{:S(2)}, u32[]{:S(2)}) %collective-permute-start.31) | collective-permute-done | bytes 49184 | tf_op jit(solution)/shard_map/ppermute | solution.py:24
  114.3 2.1 %collective-permute-done.32 = f32[32,384]{1,0:T(8,128)S(1)} collective-permute-done((f32[32,384]{1,0:T(8,128)S(1)}, f32[32,384]{1,0:T(8,128)S(1)}, u32[]{:S(2)}, u32[]{:S(2)}) %collective-permute-start.32) | collective-permute-done | bytes 49184 | tf_op jit(solution)/shard_map/ppermute | solution.py:24
  117.1 1.9 %collective-permute-start.37 = (f32[32,384]{1,0:T(8,128)S(1)}, f32[32,384]{1,0:T(8,128)S(1)}, u32[]{:S(2)}, u32[]{:S(2)}) collective-permute-start(f32[32,384]{1,0:T(8,128)S(1)} %convolution_add_fusion.1), channel_id=1, source_target_pairs={{0,65},{1,66},{2,67},{4,69},{5,70},{6,71},{8,97},{9,98},{10,99},{1... | collective-permute-start | bytes 147464 | tf_op jit(solution)/shard_map/ppermute | solution.py:24
  119.1 3.5 %collective-permute-start.38 = (f32[32,384]{1,0:T(8,128)S(1)}, f32[32,384]{1,0:T(8,128)S(1)}, u32[]{:S(2)}, u32[]{:S(2)}) collective-permute-start(f32[32,384]{1,0:T(8,128)S(1)} %convolution_add_fusion.1), channel_id=1, source_target_pairs={{0,97},{1,98},{2,99},{4,101},{5,102},{6,103},{8,1},{9,2},{10,3},{1... | collective-permute-start | bytes 147464 | tf_op jit(solution)/shard_map/ppermute | solution.py:24
  122.5 1.9 %collective-permute-start.35 = (f32[32,384]{1,0:T(8,128)S(1)}, f32[32,384]{1,0:T(8,128)S(1)}, u32[]{:S(2)}, u32[]{:S(2)}) collective-permute-start(f32[32,384]{1,0:T(8,128)S(1)} %convolution_add_fusion.1), channel_id=1, source_target_pairs={{0,1},{1,2},{2,3},{4,5},{5,6},{6,7},{8,33},{9,34},{10,35},{12,37},... | collective-permute-start | bytes 147464 | tf_op jit(solution)/shard_map/ppermute | solution.py:24
  124.5 1.9 %collective-permute-start.36 = (f32[32,384]{1,0:T(8,128)S(1)}, f32[32,384]{1,0:T(8,128)S(1)}, u32[]{:S(2)}, u32[]{:S(2)}) collective-permute-start(f32[32,384]{1,0:T(8,128)S(1)} %convolution_add_fusion.1), channel_id=1, source_target_pairs={{0,33},{1,34},{2,35},{4,37},{5,38},{6,39},{8,65},{9,66},{10,67},{1... | collective-permute-start | bytes 147464 | tf_op jit(solution)/shard_map/ppermute | solution.py:24
  126.4 2.2 %collective-permute-done.38 = f32[32,384]{1,0:T(8,128)S(1)} collective-permute-done((f32[32,384]{1,0:T(8,128)S(1)}, f32[32,384]{1,0:T(8,128)S(1)}, u32[]{:S(2)}, u32[]{:S(2)}) %collective-permute-start.38) | collective-permute-done | bytes 49184 | tf_op jit(solution)/shard_map/ppermute | solution.py:24
  128.6 2.2 %collective-permute-done.35 = f32[32,384]{1,0:T(8,128)S(1)} collective-permute-done((f32[32,384]{1,0:T(8,128)S(1)}, f32[32,384]{1,0:T(8,128)S(1)}, u32[]{:S(2)}, u32[]{:S(2)}) %collective-permute-start.35) | collective-permute-done | bytes 49184 | tf_op jit(solution)/shard_map/ppermute | solution.py:24
  134.7 6.5 %collective-permute-start.41 = (f32[2,48,32]{1,2,0:T(8,128)S(1)}, f32[2,48,32]{1,2,0:T(8,128)S(1)}, u32[]{:S(2)}, u32[]{:S(2)}) collective-permute-start(f32[2,48,32]{1,2,0:T(8,128)S(1)} %get-tuple-element.44), channel_id=1, source_target_pairs={{0,24},{1,25},{2,26},{3,27},{4,28},{5,29},{6,30},{7,31},{8,0},{9,1... | collective-permute-start | bytes 36872 | tf_op jit(solution)/shard_map/ppermute | solution.py:24
  142.8 3.9 %collective-permute-done.40 = f32[2,48,32]{1,2,0:T(8,128)S(1)} collective-permute-done((f32[2,48,32]{1,2,0:T(8,128)S(1)}, f32[2,48,32]{1,2,0:T(8,128)S(1)}, u32[]{:S(2)}, u32[]{:S(2)}) %collective-permute-start.40) | collective-permute-done | bytes 12320 | tf_op jit(solution)/shard_map/ppermute | solution.py:24
  (109 shorter events, 44.2 us)
Async XLA Ops:
  2.6 12.7 %collective-permute-start.11 = (bf16[48,1536]{1,0:T(8,128)(2,1)S(1)}, bf16[48,1536]{1,0:T(8,128)(2,1)S(1)}, u32[]{:S(2)}, u32[]{:S(2)}) collective-permute-start(bf16[48,1536]{1,0:T(8,128)(2,1)S(1)} %get-tuple-element.33), channel_id=1, source_target_pairs={{0,4},{1,5},{2,6},{3,7},{4,0},{5,1},{6,2},{7,3},{8,12},{9,13},{10,... | collective-permute-start | bytes 442376 | tf_op jit(solution)/shard_map/ppermute | solution.py:24
  7.8 9.4 %collective-permute-start.7 = (bf16[48,1536]{1,0:T(8,128)(2,1)S(1)}, bf16[48,1536]{1,0:T(8,128)(2,1)S(1)}, u32[]{:S(2)}, u32[]{:S(2)}) collective-permute-start(bf16[48,1536]{1,0:T(8,128)(2,1)S(1)} %get-tuple-element.28), channel_id=1, source_target_pairs={{0,4},{1,5},{2,6},{3,7},{4,0},{5,1},{6,2},{7,3},{8,12},{9,13},{10,... | collective-permute-start | bytes 442376 | tf_op jit(solution)/shard_map/ppermute | solution.py:24
  12.2 39.9 %collective-permute-start.4 = (f32[64,384]{1,0:T(8,128)S(1)}, f32[64,384]{1,0:T(8,128)S(1)}, u32[]{:S(2)}, u32[]{:S(2)}) collective-permute-start(f32[64,384]{1,0:T(8,128)S(1)} %pad_maximum_fusion.7), channel_id=1, source_target_pairs={{0,96},{1,97},{2,98},{3,99},{4,100},{5,101},{6,102},{7,103},{8,104... | collective-permute-start | bytes 294920 | tf_op jit(solution)/shard_map/ppermute | solution.py:24
  12.7 40.3 %collective-permute-start.5 = (f32[64,384]{1,0:T(8,128)S(1)}, f32[64,384]{1,0:T(8,128)S(1)}, u32[]{:S(2)}, u32[]{:S(2)}) collective-permute-start(f32[64,384]{1,0:T(8,128)S(1)} %pad_maximum_fusion.7), channel_id=1, source_target_pairs={{0,64},{1,65},{2,66},{3,67},{4,68},{5,69},{6,70},{7,71},{8,72},{9,... | collective-permute-start | bytes 294920 | tf_op jit(solution)/shard_map/ppermute | solution.py:24
  15.9 5.9 %collective-permute-start.13 = (bf16[96,384]{1,0:T(8,128)(2,1)S(1)}, bf16[96,384]{1,0:T(8,128)(2,1)S(1)}, u32[]{:S(2)}, u32[]{:S(2)}) collective-permute-start(bf16[96,384]{1,0:T(8,128)(2,1)S(1)} %get-tuple-element.30), channel_id=1, source_target_pairs={{0,16},{1,17},{2,18},{3,19},{4,20},{5,21},{6,22},{7,23},{8,24},{9,... | collective-permute-start | bytes 221192 | tf_op jit(solution)/shard_map/ppermute | solution.py:24
  17.2 5.9 %collective-permute-start.14 = (bf16[96,384]{1,0:T(8,128)(2,1)S(1)}, bf16[96,384]{1,0:T(8,128)(2,1)S(1)}, u32[]{:S(2)}, u32[]{:S(2)}) collective-permute-start(bf16[96,384]{1,0:T(8,128)(2,1)S(1)} %get-tuple-element.29), channel_id=1, source_target_pairs={{0,8},{1,9},{2,10},{3,11},{4,12},{5,13},{6,14},{7,15},{8,16},{9,17... | collective-permute-start | bytes 221192 | tf_op jit(solution)/shard_map/ppermute | solution.py:24
  20.3 9.8 %collective-permute-start.8 = (bf16[96,1536]{1,0:T(8,128)(2,1)S(1)}, bf16[96,1536]{1,0:T(8,128)(2,1)S(1)}, u32[]{:S(2)}, u32[]{:S(2)}) collective-permute-start(bf16[96,1536]{1,0:T(8,128)(2,1)S(1)} %maximum_select_fusion), channel_id=1, source_target_pairs={{0,24},{1,25},{2,26},{3,27},{4,28},{5,29},{6,30},{7,31},{8,0},{9,1... | collective-permute-start | bytes 884744 | tf_op jit(solution)/shard_map/ppermute | solution.py:24
  21.7 11.3 %collective-permute-start.9 = (bf16[96,1536]{1,0:T(8,128)(2,1)S(1)}, bf16[96,1536]{1,0:T(8,128)(2,1)S(1)}, u32[]{:S(2)}, u32[]{:S(2)}) collective-permute-start(bf16[96,1536]{1,0:T(8,128)(2,1)S(1)} %maximum_select_fusion), channel_id=1, source_target_pairs={{0,16},{1,17},{2,18},{3,19},{4,20},{5,21},{6,22},{7,23},{8,24},{9,... | collective-permute-start | bytes 884744 | tf_op jit(solution)/shard_map/ppermute | solution.py:24
  23.1 12.6 %collective-permute-start.10 = (bf16[96,1536]{1,0:T(8,128)(2,1)S(1)}, bf16[96,1536]{1,0:T(8,128)(2,1)S(1)}, u32[]{:S(2)}, u32[]{:S(2)}) collective-permute-start(bf16[96,1536]{1,0:T(8,128)(2,1)S(1)} %maximum_select_fusion), channel_id=1, source_target_pairs={{0,8},{1,9},{2,10},{3,11},{4,12},{5,13},{6,14},{7,15},{8,16},{9,17... | collective-permute-start | bytes 884744 | tf_op jit(solution)/shard_map/ppermute | solution.py:24
  30.1 7.6 %collective-permute-start.15 = (bf16[384,384]{1,0:T(8,128)(2,1)S(1)}, bf16[384,384]{1,0:T(8,128)(2,1)S(1)}, u32[]{:S(2)}, u32[]{:S(2)}) collective-permute-start(bf16[384,384]{1,0:T(8,128)(2,1)S(1)} %pad_maximum_fusion.3), channel_id=1, source_target_pairs={{0,96},{1,97},{2,98},{3,99},{4,100},{5,101},{6,102},{7,103},{8,104... | collective-permute-start | bytes 884744 | tf_op jit(solution)/shard_map/ppermute | solution.py:24
  33.0 8.3 %collective-permute-start.16 = (bf16[384,384]{1,0:T(8,128)(2,1)S(1)}, bf16[384,384]{1,0:T(8,128)(2,1)S(1)}, u32[]{:S(2)}, u32[]{:S(2)}) collective-permute-start(bf16[384,384]{1,0:T(8,128)(2,1)S(1)} %pad_maximum_fusion.3), channel_id=1, source_target_pairs={{0,64},{1,65},{2,66},{3,67},{4,68},{5,69},{6,70},{7,71},{8,72},{9,... | collective-permute-start | bytes 884744 | tf_op jit(solution)/shard_map/ppermute | solution.py:24
  35.7 11.7 %collective-permute-start.17 = (bf16[384,384]{1,0:T(8,128)(2,1)S(1)}, bf16[384,384]{1,0:T(8,128)(2,1)S(1)}, u32[]{:S(2)}, u32[]{:S(2)}) collective-permute-start(bf16[384,384]{1,0:T(8,128)(2,1)S(1)} %pad_maximum_fusion.3), channel_id=1, source_target_pairs={{0,32},{1,33},{2,34},{3,35},{4,36},{5,37},{6,38},{7,39},{8,40},{9,... | collective-permute-start | bytes 884744 | tf_op jit(solution)/shard_map/ppermute | solution.py:24
  37.7 15.2 %collective-permute-start.6 = (f32[64,384]{1,0:T(8,128)S(1)}, f32[64,384]{1,0:T(8,128)S(1)}, u32[]{:S(2)}, u32[]{:S(2)}) collective-permute-start(f32[64,384]{1,0:T(8,128)S(1)} %pad_maximum_fusion.7), channel_id=1, source_target_pairs={{0,32},{1,33},{2,34},{3,35},{4,36},{5,37},{6,38},{7,39},{8,40},{9,... | collective-permute-start | bytes 294920 | tf_op jit(solution)/shard_map/ppermute | solution.py:24
  48.6 6.8 %collective-permute-start.23 = (bf16[384,384]{1,0:T(8,128)(2,1)S(1)}, bf16[384,384]{1,0:T(8,128)(2,1)S(1)}, u32[]{:S(2)}, u32[]{:S(2)}) collective-permute-start(bf16[384,384]{1,0:T(8,128)(2,1)S(1)} %convolution_convert_fusion), channel_id=1, source_target_pairs={{0,96},{1,97},{2,98},{3,99},{4,28},{5,29},{6,30},{7,31},{8,104},{9... | collective-permute-start | bytes 884744 | tf_op jit(solution)/shard_map/ppermute | solution.py:24
  50.7 9.2 %collective-permute-start.24 = (bf16[384,384]{1,0:T(8,128)(2,1)S(1)}, bf16[384,384]{1,0:T(8,128)(2,1)S(1)}, u32[]{:S(2)}, u32[]{:S(2)}) collective-permute-start(bf16[384,384]{1,0:T(8,128)(2,1)S(1)} %convolution_convert_fusion), channel_id=1, source_target_pairs={{0,64},{1,65},{2,66},{3,67},{4,20},{5,21},{6,22},{7,23},{8,72},{9,... | collective-permute-start | bytes 884744 | tf_op jit(solution)/shard_map/ppermute | solution.py:24
  52.1 8.6 %collective-permute-start.25 = (bf16[384,384]{1,0:T(8,128)(2,1)S(1)}, bf16[384,384]{1,0:T(8,128)(2,1)S(1)}, u32[]{:S(2)}, u32[]{:S(2)}) collective-permute-start(bf16[384,384]{1,0:T(8,128)(2,1)S(1)} %convolution_convert_fusion), channel_id=1, source_target_pairs={{0,32},{1,33},{2,34},{3,35},{4,12},{5,13},{6,14},{7,15},{8,40},{9,... | collective-permute-start | bytes 884744 | tf_op jit(solution)/shard_map/ppermute | solution.py:24
  61.0 11.9 %collective-permute-start.26 = (bf16[1536,384]{1,0:T(8,128)(2,1)S(1)}, bf16[1536,384]{1,0:T(8,128)(2,1)S(1)}, u32[]{:S(2)}, u32[]{:S(2)}) collective-permute-start(bf16[1536,384]{1,0:T(8,128)(2,1)S(1)} %pad_maximum_fusion.1), channel_id=1, source_target_pairs={{0,4},{1,5},{2,6},{3,7},{4,0},{5,1},{6,2},{7,3},{8,12},{9,13},{10,... | collective-permute-start | bytes 3538952 | tf_op jit(solution)/shard_map/ppermute | solution.py:24
  64.9 5.8 %collective-permute-start.20 = (f32[32,384]{1,0:T(8,128)}, f32[32,384]{1,0:T(8,128)S(1)}, u32[]{:S(2)}, u32[]{:S(2)}) collective-permute-start(f32[32,384]{1,0:T(8,128)} %fusion.8), channel_id=1, source_target_pairs={{0,64},{1,65},{2,66},{3,67},{4,20},{5,21},{6,22},{7,23},{8,72},{9,... | collective-permute-start | bytes 147464 | tf_op jit(solution)/shard_map/ppermute | solution.py:24
  67.0 8.1 %collective-permute-start.18 = (f32[32,384]{1,0:T(8,128)}, f32[32,384]{1,0:T(8,128)}, u32[]{:S(2)}, u32[]{:S(2)}) collective-permute-start(f32[32,384]{1,0:T(8,128)} %fusion.8), channel_id=1, source_target_pairs={{0,4},{1,5},{2,6},{3,7},{4,0},{5,1},{6,2},{7,3},{8,12},{9,13},{10,... | collective-permute-start | bytes 147464 | tf_op jit(solution)/shard_map/ppermute | solution.py:24
  77.2 13.6 %collective-permute-start.29 = (f32[32,384]{1,0:T(8,128)S(1)}, f32[32,384]{1,0:T(8,128)S(1)}, u32[]{:S(2)}, u32[]{:S(2)}) collective-permute-start(f32[32,384]{1,0:T(8,128)S(1)} %convolution_add_fusion.3), channel_id=1, source_target_pairs={{0,65},{1,66},{2,67},{4,69},{5,70},{6,71},{8,97},{9,98},{10,99},{1... | collective-permute-start | bytes 147464 | tf_op jit(solution)/shard_map/ppermute | solution.py:24
  80.9 9.9 %collective-permute-start.30 = (f32[32,384]{1,0:T(8,128)S(1)}, f32[32,384]{1,0:T(8,128)S(1)}, u32[]{:S(2)}, u32[]{:S(2)}) collective-permute-start(f32[32,384]{1,0:T(8,128)S(1)} %convolution_add_fusion.3), channel_id=1, source_target_pairs={{0,97},{1,98},{2,99},{4,101},{5,102},{6,103},{8,1},{9,2},{10,3},{1... | collective-permute-start | bytes 147464 | tf_op jit(solution)/shard_map/ppermute | solution.py:24
  86.9 7.8 %collective-permute-start.27 = (f32[32,384]{1,0:T(8,128)S(1)}, f32[32,384]{1,0:T(8,128)S(1)}, u32[]{:S(2)}, u32[]{:S(2)}) collective-permute-start(f32[32,384]{1,0:T(8,128)S(1)} %convolution_add_fusion.3), channel_id=1, source_target_pairs={{0,1},{1,2},{2,3},{4,5},{5,6},{6,7},{8,33},{9,34},{10,35},{12,37},... | collective-permute-start | bytes 147464 | tf_op jit(solution)/shard_map/ppermute | solution.py:24
  88.9 6.9 %collective-permute-start.28 = (f32[32,384]{1,0:T(8,128)S(1)}, f32[32,384]{1,0:T(8,128)S(1)}, u32[]{:S(2)}, u32[]{:S(2)}) collective-permute-start(f32[32,384]{1,0:T(8,128)S(1)} %convolution_add_fusion.3), channel_id=1, source_target_pairs={{0,33},{1,34},{2,35},{4,37},{5,38},{6,39},{8,65},{9,66},{10,67},{1... | collective-permute-start | bytes 147464 | tf_op jit(solution)/shard_map/ppermute | solution.py:24
  96.5 13.6 %collective-permute-start.33 = (f32[32,384]{1,0:T(8,128)S(1)}, f32[32,384]{1,0:T(8,128)S(1)}, u32[]{:S(2)}, u32[]{:S(2)}) collective-permute-start(f32[32,384]{1,0:T(8,128)S(1)} %convolution_add_fusion.2), channel_id=1, source_target_pairs={{0,65},{1,66},{2,67},{4,69},{5,70},{6,71},{8,97},{9,98},{10,99},{1... | collective-permute-start | bytes 147464 | tf_op jit(solution)/shard_map/ppermute | solution.py:24
  98.4 11.7 %collective-permute-start.34 = (f32[32,384]{1,0:T(8,128)S(1)}, f32[32,384]{1,0:T(8,128)S(1)}, u32[]{:S(2)}, u32[]{:S(2)}) collective-permute-start(f32[32,384]{1,0:T(8,128)S(1)} %convolution_add_fusion.2), channel_id=1, source_target_pairs={{0,97},{1,98},{2,99},{4,101},{5,102},{6,103},{8,1},{9,2},{10,3},{1... | collective-permute-start | bytes 147464 | tf_op jit(solution)/shard_map/ppermute | solution.py:24
  106.2 8.1 %collective-permute-start.31 = (f32[32,384]{1,0:T(8,128)S(1)}, f32[32,384]{1,0:T(8,128)S(1)}, u32[]{:S(2)}, u32[]{:S(2)}) collective-permute-start(f32[32,384]{1,0:T(8,128)S(1)} %convolution_add_fusion.2), channel_id=1, source_target_pairs={{0,1},{1,2},{2,3},{4,5},{5,6},{6,7},{8,33},{9,34},{10,35},{12,37},... | collective-permute-start | bytes 147464 | tf_op jit(solution)/shard_map/ppermute | solution.py:24
  108.2 8.3 %collective-permute-start.32 = (f32[32,384]{1,0:T(8,128)S(1)}, f32[32,384]{1,0:T(8,128)S(1)}, u32[]{:S(2)}, u32[]{:S(2)}) collective-permute-start(f32[32,384]{1,0:T(8,128)S(1)} %convolution_add_fusion.2), channel_id=1, source_target_pairs={{0,33},{1,34},{2,35},{4,37},{5,38},{6,39},{8,65},{9,66},{10,67},{1... | collective-permute-start | bytes 147464 | tf_op jit(solution)/shard_map/ppermute | solution.py:24
  117.1 9.3 %collective-permute-start.37 = (f32[32,384]{1,0:T(8,128)S(1)}, f32[32,384]{1,0:T(8,128)S(1)}, u32[]{:S(2)}, u32[]{:S(2)}) collective-permute-start(f32[32,384]{1,0:T(8,128)S(1)} %convolution_add_fusion.1), channel_id=1, source_target_pairs={{0,65},{1,66},{2,67},{4,69},{5,70},{6,71},{8,97},{9,98},{10,99},{1... | collective-permute-start | bytes 147464 | tf_op jit(solution)/shard_map/ppermute | solution.py:24
  119.1 9.6 %collective-permute-start.38 = (f32[32,384]{1,0:T(8,128)S(1)}, f32[32,384]{1,0:T(8,128)S(1)}, u32[]{:S(2)}, u32[]{:S(2)}) collective-permute-start(f32[32,384]{1,0:T(8,128)S(1)} %convolution_add_fusion.1), channel_id=1, source_target_pairs={{0,97},{1,98},{2,99},{4,101},{5,102},{6,103},{8,1},{9,2},{10,3},{1... | collective-permute-start | bytes 147464 | tf_op jit(solution)/shard_map/ppermute | solution.py:24
  122.5 8.3 %collective-permute-start.35 = (f32[32,384]{1,0:T(8,128)S(1)}, f32[32,384]{1,0:T(8,128)S(1)}, u32[]{:S(2)}, u32[]{:S(2)}) collective-permute-start(f32[32,384]{1,0:T(8,128)S(1)} %convolution_add_fusion.1), channel_id=1, source_target_pairs={{0,1},{1,2},{2,3},{4,5},{5,6},{6,7},{8,33},{9,34},{10,35},{12,37},... | collective-permute-start | bytes 147464 | tf_op jit(solution)/shard_map/ppermute | solution.py:24
  124.5 8.2 %collective-permute-start.36 = (f32[32,384]{1,0:T(8,128)S(1)}, f32[32,384]{1,0:T(8,128)S(1)}, u32[]{:S(2)}, u32[]{:S(2)}) collective-permute-start(f32[32,384]{1,0:T(8,128)S(1)} %convolution_add_fusion.1), channel_id=1, source_target_pairs={{0,33},{1,34},{2,35},{4,37},{5,38},{6,39},{8,65},{9,66},{10,67},{1... | collective-permute-start | bytes 147464 | tf_op jit(solution)/shard_map/ppermute | solution.py:24
  134.7 8.1 %collective-permute-start.41 = (f32[2,48,32]{1,2,0:T(8,128)S(1)}, f32[2,48,32]{1,2,0:T(8,128)S(1)}, u32[]{:S(2)}, u32[]{:S(2)}) collective-permute-start(f32[2,48,32]{1,2,0:T(8,128)S(1)} %get-tuple-element.44), channel_id=1, source_target_pairs={{0,24},{1,25},{2,26},{3,27},{4,28},{5,29},{6,30},{7,31},{8,0},{9,1... | collective-permute-start | bytes 36872 | tf_op jit(solution)/shard_map/ppermute | solution.py:24
  (19 other events, 61.6 us)

commit v2 on v0

v2 whole, which is shorter than its diff:
```python
import jax
import jax.numpy as jnp
from jax import lax
from jax.experimental import pallas as pl
from jax.experimental.pallas import tpu as pltpu
from jax.sharding import PartitionSpec as P

Y, X, CORES, Z = 4, 4, 2, 4
AXES = ("group", "blk")
ROWS = 48
CHIP = ROWS * CORES
BLOCK = CHIP * X
N = BLOCK * Y
R = 32
F32, BF16 = jnp.float32, jnp.bfloat16


def send(value, target):
    pairs = []
    for y in range(Y):
        for x in range(X):
            for c in range(CORES):
                for z in range(Z):
                    to = target(y, x, c, z)
                    if to is not None:
                        ty, tx, tc, tz = to
                        pairs.append((
                            ((y * X + x) * CORES + c) * Z + z,
                            ((ty % Y * X + tx % X) * CORES + tc) * Z + tz,
                        ))
    return lax.ppermute(value, AXES, pairs)


def to_peer(value):
    return send(value, lambda y, x, c, z: (y, x, 1 - c, z))


def along_x(d):
    return lambda y, x, c, z: (y, x + d, c, z)


def along_y(d):
    return lambda y, x, c, z: (y + d, x, c, z)


def across(d):
    return lambda y, x, c, z: (y + d, x, c, z) if c == 0 else (y, x + d, c, z)


def place():
    group = lax.axis_index("group")
    return group // (X * CORES), (group // CORES) % X, group % CORES, lax.axis_index("blk")


def call(kernel, out, *args, scratch=(), flops=0):
    moved = sum(a.size * a.dtype.itemsize for a in args)
    return pl.pallas_call(
        kernel,
        out_shape=out,
        in_specs=[pl.BlockSpec(memory_space=pltpu.VMEM)] * len(args),
        out_specs=jax.tree.map(lambda _: pl.BlockSpec(memory_space=pltpu.VMEM), out),
        scratch_shapes=list(scratch),
        cost_estimate=pl.CostEstimate(flops=flops, bytes_accessed=moved, transcendentals=0),
        compiler_params=pltpu.CompilerParams(vmem_limit_bytes=24 * 2**20),
    )(*args)


def shape(dims, kind=BF16):
    return jax.ShapeDtypeStruct(dims, kind)


def nt(a, b):
    return lax.dot_general(a, b, (((1,), (1,)), ((), ())), preferred_element_type=F32)


def halves(value):
    high = value.astype(BF16)
    return high, (value - high.astype(F32)).astype(BF16)


def wide_nt(value, matrix):
    high, low = halves(value)
    return nt(high, matrix) + nt(low, matrix)


def lower_pieces(own, peer, *outs):
    y, x, c, _ = place()
    for d in range(X):
        columns = pl.ds(pl.multiple_of(lax.rem(x + d, X) * BLOCK, 128), BLOCK)
        outs[d][pl.ds(pl.multiple_of(c * ROWS, 16), ROWS), :] = own[c, :, columns]
        outs[d][pl.ds(pl.multiple_of((1 - c) * ROWS, 16), ROWS), :] = peer[c, :, columns]


def inverse_piece(own, peer, out):
    c = place()[2]
    out[pl.ds(pl.multiple_of(c * ROWS, 16), ROWS), :] = own[c]
    out[pl.ds(pl.multiple_of((1 - c) * ROWS, 16), ROWS), :] = peer[c]


def lower_block(p0, p1, p2, p3, forcing, out):
    x = place()[1]
    for d, piece in enumerate((p0, p1, p2, p3)):
        at = lax.rem(x - d + X, X) * CHIP
        out[pl.ds(pl.multiple_of(at, 16), CHIP), :] = piece[...]
    out[BLOCK:, :] = forcing[...]


def coupling_block(a0, a1, a2, a3, l0, l1, l2, l3, r0, r1, s0, s1, out, panel):
    y, x, c, z = place()
    for d, piece in enumerate((a0, a1, a2, a3)):
        at = lax.rem(x - d + X, X) * CHIP
        panel[pl.ds(pl.multiple_of(at, 16), CHIP), :] = piece[...]
    total = jnp.zeros((BLOCK, BLOCK), F32)
    share = jnp.zeros((R, BLOCK), F32)
    for d, piece in enumerate((l0, l1, l2, l3)):
        at = pl.multiple_of(lax.rem(y - d + Y, Y) * BLOCK, 128)
        part = panel[:, pl.ds(at, BLOCK)]
        total += jnp.dot(part, piece[:BLOCK, :], preferred_element_type=F32)
        share += nt(piece[BLOCK:, :], part)
    block = total.astype(BF16)
    entry = (r0[...] + r1[...]) + (s0[...] + s1[...])
    entry = jnp.where((z == 0) & (c == 0), entry, 0.0)
    share = share - wide_nt(entry, block)
    high, low = halves(share)
    out[:BLOCK, :] = block
    out[BLOCK:BLOCK + R, :] = high
    out[BLOCK + R:, :] = low


def product_block(o0, o1, o2, o3, p0, p1, p2, p3, high_out, low_out, base_out, second):
    y, x, c, _ = place()

    def run(firsts, seconds):
        for d, piece in enumerate(seconds):
            second[lax.rem(x - d + X, X)] = piece[:BLOCK, :]
        total = jnp.zeros((BLOCK, BLOCK), F32)
        base = seconds[0][BLOCK:BLOCK + R, :].astype(F32) + seconds[0][BLOCK + R:, :].astype(F32)
        for d, piece in enumerate(firsts):
            mine = second[lax.rem(y - d + Y, Y)]
            total += jnp.dot(mine, piece[:BLOCK, :], preferred_element_type=F32)
            both = nt(piece[BLOCK:, :], mine)
            base -= both[:R] + both[R:]
        high, low = halves(total)
        high_out[...] = high
        low_out[...] = low
        base_out[...] = base

    own, peer = (o0, o1, o2, o3), (p0, p1, p2, p3)

    @pl.when(c == 0)
    def _():
        run(own, peer)

    @pl.when(c != 0)
    def _():
        run(peer, own)


def gathered(r0, r1, s0, s1):
    return (r0[...] + r1[...]) + (s0[...] + s1[...])


def hop_block(r0, r1, s0, s1, p_high, p_low, base, out):
    entry = gathered(r0, r1, s0, s1)
    high, low = halves(entry)
    out[...] = base[...] + (nt(high, p_high[...]) + (nt(low, p_high[...]) + nt(high, p_low[...])))


def final_block(r0, r1, s0, s1, p_high, p_low, base, own, peer, *outs):
    y, x, c, _ = place()
    scratch = outs[-1]
    outs = outs[:-1]
    entry = gathered(r0, r1, s0, s1)
    high, low = halves(entry)
    second = base[...] + (nt(high, p_high[...]) + (nt(low, p_high[...]) + nt(high, p_low[...])))
    first_block = jnp.where(c == 0, own[...], peer[...])
    first = first_block[BLOCK:BLOCK + R, :].astype(F32) + first_block[BLOCK + R:, :].astype(F32)
    first = first - (nt(high, first_block[:BLOCK, :]) + nt(low, first_block[:BLOCK, :]))
    scratch[0] = first.T
    scratch[1] = second.T
    for d in range(X):
        at = lax.rem(x + d, X) * CHIP + c * ROWS
        outs[d][...] = scratch[:, pl.ds(pl.multiple_of(at, 16), ROWS), :]


def hop(out, shift):
    arrived = []
    for j in range(2):
        def target(y, x, c, z, j=j):
            if shift == 0:
                return (x + 2 * j + c, y, c, z) if z == 0 else None
            return (x + 2 * j + c, y, c, z + 1) if z + 1 < Z else None
        arrived.append(send(out, target))
    return arrived + [to_peer(value) for value in arrived]


def local(inverses, lower, forcing, inflow):
    y, x, c, z = place()

    forcing_t = jnp.swapaxes(forcing, 1, 2).astype(F32).reshape(2 * R, ROWS)
    small = jnp.concatenate([forcing_t, inflow.T], axis=0)
    lower_peer = to_peer(lower)
    small_peer = to_peer(small)
    inverses_peer = to_peer(inverses)
    small = jnp.where(
        c == 0,
        jnp.concatenate([small, small_peer], axis=1),
        jnp.concatenate([small_peer, small], axis=1),
    )
    at_x = jnp.zeros((3 * R, BLOCK), F32)
    at_x = lax.dynamic_update_slice(at_x, small, (0, x * CHIP))
    forcing_x = lax.dynamic_slice_in_dim(at_x, c * R, R, 0).astype(BF16)
    inflow_x = at_x[2 * R:]

    piece = shape((CHIP, BLOCK))
    low = call(lower_pieces, [piece] * X, lower, lower_peer)
    low = [low[0]] + [send(low[d], along_x(d)) for d in range(1, X)]
    own = call(lower_block, shape((BLOCK + R, BLOCK)), *low, forcing_x)
    inverses, inverses_peer, own = lax.optimization_barrier((inverses, inverses_peer, own))
    panel = [own] + [send(own, along_y(d)) for d in range(1, Y)]
    inv = call(inverse_piece, shape((CHIP, N)), inverses, inverses_peer)
    inv = [inv] + [send(inv, along_x(d)) for d in range(1, X)]
    entry = hop(inflow_x, 0)

    message = call(
        coupling_block, shape((BLOCK + 2 * R, BLOCK)), *inv, *panel, *entry,
        scratch=[pltpu.VMEM((BLOCK, N), BF16)], flops=2 * BLOCK * BLOCK * N,
    )
    turn = [message] + [send(message, across(d)) for d in range(1, X)]
    turn_peer = [to_peer(value) for value in turn]
    p_high, p_low, base = call(
        product_block, [shape((BLOCK, BLOCK)), shape((BLOCK, BLOCK)), shape((R, BLOCK), F32)],
        *turn, *turn_peer, scratch=[pltpu.VMEM((X, BLOCK, BLOCK), BF16)], flops=2 * BLOCK * BLOCK * N,
    )

    out = base
    for step in range(Z - 1):
        entry = hop(out, 1)
        if step + 1 < Z - 1:
            out = call(hop_block, shape((R, BLOCK), F32), *entry, p_high, p_low, base)
    part = shape((2, ROWS, R), F32)
    finals = call(
        final_block, [part] * X, *entry, p_high, p_low, base, turn[0], turn_peer[0],
        scratch=[pltpu.VMEM((2, BLOCK, R), F32)],
    )
    total = finals[0]
    for d in range(1, X):
        total = total + send(finals[d], along_x(d))
    return total


def solution(mesh):
    placed = (
        P("blk", "group", None),
        P("blk", "group", None),
        P("blk", "group", None),
        P("group", None),
    )
    return jax.shard_map(
        local, mesh=mesh, in_specs=placed, out_specs=P("blk", "group", None), check_vma=False
    )
```

time: 281 us -> 114 us (0.41)
  the two profiles are of different devices: /device:TPU:96 before, /device:TPU:32 now
where the time goes in v2:
time: 114 us
  waiting for transfers between devices  55.3 us (49%)
  starting transfers between devices  50.8 us (45%)
  Pallas kernels  4.43 us (4%)
  local copies, waits for them, and re-layouts  2.18 us (2%)
    ppermute x38, waiting for transfers between devices, send(): return lax.ppermute(value, AXES, pairs)  55.3 us
    ppermute x38, starting transfers between devices, send(): return lax.ppermute(value, AXES, pairs)  50.8 us
    pallas_call x8, Pallas kernels, call(): pl.pallas_call(kernel, out_shape=out, in_specs=[pl.BlockSpec(memory_space...  4.43 us
  transfers between devices with their start and end apart: 38, of which 21 were waited for; matrix products, arithmetic and copies ran while one was open for 1% of the time, Pallas kernels for 0%

profile of v2, /device:TPU:32, one launch (start us, length us, event | category | flops | bytes accessed | tf_op | source)
XLA Modules:
  0.0 113.8 jit_solution(16576840313361572381)
XLA Ops:
  3.3 1.7 %collective-permute-start.2 = (bf16[96,384]{1,0:T(8,128)(2,1)S(1)}, bf16[96,384]{1,0:T(8,128)(2,1)S(1)}, u32[]{:S(2)}, u32[]{:S(2)}) collective-permute-start(bf16[96,384]{1,0:T(8,128)(2,1)S(1)} %get-tuple-element.20), channel_id=1, source_target_pairs={{0,8},{1,9},{2,10},{3,11},{4,12},{5,13},{6,14},{7,15},{8,16},{9,17... | collective-permute-start | bytes 221192 | tf_op jit(solution)/shard_map/ppermute | solution.py:31
  5.1 2.5 %collective-permute-start.3 = (bf16[96,384]{1,0:T(8,128)(2,1)S(1)}, bf16[96,384]{1,0:T(8,128)(2,1)S(1)}, u32[]{:S(2)}, u32[]{:S(2)}) collective-permute-start(bf16[96,384]{1,0:T(8,128)(2,1)S(1)} %get-tuple-element.21), channel_id=1, source_target_pairs={{0,16},{1,17},{2,18},{3,19},{4,20},{5,21},{6,22},{7,23},{8,24},{9,... | collective-permute-start | bytes 221192 | tf_op jit(solution)/shard_map/ppermute | solution.py:31
  7.6 1.6 %collective-permute-start.4 = (bf16[96,384]{1,0:T(8,128)(2,1)S(1)}, bf16[96,384]{1,0:T(8,128)(2,1)S(1)}, u32[]{:S(2)}, u32[]{:S(2)}) collective-permute-start(bf16[96,384]{1,0:T(8,128)(2,1)S(1)} %get-tuple-element.22), channel_id=1, source_target_pairs={{0,24},{1,25},{2,26},{3,27},{4,28},{5,29},{6,30},{7,31},{8,0},{9,1... | collective-permute-start | bytes 221192 | tf_op jit(solution)/shard_map/ppermute | solution.py:31
  9.2 2.2 %collective-permute-done.3.p2 = bf16[96,384]{1,0:T(8,128)(2,1)S(1)} collective-permute-done((bf16[96,384]{1,0:T(8,128)(2,1)S(1)}, bf16[96,384]{1,0:T(8,128)(2,1)S(1)}, u32[]{:S(2)}, u32[]{:S(2)}) %collective-permute-start.3) | collective-permute-done | bytes 73760 | tf_op jit(solution)/shard_map/ppermute | solution.py:31
  12.9 2.9 %collective-permute-start.8 = (bf16[96,1536]{1,0:T(8,128)(2,1)S(1)}, bf16[96,1536]{1,0:T(8,128)(2,1)S(1)}, u32[]{:S(2)}, u32[]{:S(2)}) collective-permute-start(bf16[96,1536]{1,0:T(8,128)(2,1)S(1)} %shard_map.48.a0), channel_id=1, source_target_pairs={{0,24},{1,25},{2,26},{3,27},{4,28},{5,29},{6,30},{7,31},{8,0},{9,1... | collective-permute-start | bytes 884744 | tf_op jit(solution)/shard_map/ppermute | solution.py:31
  17.8 3.0 %collective-permute-start.11 = (bf16[416,384]{1,0:T(8,128)(2,1)S(1)}, bf16[416,384]{1,0:T(8,128)(2,1)S(1)}, u32[]{:S(2)}, u32[]{:S(2)}) collective-permute-start(bf16[416,384]{1,0:T(8,128)(2,1)S(1)} %shard_map.47.l0), channel_id=1, source_target_pairs={{0,96},{1,97},{2,98},{3,99},{4,100},{5,101},{6,102},{7,103},{8,104... | collective-permute-start | bytes 958472 | tf_op jit(solution)/shard_map/ppermute | solution.py:31
  23.3 10.5 %collective-permute-done.7.a2 = bf16[96,1536]{1,0:T(8,128)(2,1)S(1)} collective-permute-done((bf16[96,1536]{1,0:T(8,128)(2,1)S(1)}, bf16[96,1536]{1,0:T(8,128)(2,1)S(1)}, u32[]{:S(2)}, u32[]{:S(2)}) %collective-permute-start.7) | collective-permute-done | bytes 294944 | tf_op jit(solution)/shard_map/ppermute | solution.py:31
  33.9 4.3 %collective-permute-done.6.a1 = bf16[96,1536]{1,0:T(8,128)(2,1)S(1)} collective-permute-done((bf16[96,1536]{1,0:T(8,128)(2,1)S(1)}, bf16[96,1536]{1,0:T(8,128)(2,1)S(1)}, u32[]{:S(2)}, u32[]{:S(2)}) %collective-permute-start.6) | collective-permute-done | bytes 294944 | tf_op jit(solution)/shard_map/ppermute | solution.py:31
  38.4 1.5 %shard_map.49.o0.own = bf16[448,384]{1,0:T(8,128)(2,1)S(1)} custom-call(bf16[96,1536]{1,0:T(8,128)(2,1)S(1)} %shard_map.48.a0, bf16[96,1536]{1,0:T(8,128)(2,1)S(1)} %collective-permute-done.6.a1, bf16[96,1536]{1,0:T(8,128)(2,1)S(1)} %collective-permute-done.7.a2, bf16[96,1536]{1,0:T(8,128)(2,1)S(1)} %collective-permute-done.8.a3, ...), custom_call_target="tpu_custom_call" | custom-call | flops 452984832 | bytes 2654208 | tf_op jit(solution)/shard_map/pallas_call | solution.py:57
  39.9 2.1 %collective-permute-start.18 = (bf16[448,384]{1,0:T(8,128)(2,1)S(1)}, bf16[448,384]{1,0:T(8,128)(2,1)S(1)}, u32[]{:S(2)}, u32[]{:S(2)}) collective-permute-start(bf16[448,384]{1,0:T(8,128)(2,1)S(1)} %shard_map.49.o0.own), channel_id=1, source_target_pairs={{0,96},{1,97},{2,98},{3,99},{4,28},{5,29},{6,30},{7,31},{8,104},{9... | collective-permute-start | bytes 1032200 | tf_op jit(solution)/shard_map/ppermute | solution.py:31
  42.0 1.7 %collective-permute-start.17 = (bf16[448,384]{1,0:T(8,128)(2,1)S(1)}, bf16[448,384]{1,0:T(8,128)(2,1)S(1)}, u32[]{:S(2)}, u32[]{:S(2)}) collective-permute-start(bf16[448,384]{1,0:T(8,128)(2,1)S(1)} %shard_map.49.o0.own), channel_id=1, source_target_pairs={{0,64},{1,65},{2,66},{3,67},{4,20},{5,21},{6,22},{7,23},{8,72},{9,... | collective-permute-start | bytes 1032200 | tf_op jit(solution)/shard_map/ppermute | solution.py:31
  43.7 6.8 %collective-permute-done.18.o3 = bf16[448,384]{1,0:T(8,128)(2,1)S(1)} collective-permute-done((bf16[448,384]{1,0:T(8,128)(2,1)S(1)}, bf16[448,384]{1,0:T(8,128)(2,1)S(1)}, u32[]{:S(2)}, u32[]{:S(2)}) %collective-permute-start.18) | collective-permute-done | bytes 344096 | tf_op jit(solution)/shard_map/ppermute | solution.py:31
  51.0 3.4 %collective-permute-done.16.o1 = bf16[448,384]{1,0:T(8,128)(2,1)S(1)} collective-permute-done((bf16[448,384]{1,0:T(8,128)(2,1)S(1)}, bf16[448,384]{1,0:T(8,128)(2,1)S(1)}, u32[]{:S(2)}, u32[]{:S(2)}) %collective-permute-start.16) | collective-permute-done | bytes 344096 | tf_op jit(solution)/shard_map/ppermute | solution.py:31
  54.5 1.6 %collective-permute-done.20.p1 = bf16[448,384]{1,0:T(8,128)(2,1)S(1)} collective-permute-done((bf16[448,384]{1,0:T(8,128)(2,1)S(1)}, bf16[448,384]{1,0:T(8,128)(2,1)S(1)}, u32[]{:S(2)}, u32[]{:S(2)}) %collective-permute-start.20) | collective-permute-done | bytes 344096 | tf_op jit(solution)/shard_map/ppermute | solution.py:31
  56.1 1.3 %shard_map.50 = (bf16[384,384]{1,0:T(8,128)(2,1)S(1)}, bf16[384,384]{1,0:T(8,128)(2,1)S(1)}, f32[32,384]{1,0:T(8,128)S(1)}) custom-call(bf16[448,384]{1,0:T(8,128)(2,1)S(1)} %shard_map.49.o0.own, bf16[448,384]{1,0:T(8,128)(2,1)S(1)} %collective-permute-done.16.o1, bf16[448,384]{1,0:T(8,128)(2,1)S(1)} %collective-permute-done.17.o2, ...), custom_call_target="tpu_custom_call" | custom-call | flops 452984832 | bytes 2752512 | tf_op jit(solution)/shard_map/pallas_call | solution.py:57
  57.4 5.0 %collective-permute-start.24 = (f32[32,384]{1,0:T(8,128)S(1)}, f32[32,384]{1,0:T(8,128)S(1)}, u32[]{:S(2)}, u32[]{:S(2)}) collective-permute-start(f32[32,384]{1,0:T(8,128)S(1)} %get-tuple-element.26.base), channel_id=1, source_target_pairs={{0,65},{1,66},{2,67},{4,101},{5,102},{6,103},{8,97},{9,98},{10,99}... | collective-permute-start | bytes 147464 | tf_op jit(solution)/shard_map/ppermute | solution.py:31
  62.4 3.5 %collective-permute-start.23 = (f32[32,384]{1,0:T(8,128)S(1)}, f32[32,384]{1,0:T(8,128)S(1)}, u32[]{:S(2)}, u32[]{:S(2)}) collective-permute-start(f32[32,384]{1,0:T(8,128)S(1)} %get-tuple-element.26.base), channel_id=1, source_target_pairs={{0,1},{1,2},{2,3},{4,37},{5,38},{6,39},{8,33},{9,34},{10,35},{12,6... | collective-permute-start | bytes 147464 | tf_op jit(solution)/shard_map/ppermute | solution.py:31
  66.0 6.7 %collective-permute-done.24.r1 = f32[32,384]{1,0:T(8,128)S(1)} collective-permute-done((f32[32,384]{1,0:T(8,128)S(1)}, f32[32,384]{1,0:T(8,128)S(1)}, u32[]{:S(2)}, u32[]{:S(2)}) %collective-permute-start.24) | collective-permute-done | bytes 49184 | tf_op jit(solution)/shard_map/ppermute | solution.py:31
  73.2 1.3 %collective-permute-start.25 = (f32[32,384]{1,0:T(8,128)S(1)}, f32[32,384]{1,0:T(8,128)S(1)}, u32[]{:S(2)}, u32[]{:S(2)}) collective-permute-start(f32[32,384]{1,0:T(8,128)S(1)} %collective-permute-done.23.r0), channel_id=1, source_target_pairs={{0,4},{1,5},{2,6},{3,7},{4,0},{5,1},{6,2},{7,3},{8,12},{9,13},{10,... | collective-permute-start | bytes 147464 | tf_op jit(solution)/shard_map/ppermute | solution.py:31
  75.8 2.6 %collective-permute-start.28 = (f32[32,384]{1,0:T(8,128)S(1)}, f32[32,384]{1,0:T(8,128)S(1)}, u32[]{:S(2)}, u32[]{:S(2)}) collective-permute-start(f32[32,384]{1,0:T(8,128)S(1)} %shard_map.51), channel_id=1, source_target_pairs={{0,65},{1,66},{2,67},{4,101},{5,102},{6,103},{8,97},{9,98},{10,99}... | collective-permute-start | bytes 147464 | tf_op jit(solution)/shard_map/ppermute | solution.py:31
  78.3 1.9 %collective-permute-start.27 = (f32[32,384]{1,0:T(8,128)S(1)}, f32[32,384]{1,0:T(8,128)S(1)}, u32[]{:S(2)}, u32[]{:S(2)}) collective-permute-start(f32[32,384]{1,0:T(8,128)S(1)} %shard_map.51), channel_id=1, source_target_pairs={{0,1},{1,2},{2,3},{4,37},{5,38},{6,39},{8,33},{9,34},{10,35},{12,6... | collective-permute-start | bytes 147464 | tf_op jit(solution)/shard_map/ppermute | solution.py:31
  80.3 4.2 %collective-permute-done.28.r1 = f32[32,384]{1,0:T(8,128)S(1)} collective-permute-done((f32[32,384]{1,0:T(8,128)S(1)}, f32[32,384]{1,0:T(8,128)S(1)}, u32[]{:S(2)}, u32[]{:S(2)}) %collective-permute-start.28) | collective-permute-done | bytes 49184 | tf_op jit(solution)/shard_map/ppermute | solution.py:31
  84.5 1.6 %collective-permute-done.27.r0 = f32[32,384]{1,0:T(8,128)S(1)} collective-permute-done((f32[32,384]{1,0:T(8,128)S(1)}, f32[32,384]{1,0:T(8,128)S(1)}, u32[]{:S(2)}, u32[]{:S(2)}) %collective-permute-start.27) | collective-permute-done | bytes 49184 | tf_op jit(solution)/shard_map/ppermute | solution.py:31
  86.0 1.3 %collective-permute-start.29 = (f32[32,384]{1,0:T(8,128)S(1)}, f32[32,384]{1,0:T(8,128)S(1)}, u32[]{:S(2)}, u32[]{:S(2)}) collective-permute-start(f32[32,384]{1,0:T(8,128)S(1)} %collective-permute-done.27.r0), channel_id=1, source_target_pairs={{0,4},{1,5},{2,6},{3,7},{4,0},{5,1},{6,2},{7,3},{8,12},{9,13},{10,... | collective-permute-start | bytes 147464 | tf_op jit(solution)/shard_map/ppermute | solution.py:31
  88.6 4.1 %collective-permute-start.32 = (f32[32,384]{1,0:T(8,128)S(1)}, f32[32,384]{1,0:T(8,128)S(1)}, u32[]{:S(2)}, u32[]{:S(2)}) collective-permute-start(f32[32,384]{1,0:T(8,128)S(1)} %shard_map.52), channel_id=1, source_target_pairs={{0,65},{1,66},{2,67},{4,101},{5,102},{6,103},{8,97},{9,98},{10,99}... | collective-permute-start | bytes 147464 | tf_op jit(solution)/shard_map/ppermute | solution.py:31
  92.7 1.9 %collective-permute-start.31 = (f32[32,384]{1,0:T(8,128)S(1)}, f32[32,384]{1,0:T(8,128)S(1)}, u32[]{:S(2)}, u32[]{:S(2)}) collective-permute-start(f32[32,384]{1,0:T(8,128)S(1)} %shard_map.52), channel_id=1, source_target_pairs={{0,1},{1,2},{2,3},{4,37},{5,38},{6,39},{8,33},{9,34},{10,35},{12,6... | collective-permute-start | bytes 147464 | tf_op jit(solution)/shard_map/ppermute | solution.py:31
  94.6 2.5 %collective-permute-done.32.r1 = f32[32,384]{1,0:T(8,128)S(1)} collective-permute-done((f32[32,384]{1,0:T(8,128)S(1)}, f32[32,384]{1,0:T(8,128)S(1)}, u32[]{:S(2)}, u32[]{:S(2)}) %collective-permute-start.32) | collective-permute-done | bytes 49184 | tf_op jit(solution)/shard_map/ppermute | solution.py:31
  97.1 3.3 %collective-permute-done.31.r0 = f32[32,384]{1,0:T(8,128)S(1)} collective-permute-done((f32[32,384]{1,0:T(8,128)S(1)}, f32[32,384]{1,0:T(8,128)S(1)}, u32[]{:S(2)}, u32[]{:S(2)}) %collective-permute-start.31) | collective-permute-done | bytes 49184 | tf_op jit(solution)/shard_map/ppermute | solution.py:31
  103.1 1.6 %collective-permute-start.35 = (f32[2,48,32]{2,1,0:T(8,128)S(1)}, f32[2,48,32]{2,1,0:T(8,128)S(1)}, u32[]{:S(2)}, u32[]{:S(2)}) collective-permute-start(f32[2,48,32]{2,1,0:T(8,128)S(1)} %get-tuple-element.30), channel_id=1, source_target_pairs={{0,8},{1,9},{2,10},{3,11},{4,12},{5,13},{6,14},{7,15},{8,16},{9,17... | collective-permute-start | bytes 36872 | tf_op jit(solution)/shard_map/ppermute | solution.py:31
  104.7 4.3 %collective-permute-start.36 = (f32[2,48,32]{2,1,0:T(8,128)S(1)}, f32[2,48,32]{2,1,0:T(8,128)S(1)}, u32[]{:S(2)}, u32[]{:S(2)}) collective-permute-start(f32[2,48,32]{2,1,0:T(8,128)S(1)} %get-tuple-element.31), channel_id=1, source_target_pairs={{0,16},{1,17},{2,18},{3,19},{4,20},{5,21},{6,22},{7,23},{8,24},{9,... | collective-permute-start | bytes 36872 | tf_op jit(solution)/shard_map/ppermute | solution.py:31
  109.0 1.4 %collective-permute-start.37 = (f32[2,48,32]{2,1,0:T(8,128)S(1)}, f32[2,48,32]{2,1,0:T(8,128)S(1)}, u32[]{:S(2)}, u32[]{:S(2)}) collective-permute-start(f32[2,48,32]{2,1,0:T(8,128)S(1)} %get-tuple-element.32), channel_id=1, source_target_pairs={{0,24},{1,25},{2,26},{3,27},{4,28},{5,29},{6,30},{7,31},{8,0},{9,1... | collective-permute-start | bytes 36872 | tf_op jit(solution)/shard_map/ppermute | solution.py:31
  110.4 1.5 %collective-permute-done.36 = f32[2,48,32]{2,1,0:T(8,128)S(1)} collective-permute-done((f32[2,48,32]{2,1,0:T(8,128)S(1)}, f32[2,48,32]{2,1,0:T(8,128)S(1)}, u32[]{:S(2)}, u32[]{:S(2)}) %collective-permute-start.36) | collective-permute-done | bytes 12320 | tf_op jit(solution)/shard_map/ppermute | solution.py:31
  (67 shorter events, 17.7 us)
Async XLA Ops:
  0.0 3.3 %collective-permute-start.1 = (bf16[2,48,1536]{2,1,0:T(8,128)(2,1)}, bf16[2,48,1536]{2,1,0:T(8,128)(2,1)S(1)}, u32[]{:S(2)}, u32[]{:S(2)}) collective-permute-start(bf16[2,48,1536]{2,1,0:T(8,128)(2,1)} %own.1), channel_id=1, source_target_pairs={{0,4},{1,5},{2,6},{3,7},{4,0},{5,1},{6,2},{7,3},{8,12},{9,13},{10,... | collective-permute-start | bytes 884744 | tf_op jit(solution)/shard_map/ppermute | solution.py:31
  0.0 12.0 %collective-permute-start = (bf16[2,48,1536]{2,1,0:T(8,128)(2,1)}, bf16[2,48,1536]{2,1,0:T(8,128)(2,1)S(1)}, u32[]{:S(2)}, u32[]{:S(2)}) collective-permute-start(bf16[2,48,1536]{2,1,0:T(8,128)(2,1)} %own.2), channel_id=1, source_target_pairs={{0,4},{1,5},{2,6},{3,7},{4,0},{5,1},{6,2},{7,3},{8,12},{9,13},{10,... | collective-permute-start | bytes 884744 | tf_op jit(solution)/shard_map/ppermute | solution.py:31
  3.3 5.9 %collective-permute-start.2 = (bf16[96,384]{1,0:T(8,128)(2,1)S(1)}, bf16[96,384]{1,0:T(8,128)(2,1)S(1)}, u32[]{:S(2)}, u32[]{:S(2)}) collective-permute-start(bf16[96,384]{1,0:T(8,128)(2,1)S(1)} %get-tuple-element.20), channel_id=1, source_target_pairs={{0,8},{1,9},{2,10},{3,11},{4,12},{5,13},{6,14},{7,15},{8,16},{9,17... | collective-permute-start | bytes 221192 | tf_op jit(solution)/shard_map/ppermute | solution.py:31
  5.1 6.4 %collective-permute-start.3 = (bf16[96,384]{1,0:T(8,128)(2,1)S(1)}, bf16[96,384]{1,0:T(8,128)(2,1)S(1)}, u32[]{:S(2)}, u32[]{:S(2)}) collective-permute-start(bf16[96,384]{1,0:T(8,128)(2,1)S(1)} %get-tuple-element.21), channel_id=1, source_target_pairs={{0,16},{1,17},{2,18},{3,19},{4,20},{5,21},{6,22},{7,23},{8,24},{9,... | collective-permute-start | bytes 221192 | tf_op jit(solution)/shard_map/ppermute | solution.py:31
  7.6 4.4 %collective-permute-start.4 = (bf16[96,384]{1,0:T(8,128)(2,1)S(1)}, bf16[96,384]{1,0:T(8,128)(2,1)S(1)}, u32[]{:S(2)}, u32[]{:S(2)}) collective-permute-start(bf16[96,384]{1,0:T(8,128)(2,1)S(1)} %get-tuple-element.22), channel_id=1, source_target_pairs={{0,24},{1,25},{2,26},{3,27},{4,28},{5,29},{6,30},{7,31},{8,0},{9,1... | collective-permute-start | bytes 221192 | tf_op jit(solution)/shard_map/ppermute | solution.py:31
  12.9 9.7 %collective-permute-start.8 = (bf16[96,1536]{1,0:T(8,128)(2,1)S(1)}, bf16[96,1536]{1,0:T(8,128)(2,1)S(1)}, u32[]{:S(2)}, u32[]{:S(2)}) collective-permute-start(bf16[96,1536]{1,0:T(8,128)(2,1)S(1)} %shard_map.48.a0), channel_id=1, source_target_pairs={{0,24},{1,25},{2,26},{3,27},{4,28},{5,29},{6,30},{7,31},{8,0},{9,1... | collective-permute-start | bytes 884744 | tf_op jit(solution)/shard_map/ppermute | solution.py:31
  17.2 4.2 %collective-permute-start.15 = (f32[32,384]{1,0:T(8,128)S(1)}, f32[32,384]{1,0:T(8,128)S(1)}, u32[]{:S(2)}, u32[]{:S(2)}) collective-permute-start(f32[32,384]{1,0:T(8,128)S(1)} %collective-permute-done.13.r1), channel_id=1, source_target_pairs={{0,4},{1,5},{2,6},{3,7},{4,0},{5,1},{6,2},{7,3},{8,12},{9,13},{10,... | collective-permute-start | bytes 147464 | tf_op jit(solution)/shard_map/ppermute | solution.py:31
  17.3 5.1 %collective-permute-start.14 = (f32[32,384]{1,0:T(8,128)S(1)}, f32[32,384]{1,0:T(8,128)S(1)}, u32[]{:S(2)}, u32[]{:S(2)}) collective-permute-start(f32[32,384]{1,0:T(8,128)S(1)} %collective-permute-done.12.r0), channel_id=1, source_target_pairs={{0,4},{1,5},{2,6},{3,7},{4,0},{5,1},{6,2},{7,3},{8,12},{9,13},{10,... | collective-permute-start | bytes 147464 | tf_op jit(solution)/shard_map/ppermute | solution.py:31
  17.8 20.4 %collective-permute-start.11 = (bf16[416,384]{1,0:T(8,128)(2,1)S(1)}, bf16[416,384]{1,0:T(8,128)(2,1)S(1)}, u32[]{:S(2)}, u32[]{:S(2)}) collective-permute-start(bf16[416,384]{1,0:T(8,128)(2,1)S(1)} %shard_map.47.l0), channel_id=1, source_target_pairs={{0,96},{1,97},{2,98},{3,99},{4,100},{5,101},{6,102},{7,103},{8,104... | collective-permute-start | bytes 958472 | tf_op jit(solution)/shard_map/ppermute | solution.py:31
  20.8 17.4 %collective-permute-start.10 = (bf16[416,384]{1,0:T(8,128)(2,1)S(1)}, bf16[416,384]{1,0:T(8,128)(2,1)S(1)}, u32[]{:S(2)}, u32[]{:S(2)}) collective-permute-start(bf16[416,384]{1,0:T(8,128)(2,1)S(1)} %shard_map.47.l0), channel_id=1, source_target_pairs={{0,64},{1,65},{2,66},{3,67},{4,68},{5,69},{6,70},{7,71},{8,72},{9,... | collective-permute-start | bytes 958472 | tf_op jit(solution)/shard_map/ppermute | solution.py:31
  21.4 17.0 %collective-permute-start.9 = (bf16[416,384]{1,0:T(8,128)(2,1)S(1)}, bf16[416,384]{1,0:T(8,128)(2,1)S(1)}, u32[]{:S(2)}, u32[]{:S(2)}) collective-permute-start(bf16[416,384]{1,0:T(8,128)(2,1)S(1)} %shard_map.47.l0), channel_id=1, source_target_pairs={{0,32},{1,33},{2,34},{3,35},{4,36},{5,37},{6,38},{7,39},{8,40},{9,... | collective-permute-start | bytes 958472 | tf_op jit(solution)/shard_map/ppermute | solution.py:31
  22.4 11.5 %collective-permute-start.7 = (bf16[96,1536]{1,0:T(8,128)(2,1)S(1)}, bf16[96,1536]{1,0:T(8,128)(2,1)S(1)}, u32[]{:S(2)}, u32[]{:S(2)}) collective-permute-start(bf16[96,1536]{1,0:T(8,128)(2,1)S(1)} %shard_map.48.a0), channel_id=1, source_target_pairs={{0,16},{1,17},{2,18},{3,19},{4,20},{5,21},{6,22},{7,23},{8,24},{9,... | collective-permute-start | bytes 884744 | tf_op jit(solution)/shard_map/ppermute | solution.py:31
  22.6 15.6 %collective-permute-start.6 = (bf16[96,1536]{1,0:T(8,128)(2,1)S(1)}, bf16[96,1536]{1,0:T(8,128)(2,1)S(1)}, u32[]{:S(2)}, u32[]{:S(2)}) collective-permute-start(bf16[96,1536]{1,0:T(8,128)(2,1)S(1)} %shard_map.48.a0), channel_id=1, source_target_pairs={{0,8},{1,9},{2,10},{3,11},{4,12},{5,13},{6,14},{7,15},{8,16},{9,17... | collective-permute-start | bytes 884744 | tf_op jit(solution)/shard_map/ppermute | solution.py:31
  39.9 10.6 %collective-permute-start.18 = (bf16[448,384]{1,0:T(8,128)(2,1)S(1)}, bf16[448,384]{1,0:T(8,128)(2,1)S(1)}, u32[]{:S(2)}, u32[]{:S(2)}) collective-permute-start(bf16[448,384]{1,0:T(8,128)(2,1)S(1)} %shard_map.49.o0.own), channel_id=1, source_target_pairs={{0,96},{1,97},{2,98},{3,99},{4,28},{5,29},{6,30},{7,31},{8,104},{9... | collective-permute-start | bytes 1032200 | tf_op jit(solution)/shard_map/ppermute | solution.py:31
  42.0 8.9 %collective-permute-start.17 = (bf16[448,384]{1,0:T(8,128)(2,1)S(1)}, bf16[448,384]{1,0:T(8,128)(2,1)S(1)}, u32[]{:S(2)}, u32[]{:S(2)}) collective-permute-start(bf16[448,384]{1,0:T(8,128)(2,1)S(1)} %shard_map.49.o0.own), channel_id=1, source_target_pairs={{0,64},{1,65},{2,66},{3,67},{4,20},{5,21},{6,22},{7,23},{8,72},{9,... | collective-permute-start | bytes 1032200 | tf_op jit(solution)/shard_map/ppermute | solution.py:31
  43.7 10.7 %collective-permute-start.16 = (bf16[448,384]{1,0:T(8,128)(2,1)S(1)}, bf16[448,384]{1,0:T(8,128)(2,1)S(1)}, u32[]{:S(2)}, u32[]{:S(2)}) collective-permute-start(bf16[448,384]{1,0:T(8,128)(2,1)S(1)} %shard_map.49.o0.own), channel_id=1, source_target_pairs={{0,32},{1,33},{2,34},{3,35},{4,12},{5,13},{6,14},{7,15},{8,40},{9,... | collective-permute-start | bytes 1032200 | tf_op jit(solution)/shard_map/ppermute | solution.py:31
  43.7 10.8 %collective-permute-start.19 = (bf16[448,384]{1,0:T(8,128)(2,1)S(1)}, bf16[448,384]{1,0:T(8,128)(2,1)S(1)}, u32[]{:S(2)}, u32[]{:S(2)}) collective-permute-start(bf16[448,384]{1,0:T(8,128)(2,1)S(1)} %shard_map.49.o0.own), channel_id=1, source_target_pairs={{0,4},{1,5},{2,6},{3,7},{4,0},{5,1},{6,2},{7,3},{8,12},{9,13},{10,... | collective-permute-start | bytes 1032200 | tf_op jit(solution)/shard_map/ppermute | solution.py:31
  50.5 4.0 %collective-permute-start.22 = (bf16[448,384]{1,0:T(8,128)(2,1)S(1)}, bf16[448,384]{1,0:T(8,128)(2,1)S(1)}, u32[]{:S(2)}, u32[]{:S(2)}) collective-permute-start(bf16[448,384]{1,0:T(8,128)(2,1)S(1)} %collective-permute-done.18.o3), channel_id=1, source_target_pairs={{0,4},{1,5},{2,6},{3,7},{4,0},{5,1},{6,2},{7,3},{8,12},{9,13},{10,... | collective-permute-start | bytes 1032200 | tf_op jit(solution)/shard_map/ppermute | solution.py:31
  50.9 3.6 %collective-permute-start.21 = (bf16[448,384]{1,0:T(8,128)(2,1)S(1)}, bf16[448,384]{1,0:T(8,128)(2,1)S(1)}, u32[]{:S(2)}, u32[]{:S(2)}) collective-permute-start(bf16[448,384]{1,0:T(8,128)(2,1)S(1)} %collective-permute-done.17.o2), channel_id=1, source_target_pairs={{0,4},{1,5},{2,6},{3,7},{4,0},{5,1},{6,2},{7,3},{8,12},{9,13},{10,... | collective-permute-start | bytes 1032200 | tf_op jit(solution)/shard_map/ppermute | solution.py:31
  57.4 15.2 %collective-permute-start.24 = (f32[32,384]{1,0:T(8,128)S(1)}, f32[32,384]{1,0:T(8,128)S(1)}, u32[]{:S(2)}, u32[]{:S(2)}) collective-permute-start(f32[32,384]{1,0:T(8,128)S(1)} %get-tuple-element.26.base), channel_id=1, source_target_pairs={{0,65},{1,66},{2,67},{4,101},{5,102},{6,103},{8,97},{9,98},{10,99}... | collective-permute-start | bytes 147464 | tf_op jit(solution)/shard_map/ppermute | solution.py:31
  62.4 10.8 %collective-permute-start.23 = (f32[32,384]{1,0:T(8,128)S(1)}, f32[32,384]{1,0:T(8,128)S(1)}, u32[]{:S(2)}, u32[]{:S(2)}) collective-permute-start(f32[32,384]{1,0:T(8,128)S(1)} %get-tuple-element.26.base), channel_id=1, source_target_pairs={{0,1},{1,2},{2,3},{4,37},{5,38},{6,39},{8,33},{9,34},{10,35},{12,6... | collective-permute-start | bytes 147464 | tf_op jit(solution)/shard_map/ppermute | solution.py:31
  73.2 2.2 %collective-permute-start.25 = (f32[32,384]{1,0:T(8,128)S(1)}, f32[32,384]{1,0:T(8,128)S(1)}, u32[]{:S(2)}, u32[]{:S(2)}) collective-permute-start(f32[32,384]{1,0:T(8,128)S(1)} %collective-permute-done.23.r0), channel_id=1, source_target_pairs={{0,4},{1,5},{2,6},{3,7},{4,0},{5,1},{6,2},{7,3},{8,12},{9,13},{10,... | collective-permute-start | bytes 147464 | tf_op jit(solution)/shard_map/ppermute | solution.py:31
  75.8 8.7 %collective-permute-start.28 = (f32[32,384]{1,0:T(8,128)S(1)}, f32[32,384]{1,0:T(8,128)S(1)}, u32[]{:S(2)}, u32[]{:S(2)}) collective-permute-start(f32[32,384]{1,0:T(8,128)S(1)} %shard_map.51), channel_id=1, source_target_pairs={{0,65},{1,66},{2,67},{4,101},{5,102},{6,103},{8,97},{9,98},{10,99}... | collective-permute-start | bytes 147464 | tf_op jit(solution)/shard_map/ppermute | solution.py:31
  78.3 7.7 %collective-permute-start.27 = (f32[32,384]{1,0:T(8,128)S(1)}, f32[32,384]{1,0:T(8,128)S(1)}, u32[]{:S(2)}, u32[]{:S(2)}) collective-permute-start(f32[32,384]{1,0:T(8,128)S(1)} %shard_map.51), channel_id=1, source_target_pairs={{0,1},{1,2},{2,3},{4,37},{5,38},{6,39},{8,33},{9,34},{10,35},{12,6... | collective-permute-start | bytes 147464 | tf_op jit(solution)/shard_map/ppermute | solution.py:31
  84.5 2.9 %collective-permute-start.30 = (f32[32,384]{1,0:T(8,128)S(1)}, f32[32,384]{1,0:T(8,128)S(1)}, u32[]{:S(2)}, u32[]{:S(2)}) collective-permute-start(f32[32,384]{1,0:T(8,128)S(1)} %collective-permute-done.28.r1), channel_id=1, source_target_pairs={{0,4},{1,5},{2,6},{3,7},{4,0},{5,1},{6,2},{7,3},{8,12},{9,13},{10,... | collective-permute-start | bytes 147464 | tf_op jit(solution)/shard_map/ppermute | solution.py:31
  86.0 2.2 %collective-permute-start.29 = (f32[32,384]{1,0:T(8,128)S(1)}, f32[32,384]{1,0:T(8,128)S(1)}, u32[]{:S(2)}, u32[]{:S(2)}) collective-permute-start(f32[32,384]{1,0:T(8,128)S(1)} %collective-permute-done.27.r0), channel_id=1, source_target_pairs={{0,4},{1,5},{2,6},{3,7},{4,0},{5,1},{6,2},{7,3},{8,12},{9,13},{10,... | collective-permute-start | bytes 147464 | tf_op jit(solution)/shard_map/ppermute | solution.py:31
  88.6 8.5 %collective-permute-start.32 = (f32[32,384]{1,0:T(8,128)S(1)}, f32[32,384]{1,0:T(8,128)S(1)}, u32[]{:S(2)}, u32[]{:S(2)}) collective-permute-start(f32[32,384]{1,0:T(8,128)S(1)} %shard_map.52), channel_id=1, source_target_pairs={{0,65},{1,66},{2,67},{4,101},{5,102},{6,103},{8,97},{9,98},{10,99}... | collective-permute-start | bytes 147464 | tf_op jit(solution)/shard_map/ppermute | solution.py:31
  92.7 7.7 %collective-permute-start.31 = (f32[32,384]{1,0:T(8,128)S(1)}, f32[32,384]{1,0:T(8,128)S(1)}, u32[]{:S(2)}, u32[]{:S(2)}) collective-permute-start(f32[32,384]{1,0:T(8,128)S(1)} %shard_map.52), channel_id=1, source_target_pairs={{0,1},{1,2},{2,3},{4,37},{5,38},{6,39},{8,33},{9,34},{10,35},{12,6... | collective-permute-start | bytes 147464 | tf_op jit(solution)/shard_map/ppermute | solution.py:31
  97.1 4.4 %collective-permute-start.34 = (f32[32,384]{1,0:T(8,128)S(1)}, f32[32,384]{1,0:T(8,128)S(1)}, u32[]{:S(2)}, u32[]{:S(2)}) collective-permute-start(f32[32,384]{1,0:T(8,128)S(1)} %collective-permute-done.32.r1), channel_id=1, source_target_pairs={{0,4},{1,5},{2,6},{3,7},{4,0},{5,1},{6,2},{7,3},{8,12},{9,13},{10,... | collective-permute-start | bytes 147464 | tf_op jit(solution)/shard_map/ppermute | solution.py:31
  103.1 7.2 %collective-permute-start.35 = (f32[2,48,32]{2,1,0:T(8,128)S(1)}, f32[2,48,32]{2,1,0:T(8,128)S(1)}, u32[]{:S(2)}, u32[]{:S(2)}) collective-permute-start(f32[2,48,32]{2,1,0:T(8,128)S(1)} %get-tuple-element.30), channel_id=1, source_target_pairs={{0,8},{1,9},{2,10},{3,11},{4,12},{5,13},{6,14},{7,15},{8,16},{9,17... | collective-permute-start | bytes 36872 | tf_op jit(solution)/shard_map/ppermute | solution.py:31
  104.7 7.1 %collective-permute-start.36 = (f32[2,48,32]{2,1,0:T(8,128)S(1)}, f32[2,48,32]{2,1,0:T(8,128)S(1)}, u32[]{:S(2)}, u32[]{:S(2)}) collective-permute-start(f32[2,48,32]{2,1,0:T(8,128)S(1)} %get-tuple-element.31), channel_id=1, source_target_pairs={{0,16},{1,17},{2,18},{3,19},{4,20},{5,21},{6,22},{7,23},{8,24},{9,... | collective-permute-start | bytes 36872 | tf_op jit(solution)/shard_map/ppermute | solution.py:31
  109.0 4.1 %collective-permute-start.37 = (f32[2,48,32]{2,1,0:T(8,128)S(1)}, f32[2,48,32]{2,1,0:T(8,128)S(1)}, u32[]{:S(2)}, u32[]{:S(2)}) collective-permute-start(f32[2,48,32]{2,1,0:T(8,128)S(1)} %get-tuple-element.32), channel_id=1, source_target_pairs={{0,24},{1,25},{2,26},{3,27},{4,28},{5,29},{6,30},{7,31},{8,0},{9,1... | collective-permute-start | bytes 36872 | tf_op jit(solution)/shard_map/ppermute | solution.py:31
  (9 other events, 13.2 us)

commit v3 on v2

v3 whole, which is shorter than its diff:
```python
import jax
import jax.numpy as jnp
from jax import lax
from jax.experimental import pallas as pl
from jax.experimental.pallas import tpu as pltpu
from jax.sharding import PartitionSpec as P

Y, X, CORES, Z = 4, 4, 2, 4
AXES = ("group", "blk")
ROWS = 48
CHIP = ROWS * CORES
BLOCK = CHIP * X
N = BLOCK * Y
R = 32
LANES = 128
F32, BF16 = jnp.float32, jnp.bfloat16


def send(value, target):
    pairs = []
    for y in range(Y):
        for x in range(X):
            for c in range(CORES):
                for z in range(Z):
                    to = target(y, x, c, z)
                    if to is not None:
                        ty, tx, tc, tz = to
                        pairs.append((
                            ((y * X + x) * CORES + c) * Z + z,
                            ((ty % Y * X + tx % X) * CORES + tc) * Z + tz,
                        ))
    return lax.ppermute(value, AXES, pairs)


def to_peer(value):
    return send(value, lambda y, x, c, z: (y, x, 1 - c, z))


def along_v(d):
    return lambda y, x, c, z: (y, x + d, c, z) if z % 2 == 0 else (y + d, x, c, z)


def along_u(d):
    return lambda y, x, c, z: (y + d, x, c, z) if z % 2 == 0 else (y, x + d, c, z)


def across(d):
    return lambda y, x, c, z: (along_u(d) if c == 0 else along_v(d))(y, x, c, z)


def place():
    group, z = lax.axis_index("group"), lax.axis_index("blk")
    y, x = group // (X * CORES), (group // CORES) % X
    even = z % 2 == 0
    return jnp.where(even, y, x), jnp.where(even, x, y), group % CORES, z


def chunk(u, v, z):
    return pl.multiple_of(jnp.where(z % 2 == 0, u * BLOCK + v * CHIP, v * BLOCK + u * CHIP), 32)


def rows_at(start, size):
    return pl.ds(pl.multiple_of(start, 16), size)


def lanes_at(start, size):
    return pl.ds(pl.multiple_of(start, 128), size)


def behind(me, d):
    return lax.rem(me - d + 4, 4)


def call(kernel, out, *args, scratch=(), flops=0):
    moved = sum(a.size * a.dtype.itemsize for a in args)
    return pl.pallas_call(
        kernel,
        out_shape=out,
        in_specs=[pl.BlockSpec(memory_space=pltpu.VMEM)] * len(args),
        out_specs=jax.tree.map(lambda _: pl.BlockSpec(memory_space=pltpu.VMEM), out),
        scratch_shapes=list(scratch),
        cost_estimate=pl.CostEstimate(flops=flops, bytes_accessed=moved, transcendentals=0),
        compiler_params=pltpu.CompilerParams(vmem_limit_bytes=24 * 2**20),
    )(*args)


def shape(dims, kind=BF16):
    return jax.ShapeDtypeStruct(dims, kind)


def nt(a, b):
    return lax.dot_general(a, b, (((1,), (1,)), ((), ())), preferred_element_type=F32)


def halves(value):
    high = value.astype(BF16)
    return high, (value - high.astype(F32)).astype(BF16)


def lower_pieces(own, peer, *refs):
    outs, rows, cut = refs[:4], refs[4], refs[5]
    _, v, c, z = place()
    rows[rows_at(c * ROWS, ROWS), :] = own[c]
    rows[rows_at((1 - c) * ROWS, ROWS), :] = peer[c]

    @pl.when(z % 2 == 0)
    def _():
        for b in range(4):
            cut[b] = jnp.concatenate(
                [rows[:, i * BLOCK + b * CHIP:i * BLOCK + (b + 1) * CHIP] for i in range(4)], axis=1
            )

    @pl.when(z % 2 == 1)
    def _():
        for b in range(4):
            cut[b] = rows[:, b * BLOCK:(b + 1) * BLOCK]

    for d in range(4):
        outs[d][...] = cut[lax.rem(v + d, 4)]


def inverse_piece(own, peer, out):
    c = place()[2]
    out[rows_at(c * ROWS, ROWS), :] = own[c]
    out[rows_at((1 - c) * ROWS, ROWS), :] = peer[c]


def lower_block(p0, p1, p2, p3, forcing, forcing_peer, inflow, inflow_peer, out, sides):
    _, v, c, _ = place()
    for d, piece in enumerate((p0, p1, p2, p3)):
        out[rows_at(behind(v, d) * CHIP, CHIP), :] = piece[...]
    sides[...] = jnp.zeros_like(sides)
    for f, e, at in ((forcing, inflow, c * ROWS), (forcing_peer, inflow_peer, (1 - c) * ROWS)):
        high, low = halves(e[...])
        sides[rows_at(at, ROWS), 0:R] = f[c].astype(F32)
        sides[rows_at(at, ROWS), R:2 * R] = high.astype(F32)
        sides[rows_at(at, ROWS), 2 * R:3 * R] = low.astype(F32)
    for g in range(3):
        out[BLOCK:, g * LANES:(g + 1) * LANES] = sides[g * R:(g + 1) * R, :].astype(BF16)


def coupling_block(a0, a1, a2, a3, l0, l1, l2, l3, out, panel, lower, sides, entry):
    u, v, c, z = place()
    for d, piece in enumerate((a0, a1, a2, a3)):
        panel[rows_at(behind(v, d) * CHIP, CHIP), :] = piece[...]
    sides[...] = jnp.zeros_like(sides)
    for d, piece in enumerate((l0, l1, l2, l3)):
        from_u = behind(u, d)
        for j in range(4):
            lower[rows_at(chunk(from_u, j, z), CHIP), :] = piece[j * CHIP:(j + 1) * CHIP, :]
        at = chunk(from_u, v, z)
        for g in range(3):
            part = piece[BLOCK:, g * LANES:(g + 1) * LANES]
            sides[rows_at(at + g * R, R), :] = part
            entry[rows_at(from_u * CHIP + g * R, R), :] = part
    block = jnp.dot(panel[...], lower[...], preferred_element_type=F32).astype(BF16)
    share = jnp.dot(panel[...], sides[...], preferred_element_type=F32)[:, :R]
    known = jnp.dot(block, entry[...], preferred_element_type=F32)
    known = known[:, R:2 * R] + known[:, 2 * R:3 * R]
    share = share - jnp.where((z == 0) & (c == 0), known, 0.0)
    share = jnp.concatenate([share, jnp.zeros((BLOCK, LANES - R), F32)], axis=1).T[:R]
    high, low = halves(share)
    out[:BLOCK, :] = block
    out[BLOCK:BLOCK + R, :] = high
    out[BLOCK + R:, :] = low


def product_block(o0, o1, o2, o3, p0, p1, p2, p3, high_out, low_out, base_out, second, first, shares):
    u, v, c, _ = place()

    def run(firsts, seconds):
        for d, piece in enumerate(seconds):
            second[:, lanes_at(behind(v, d) * BLOCK, BLOCK)] = piece[:BLOCK, :]
        for d, piece in enumerate(firsts):
            from_u = behind(u, d)
            side = piece[BLOCK:, :].astype(F32)
            side = jnp.concatenate([side, jnp.zeros((LANES - 2 * R, BLOCK), F32)], axis=0).T.astype(BF16)
            for j in range(4):
                at = rows_at(j * BLOCK + from_u * CHIP, CHIP)
                first[at, :] = piece[j * CHIP:(j + 1) * CHIP, :]
                shares[at, :] = side[j * CHIP:(j + 1) * CHIP, :]
        total = jnp.dot(second[...], first[...], preferred_element_type=F32)
        taken = jnp.dot(second[...], shares[...], preferred_element_type=F32).T
        high, low = halves(total)
        high_out[...] = high
        low_out[...] = low
        own = seconds[0][BLOCK:BLOCK + R, :].astype(F32) + seconds[0][BLOCK + R:, :].astype(F32)
        base_out[...] = own - (taken[:R] + taken[R:2 * R])

    own, peer = (o0, o1, o2, o3), (p0, p1, p2, p3)

    @pl.when(c == 0)
    def _():
        run(own, peer)

    @pl.when(c != 0)
    def _():
        run(peer, own)


def gathered(r0, r1, s0, s1):
    return (r0[...] + r1[...]) + (s0[...] + s1[...])


def hop_block(r0, r1, s0, s1, p_high, p_low, base, out):
    entry = gathered(r0, r1, s0, s1)
    high, low = halves(entry)
    out[...] = base[...] + (nt(high, p_high[...]) + (nt(low, p_high[...]) + nt(high, p_low[...])))


def final_block(r0, r1, s0, s1, p_high, p_low, base, own, peer, *outs):
    c = place()[2]
    v = place()[1]
    scratch = outs[-1]
    outs = outs[:-1]
    entry = gathered(r0, r1, s0, s1)
    high, low = halves(entry)
    second = base[...] + (nt(high, p_high[...]) + (nt(low, p_high[...]) + nt(high, p_low[...])))
    first_block = jnp.where(c == 0, own[...], peer[...])
    first = first_block[BLOCK:BLOCK + R, :].astype(F32) + first_block[BLOCK + R:, :].astype(F32)
    first = first - (nt(high, first_block[:BLOCK, :]) + nt(low, first_block[:BLOCK, :]))
    scratch[0] = first.T
    scratch[1] = second.T
    for d in range(X):
        outs[d][...] = scratch[:, rows_at(lax.rem(v + d, 4) * CHIP + c * ROWS, ROWS), :]


def hop(out):
    arrived = []
    for j in range(2):
        def target(y, x, c, z, j=j):
            y, x, c, _ = along_v(2 * j + c)(y, x, c, z)
            return (y, x, c, z + 1) if z + 1 < Z else None
        arrived.append(send(out, target))
    return arrived + [to_peer(value) for value in arrived]


def local(inverses, lower, forcing, inflow):
    lower_peer = to_peer(lower)
    piece = shape((CHIP, BLOCK))
    low = call(
        lower_pieces, [piece] * 4, lower, lower_peer,
        scratch=[pltpu.VMEM((CHIP, N), BF16), pltpu.VMEM((4, CHIP, BLOCK), BF16)],
    )
    low = [low[0]] + [send(low[d], along_v(d)) for d in range(1, 4)]
    forcing_peer = to_peer(forcing)
    inflow_peer = to_peer(inflow)
    own = call(
        lower_block, shape((BLOCK + R, BLOCK)), *low, forcing, forcing_peer, inflow, inflow_peer,
        scratch=[pltpu.VMEM((CHIP, LANES), F32)],
    )
    inverses, own = lax.optimization_barrier((inverses, own))
    panel = [own] + [send(own, along_u(d)) for d in range(1, 4)]
    inverses_peer = to_peer(inverses)
    inv = call(inverse_piece, shape((CHIP, N)), inverses, inverses_peer)
    inv = [inv] + [send(inv, along_v(d)) for d in range(1, 4)]

    message = call(
        coupling_block, shape((BLOCK + 2 * R, BLOCK)), *inv, *panel,
        scratch=[
            pltpu.VMEM((BLOCK, N), BF16), pltpu.VMEM((N, BLOCK), BF16),
            pltpu.VMEM((N, LANES), BF16), pltpu.VMEM((BLOCK, LANES), BF16),
        ],
        flops=2 * BLOCK * BLOCK * N,
    )
    turn = [message] + [send(message, across(d)) for d in range(1, 4)]
    turn_peer = [to_peer(value) for value in turn]
    p_high, p_low, base = call(
        product_block, [shape((BLOCK, BLOCK)), shape((BLOCK, BLOCK)), shape((R, BLOCK), F32)],
        *turn, *turn_peer,
        scratch=[pltpu.VMEM((BLOCK, N), BF16), pltpu.VMEM((N, BLOCK), BF16), pltpu.VMEM((N, LANES), BF16)],
        flops=2 * BLOCK * BLOCK * N,
    )

    out = base
    for step in range(Z - 1):
        entry = hop(out)
        if step + 1 < Z - 1:
            out = call(hop_block, shape((R, BLOCK), F32), *entry, p_high, p_low, base)
    part = shape((2, ROWS, R), F32)
    finals = call(
        final_block, [part] * 4, *entry, p_high, p_low, base, turn[0], turn_peer[0],
        scratch=[pltpu.VMEM((2, BLOCK, R), F32)],
    )
    total = finals[0]
    for d in range(1, 4):
        total = total + send(finals[d], along_v(d))
    return total


def solution(mesh):
    placed = (
        P("blk", "group", None),
        P("blk", "group", None),
        P("blk", "group", None),
        P("group", None),
    )
    return jax.shard_map(
        local, mesh=mesh, in_specs=placed, out_specs=P("blk", "group", None), check_vma=False
    )
```

time: 114 us -> 100 us (0.88)
  the two profiles are of different devices: /device:TPU:32 before, /device:TPU:56 now
where the time goes in v3:
time: 100 us
  waiting for transfers between devices  51.3 us (51%)
  starting transfers between devices  41.5 us (42%)
  Pallas kernels  4.71 us (5%)
  local copies, waits for them, and re-layouts  2.43 us (2%)
    ppermute x35, waiting for transfers between devices, send(): return lax.ppermute(value, AXES, pairs)  51.3 us
    ppermute x35, starting transfers between devices, send(): return lax.ppermute(value, AXES, pairs)  41.5 us
    pallas_call x8, Pallas kernels, call(): pl.pallas_call(kernel, out_shape=out, in_specs=[pl.BlockSpec(memory_space...  4.71 us
  transfers between devices with their start and end apart: 35, of which 24 were waited for; matrix products, arithmetic and copies ran while one was open for 0% of the time, Pallas kernels for 0%

profile of v3, /device:TPU:56, one launch (start us, length us, event | category | flops | bytes accessed | tf_op | source)
XLA Modules:
  0.0 100.1 jit_solution(2109332761346457595)
XLA Ops:
  0.0 1.8 %collective-permute-done.peer = bf16[2,48,1536]{2,1,0:T(8,128)(2,1)S(1)} collective-permute-done((bf16[2,48,1536]{2,1,0:T(8,128)(2,1)}, bf16[2,48,1536]{2,1,0:T(8,128)(2,1)S(1)}, u32[]{:S(2)}, u32[]{:S(2)}) %collective-permute-start) | collective-permute-done | bytes 294944 | tf_op jit(solution)/shard_map/ppermute | solution.py:32
  3.1 2.6 %collective-permute-start.2 = (bf16[96,384]{1,0:T(8,128)(2,1)S(1)}, bf16[96,384]{1,0:T(8,128)(2,1)S(1)}, u32[]{:S(2)}, u32[]{:S(2)}) collective-permute-start(bf16[96,384]{1,0:T(8,128)(2,1)S(1)} %get-tuple-element.20), channel_id=1, source_target_pairs={{0,16},{1,65},{2,18},{3,67},{4,20},{5,69},{6,22},{7,71},{8,24},{9,... | collective-permute-start | bytes 221192 | tf_op jit(solution)/shard_map/ppermute | solution.py:32
  9.0 2.3 %collective-permute-done.3.p3 = bf16[96,384]{1,0:T(8,128)(2,1)S(1)} collective-permute-done((bf16[96,384]{1,0:T(8,128)(2,1)S(1)}, bf16[96,384]{1,0:T(8,128)(2,1)S(1)}, u32[]{:S(2)}, u32[]{:S(2)}) %collective-permute-start.3) | collective-permute-done | bytes 73760 | tf_op jit(solution)/shard_map/ppermute | solution.py:32
  11.4 2.8 %collective-permute-start.12 = (bf16[416,384]{1,0:T(8,128)(2,1)S(1)}, bf16[416,384]{1,0:T(8,128)(2,1)S(1)}, u32[]{:S(2)}, u32[]{:S(2)}) collective-permute-start(bf16[416,384]{1,0:T(8,128)(2,1)S(1)} %shard_map.47.l0), channel_id=1, source_target_pairs={{0,96},{1,25},{2,98},{3,27},{4,100},{5,29},{6,102},{7,31},{8,104},... | collective-permute-start | bytes 958472 | tf_op jit(solution)/shard_map/ppermute | solution.py:32
  14.2 1.1 %collective-permute-start.11 = (bf16[416,384]{1,0:T(8,128)(2,1)S(1)}, bf16[416,384]{1,0:T(8,128)(2,1)S(1)}, u32[]{:S(2)}, u32[]{:S(2)}) collective-permute-start(bf16[416,384]{1,0:T(8,128)(2,1)S(1)} %shard_map.47.l0), channel_id=1, source_target_pairs={{0,64},{1,17},{2,66},{3,19},{4,68},{5,21},{6,70},{7,23},{8,72},{9,... | collective-permute-start | bytes 958472 | tf_op jit(solution)/shard_map/ppermute | solution.py:32
  16.0 2.1 %collective-permute-start.8 = (bf16[96,1536]{1,0:T(8,128)(2,1)S(1)}, bf16[96,1536]{1,0:T(8,128)(2,1)S(1)}, u32[]{:S(2)}, u32[]{:S(2)}) collective-permute-start(bf16[96,1536]{1,0:T(8,128)(2,1)S(1)} %shard_map.48.a0), channel_id=1, source_target_pairs={{0,16},{1,65},{2,18},{3,67},{4,20},{5,69},{6,22},{7,71},{8,24},{9,... | collective-permute-start | bytes 884744 | tf_op jit(solution)/shard_map/ppermute | solution.py:32
  18.1 8.3 %collective-permute-done.12.l3 = bf16[416,384]{1,0:T(8,128)(2,1)S(1)} collective-permute-done((bf16[416,384]{1,0:T(8,128)(2,1)S(1)}, bf16[416,384]{1,0:T(8,128)(2,1)S(1)}, u32[]{:S(2)}, u32[]{:S(2)}) %collective-permute-start.12) | collective-permute-done | bytes 319520 | tf_op jit(solution)/shard_map/ppermute | solution.py:32
  26.5 1.2 %collective-permute-start.7 = (bf16[96,1536]{1,0:T(8,128)(2,1)S(1)}, bf16[96,1536]{1,0:T(8,128)(2,1)S(1)}, u32[]{:S(2)}, u32[]{:S(2)}) collective-permute-start(bf16[96,1536]{1,0:T(8,128)(2,1)S(1)} %shard_map.48.a0), channel_id=1, source_target_pairs={{0,8},{1,33},{2,10},{3,35},{4,12},{5,37},{6,14},{7,39},{8,16},{9,4... | collective-permute-start | bytes 884744 | tf_op jit(solution)/shard_map/ppermute | solution.py:32
  27.7 4.8 %collective-permute-done.10.l1 = bf16[416,384]{1,0:T(8,128)(2,1)S(1)} collective-permute-done((bf16[416,384]{1,0:T(8,128)(2,1)S(1)}, bf16[416,384]{1,0:T(8,128)(2,1)S(1)}, u32[]{:S(2)}, u32[]{:S(2)}) %collective-permute-start.10) | collective-permute-done | bytes 319520 | tf_op jit(solution)/shard_map/ppermute | solution.py:32
  33.2 1.6 %shard_map.49.o0.own = bf16[448,384]{1,0:T(8,128)(2,1)S(1)} custom-call(bf16[96,1536]{1,0:T(8,128)(2,1)S(1)} %shard_map.48.a0, bf16[96,1536]{1,0:T(8,128)(2,1)S(1)} %collective-permute-done.7.a1, bf16[96,1536]{1,0:T(8,128)(2,1)S(1)} %collective-permute-done.8.a2, bf16[96,1536]{1,0:T(8,128)(2,1)S(1)} %collective-permute-done.9.a3, ...), custom_call_target="tpu_custom_call" | custom-call | flops 452984832 | bytes 2457600 | tf_op jit(solution)/shard_map/pallas_call | solution.py:76
  34.8 3.7 %collective-permute-start.15 = (bf16[448,384]{1,0:T(8,128)(2,1)S(1)}, bf16[448,384]{1,0:T(8,128)(2,1)S(1)}, u32[]{:S(2)}, u32[]{:S(2)}) collective-permute-start(bf16[448,384]{1,0:T(8,128)(2,1)S(1)} %shard_map.49.o0.own), channel_id=1, source_target_pairs={{0,96},{1,25},{2,98},{3,27},{4,28},{5,101},{6,30},{7,103},{8,104},... | collective-permute-start | bytes 1032200 | tf_op jit(solution)/shard_map/ppermute | solution.py:32
  39.5 7.5 %collective-permute-done.15.o3 = bf16[448,384]{1,0:T(8,128)(2,1)S(1)} collective-permute-done((bf16[448,384]{1,0:T(8,128)(2,1)S(1)}, bf16[448,384]{1,0:T(8,128)(2,1)S(1)}, u32[]{:S(2)}, u32[]{:S(2)}) %collective-permute-start.15) | collective-permute-done | bytes 344096 | tf_op jit(solution)/shard_map/ppermute | solution.py:32
  47.5 3.2 %collective-permute-done.13.o1 = bf16[448,384]{1,0:T(8,128)(2,1)S(1)} collective-permute-done((bf16[448,384]{1,0:T(8,128)(2,1)S(1)}, bf16[448,384]{1,0:T(8,128)(2,1)S(1)}, u32[]{:S(2)}, u32[]{:S(2)}) %collective-permute-start.13) | collective-permute-done | bytes 344096 | tf_op jit(solution)/shard_map/ppermute | solution.py:32
  50.7 1.6 %collective-permute-done.17.p1 = bf16[448,384]{1,0:T(8,128)(2,1)S(1)} collective-permute-done((bf16[448,384]{1,0:T(8,128)(2,1)S(1)}, bf16[448,384]{1,0:T(8,128)(2,1)S(1)}, u32[]{:S(2)}, u32[]{:S(2)}) %collective-permute-start.17) | collective-permute-done | bytes 344096 | tf_op jit(solution)/shard_map/ppermute | solution.py:32
  52.3 1.4 %shard_map.50 = (bf16[384,384]{1,0:T(8,128)(2,1)S(1)}, bf16[384,384]{1,0:T(8,128)(2,1)S(1)}, f32[32,384]{1,0:T(8,128)S(1)}) custom-call(bf16[448,384]{1,0:T(8,128)(2,1)S(1)} %shard_map.49.o0.own, bf16[448,384]{1,0:T(8,128)(2,1)S(1)} %collective-permute-done.13.o1, bf16[448,384]{1,0:T(8,128)(2,1)S(1)} %collective-permute-done.14.o2, ...), custom_call_target="tpu_custom_call" | custom-call | flops 452984832 | bytes 2752512 | tf_op jit(solution)/shard_map/pallas_call | solution.py:76
  53.8 4.2 %collective-permute-start.21 = (f32[32,384]{1,0:T(8,128)S(1)}, f32[32,384]{1,0:T(8,128)S(1)}, u32[]{:S(2)}, u32[]{:S(2)}) collective-permute-start(f32[32,384]{1,0:T(8,128)S(1)} %get-tuple-element.24.base), channel_id=1, source_target_pairs={{0,17},{1,66},{2,19},{4,29},{5,102},{6,31},{8,25},{9,74},{10,27},{... | collective-permute-start | bytes 147464 | tf_op jit(solution)/shard_map/ppermute | solution.py:32
  58.0 2.9 %collective-permute-start.20 = (f32[32,384]{1,0:T(8,128)S(1)}, f32[32,384]{1,0:T(8,128)S(1)}, u32[]{:S(2)}, u32[]{:S(2)}) collective-permute-start(f32[32,384]{1,0:T(8,128)S(1)} %get-tuple-element.24.base), channel_id=1, source_target_pairs={{0,1},{1,2},{2,3},{4,13},{5,38},{6,15},{8,9},{9,10},{10,11},{12,21... | collective-permute-start | bytes 147464 | tf_op jit(solution)/shard_map/ppermute | solution.py:32
  60.9 1.3 %collective-permute-done.21.r1 = f32[32,384]{1,0:T(8,128)S(1)} collective-permute-done((f32[32,384]{1,0:T(8,128)S(1)}, f32[32,384]{1,0:T(8,128)S(1)}, u32[]{:S(2)}, u32[]{:S(2)}) %collective-permute-start.21) | collective-permute-done | bytes 49184 | tf_op jit(solution)/shard_map/ppermute | solution.py:32
  63.1 1.4 %collective-permute-done.20.r0 = f32[32,384]{1,0:T(8,128)S(1)} collective-permute-done((f32[32,384]{1,0:T(8,128)S(1)}, f32[32,384]{1,0:T(8,128)S(1)}, u32[]{:S(2)}, u32[]{:S(2)}) %collective-permute-start.20) | collective-permute-done | bytes 49184 | tf_op jit(solution)/shard_map/ppermute | solution.py:32
  64.5 1.2 %collective-permute-done.22.s0 = f32[32,384]{1,0:T(8,128)S(1)} collective-permute-done((f32[32,384]{1,0:T(8,128)S(1)}, f32[32,384]{1,0:T(8,128)S(1)}, u32[]{:S(2)}, u32[]{:S(2)}) %collective-permute-start.22) | collective-permute-done | bytes 49184 | tf_op jit(solution)/shard_map/ppermute | solution.py:32
  66.1 4.2 %collective-permute-start.25 = (f32[32,384]{1,0:T(8,128)S(1)}, f32[32,384]{1,0:T(8,128)S(1)}, u32[]{:S(2)}, u32[]{:S(2)}) collective-permute-start(f32[32,384]{1,0:T(8,128)S(1)} %shard_map.51), channel_id=1, source_target_pairs={{0,17},{1,66},{2,19},{4,29},{5,102},{6,31},{8,25},{9,74},{10,27},{... | collective-permute-start | bytes 147464 | tf_op jit(solution)/shard_map/ppermute | solution.py:32
  70.3 2.8 %collective-permute-start.24 = (f32[32,384]{1,0:T(8,128)S(1)}, f32[32,384]{1,0:T(8,128)S(1)}, u32[]{:S(2)}, u32[]{:S(2)}) collective-permute-start(f32[32,384]{1,0:T(8,128)S(1)} %shard_map.51), channel_id=1, source_target_pairs={{0,1},{1,2},{2,3},{4,13},{5,38},{6,15},{8,9},{9,10},{10,11},{12,21... | collective-permute-start | bytes 147464 | tf_op jit(solution)/shard_map/ppermute | solution.py:32
  73.1 1.4 %collective-permute-done.25.r1 = f32[32,384]{1,0:T(8,128)S(1)} collective-permute-done((f32[32,384]{1,0:T(8,128)S(1)}, f32[32,384]{1,0:T(8,128)S(1)}, u32[]{:S(2)}, u32[]{:S(2)}) %collective-permute-start.25) | collective-permute-done | bytes 49184 | tf_op jit(solution)/shard_map/ppermute | solution.py:32
  74.5 2.3 %collective-permute-done.24.r0 = f32[32,384]{1,0:T(8,128)S(1)} collective-permute-done((f32[32,384]{1,0:T(8,128)S(1)}, f32[32,384]{1,0:T(8,128)S(1)}, u32[]{:S(2)}, u32[]{:S(2)}) %collective-permute-start.24) | collective-permute-done | bytes 49184 | tf_op jit(solution)/shard_map/ppermute | solution.py:32
  76.8 1.2 %collective-permute-done.26.s0 = f32[32,384]{1,0:T(8,128)S(1)} collective-permute-done((f32[32,384]{1,0:T(8,128)S(1)}, f32[32,384]{1,0:T(8,128)S(1)}, u32[]{:S(2)}, u32[]{:S(2)}) %collective-permute-start.26) | collective-permute-done | bytes 49184 | tf_op jit(solution)/shard_map/ppermute | solution.py:32
  78.4 3.1 %collective-permute-start.29 = (f32[32,384]{1,0:T(8,128)S(1)}, f32[32,384]{1,0:T(8,128)S(1)}, u32[]{:S(2)}, u32[]{:S(2)}) collective-permute-start(f32[32,384]{1,0:T(8,128)S(1)} %shard_map.52), channel_id=1, source_target_pairs={{0,17},{1,66},{2,19},{4,29},{5,102},{6,31},{8,25},{9,74},{10,27},{... | collective-permute-start | bytes 147464 | tf_op jit(solution)/shard_map/ppermute | solution.py:32
  81.5 2.3 %collective-permute-start.28 = (f32[32,384]{1,0:T(8,128)S(1)}, f32[32,384]{1,0:T(8,128)S(1)}, u32[]{:S(2)}, u32[]{:S(2)}) collective-permute-start(f32[32,384]{1,0:T(8,128)S(1)} %shard_map.52), channel_id=1, source_target_pairs={{0,1},{1,2},{2,3},{4,13},{5,38},{6,15},{8,9},{9,10},{10,11},{12,21... | collective-permute-start | bytes 147464 | tf_op jit(solution)/shard_map/ppermute | solution.py:32
  83.8 3.2 %collective-permute-done.29.r1 = f32[32,384]{1,0:T(8,128)S(1)} collective-permute-done((f32[32,384]{1,0:T(8,128)S(1)}, f32[32,384]{1,0:T(8,128)S(1)}, u32[]{:S(2)}, u32[]{:S(2)}) %collective-permute-start.29) | collective-permute-done | bytes 49184 | tf_op jit(solution)/shard_map/ppermute | solution.py:32
  89.8 2.8 %collective-permute-start.32 = (f32[2,48,32]{2,1,0:T(8,128)S(1)}, f32[2,48,32]{2,1,0:T(8,128)S(1)}, u32[]{:S(2)}, u32[]{:S(2)}) collective-permute-start(f32[2,48,32]{2,1,0:T(8,128)S(1)} %get-tuple-element.28), channel_id=1, source_target_pairs={{0,8},{1,33},{2,10},{3,35},{4,12},{5,37},{6,14},{7,39},{8,16},{9,4... | collective-permute-start | bytes 36872 | tf_op jit(solution)/shard_map/ppermute | solution.py:32
  92.6 1.5 %collective-permute-start.33 = (f32[2,48,32]{2,1,0:T(8,128)S(1)}, f32[2,48,32]{2,1,0:T(8,128)S(1)}, u32[]{:S(2)}, u32[]{:S(2)}) collective-permute-start(f32[2,48,32]{2,1,0:T(8,128)S(1)} %get-tuple-element.29), channel_id=1, source_target_pairs={{0,16},{1,65},{2,18},{3,67},{4,20},{5,69},{6,22},{7,71},{8,24},{9,... | collective-permute-start | bytes 36872 | tf_op jit(solution)/shard_map/ppermute | solution.py:32
  94.5 3.8 %collective-permute-done.33 = f32[2,48,32]{2,1,0:T(8,128)S(1)} collective-permute-done((f32[2,48,32]{2,1,0:T(8,128)S(1)}, f32[2,48,32]{2,1,0:T(8,128)S(1)}, u32[]{:S(2)}, u32[]{:S(2)}) %collective-permute-start.33) | collective-permute-done | bytes 12320 | tf_op jit(solution)/shard_map/ppermute | solution.py:32
  98.3 1.1 %collective-permute-done.34 = f32[2,48,32]{2,1,0:T(8,128)S(1)} collective-permute-done((f32[2,48,32]{2,1,0:T(8,128)S(1)}, f32[2,48,32]{2,1,0:T(8,128)S(1)}, u32[]{:S(2)}, u32[]{:S(2)}) %collective-permute-start.34) | collective-permute-done | bytes 12320 | tf_op jit(solution)/shard_map/ppermute | solution.py:32
  (58 shorter events, 13.3 us)
Async XLA Ops:
  0.0 1.8 %collective-permute-start = (bf16[2,48,1536]{2,1,0:T(8,128)(2,1)}, bf16[2,48,1536]{2,1,0:T(8,128)(2,1)S(1)}, u32[]{:S(2)}, u32[]{:S(2)}) collective-permute-start(bf16[2,48,1536]{2,1,0:T(8,128)(2,1)} %own.1), channel_id=1, source_target_pairs={{0,4},{1,5},{2,6},{3,7},{4,0},{5,1},{6,2},{7,3},{8,12},{9,13},{10,... | collective-permute-start | bytes 884744 | tf_op jit(solution)/shard_map/ppermute | solution.py:32
  2.8 5.2 %collective-permute-start.1 = (bf16[96,384]{1,0:T(8,128)(2,1)S(1)}, bf16[96,384]{1,0:T(8,128)(2,1)S(1)}, u32[]{:S(2)}, u32[]{:S(2)}) collective-permute-start(bf16[96,384]{1,0:T(8,128)(2,1)S(1)} %get-tuple-element.19), channel_id=1, source_target_pairs={{0,8},{1,33},{2,10},{3,35},{4,12},{5,37},{6,14},{7,39},{8,16},{9,4... | collective-permute-start | bytes 221192 | tf_op jit(solution)/shard_map/ppermute | solution.py:32
  3.1 5.9 %collective-permute-start.2 = (bf16[96,384]{1,0:T(8,128)(2,1)S(1)}, bf16[96,384]{1,0:T(8,128)(2,1)S(1)}, u32[]{:S(2)}, u32[]{:S(2)}) collective-permute-start(bf16[96,384]{1,0:T(8,128)(2,1)S(1)} %get-tuple-element.20), channel_id=1, source_target_pairs={{0,16},{1,65},{2,18},{3,67},{4,20},{5,69},{6,22},{7,71},{8,24},{9,... | collective-permute-start | bytes 221192 | tf_op jit(solution)/shard_map/ppermute | solution.py:32
  5.7 5.6 %collective-permute-start.3 = (bf16[96,384]{1,0:T(8,128)(2,1)S(1)}, bf16[96,384]{1,0:T(8,128)(2,1)S(1)}, u32[]{:S(2)}, u32[]{:S(2)}) collective-permute-start(bf16[96,384]{1,0:T(8,128)(2,1)S(1)} %get-tuple-element.21), channel_id=1, source_target_pairs={{0,24},{1,97},{2,26},{3,99},{4,28},{5,101},{6,30},{7,103},{8,0},{9... | collective-permute-start | bytes 221192 | tf_op jit(solution)/shard_map/ppermute | solution.py:32
  6.5 1.3 %collective-permute-start.4 = (bf16[2,48,32]{2,1,0:T(8,128)(2,1)S(1)}, bf16[2,48,32]{2,1,0:T(8,128)(2,1)S(1)}, u32[]{:S(2)}, u32[]{:S(2)}) collective-permute-start(bf16[2,48,32]{2,1,0:T(8,128)(2,1)S(1)} %copy.7.forcing), channel_id=1, source_target_pairs={{0,4},{1,5},{2,6},{3,7},{4,0},{5,1},{6,2},{7,3},{8,12},{9,13},{10,... | collective-permute-start | bytes 18440 | tf_op jit(solution)/shard_map/ppermute | solution.py:32
  11.4 15.1 %collective-permute-start.12 = (bf16[416,384]{1,0:T(8,128)(2,1)S(1)}, bf16[416,384]{1,0:T(8,128)(2,1)S(1)}, u32[]{:S(2)}, u32[]{:S(2)}) collective-permute-start(bf16[416,384]{1,0:T(8,128)(2,1)S(1)} %shard_map.47.l0), channel_id=1, source_target_pairs={{0,96},{1,25},{2,98},{3,27},{4,100},{5,29},{6,102},{7,31},{8,104},... | collective-permute-start | bytes 958472 | tf_op jit(solution)/shard_map/ppermute | solution.py:32
  14.2 1.7 %collective-permute-start.6 = (bf16[2,48,1536]{2,1,0:T(8,128)(2,1)S(1)}, bf16[2,48,1536]{2,1,0:T(8,128)(2,1)S(1)}, u32[]{:S(2)}, u32[]{:S(2)}) collective-permute-start(bf16[2,48,1536]{2,1,0:T(8,128)(2,1)S(1)} %copy-done), channel_id=1, source_target_pairs={{0,4},{1,5},{2,6},{3,7},{4,0},{5,1},{6,2},{7,3},{8,12},{9,13},{10,... | collective-permute-start | bytes 884744 | tf_op jit(solution)/shard_map/ppermute | solution.py:32
  14.2 13.5 %collective-permute-start.11 = (bf16[416,384]{1,0:T(8,128)(2,1)S(1)}, bf16[416,384]{1,0:T(8,128)(2,1)S(1)}, u32[]{:S(2)}, u32[]{:S(2)}) collective-permute-start(bf16[416,384]{1,0:T(8,128)(2,1)S(1)} %shard_map.47.l0), channel_id=1, source_target_pairs={{0,64},{1,17},{2,66},{3,19},{4,68},{5,21},{6,70},{7,23},{8,72},{9,... | collective-permute-start | bytes 958472 | tf_op jit(solution)/shard_map/ppermute | solution.py:32
  15.3 17.2 %collective-permute-start.10 = (bf16[416,384]{1,0:T(8,128)(2,1)S(1)}, bf16[416,384]{1,0:T(8,128)(2,1)S(1)}, u32[]{:S(2)}, u32[]{:S(2)}) collective-permute-start(bf16[416,384]{1,0:T(8,128)(2,1)S(1)} %shard_map.47.l0), channel_id=1, source_target_pairs={{0,32},{1,9},{2,34},{3,11},{4,36},{5,13},{6,38},{7,15},{8,40},{9,1... | collective-permute-start | bytes 958472 | tf_op jit(solution)/shard_map/ppermute | solution.py:32
  15.9 16.6 %collective-permute-start.9 = (bf16[96,1536]{1,0:T(8,128)(2,1)S(1)}, bf16[96,1536]{1,0:T(8,128)(2,1)S(1)}, u32[]{:S(2)}, u32[]{:S(2)}) collective-permute-start(bf16[96,1536]{1,0:T(8,128)(2,1)S(1)} %shard_map.48.a0), channel_id=1, source_target_pairs={{0,24},{1,97},{2,26},{3,99},{4,28},{5,101},{6,30},{7,103},{8,0},{9... | collective-permute-start | bytes 884744 | tf_op jit(solution)/shard_map/ppermute | solution.py:32
  16.0 16.5 %collective-permute-start.8 = (bf16[96,1536]{1,0:T(8,128)(2,1)S(1)}, bf16[96,1536]{1,0:T(8,128)(2,1)S(1)}, u32[]{:S(2)}, u32[]{:S(2)}) collective-permute-start(bf16[96,1536]{1,0:T(8,128)(2,1)S(1)} %shard_map.48.a0), channel_id=1, source_target_pairs={{0,16},{1,65},{2,18},{3,67},{4,20},{5,69},{6,22},{7,71},{8,24},{9,... | collective-permute-start | bytes 884744 | tf_op jit(solution)/shard_map/ppermute | solution.py:32
  26.5 6.7 %collective-permute-start.7 = (bf16[96,1536]{1,0:T(8,128)(2,1)S(1)}, bf16[96,1536]{1,0:T(8,128)(2,1)S(1)}, u32[]{:S(2)}, u32[]{:S(2)}) collective-permute-start(bf16[96,1536]{1,0:T(8,128)(2,1)S(1)} %shard_map.48.a0), channel_id=1, source_target_pairs={{0,8},{1,33},{2,10},{3,35},{4,12},{5,37},{6,14},{7,39},{8,16},{9,4... | collective-permute-start | bytes 884744 | tf_op jit(solution)/shard_map/ppermute | solution.py:32
  34.8 12.2 %collective-permute-start.15 = (bf16[448,384]{1,0:T(8,128)(2,1)S(1)}, bf16[448,384]{1,0:T(8,128)(2,1)S(1)}, u32[]{:S(2)}, u32[]{:S(2)}) collective-permute-start(bf16[448,384]{1,0:T(8,128)(2,1)S(1)} %shard_map.49.o0.own), channel_id=1, source_target_pairs={{0,96},{1,25},{2,98},{3,27},{4,28},{5,101},{6,30},{7,103},{8,104},... | collective-permute-start | bytes 1032200 | tf_op jit(solution)/shard_map/ppermute | solution.py:32
  38.5 8.9 %collective-permute-start.14 = (bf16[448,384]{1,0:T(8,128)(2,1)S(1)}, bf16[448,384]{1,0:T(8,128)(2,1)S(1)}, u32[]{:S(2)}, u32[]{:S(2)}) collective-permute-start(bf16[448,384]{1,0:T(8,128)(2,1)S(1)} %shard_map.49.o0.own), channel_id=1, source_target_pairs={{0,64},{1,17},{2,66},{3,19},{4,20},{5,69},{6,22},{7,71},{8,72},{9,... | collective-permute-start | bytes 1032200 | tf_op jit(solution)/shard_map/ppermute | solution.py:32
  38.5 12.1 %collective-permute-start.13 = (bf16[448,384]{1,0:T(8,128)(2,1)S(1)}, bf16[448,384]{1,0:T(8,128)(2,1)S(1)}, u32[]{:S(2)}, u32[]{:S(2)}) collective-permute-start(bf16[448,384]{1,0:T(8,128)(2,1)S(1)} %shard_map.49.o0.own), channel_id=1, source_target_pairs={{0,32},{1,9},{2,34},{3,11},{4,12},{5,37},{6,14},{7,39},{8,40},{9,1... | collective-permute-start | bytes 1032200 | tf_op jit(solution)/shard_map/ppermute | solution.py:32
  39.5 11.2 %collective-permute-start.16 = (bf16[448,384]{1,0:T(8,128)(2,1)S(1)}, bf16[448,384]{1,0:T(8,128)(2,1)S(1)}, u32[]{:S(2)}, u32[]{:S(2)}) collective-permute-start(bf16[448,384]{1,0:T(8,128)(2,1)S(1)} %shard_map.49.o0.own), channel_id=1, source_target_pairs={{0,4},{1,5},{2,6},{3,7},{4,0},{5,1},{6,2},{7,3},{8,12},{9,13},{10,... | collective-permute-start | bytes 1032200 | tf_op jit(solution)/shard_map/ppermute | solution.py:32
  47.0 3.7 %collective-permute-start.19 = (bf16[448,384]{1,0:T(8,128)(2,1)S(1)}, bf16[448,384]{1,0:T(8,128)(2,1)S(1)}, u32[]{:S(2)}, u32[]{:S(2)}) collective-permute-start(bf16[448,384]{1,0:T(8,128)(2,1)S(1)} %collective-permute-done.15.o3), channel_id=1, source_target_pairs={{0,4},{1,5},{2,6},{3,7},{4,0},{5,1},{6,2},{7,3},{8,12},{9,13},{10,... | collective-permute-start | bytes 1032200 | tf_op jit(solution)/shard_map/ppermute | solution.py:32
  47.4 3.3 %collective-permute-start.18 = (bf16[448,384]{1,0:T(8,128)(2,1)S(1)}, bf16[448,384]{1,0:T(8,128)(2,1)S(1)}, u32[]{:S(2)}, u32[]{:S(2)}) collective-permute-start(bf16[448,384]{1,0:T(8,128)(2,1)S(1)} %collective-permute-done.14.o2), channel_id=1, source_target_pairs={{0,4},{1,5},{2,6},{3,7},{4,0},{5,1},{6,2},{7,3},{8,12},{9,13},{10,... | collective-permute-start | bytes 1032200 | tf_op jit(solution)/shard_map/ppermute | solution.py:32
  50.7 1.7 %collective-permute-start.17 = (bf16[448,384]{1,0:T(8,128)(2,1)S(1)}, bf16[448,384]{1,0:T(8,128)(2,1)S(1)}, u32[]{:S(2)}, u32[]{:S(2)}) collective-permute-start(bf16[448,384]{1,0:T(8,128)(2,1)S(1)} %collective-permute-done.13.o1), channel_id=1, source_target_pairs={{0,4},{1,5},{2,6},{3,7},{4,0},{5,1},{6,2},{7,3},{8,12},{9,13},{10,... | collective-permute-start | bytes 1032200 | tf_op jit(solution)/shard_map/ppermute | solution.py:32
  53.8 8.4 %collective-permute-start.21 = (f32[32,384]{1,0:T(8,128)S(1)}, f32[32,384]{1,0:T(8,128)S(1)}, u32[]{:S(2)}, u32[]{:S(2)}) collective-permute-start(f32[32,384]{1,0:T(8,128)S(1)} %get-tuple-element.24.base), channel_id=1, source_target_pairs={{0,17},{1,66},{2,19},{4,29},{5,102},{6,31},{8,25},{9,74},{10,27},{... | collective-permute-start | bytes 147464 | tf_op jit(solution)/shard_map/ppermute | solution.py:32
  58.0 6.5 %collective-permute-start.20 = (f32[32,384]{1,0:T(8,128)S(1)}, f32[32,384]{1,0:T(8,128)S(1)}, u32[]{:S(2)}, u32[]{:S(2)}) collective-permute-start(f32[32,384]{1,0:T(8,128)S(1)} %get-tuple-element.24.base), channel_id=1, source_target_pairs={{0,1},{1,2},{2,3},{4,13},{5,38},{6,15},{8,9},{9,10},{10,11},{12,21... | collective-permute-start | bytes 147464 | tf_op jit(solution)/shard_map/ppermute | solution.py:32
  62.2 2.3 %collective-permute-start.23 = (f32[32,384]{1,0:T(8,128)S(1)}, f32[32,384]{1,0:T(8,128)S(1)}, u32[]{:S(2)}, u32[]{:S(2)}) collective-permute-start(f32[32,384]{1,0:T(8,128)S(1)} %collective-permute-done.21.r1), channel_id=1, source_target_pairs={{0,4},{1,5},{2,6},{3,7},{4,0},{5,1},{6,2},{7,3},{8,12},{9,13},{10,... | collective-permute-start | bytes 147464 | tf_op jit(solution)/shard_map/ppermute | solution.py:32
  66.1 8.4 %collective-permute-start.25 = (f32[32,384]{1,0:T(8,128)S(1)}, f32[32,384]{1,0:T(8,128)S(1)}, u32[]{:S(2)}, u32[]{:S(2)}) collective-permute-start(f32[32,384]{1,0:T(8,128)S(1)} %shard_map.51), channel_id=1, source_target_pairs={{0,17},{1,66},{2,19},{4,29},{5,102},{6,31},{8,25},{9,74},{10,27},{... | collective-permute-start | bytes 147464 | tf_op jit(solution)/shard_map/ppermute | solution.py:32
  70.3 6.5 %collective-permute-start.24 = (f32[32,384]{1,0:T(8,128)S(1)}, f32[32,384]{1,0:T(8,128)S(1)}, u32[]{:S(2)}, u32[]{:S(2)}) collective-permute-start(f32[32,384]{1,0:T(8,128)S(1)} %shard_map.51), channel_id=1, source_target_pairs={{0,1},{1,2},{2,3},{4,13},{5,38},{6,15},{8,9},{9,10},{10,11},{12,21... | collective-permute-start | bytes 147464 | tf_op jit(solution)/shard_map/ppermute | solution.py:32
  74.5 2.3 %collective-permute-start.27 = (f32[32,384]{1,0:T(8,128)S(1)}, f32[32,384]{1,0:T(8,128)S(1)}, u32[]{:S(2)}, u32[]{:S(2)}) collective-permute-start(f32[32,384]{1,0:T(8,128)S(1)} %collective-permute-done.25.r1), channel_id=1, source_target_pairs={{0,4},{1,5},{2,6},{3,7},{4,0},{5,1},{6,2},{7,3},{8,12},{9,13},{10,... | collective-permute-start | bytes 147464 | tf_op jit(solution)/shard_map/ppermute | solution.py:32
  76.8 1.2 %collective-permute-start.26 = (f32[32,384]{1,0:T(8,128)S(1)}, f32[32,384]{1,0:T(8,128)S(1)}, u32[]{:S(2)}, u32[]{:S(2)}) collective-permute-start(f32[32,384]{1,0:T(8,128)S(1)} %collective-permute-done.24.r0), channel_id=1, source_target_pairs={{0,4},{1,5},{2,6},{3,7},{4,0},{5,1},{6,2},{7,3},{8,12},{9,13},{10,... | collective-permute-start | bytes 147464 | tf_op jit(solution)/shard_map/ppermute | solution.py:32
  78.4 8.6 %collective-permute-start.29 = (f32[32,384]{1,0:T(8,128)S(1)}, f32[32,384]{1,0:T(8,128)S(1)}, u32[]{:S(2)}, u32[]{:S(2)}) collective-permute-start(f32[32,384]{1,0:T(8,128)S(1)} %shard_map.52), channel_id=1, source_target_pairs={{0,17},{1,66},{2,19},{4,29},{5,102},{6,31},{8,25},{9,74},{10,27},{... | collective-permute-start | bytes 147464 | tf_op jit(solution)/shard_map/ppermute | solution.py:32
  81.5 6.0 %collective-permute-start.28 = (f32[32,384]{1,0:T(8,128)S(1)}, f32[32,384]{1,0:T(8,128)S(1)}, u32[]{:S(2)}, u32[]{:S(2)}) collective-permute-start(f32[32,384]{1,0:T(8,128)S(1)} %shard_map.52), channel_id=1, source_target_pairs={{0,1},{1,2},{2,3},{4,13},{5,38},{6,15},{8,9},{9,10},{10,11},{12,21... | collective-permute-start | bytes 147464 | tf_op jit(solution)/shard_map/ppermute | solution.py:32
  87.5 1.6 %collective-permute-start.30 = (f32[32,384]{1,0:T(8,128)S(1)}, f32[32,384]{1,0:T(8,128)S(1)}, u32[]{:S(2)}, u32[]{:S(2)}) collective-permute-start(f32[32,384]{1,0:T(8,128)S(1)} %collective-permute-done.28.r0), channel_id=1, source_target_pairs={{0,4},{1,5},{2,6},{3,7},{4,0},{5,1},{6,2},{7,3},{8,12},{9,13},{10,... | collective-permute-start | bytes 147464 | tf_op jit(solution)/shard_map/ppermute | solution.py:32
  89.8 4.7 %collective-permute-start.32 = (f32[2,48,32]{2,1,0:T(8,128)S(1)}, f32[2,48,32]{2,1,0:T(8,128)S(1)}, u32[]{:S(2)}, u32[]{:S(2)}) collective-permute-start(f32[2,48,32]{2,1,0:T(8,128)S(1)} %get-tuple-element.28), channel_id=1, source_target_pairs={{0,8},{1,33},{2,10},{3,35},{4,12},{5,37},{6,14},{7,39},{8,16},{9,4... | collective-permute-start | bytes 36872 | tf_op jit(solution)/shard_map/ppermute | solution.py:32
  92.6 5.7 %collective-permute-start.33 = (f32[2,48,32]{2,1,0:T(8,128)S(1)}, f32[2,48,32]{2,1,0:T(8,128)S(1)}, u32[]{:S(2)}, u32[]{:S(2)}) collective-permute-start(f32[2,48,32]{2,1,0:T(8,128)S(1)} %get-tuple-element.29), channel_id=1, source_target_pairs={{0,16},{1,65},{2,18},{3,67},{4,20},{5,69},{6,22},{7,71},{8,24},{9,... | collective-permute-start | bytes 36872 | tf_op jit(solution)/shard_map/ppermute | solution.py:32
  94.1 5.3 %collective-permute-start.34 = (f32[2,48,32]{2,1,0:T(8,128)S(1)}, f32[2,48,32]{2,1,0:T(8,128)S(1)}, u32[]{:S(2)}, u32[]{:S(2)}) collective-permute-start(f32[2,48,32]{2,1,0:T(8,128)S(1)} %get-tuple-element.30), channel_id=1, source_target_pairs={{0,24},{1,97},{2,26},{3,99},{4,28},{5,101},{6,30},{7,103},{8,0},{9... | collective-permute-start | bytes 36872 | tf_op jit(solution)/shard_map/ppermute | solution.py:32
  (7 other events, 11.3 us)

commit v4 on v3

--- a/solution.py
+++ b/solution.py
@@ -97,10 +97,14 @@
     return high, (value - high.astype(F32)).astype(BF16)
 
 
+def hold(own, out):
+    out[...] = own[place()[2]]
+
+
 def lower_pieces(own, peer, *refs):
     outs, rows, cut = refs[:4], refs[4], refs[5]
     _, v, c, z = place()
-    rows[rows_at(c * ROWS, ROWS), :] = own[c]
+    rows[rows_at(c * ROWS, ROWS), :] = own[...]
     rows[rows_at((1 - c) * ROWS, ROWS), :] = peer[c]
 
     @pl.when(z % 2 == 0)
@@ -129,12 +133,11 @@
     _, v, c, _ = place()
     for d, piece in enumerate((p0, p1, p2, p3)):
         out[rows_at(behind(v, d) * CHIP, CHIP), :] = piece[...]
-    sides[...] = jnp.zeros_like(sides)
     for f, e, at in ((forcing, inflow, c * ROWS), (forcing_peer, inflow_peer, (1 - c) * ROWS)):
         high, low = halves(e[...])
-        sides[rows_at(at, ROWS), 0:R] = f[c].astype(F32)
-        sides[rows_at(at, ROWS), R:2 * R] = high.astype(F32)
-        sides[rows_at(at, ROWS), 2 * R:3 * R] = low.astype(F32)
+        side = jnp.concatenate([f[c].astype(F32), high.astype(F32), low.astype(F32), jnp.zeros((R, ROWS), F32)], axis=0)
+        side = jnp.concatenate([side, jnp.zeros((LANES, LANES - ROWS), F32)], axis=1).T
+        sides[rows_at(at, ROWS), :] = side[:ROWS]
     for g in range(3):
         out[BLOCK:, g * LANES:(g + 1) * LANES] = sides[g * R:(g + 1) * R, :].astype(BF16)
 
@@ -165,7 +168,7 @@
     out[BLOCK + R:, :] = low
 
 
-def product_block(o0, o1, o2, o3, p0, p1, p2, p3, high_out, low_out, base_out, second, first, shares):
+def product_block(o0, o1, o2, o3, p0, p1, p2, p3, high_out, low_out, base_out, start_out, second, first, shares):
     u, v, c, _ = place()
 
     def run(firsts, seconds):
@@ -185,7 +188,9 @@
         high_out[...] = high
         low_out[...] = low
         own = seconds[0][BLOCK:BLOCK + R, :].astype(F32) + seconds[0][BLOCK + R:, :].astype(F32)
-        base_out[...] = own - (taken[:R] + taken[R:2 * R])
+        base = own - (taken[:R] + taken[R:2 * R])
+        base_out[...] = base
+        start_out[...] = base.astype(BF16)
 
     own, peer = (o0, o1, o2, o3), (p0, p1, p2, p3)
 
@@ -198,31 +203,31 @@
         run(peer, own)
 
 
-def gathered(r0, r1, s0, s1):
-    return (r0[...] + r1[...]) + (s0[...] + s1[...])
-
-
-def hop_block(r0, r1, s0, s1, p_high, p_low, base, out):
-    entry = gathered(r0, r1, s0, s1)
+def pair_sum(r0, r1, out):
+    out[...] = r0[...].astype(F32) + r1[...].astype(F32)
+
+
+def onward(entry, p_high, p_low, base):
     high, low = halves(entry)
-    out[...] = base[...] + (nt(high, p_high[...]) + (nt(low, p_high[...]) + nt(high, p_low[...])))
-
-
-def final_block(r0, r1, s0, s1, p_high, p_low, base, own, peer, *outs):
-    c = place()[2]
-    v = place()[1]
-    scratch = outs[-1]
-    outs = outs[:-1]
-    entry = gathered(r0, r1, s0, s1)
+    return base + (nt(high, p_high) + (nt(low, p_high) + nt(high, p_low)))
+
+
+def hop_block(own, peer, p_high, p_low, base, out):
+    out[...] = onward(own[...] + peer[...], p_high[...], p_low[...], base[...]).astype(BF16)
+
+
+def final_block(own, peer, p_high, p_low, base, message, message_peer, *outs):
+    _, v, c, _ = place()
+    entry = own[...] + peer[...]
     high, low = halves(entry)
-    second = base[...] + (nt(high, p_high[...]) + (nt(low, p_high[...]) + nt(high, p_low[...])))
-    first_block = jnp.where(c == 0, own[...], peer[...])
+    second = onward(entry, p_high[...], p_low[...], base[...])
+    first_block = jnp.where(c == 0, message[...], message_peer[...])
     first = first_block[BLOCK:BLOCK + R, :].astype(F32) + first_block[BLOCK + R:, :].astype(F32)
     first = first - (nt(high, first_block[:BLOCK, :]) + nt(low, first_block[:BLOCK, :]))
-    scratch[0] = first.T
-    scratch[1] = second.T
-    for d in range(X):
-        outs[d][...] = scratch[:, rows_at(lax.rem(v + d, 4) * CHIP + c * ROWS, ROWS), :]
+    states = jnp.concatenate([first, second], axis=0)
+    for d in range(4):
+        at = lax.rem(v + d, 4) * CHIP + c * ROWS
+        outs[d][...] = pltpu.roll(states, lax.rem(BLOCK - at, BLOCK), 1)[:, :ROWS]
 
 
 def hop(out):
@@ -232,28 +237,35 @@
             y, x, c, _ = along_v(2 * j + c)(y, x, c, z)
             return (y, x, c, z + 1) if z + 1 < Z else None
         arrived.append(send(out, target))
-    return arrived + [to_peer(value) for value in arrived]
+    own = call(pair_sum, shape((R, BLOCK), F32), *arrived)
+    return own, to_peer(own)
 
 
 def local(inverses, lower, forcing, inflow):
+    forcing = jnp.swapaxes(forcing, 1, 2)
+    inflow = inflow.T
+    inverses_peer = to_peer(inverses)
     lower_peer = to_peer(lower)
+    inv_own = call(inverse_piece, shape((CHIP, N)), inverses, inverses_peer)
+    lower_own = call(hold, shape((ROWS, N)), lower)
+    inv_own, lower_own = lax.optimization_barrier((inv_own, lower_own))
     piece = shape((CHIP, BLOCK))
     low = call(
-        lower_pieces, [piece] * 4, lower, lower_peer,
+        lower_pieces, [piece] * 4, lower_own, lower_peer,
         scratch=[pltpu.VMEM((CHIP, N), BF16), pltpu.VMEM((4, CHIP, BLOCK), BF16)],
     )
+    inv = {0: inv_own, 1: send(inv_own, along_v(1)), 3: send(inv_own, along_v(3))}
     low = [low[0]] + [send(low[d], along_v(d)) for d in range(1, 4)]
     forcing_peer = to_peer(forcing)
     inflow_peer = to_peer(inflow)
+    inv, low = lax.optimization_barrier((inv, low))
+    inv[2] = send(inv[0], along_v(2))
+    inv = [inv[d] for d in range(4)]
     own = call(
         lower_block, shape((BLOCK + R, BLOCK)), *low, forcing, forcing_peer, inflow, inflow_peer,
         scratch=[pltpu.VMEM((CHIP, LANES), F32)],
     )
-    inverses, own = lax.optimization_barrier((inverses, own))
     panel = [own] + [send(own, along_u(d)) for d in range(1, 4)]
-    inverses_peer = to_peer(inverses)
-    inv = call(inverse_piece, shape((CHIP, N)), inverses, inverses_peer)
-    inv = [inv] + [send(inv, along_v(d)) for d in range(1, 4)]
 
     message = call(
         coupling_block, shape((BLOCK + 2 * R, BLOCK)), *inv, *panel,
@@ -265,27 +277,25 @@
     )
     turn = [message] + [send(message, across(d)) for d in range(1, 4)]
     turn_peer = [to_peer(value) for value in turn]
-    p_high, p_low, base = call(
-        product_block, [shape((BLOCK, BLOCK)), shape((BLOCK, BLOCK)), shape((R, BLOCK), F32)],
+    p_high, p_low, base, out = call(
+        product_block,
+        [shape((BLOCK, BLOCK)), shape((BLOCK, BLOCK)), shape((R, BLOCK), F32), shape((R, BLOCK))],
         *turn, *turn_peer,
         scratch=[pltpu.VMEM((BLOCK, N), BF16), pltpu.VMEM((N, BLOCK), BF16), pltpu.VMEM((N, LANES), BF16)],
         flops=2 * BLOCK * BLOCK * N,
     )
 
-    out = base
     for step in range(Z - 1):
         entry = hop(out)
         if step + 1 < Z - 1:
-            out = call(hop_block, shape((R, BLOCK), F32), *entry, p_high, p_low, base)
-    part = shape((2, ROWS, R), F32)
+            out = call(hop_block, shape((R, BLOCK)), *entry, p_high, p_low, base)
     finals = call(
-        final_block, [part] * 4, *entry, p_high, p_low, base, turn[0], turn_peer[0],
-        scratch=[pltpu.VMEM((2, BLOCK, R), F32)],
+        final_block, [shape((2 * R, ROWS), F32)] * 4, *entry, p_high, p_low, base, turn[0], turn_peer[0]
     )
     total = finals[0]
     for d in range(1, 4):
         total = total + send(finals[d], along_v(d))
-    return total
+    return jnp.swapaxes(total.reshape(2, R, ROWS), 1, 2)
 
 
 def solution(mesh):

time: 100 us -> 101 us (1.010)
  starting transfers between devices: 41.5 us -> 47.1 us
  waiting for transfers between devices: 51.3 us -> 47.4 us
  local copies, waits for them, and re-layouts: 2.43 us -> 0.98 us
    ppermute x35 -> x32, starting transfers between devices: 41.5 us -> 47.1 us  [send(): return lax.ppermute(value, AXES, pairs)]
    ppermute x35 -> x32, waiting for transfers between devices: 51.3 us -> 47.4 us  [send(): return lax.ppermute(value, AXES, pairs)]
    pallas_call x8 -> x12, Pallas kernels: 4.71 us -> 4.73 us  [call(): pl.pallas_call(kernel, out_shape=out, in_specs=[pl.BlockSpec(memory_space...]
  transfers between devices with their start and end apart: 35 -> 32, of which waited for: 24 -> 24; matrix products, arithmetic and copies ran while one was open for 0% -> 0% of each run, Pallas kernels for 0% -> 0%
where the time goes in v4:
time: 101 us
  waiting for transfers between devices  47.4 us (47%)
  starting transfers between devices  47.1 us (47%)
  Pallas kernels  4.73 us (5%)
    ppermute x32, waiting for transfers between devices, send(): return lax.ppermute(value, AXES, pairs)  47.4 us
    ppermute x32, starting transfers between devices, send(): return lax.ppermute(value, AXES, pairs)  47.1 us
    pallas_call x12, Pallas kernels, call(): pl.pallas_call(kernel, out_shape=out, in_specs=[pl.BlockSpec(memory_space...  4.73 us
  transfers between devices with their start and end apart: 32, of which 24 were waited for; matrix products, arithmetic and copies ran while one was open for 0% of the time, Pallas kernels for 0%

profile of v4, /device:TPU:56, one launch (start us, length us, event | category | flops | bytes accessed | tf_op | source)
XLA Modules:
  0.0 101.0 jit_solution(4139794883908858231)
XLA Ops:
  2.7 2.5 %collective-permute-start.1 = (bf16[96,1536]{1,0:T(8,128)(2,1)S(1)}, bf16[96,1536]{1,0:T(8,128)(2,1)S(1)}, u32[]{:S(2)}, u32[]{:S(2)}) collective-permute-start(bf16[96,1536]{1,0:T(8,128)(2,1)S(1)} %shard_map.46.a0), channel_id=1, source_target_pairs={{0,8},{1,33},{2,10},{3,35},{4,12},{5,37},{6,14},{7,39},{8,16},{9,4... | collective-permute-start | bytes 884744 | tf_op jit(solution)/shard_map/ppermute | solution.py:32
  5.3 1.6 %collective-permute-start.5 = (bf16[96,384]{1,0:T(8,128)(2,1)S(1)}, bf16[96,384]{1,0:T(8,128)(2,1)S(1)}, u32[]{:S(2)}, u32[]{:S(2)}) collective-permute-start(bf16[96,384]{1,0:T(8,128)(2,1)S(1)} %get-tuple-element.30), channel_id=1, source_target_pairs={{0,16},{1,65},{2,18},{3,67},{4,20},{5,69},{6,22},{7,71},{8,24},{9,... | collective-permute-start | bytes 221192 | tf_op jit(solution)/shard_map/ppermute | solution.py:32
  7.4 7.3 %collective-permute-done.4.p1 = bf16[96,384]{1,0:T(8,128)(2,1)S(1)} collective-permute-done((bf16[96,384]{1,0:T(8,128)(2,1)S(1)}, bf16[96,384]{1,0:T(8,128)(2,1)S(1)}, u32[]{:S(2)}, u32[]{:S(2)}) %collective-permute-start.4) | collective-permute-done | bytes 73760 | tf_op jit(solution)/shard_map/ppermute | solution.py:32
  16.1 2.8 %collective-permute-start.12 = (bf16[416,384]{1,0:T(8,128)(2,1)S(1)}, bf16[416,384]{1,0:T(8,128)(2,1)S(1)}, u32[]{:S(2)}, u32[]{:S(2)}) collective-permute-start(bf16[416,384]{1,0:T(8,128)(2,1)S(1)} %shard_map.49.l0), channel_id=1, source_target_pairs={{0,96},{1,25},{2,98},{3,27},{4,100},{5,29},{6,102},{7,31},{8,104},... | collective-permute-start | bytes 958472 | tf_op jit(solution)/shard_map/ppermute | solution.py:32
  20.6 1.4 %collective-permute-start.7 = (bf16[96,1536]{1,0:T(8,128)(2,1)S(1)}, bf16[96,1536]{1,0:T(8,128)(2,1)S(1)}, u32[]{:S(2)}, u32[]{:S(2)}) collective-permute-start(bf16[96,1536]{1,0:T(8,128)(2,1)S(1)} %shard_map.46.a0), channel_id=1, source_target_pairs={{0,16},{1,65},{2,18},{3,67},{4,20},{5,69},{6,22},{7,71},{8,24},{9,... | collective-permute-start | bytes 884744 | tf_op jit(solution)/shard_map/ppermute | solution.py:32
  22.0 8.5 %collective-permute-done.7.a2 = bf16[96,1536]{1,0:T(8,128)(2,1)S(1)} collective-permute-done((bf16[96,1536]{1,0:T(8,128)(2,1)S(1)}, bf16[96,1536]{1,0:T(8,128)(2,1)S(1)}, u32[]{:S(2)}, u32[]{:S(2)}) %collective-permute-start.7) | collective-permute-done | bytes 294944 | tf_op jit(solution)/shard_map/ppermute | solution.py:32
  30.6 2.6 %collective-permute-done.12.l3 = bf16[416,384]{1,0:T(8,128)(2,1)S(1)} collective-permute-done((bf16[416,384]{1,0:T(8,128)(2,1)S(1)}, bf16[416,384]{1,0:T(8,128)(2,1)S(1)}, u32[]{:S(2)}, u32[]{:S(2)}) %collective-permute-start.12) | collective-permute-done | bytes 319520 | tf_op jit(solution)/shard_map/ppermute | solution.py:32
  33.1 3.7 %collective-permute-done.10.l1 = bf16[416,384]{1,0:T(8,128)(2,1)S(1)} collective-permute-done((bf16[416,384]{1,0:T(8,128)(2,1)S(1)}, bf16[416,384]{1,0:T(8,128)(2,1)S(1)}, u32[]{:S(2)}, u32[]{:S(2)}) %collective-permute-start.10) | collective-permute-done | bytes 319520 | tf_op jit(solution)/shard_map/ppermute | solution.py:32
  36.8 1.6 %shard_map.50.o0.message = bf16[448,384]{1,0:T(8,128)(2,1)S(1)} custom-call(bf16[96,1536]{1,0:T(8,128)(2,1)S(1)} %shard_map.46.a0, bf16[96,1536]{1,0:T(8,128)(2,1)S(1)} %collective-permute-done.1.a1, bf16[96,1536]{1,0:T(8,128)(2,1)S(1)} %collective-permute-done.7.a2, bf16[96,1536]{1,0:T(8,128)(2,1)S(1)} %collective-permute-done.2.a3, ...), custom_call_target="tpu_custom_call" | custom-call | flops 452984832 | bytes 2457600 | tf_op jit(solution)/shard_map/pallas_call | solution.py:76
  40.7 2.4 %collective-permute-start.16 = (bf16[448,384]{1,0:T(8,128)(2,1)S(1)}, bf16[448,384]{1,0:T(8,128)(2,1)S(1)}, u32[]{:S(2)}, u32[]{:S(2)}) collective-permute-start(bf16[448,384]{1,0:T(8,128)(2,1)S(1)} %shard_map.50.o0.message), channel_id=1, source_target_pairs={{0,4},{1,5},{2,6},{3,7},{4,0},{5,1},{6,2},{7,3},{8,12},{9,13},{10,... | collective-permute-start | bytes 1032200 | tf_op jit(solution)/shard_map/ppermute | solution.py:32
  43.0 2.7 %collective-permute-done.15.o3 = bf16[448,384]{1,0:T(8,128)(2,1)S(1)} collective-permute-done((bf16[448,384]{1,0:T(8,128)(2,1)S(1)}, bf16[448,384]{1,0:T(8,128)(2,1)S(1)}, u32[]{:S(2)}, u32[]{:S(2)}) %collective-permute-start.15) | collective-permute-done | bytes 344096 | tf_op jit(solution)/shard_map/ppermute | solution.py:32
  45.7 1.1 %collective-permute-start.19 = (bf16[448,384]{1,0:T(8,128)(2,1)S(1)}, bf16[448,384]{1,0:T(8,128)(2,1)S(1)}, u32[]{:S(2)}, u32[]{:S(2)}) collective-permute-start(bf16[448,384]{1,0:T(8,128)(2,1)S(1)} %collective-permute-done.15.o3), channel_id=1, source_target_pairs={{0,4},{1,5},{2,6},{3,7},{4,0},{5,1},{6,2},{7,3},{8,12},{9,13},{10,... | collective-permute-start | bytes 1032200 | tf_op jit(solution)/shard_map/ppermute | solution.py:32
  46.8 1.1 %collective-permute-done.14.o2 = bf16[448,384]{1,0:T(8,128)(2,1)S(1)} collective-permute-done((bf16[448,384]{1,0:T(8,128)(2,1)S(1)}, bf16[448,384]{1,0:T(8,128)(2,1)S(1)}, u32[]{:S(2)}, u32[]{:S(2)}) %collective-permute-start.14) | collective-permute-done | bytes 344096 | tf_op jit(solution)/shard_map/ppermute | solution.py:32
  47.9 3.4 %collective-permute-start.18 = (bf16[448,384]{1,0:T(8,128)(2,1)S(1)}, bf16[448,384]{1,0:T(8,128)(2,1)S(1)}, u32[]{:S(2)}, u32[]{:S(2)}) collective-permute-start(bf16[448,384]{1,0:T(8,128)(2,1)S(1)} %collective-permute-done.14.o2), channel_id=1, source_target_pairs={{0,4},{1,5},{2,6},{3,7},{4,0},{5,1},{6,2},{7,3},{8,12},{9,13},{10,... | collective-permute-start | bytes 1032200 | tf_op jit(solution)/shard_map/ppermute | solution.py:32
  51.5 1.1 %collective-permute-done.18.p2 = bf16[448,384]{1,0:T(8,128)(2,1)S(1)} collective-permute-done((bf16[448,384]{1,0:T(8,128)(2,1)S(1)}, bf16[448,384]{1,0:T(8,128)(2,1)S(1)}, u32[]{:S(2)}, u32[]{:S(2)}) %collective-permute-start.18) | collective-permute-done | bytes 344096 | tf_op jit(solution)/shard_map/ppermute | solution.py:32
  53.2 1.4 %shard_map.51 = (bf16[384,384]{1,0:T(8,128)(2,1)S(1)}, bf16[384,384]{1,0:T(8,128)(2,1)S(1)}, f32[32,384]{1,0:T(8,128)S(1)}, bf16[32,384]{1,0:T(8,128)(2,1)S(1)}) custom-call(bf16[448,384]{1,0:T(8,128)(2,1)S(1)} %shard_map.50.o0.message, bf16[448,384]{1,0:T(8,128)(2,1)S(1)} %collective-permute-done.13.o1, bf16[448,384]{1,0:T(8,128)(2,1)S(1)} %collective-permute-done.14.o2, ...), custom_call_target="tpu_custom_call" | custom-call | flops 452984832 | bytes 2752512 | tf_op jit(solution)/shard_map/pallas_call | solution.py:76
  54.6 5.5 %collective-permute-start.21 = (bf16[32,384]{1,0:T(8,128)(2,1)S(1)}, bf16[32,384]{1,0:T(8,128)(2,1)S(1)}, u32[]{:S(2)}, u32[]{:S(2)}) collective-permute-start(bf16[32,384]{1,0:T(8,128)(2,1)S(1)} %get-tuple-element.39), channel_id=1, source_target_pairs={{0,17},{1,66},{2,19},{4,29},{5,102},{6,31},{8,25},{9,74},{10,27},{... | collective-permute-start | bytes 73736 | tf_op jit(solution)/shard_map/ppermute | solution.py:32
  60.1 2.1 %collective-permute-start.20 = (bf16[32,384]{1,0:T(8,128)(2,1)S(1)}, bf16[32,384]{1,0:T(8,128)(2,1)S(1)}, u32[]{:S(2)}, u32[]{:S(2)}) collective-permute-start(bf16[32,384]{1,0:T(8,128)(2,1)S(1)} %get-tuple-element.39), channel_id=1, source_target_pairs={{0,1},{1,2},{2,3},{4,13},{5,38},{6,15},{8,9},{9,10},{10,11},{12,21... | collective-permute-start | bytes 73736 | tf_op jit(solution)/shard_map/ppermute | solution.py:32
  62.7 3.1 %collective-permute-done.20.r0 = bf16[32,384]{1,0:T(8,128)(2,1)S(1)} collective-permute-done((bf16[32,384]{1,0:T(8,128)(2,1)S(1)}, bf16[32,384]{1,0:T(8,128)(2,1)S(1)}, u32[]{:S(2)}, u32[]{:S(2)}) %collective-permute-start.20) | collective-permute-done | bytes 24608 | tf_op jit(solution)/shard_map/ppermute | solution.py:32
  66.1 1.0 %collective-permute-done.22.peer = f32[32,384]{1,0:T(8,128)S(1)} collective-permute-done((f32[32,384]{1,0:T(8,128)S(1)}, f32[32,384]{1,0:T(8,128)S(1)}, u32[]{:S(2)}, u32[]{:S(2)}) %collective-permute-start.22) | collective-permute-done | bytes 49184 | tf_op jit(solution)/shard_map/ppermute | solution.py:32
  67.6 4.1 %collective-permute-start.24 = (bf16[32,384]{1,0:T(8,128)(2,1)S(1)}, bf16[32,384]{1,0:T(8,128)(2,1)S(1)}, u32[]{:S(2)}, u32[]{:S(2)}) collective-permute-start(bf16[32,384]{1,0:T(8,128)(2,1)S(1)} %shard_map.53), channel_id=1, source_target_pairs={{0,17},{1,66},{2,19},{4,29},{5,102},{6,31},{8,25},{9,74},{10,27},{... | collective-permute-start | bytes 73736 | tf_op jit(solution)/shard_map/ppermute | solution.py:32
  71.7 2.0 %collective-permute-start.23 = (bf16[32,384]{1,0:T(8,128)(2,1)S(1)}, bf16[32,384]{1,0:T(8,128)(2,1)S(1)}, u32[]{:S(2)}, u32[]{:S(2)}) collective-permute-start(bf16[32,384]{1,0:T(8,128)(2,1)S(1)} %shard_map.53), channel_id=1, source_target_pairs={{0,1},{1,2},{2,3},{4,13},{5,38},{6,15},{8,9},{9,10},{10,11},{12,21... | collective-permute-start | bytes 73736 | tf_op jit(solution)/shard_map/ppermute | solution.py:32
  73.7 2.0 %collective-permute-done.24.r1 = bf16[32,384]{1,0:T(8,128)(2,1)S(1)} collective-permute-done((bf16[32,384]{1,0:T(8,128)(2,1)S(1)}, bf16[32,384]{1,0:T(8,128)(2,1)S(1)}, u32[]{:S(2)}, u32[]{:S(2)}) %collective-permute-start.24) | collective-permute-done | bytes 24608 | tf_op jit(solution)/shard_map/ppermute | solution.py:32
  75.7 1.7 %collective-permute-done.23.r0 = bf16[32,384]{1,0:T(8,128)(2,1)S(1)} collective-permute-done((bf16[32,384]{1,0:T(8,128)(2,1)S(1)}, bf16[32,384]{1,0:T(8,128)(2,1)S(1)}, u32[]{:S(2)}, u32[]{:S(2)}) %collective-permute-start.23) | collective-permute-done | bytes 24608 | tf_op jit(solution)/shard_map/ppermute | solution.py:32
  79.1 3.0 %collective-permute-start.27 = (bf16[32,384]{1,0:T(8,128)(2,1)S(1)}, bf16[32,384]{1,0:T(8,128)(2,1)S(1)}, u32[]{:S(2)}, u32[]{:S(2)}) collective-permute-start(bf16[32,384]{1,0:T(8,128)(2,1)S(1)} %shard_map.55), channel_id=1, source_target_pairs={{0,17},{1,66},{2,19},{4,29},{5,102},{6,31},{8,25},{9,74},{10,27},{... | collective-permute-start | bytes 73736 | tf_op jit(solution)/shard_map/ppermute | solution.py:32
  82.1 1.9 %collective-permute-start.26 = (bf16[32,384]{1,0:T(8,128)(2,1)S(1)}, bf16[32,384]{1,0:T(8,128)(2,1)S(1)}, u32[]{:S(2)}, u32[]{:S(2)}) collective-permute-start(bf16[32,384]{1,0:T(8,128)(2,1)S(1)} %shard_map.55), channel_id=1, source_target_pairs={{0,1},{1,2},{2,3},{4,13},{5,38},{6,15},{8,9},{9,10},{10,11},{12,21... | collective-permute-start | bytes 73736 | tf_op jit(solution)/shard_map/ppermute | solution.py:32
  84.1 3.2 %collective-permute-done.27.r1 = bf16[32,384]{1,0:T(8,128)(2,1)S(1)} collective-permute-done((bf16[32,384]{1,0:T(8,128)(2,1)S(1)}, bf16[32,384]{1,0:T(8,128)(2,1)S(1)}, u32[]{:S(2)}, u32[]{:S(2)}) %collective-permute-start.27) | collective-permute-done | bytes 24608 | tf_op jit(solution)/shard_map/ppermute | solution.py:32
  87.9 1.9 %collective-permute-start.28 = (f32[32,384]{1,0:T(8,128)S(1)}, f32[32,384]{1,0:T(8,128)S(1)}, u32[]{:S(2)}, u32[]{:S(2)}) collective-permute-start(f32[32,384]{1,0:T(8,128)S(1)} %shard_map.56.own), channel_id=1, source_target_pairs={{0,4},{1,5},{2,6},{3,7},{4,0},{5,1},{6,2},{7,3},{8,12},{9,13},{10,... | collective-permute-start | bytes 147464 | tf_op jit(solution)/shard_map/ppermute | solution.py:32
  91.3 2.2 %collective-permute-start.29 = (f32[64,48]{1,0:T(8,128)S(1)}, f32[64,48]{1,0:T(8,128)S(1)}, u32[]{:S(2)}, u32[]{:S(2)}) collective-permute-start(f32[64,48]{1,0:T(8,128)S(1)} %get-tuple-element.44), channel_id=1, source_target_pairs={{0,8},{1,33},{2,10},{3,35},{4,12},{5,37},{6,14},{7,39},{8,16},{9,4... | collective-permute-start | bytes 36872 | tf_op jit(solution)/shard_map/ppermute | solution.py:32
  93.6 1.7 %collective-permute-start.30 = (f32[64,48]{1,0:T(8,128)S(1)}, f32[64,48]{1,0:T(8,128)S(1)}, u32[]{:S(2)}, u32[]{:S(2)}) collective-permute-start(f32[64,48]{1,0:T(8,128)S(1)} %get-tuple-element.45), channel_id=1, source_target_pairs={{0,16},{1,65},{2,18},{3,67},{4,20},{5,69},{6,22},{7,71},{8,24},{9,... | collective-permute-start | bytes 36872 | tf_op jit(solution)/shard_map/ppermute | solution.py:32
  95.7 3.3 %collective-permute-done.30 = f32[64,48]{1,0:T(8,128)S(1)} collective-permute-done((f32[64,48]{1,0:T(8,128)S(1)}, f32[64,48]{1,0:T(8,128)S(1)}, u32[]{:S(2)}, u32[]{:S(2)}) %collective-permute-start.30) | collective-permute-done | bytes 12320 | tf_op jit(solution)/shard_map/ppermute | solution.py:32
  99.1 1.3 %collective-permute-done.31 = f32[64,48]{1,0:T(8,128)S(1)} collective-permute-done((f32[64,48]{1,0:T(8,128)S(1)}, f32[64,48]{1,0:T(8,128)S(1)}, u32[]{:S(2)}, u32[]{:S(2)}) %collective-permute-start.31) | collective-permute-done | bytes 12320 | tf_op jit(solution)/shard_map/ppermute | solution.py:32
  (53 shorter events, 15.5 us)
Async XLA Ops:
  0.0 1.8 %collective-permute-start = (bf16[2,48,1536]{2,1,0:T(8,128)(2,1)}, bf16[2,48,1536]{2,1,0:T(8,128)(2,1)S(1)}, u32[]{:S(2)}, u32[]{:S(2)}) collective-permute-start(bf16[2,48,1536]{2,1,0:T(8,128)(2,1)} %own.2), channel_id=1, source_target_pairs={{0,4},{1,5},{2,6},{3,7},{4,0},{5,1},{6,2},{7,3},{8,12},{9,13},{10,... | collective-permute-start | bytes 884744 | tf_op jit(solution)/shard_map/ppermute | solution.py:32
  0.0 5.2 %collective-permute-start.3 = (bf16[2,48,1536]{2,1,0:T(8,128)(2,1)}, bf16[2,48,1536]{2,1,0:T(8,128)(2,1)S(1)}, u32[]{:S(2)}, u32[]{:S(2)}) collective-permute-start(bf16[2,48,1536]{2,1,0:T(8,128)(2,1)} %own.3), channel_id=1, source_target_pairs={{0,4},{1,5},{2,6},{3,7},{4,0},{5,1},{6,2},{7,3},{8,12},{9,13},{10,... | collective-permute-start | bytes 884744 | tf_op jit(solution)/shard_map/ppermute | solution.py:32
  1.8 13.5 %collective-permute-start.2 = (bf16[96,1536]{1,0:T(8,128)(2,1)S(1)}, bf16[96,1536]{1,0:T(8,128)(2,1)S(1)}, u32[]{:S(2)}, u32[]{:S(2)}) collective-permute-start(bf16[96,1536]{1,0:T(8,128)(2,1)S(1)} %shard_map.46.a0), channel_id=1, source_target_pairs={{0,24},{1,97},{2,26},{3,99},{4,28},{5,101},{6,30},{7,103},{8,0},{9... | collective-permute-start | bytes 884744 | tf_op jit(solution)/shard_map/ppermute | solution.py:32
  2.7 12.7 %collective-permute-start.1 = (bf16[96,1536]{1,0:T(8,128)(2,1)S(1)}, bf16[96,1536]{1,0:T(8,128)(2,1)S(1)}, u32[]{:S(2)}, u32[]{:S(2)}) collective-permute-start(bf16[96,1536]{1,0:T(8,128)(2,1)S(1)} %shard_map.46.a0), channel_id=1, source_target_pairs={{0,8},{1,33},{2,10},{3,35},{4,12},{5,37},{6,14},{7,39},{8,16},{9,4... | collective-permute-start | bytes 884744 | tf_op jit(solution)/shard_map/ppermute | solution.py:32
  5.3 9.4 %collective-permute-start.4 = (bf16[96,384]{1,0:T(8,128)(2,1)S(1)}, bf16[96,384]{1,0:T(8,128)(2,1)S(1)}, u32[]{:S(2)}, u32[]{:S(2)}) collective-permute-start(bf16[96,384]{1,0:T(8,128)(2,1)S(1)} %get-tuple-element.29), channel_id=1, source_target_pairs={{0,8},{1,33},{2,10},{3,35},{4,12},{5,37},{6,14},{7,39},{8,16},{9,4... | collective-permute-start | bytes 221192 | tf_op jit(solution)/shard_map/ppermute | solution.py:32
  5.3 9.3 %collective-permute-start.5 = (bf16[96,384]{1,0:T(8,128)(2,1)S(1)}, bf16[96,384]{1,0:T(8,128)(2,1)S(1)}, u32[]{:S(2)}, u32[]{:S(2)}) collective-permute-start(bf16[96,384]{1,0:T(8,128)(2,1)S(1)} %get-tuple-element.30), channel_id=1, source_target_pairs={{0,16},{1,65},{2,18},{3,67},{4,20},{5,69},{6,22},{7,71},{8,24},{9,... | collective-permute-start | bytes 221192 | tf_op jit(solution)/shard_map/ppermute | solution.py:32
  6.9 8.4 %collective-permute-start.6 = (bf16[96,384]{1,0:T(8,128)(2,1)S(1)}, bf16[96,384]{1,0:T(8,128)(2,1)S(1)}, u32[]{:S(2)}, u32[]{:S(2)}) collective-permute-start(bf16[96,384]{1,0:T(8,128)(2,1)S(1)} %get-tuple-element.31), channel_id=1, source_target_pairs={{0,24},{1,97},{2,26},{3,99},{4,28},{5,101},{6,30},{7,103},{8,0},{9... | collective-permute-start | bytes 221192 | tf_op jit(solution)/shard_map/ppermute | solution.py:32
  14.6 1.2 %collective-permute-start.8 = (bf16[2,32,48]{2,1,0:T(8,128)(2,1)S(1)}, bf16[2,32,48]{2,1,0:T(8,128)(2,1)S(1)}, u32[]{:S(2)}, u32[]{:S(2)}) collective-permute-start(bf16[2,32,48]{2,1,0:T(8,128)(2,1)S(1)} %bitcast.5), channel_id=1, source_target_pairs={{0,4},{1,5},{2,6},{3,7},{4,0},{5,1},{6,2},{7,3},{8,12},{9,13},{10,... | collective-permute-start | bytes 18440 | tf_op jit(solution)/shard_map/ppermute | solution.py:32
  14.7 1.3 %collective-permute-start.9 = (f32[32,48]{1,0:T(8,128)S(1)}, f32[32,48]{1,0:T(8,128)S(1)}, u32[]{:S(2)}, u32[]{:S(2)}) collective-permute-start(f32[32,48]{1,0:T(8,128)S(1)} %bitcast.7), channel_id=1, source_target_pairs={{0,4},{1,5},{2,6},{3,7},{4,0},{5,1},{6,2},{7,3},{8,12},{9,13},{10,... | collective-permute-start | bytes 18440 | tf_op jit(solution)/shard_map/ppermute | solution.py:32
  16.1 17.0 %collective-permute-start.12 = (bf16[416,384]{1,0:T(8,128)(2,1)S(1)}, bf16[416,384]{1,0:T(8,128)(2,1)S(1)}, u32[]{:S(2)}, u32[]{:S(2)}) collective-permute-start(bf16[416,384]{1,0:T(8,128)(2,1)S(1)} %shard_map.49.l0), channel_id=1, source_target_pairs={{0,96},{1,25},{2,98},{3,27},{4,100},{5,29},{6,102},{7,31},{8,104},... | collective-permute-start | bytes 958472 | tf_op jit(solution)/shard_map/ppermute | solution.py:32
  19.0 14.2 %collective-permute-start.11 = (bf16[416,384]{1,0:T(8,128)(2,1)S(1)}, bf16[416,384]{1,0:T(8,128)(2,1)S(1)}, u32[]{:S(2)}, u32[]{:S(2)}) collective-permute-start(bf16[416,384]{1,0:T(8,128)(2,1)S(1)} %shard_map.49.l0), channel_id=1, source_target_pairs={{0,64},{1,17},{2,66},{3,19},{4,68},{5,21},{6,70},{7,23},{8,72},{9,... | collective-permute-start | bytes 958472 | tf_op jit(solution)/shard_map/ppermute | solution.py:32
  19.8 17.1 %collective-permute-start.10 = (bf16[416,384]{1,0:T(8,128)(2,1)S(1)}, bf16[416,384]{1,0:T(8,128)(2,1)S(1)}, u32[]{:S(2)}, u32[]{:S(2)}) collective-permute-start(bf16[416,384]{1,0:T(8,128)(2,1)S(1)} %shard_map.49.l0), channel_id=1, source_target_pairs={{0,32},{1,9},{2,34},{3,11},{4,36},{5,13},{6,38},{7,15},{8,40},{9,1... | collective-permute-start | bytes 958472 | tf_op jit(solution)/shard_map/ppermute | solution.py:32
  20.6 9.9 %collective-permute-start.7 = (bf16[96,1536]{1,0:T(8,128)(2,1)S(1)}, bf16[96,1536]{1,0:T(8,128)(2,1)S(1)}, u32[]{:S(2)}, u32[]{:S(2)}) collective-permute-start(bf16[96,1536]{1,0:T(8,128)(2,1)S(1)} %shard_map.46.a0), channel_id=1, source_target_pairs={{0,16},{1,65},{2,18},{3,67},{4,20},{5,69},{6,22},{7,71},{8,24},{9,... | collective-permute-start | bytes 884744 | tf_op jit(solution)/shard_map/ppermute | solution.py:32
  38.4 7.3 %collective-permute-start.15 = (bf16[448,384]{1,0:T(8,128)(2,1)S(1)}, bf16[448,384]{1,0:T(8,128)(2,1)S(1)}, u32[]{:S(2)}, u32[]{:S(2)}) collective-permute-start(bf16[448,384]{1,0:T(8,128)(2,1)S(1)} %shard_map.50.o0.message), channel_id=1, source_target_pairs={{0,96},{1,25},{2,98},{3,27},{4,28},{5,101},{6,30},{7,103},{8,104},... | collective-permute-start | bytes 1032200 | tf_op jit(solution)/shard_map/ppermute | solution.py:32
  39.1 8.9 %collective-permute-start.14 = (bf16[448,384]{1,0:T(8,128)(2,1)S(1)}, bf16[448,384]{1,0:T(8,128)(2,1)S(1)}, u32[]{:S(2)}, u32[]{:S(2)}) collective-permute-start(bf16[448,384]{1,0:T(8,128)(2,1)S(1)} %shard_map.50.o0.message), channel_id=1, source_target_pairs={{0,64},{1,17},{2,66},{3,19},{4,20},{5,69},{6,22},{7,71},{8,72},{9,... | collective-permute-start | bytes 1032200 | tf_op jit(solution)/shard_map/ppermute | solution.py:32
  39.9 11.6 %collective-permute-start.13 = (bf16[448,384]{1,0:T(8,128)(2,1)S(1)}, bf16[448,384]{1,0:T(8,128)(2,1)S(1)}, u32[]{:S(2)}, u32[]{:S(2)}) collective-permute-start(bf16[448,384]{1,0:T(8,128)(2,1)S(1)} %shard_map.50.o0.message), channel_id=1, source_target_pairs={{0,32},{1,9},{2,34},{3,11},{4,12},{5,37},{6,14},{7,39},{8,40},{9,1... | collective-permute-start | bytes 1032200 | tf_op jit(solution)/shard_map/ppermute | solution.py:32
  40.7 10.8 %collective-permute-start.16 = (bf16[448,384]{1,0:T(8,128)(2,1)S(1)}, bf16[448,384]{1,0:T(8,128)(2,1)S(1)}, u32[]{:S(2)}, u32[]{:S(2)}) collective-permute-start(bf16[448,384]{1,0:T(8,128)(2,1)S(1)} %shard_map.50.o0.message), channel_id=1, source_target_pairs={{0,4},{1,5},{2,6},{3,7},{4,0},{5,1},{6,2},{7,3},{8,12},{9,13},{10,... | collective-permute-start | bytes 1032200 | tf_op jit(solution)/shard_map/ppermute | solution.py:32
  45.7 5.8 %collective-permute-start.19 = (bf16[448,384]{1,0:T(8,128)(2,1)S(1)}, bf16[448,384]{1,0:T(8,128)(2,1)S(1)}, u32[]{:S(2)}, u32[]{:S(2)}) collective-permute-start(bf16[448,384]{1,0:T(8,128)(2,1)S(1)} %collective-permute-done.15.o3), channel_id=1, source_target_pairs={{0,4},{1,5},{2,6},{3,7},{4,0},{5,1},{6,2},{7,3},{8,12},{9,13},{10,... | collective-permute-start | bytes 1032200 | tf_op jit(solution)/shard_map/ppermute | solution.py:32
  47.9 4.7 %collective-permute-start.18 = (bf16[448,384]{1,0:T(8,128)(2,1)S(1)}, bf16[448,384]{1,0:T(8,128)(2,1)S(1)}, u32[]{:S(2)}, u32[]{:S(2)}) collective-permute-start(bf16[448,384]{1,0:T(8,128)(2,1)S(1)} %collective-permute-done.14.o2), channel_id=1, source_target_pairs={{0,4},{1,5},{2,6},{3,7},{4,0},{5,1},{6,2},{7,3},{8,12},{9,13},{10,... | collective-permute-start | bytes 1032200 | tf_op jit(solution)/shard_map/ppermute | solution.py:32
  51.5 1.7 %collective-permute-start.17 = (bf16[448,384]{1,0:T(8,128)(2,1)S(1)}, bf16[448,384]{1,0:T(8,128)(2,1)S(1)}, u32[]{:S(2)}, u32[]{:S(2)}) collective-permute-start(bf16[448,384]{1,0:T(8,128)(2,1)S(1)} %collective-permute-done.13.o1), channel_id=1, source_target_pairs={{0,4},{1,5},{2,6},{3,7},{4,0},{5,1},{6,2},{7,3},{8,12},{9,13},{10,... | collective-permute-start | bytes 1032200 | tf_op jit(solution)/shard_map/ppermute | solution.py:32
  54.6 8.1 %collective-permute-start.21 = (bf16[32,384]{1,0:T(8,128)(2,1)S(1)}, bf16[32,384]{1,0:T(8,128)(2,1)S(1)}, u32[]{:S(2)}, u32[]{:S(2)}) collective-permute-start(bf16[32,384]{1,0:T(8,128)(2,1)S(1)} %get-tuple-element.39), channel_id=1, source_target_pairs={{0,17},{1,66},{2,19},{4,29},{5,102},{6,31},{8,25},{9,74},{10,27},{... | collective-permute-start | bytes 73736 | tf_op jit(solution)/shard_map/ppermute | solution.py:32
  60.1 5.7 %collective-permute-start.20 = (bf16[32,384]{1,0:T(8,128)(2,1)S(1)}, bf16[32,384]{1,0:T(8,128)(2,1)S(1)}, u32[]{:S(2)}, u32[]{:S(2)}) collective-permute-start(bf16[32,384]{1,0:T(8,128)(2,1)S(1)} %get-tuple-element.39), channel_id=1, source_target_pairs={{0,1},{1,2},{2,3},{4,13},{5,38},{6,15},{8,9},{9,10},{10,11},{12,21... | collective-permute-start | bytes 73736 | tf_op jit(solution)/shard_map/ppermute | solution.py:32
  65.9 1.3 %collective-permute-start.22 = (f32[32,384]{1,0:T(8,128)S(1)}, f32[32,384]{1,0:T(8,128)S(1)}, u32[]{:S(2)}, u32[]{:S(2)}) collective-permute-start(f32[32,384]{1,0:T(8,128)S(1)} %shard_map.52.own), channel_id=1, source_target_pairs={{0,4},{1,5},{2,6},{3,7},{4,0},{5,1},{6,2},{7,3},{8,12},{9,13},{10,... | collective-permute-start | bytes 147464 | tf_op jit(solution)/shard_map/ppermute | solution.py:32
  67.6 8.1 %collective-permute-start.24 = (bf16[32,384]{1,0:T(8,128)(2,1)S(1)}, bf16[32,384]{1,0:T(8,128)(2,1)S(1)}, u32[]{:S(2)}, u32[]{:S(2)}) collective-permute-start(bf16[32,384]{1,0:T(8,128)(2,1)S(1)} %shard_map.53), channel_id=1, source_target_pairs={{0,17},{1,66},{2,19},{4,29},{5,102},{6,31},{8,25},{9,74},{10,27},{... | collective-permute-start | bytes 73736 | tf_op jit(solution)/shard_map/ppermute | solution.py:32
  71.7 5.7 %collective-permute-start.23 = (bf16[32,384]{1,0:T(8,128)(2,1)S(1)}, bf16[32,384]{1,0:T(8,128)(2,1)S(1)}, u32[]{:S(2)}, u32[]{:S(2)}) collective-permute-start(bf16[32,384]{1,0:T(8,128)(2,1)S(1)} %shard_map.53), channel_id=1, source_target_pairs={{0,1},{1,2},{2,3},{4,13},{5,38},{6,15},{8,9},{9,10},{10,11},{12,21... | collective-permute-start | bytes 73736 | tf_op jit(solution)/shard_map/ppermute | solution.py:32
  77.4 1.3 %collective-permute-start.25 = (f32[32,384]{1,0:T(8,128)S(1)}, f32[32,384]{1,0:T(8,128)S(1)}, u32[]{:S(2)}, u32[]{:S(2)}) collective-permute-start(f32[32,384]{1,0:T(8,128)S(1)} %shard_map.54.own), channel_id=1, source_target_pairs={{0,4},{1,5},{2,6},{3,7},{4,0},{5,1},{6,2},{7,3},{8,12},{9,13},{10,... | collective-permute-start | bytes 147464 | tf_op jit(solution)/shard_map/ppermute | solution.py:32
  79.1 8.1 %collective-permute-start.27 = (bf16[32,384]{1,0:T(8,128)(2,1)S(1)}, bf16[32,384]{1,0:T(8,128)(2,1)S(1)}, u32[]{:S(2)}, u32[]{:S(2)}) collective-permute-start(bf16[32,384]{1,0:T(8,128)(2,1)S(1)} %shard_map.55), channel_id=1, source_target_pairs={{0,17},{1,66},{2,19},{4,29},{5,102},{6,31},{8,25},{9,74},{10,27},{... | collective-permute-start | bytes 73736 | tf_op jit(solution)/shard_map/ppermute | solution.py:32
  82.1 5.7 %collective-permute-start.26 = (bf16[32,384]{1,0:T(8,128)(2,1)S(1)}, bf16[32,384]{1,0:T(8,128)(2,1)S(1)}, u32[]{:S(2)}, u32[]{:S(2)}) collective-permute-start(bf16[32,384]{1,0:T(8,128)(2,1)S(1)} %shard_map.55), channel_id=1, source_target_pairs={{0,1},{1,2},{2,3},{4,13},{5,38},{6,15},{8,9},{9,10},{10,11},{12,21... | collective-permute-start | bytes 73736 | tf_op jit(solution)/shard_map/ppermute | solution.py:32
  87.9 2.8 %collective-permute-start.28 = (f32[32,384]{1,0:T(8,128)S(1)}, f32[32,384]{1,0:T(8,128)S(1)}, u32[]{:S(2)}, u32[]{:S(2)}) collective-permute-start(f32[32,384]{1,0:T(8,128)S(1)} %shard_map.56.own), channel_id=1, source_target_pairs={{0,4},{1,5},{2,6},{3,7},{4,0},{5,1},{6,2},{7,3},{8,12},{9,13},{10,... | collective-permute-start | bytes 147464 | tf_op jit(solution)/shard_map/ppermute | solution.py:32
  91.3 4.4 %collective-permute-start.29 = (f32[64,48]{1,0:T(8,128)S(1)}, f32[64,48]{1,0:T(8,128)S(1)}, u32[]{:S(2)}, u32[]{:S(2)}) collective-permute-start(f32[64,48]{1,0:T(8,128)S(1)} %get-tuple-element.44), channel_id=1, source_target_pairs={{0,8},{1,33},{2,10},{3,35},{4,12},{5,37},{6,14},{7,39},{8,16},{9,4... | collective-permute-start | bytes 36872 | tf_op jit(solution)/shard_map/ppermute | solution.py:32
  93.6 5.5 %collective-permute-start.30 = (f32[64,48]{1,0:T(8,128)S(1)}, f32[64,48]{1,0:T(8,128)S(1)}, u32[]{:S(2)}, u32[]{:S(2)}) collective-permute-start(f32[64,48]{1,0:T(8,128)S(1)} %get-tuple-element.45), channel_id=1, source_target_pairs={{0,16},{1,65},{2,18},{3,67},{4,20},{5,69},{6,22},{7,71},{8,24},{9,... | collective-permute-start | bytes 36872 | tf_op jit(solution)/shard_map/ppermute | solution.py:32
  95.3 5.1 %collective-permute-start.31 = (f32[64,48]{1,0:T(8,128)S(1)}, f32[64,48]{1,0:T(8,128)S(1)}, u32[]{:S(2)}, u32[]{:S(2)}) collective-permute-start(f32[64,48]{1,0:T(8,128)S(1)} %get-tuple-element.46), channel_id=1, source_target_pairs={{0,24},{1,97},{2,26},{3,99},{4,28},{5,101},{6,30},{7,103},{8,0},{9... | collective-permute-start | bytes 36872 | tf_op jit(solution)/shard_map/ppermute | solution.py:32
  (4 other events, 28.4 us)

commit v5 on v4

--- a/solution.py
+++ b/solution.py
@@ -129,6 +129,12 @@
     out[rows_at((1 - c) * ROWS, ROWS), :] = peer[c]
 
 
+def inverse_panel(a0, a1, a2, a3, out):
+    v = place()[1]
+    for d, piece in enumerate((a0, a1, a2, a3)):
+        out[rows_at(behind(v, d) * CHIP, CHIP), :] = piece[...]
+
+
 def lower_block(p0, p1, p2, p3, forcing, forcing_peer, inflow, inflow_peer, out, sides):
     _, v, c, _ = place()
     for d, piece in enumerate((p0, p1, p2, p3)):
@@ -142,10 +148,8 @@
         out[BLOCK:, g * LANES:(g + 1) * LANES] = sides[g * R:(g + 1) * R, :].astype(BF16)
 
 
-def coupling_block(a0, a1, a2, a3, l0, l1, l2, l3, out, panel, lower, sides, entry):
+def coupling_block(panel, l0, l1, l2, l3, out, lower, sides, entry):
     u, v, c, z = place()
-    for d, piece in enumerate((a0, a1, a2, a3)):
-        panel[rows_at(behind(v, d) * CHIP, CHIP), :] = piece[...]
     sides[...] = jnp.zeros_like(sides)
     for d, piece in enumerate((l0, l1, l2, l3)):
         from_u = behind(u, d)
@@ -248,30 +252,28 @@
     lower_peer = to_peer(lower)
     inv_own = call(inverse_piece, shape((CHIP, N)), inverses, inverses_peer)
     lower_own = call(hold, shape((ROWS, N)), lower)
-    inv_own, lower_own = lax.optimization_barrier((inv_own, lower_own))
     piece = shape((CHIP, BLOCK))
     low = call(
         lower_pieces, [piece] * 4, lower_own, lower_peer,
         scratch=[pltpu.VMEM((CHIP, N), BF16), pltpu.VMEM((4, CHIP, BLOCK), BF16)],
     )
-    inv = {0: inv_own, 1: send(inv_own, along_v(1)), 3: send(inv_own, along_v(3))}
     low = [low[0]] + [send(low[d], along_v(d)) for d in range(1, 4)]
     forcing_peer = to_peer(forcing)
     inflow_peer = to_peer(inflow)
-    inv, low = lax.optimization_barrier((inv, low))
-    inv[2] = send(inv[0], along_v(2))
-    inv = [inv[d] for d in range(4)]
+    inv_own, low = lax.optimization_barrier((inv_own, low))
     own = call(
         lower_block, shape((BLOCK + R, BLOCK)), *low, forcing, forcing_peer, inflow, inflow_peer,
         scratch=[pltpu.VMEM((CHIP, LANES), F32)],
     )
+    inv_own, own = lax.optimization_barrier((inv_own, own))
+    inv = [inv_own] + [send(inv_own, along_v(d)) for d in range(1, 4)]
+    inv_panel = call(inverse_panel, shape((BLOCK, N)), *inv)
     panel = [own] + [send(own, along_u(d)) for d in range(1, 4)]
 
     message = call(
-        coupling_block, shape((BLOCK + 2 * R, BLOCK)), *inv, *panel,
+        coupling_block, shape((BLOCK + 2 * R, BLOCK)), inv_panel, *panel,
         scratch=[
-            pltpu.VMEM((BLOCK, N), BF16), pltpu.VMEM((N, BLOCK), BF16),
-            pltpu.VMEM((N, LANES), BF16), pltpu.VMEM((BLOCK, LANES), BF16),
+            pltpu.VMEM((N, BLOCK), BF16), pltpu.VMEM((N, LANES), BF16), pltpu.VMEM((BLOCK, LANES), BF16),
         ],
         flops=2 * BLOCK * BLOCK * N,
     )

time: 101 us -> 96.8 us (0.958)
  the two profiles are of different devices: /device:TPU:56 before, /device:TPU:40 now
where the time goes in v5:
time: 96.8 us; the launch traced here: 96.5 us
  starting transfers between devices  46 us (48%)
  waiting for transfers between devices  43 us (44%)
  Pallas kernels  4.75 us (5%)
  local copies, waits for them, and re-layouts  1.93 us (2%)
    ppermute x32, starting transfers between devices, send(): return lax.ppermute(value, AXES, pairs)  46 us
    ppermute x32, waiting for transfers between devices, send(): return lax.ppermute(value, AXES, pairs)  43 us
    pallas_call x13, Pallas kernels, call(): pl.pallas_call(kernel, out_shape=out, in_specs=[pl.BlockSpec(memory_space...  4.75 us
  transfers between devices with their start and end apart: 32, of which 22 were waited for; matrix products, arithmetic and copies ran while one was open for 0% of the time, Pallas kernels for 0%

profile of v5, /device:TPU:40, one launch (start us, length us, event | category | flops | bytes accessed | tf_op | source)
XLA Modules:
  0.0 96.5 jit_solution(1585140175526806068)
XLA Ops:
  0.5 1.0 copy-done.1
  1.9 1.6 %collective-permute-start.2 = (bf16[96,384]{1,0:T(8,128)(2,1)S(1)}, bf16[96,384]{1,0:T(8,128)(2,1)S(1)}, u32[]{:S(2)}, u32[]{:S(2)}) collective-permute-start(bf16[96,384]{1,0:T(8,128)(2,1)S(1)} %get-tuple-element.25), channel_id=1, source_target_pairs={{0,8},{1,33},{2,10},{3,35},{4,12},{5,37},{6,14},{7,39},{8,16},{9,4... | collective-permute-start | bytes 221192 | tf_op jit(solution)/shard_map/ppermute | solution.py:32
  4.5 2.4 %collective-permute-start.4 = (bf16[96,384]{1,0:T(8,128)(2,1)S(1)}, bf16[96,384]{1,0:T(8,128)(2,1)S(1)}, u32[]{:S(2)}, u32[]{:S(2)}) collective-permute-start(bf16[96,384]{1,0:T(8,128)(2,1)S(1)} %get-tuple-element.27), channel_id=1, source_target_pairs={{0,24},{1,97},{2,26},{3,99},{4,28},{5,101},{6,30},{7,103},{8,0},{9... | collective-permute-start | bytes 221192 | tf_op jit(solution)/shard_map/ppermute | solution.py:32
  8.4 1.5 %collective-permute-done.3.p2 = bf16[96,384]{1,0:T(8,128)(2,1)S(1)} collective-permute-done((bf16[96,384]{1,0:T(8,128)(2,1)S(1)}, bf16[96,384]{1,0:T(8,128)(2,1)S(1)}, u32[]{:S(2)}, u32[]{:S(2)}) %collective-permute-start.3) | collective-permute-done | bytes 73760 | tf_op jit(solution)/shard_map/ppermute | solution.py:32
  10.1 1.4 %collective-permute-start.9 = (bf16[96,1536]{1,0:T(8,128)(2,1)S(1)}, bf16[96,1536]{1,0:T(8,128)(2,1)S(1)}, u32[]{:S(2)}, u32[]{:S(2)}) collective-permute-start(bf16[96,1536]{1,0:T(8,128)(2,1)S(1)} %shard_map.46.a0), channel_id=1, source_target_pairs={{0,24},{1,97},{2,26},{3,99},{4,28},{5,101},{6,30},{7,103},{8,0},{9... | collective-permute-start | bytes 884744 | tf_op jit(solution)/shard_map/ppermute | solution.py:32
  11.5 2.8 %collective-permute-start.12 = (bf16[416,384]{1,0:T(8,128)(2,1)S(1)}, bf16[416,384]{1,0:T(8,128)(2,1)S(1)}, u32[]{:S(2)}, u32[]{:S(2)}) collective-permute-start(bf16[416,384]{1,0:T(8,128)(2,1)S(1)} %shard_map.49.l0), channel_id=1, source_target_pairs={{0,96},{1,25},{2,98},{3,27},{4,100},{5,29},{6,102},{7,31},{8,104},... | collective-permute-start | bytes 958472 | tf_op jit(solution)/shard_map/ppermute | solution.py:32
  15.9 1.5 %collective-permute-start.8 = (bf16[96,1536]{1,0:T(8,128)(2,1)S(1)}, bf16[96,1536]{1,0:T(8,128)(2,1)S(1)}, u32[]{:S(2)}, u32[]{:S(2)}) collective-permute-start(bf16[96,1536]{1,0:T(8,128)(2,1)S(1)} %shard_map.46.a0), channel_id=1, source_target_pairs={{0,16},{1,65},{2,18},{3,67},{4,20},{5,69},{6,22},{7,71},{8,24},{9,... | collective-permute-start | bytes 884744 | tf_op jit(solution)/shard_map/ppermute | solution.py:32
  18.2 2.1 %collective-permute-start.7 = (bf16[96,1536]{1,0:T(8,128)(2,1)S(1)}, bf16[96,1536]{1,0:T(8,128)(2,1)S(1)}, u32[]{:S(2)}, u32[]{:S(2)}) collective-permute-start(bf16[96,1536]{1,0:T(8,128)(2,1)S(1)} %shard_map.46.a0), channel_id=1, source_target_pairs={{0,8},{1,33},{2,10},{3,35},{4,12},{5,37},{6,14},{7,39},{8,16},{9,4... | collective-permute-start | bytes 884744 | tf_op jit(solution)/shard_map/ppermute | solution.py:32
  20.3 4.8 %collective-permute-done.8.a2 = bf16[96,1536]{1,0:T(8,128)(2,1)S(1)} collective-permute-done((bf16[96,1536]{1,0:T(8,128)(2,1)S(1)}, bf16[96,1536]{1,0:T(8,128)(2,1)S(1)}, u32[]{:S(2)}, u32[]{:S(2)}) %collective-permute-start.8) | collective-permute-done | bytes 294944 | tf_op jit(solution)/shard_map/ppermute | solution.py:32
  25.1 4.8 %collective-permute-done.7.a1 = bf16[96,1536]{1,0:T(8,128)(2,1)S(1)} collective-permute-done((bf16[96,1536]{1,0:T(8,128)(2,1)S(1)}, bf16[96,1536]{1,0:T(8,128)(2,1)S(1)}, u32[]{:S(2)}, u32[]{:S(2)}) %collective-permute-start.7) | collective-permute-done | bytes 294944 | tf_op jit(solution)/shard_map/ppermute | solution.py:32
  30.3 1.5 %shard_map.51.o0.message = bf16[448,384]{1,0:T(8,128)(2,1)S(1)} custom-call(bf16[384,1536]{1,0:T(8,128)(2,1)S(1)} %shard_map.50.panel, bf16[416,384]{1,0:T(8,128)(2,1)S(1)} %shard_map.49.l0, bf16[416,384]{1,0:T(8,128)(2,1)S(1)} %collective-permute-done.10.l1, bf16[416,384]{1,0:T(8,128)(2,1)S(1)} %collective-permute-done.11.l2, ...), custom_call_target="tpu_custom_call" | custom-call | flops 452984832 | bytes 2457600 | tf_op jit(solution)/shard_map/pallas_call | solution.py:76
  31.8 2.6 %collective-permute-start.15 = (bf16[448,384]{1,0:T(8,128)(2,1)S(1)}, bf16[448,384]{1,0:T(8,128)(2,1)S(1)}, u32[]{:S(2)}, u32[]{:S(2)}) collective-permute-start(bf16[448,384]{1,0:T(8,128)(2,1)S(1)} %shard_map.51.o0.message), channel_id=1, source_target_pairs={{0,96},{1,25},{2,98},{3,27},{4,28},{5,101},{6,30},{7,103},{8,104},... | collective-permute-start | bytes 1032200 | tf_op jit(solution)/shard_map/ppermute | solution.py:32
  36.1 6.8 %collective-permute-done.15.o3 = bf16[448,384]{1,0:T(8,128)(2,1)S(1)} collective-permute-done((bf16[448,384]{1,0:T(8,128)(2,1)S(1)}, bf16[448,384]{1,0:T(8,128)(2,1)S(1)}, u32[]{:S(2)}, u32[]{:S(2)}) %collective-permute-start.15) | collective-permute-done | bytes 344096 | tf_op jit(solution)/shard_map/ppermute | solution.py:32
  43.4 3.4 %collective-permute-done.13.o1 = bf16[448,384]{1,0:T(8,128)(2,1)S(1)} collective-permute-done((bf16[448,384]{1,0:T(8,128)(2,1)S(1)}, bf16[448,384]{1,0:T(8,128)(2,1)S(1)}, u32[]{:S(2)}, u32[]{:S(2)}) %collective-permute-start.13) | collective-permute-done | bytes 344096 | tf_op jit(solution)/shard_map/ppermute | solution.py:32
  46.9 1.6 %collective-permute-done.17.p1 = bf16[448,384]{1,0:T(8,128)(2,1)S(1)} collective-permute-done((bf16[448,384]{1,0:T(8,128)(2,1)S(1)}, bf16[448,384]{1,0:T(8,128)(2,1)S(1)}, u32[]{:S(2)}, u32[]{:S(2)}) %collective-permute-start.17) | collective-permute-done | bytes 344096 | tf_op jit(solution)/shard_map/ppermute | solution.py:32
  48.5 1.4 %shard_map.52 = (bf16[384,384]{1,0:T(8,128)(2,1)S(1)}, bf16[384,384]{1,0:T(8,128)(2,1)S(1)}, f32[32,384]{1,0:T(8,128)S(1)}, bf16[32,384]{1,0:T(8,128)(2,1)S(1)}) custom-call(bf16[448,384]{1,0:T(8,128)(2,1)S(1)} %shard_map.51.o0.message, bf16[448,384]{1,0:T(8,128)(2,1)S(1)} %collective-permute-done.13.o1, bf16[448,384]{1,0:T(8,128)(2,1)S(1)} %collective-permute-done.14.o2, ...), custom_call_target="tpu_custom_call" | custom-call | flops 452984832 | bytes 2752512 | tf_op jit(solution)/shard_map/pallas_call | solution.py:76
  49.9 6.7 %collective-permute-start.21 = (bf16[32,384]{1,0:T(8,128)(2,1)S(1)}, bf16[32,384]{1,0:T(8,128)(2,1)S(1)}, u32[]{:S(2)}, u32[]{:S(2)}) collective-permute-start(bf16[32,384]{1,0:T(8,128)(2,1)S(1)} %get-tuple-element.35), channel_id=1, source_target_pairs={{0,17},{1,66},{2,19},{4,29},{5,102},{6,31},{8,25},{9,74},{10,27},{... | collective-permute-start | bytes 73736 | tf_op jit(solution)/shard_map/ppermute | solution.py:32
  56.7 1.9 %collective-permute-start.20 = (bf16[32,384]{1,0:T(8,128)(2,1)S(1)}, bf16[32,384]{1,0:T(8,128)(2,1)S(1)}, u32[]{:S(2)}, u32[]{:S(2)}) collective-permute-start(bf16[32,384]{1,0:T(8,128)(2,1)S(1)} %get-tuple-element.35), channel_id=1, source_target_pairs={{0,1},{1,2},{2,3},{4,13},{5,38},{6,15},{8,9},{9,10},{10,11},{12,21... | collective-permute-start | bytes 73736 | tf_op jit(solution)/shard_map/ppermute | solution.py:32
  58.6 3.8 %collective-permute-done.20.r0 = bf16[32,384]{1,0:T(8,128)(2,1)S(1)} collective-permute-done((bf16[32,384]{1,0:T(8,128)(2,1)S(1)}, bf16[32,384]{1,0:T(8,128)(2,1)S(1)}, u32[]{:S(2)}, u32[]{:S(2)}) %collective-permute-start.20) | collective-permute-done | bytes 24608 | tf_op jit(solution)/shard_map/ppermute | solution.py:32
  62.4 1.4 %collective-permute-start.22 = (f32[32,384]{1,0:T(8,128)S(1)}, f32[32,384]{1,0:T(8,128)S(1)}, u32[]{:S(2)}, u32[]{:S(2)}) collective-permute-start(f32[32,384]{1,0:T(8,128)S(1)} %shard_map.53.own), channel_id=1, source_target_pairs={{0,4},{1,5},{2,6},{3,7},{4,0},{5,1},{6,2},{7,3},{8,12},{9,13},{10,... | collective-permute-start | bytes 147464 | tf_op jit(solution)/shard_map/ppermute | solution.py:32
  65.1 3.9 %collective-permute-start.24 = (bf16[32,384]{1,0:T(8,128)(2,1)S(1)}, bf16[32,384]{1,0:T(8,128)(2,1)S(1)}, u32[]{:S(2)}, u32[]{:S(2)}) collective-permute-start(bf16[32,384]{1,0:T(8,128)(2,1)S(1)} %shard_map.54), channel_id=1, source_target_pairs={{0,17},{1,66},{2,19},{4,29},{5,102},{6,31},{8,25},{9,74},{10,27},{... | collective-permute-start | bytes 73736 | tf_op jit(solution)/shard_map/ppermute | solution.py:32
  68.9 1.9 %collective-permute-start.23 = (bf16[32,384]{1,0:T(8,128)(2,1)S(1)}, bf16[32,384]{1,0:T(8,128)(2,1)S(1)}, u32[]{:S(2)}, u32[]{:S(2)}) collective-permute-start(bf16[32,384]{1,0:T(8,128)(2,1)S(1)} %shard_map.54), channel_id=1, source_target_pairs={{0,1},{1,2},{2,3},{4,13},{5,38},{6,15},{8,9},{9,10},{10,11},{12,21... | collective-permute-start | bytes 73736 | tf_op jit(solution)/shard_map/ppermute | solution.py:32
  70.9 2.3 %collective-permute-done.24.r1 = bf16[32,384]{1,0:T(8,128)(2,1)S(1)} collective-permute-done((bf16[32,384]{1,0:T(8,128)(2,1)S(1)}, bf16[32,384]{1,0:T(8,128)(2,1)S(1)}, u32[]{:S(2)}, u32[]{:S(2)}) %collective-permute-start.24) | collective-permute-done | bytes 24608 | tf_op jit(solution)/shard_map/ppermute | solution.py:32
  73.2 1.5 %collective-permute-done.23.r0 = bf16[32,384]{1,0:T(8,128)(2,1)S(1)} collective-permute-done((bf16[32,384]{1,0:T(8,128)(2,1)S(1)}, bf16[32,384]{1,0:T(8,128)(2,1)S(1)}, u32[]{:S(2)}, u32[]{:S(2)}) %collective-permute-start.23) | collective-permute-done | bytes 24608 | tf_op jit(solution)/shard_map/ppermute | solution.py:32
  76.5 3.9 %collective-permute-start.27 = (bf16[32,384]{1,0:T(8,128)(2,1)S(1)}, bf16[32,384]{1,0:T(8,128)(2,1)S(1)}, u32[]{:S(2)}, u32[]{:S(2)}) collective-permute-start(bf16[32,384]{1,0:T(8,128)(2,1)S(1)} %shard_map.56), channel_id=1, source_target_pairs={{0,17},{1,66},{2,19},{4,29},{5,102},{6,31},{8,25},{9,74},{10,27},{... | collective-permute-start | bytes 73736 | tf_op jit(solution)/shard_map/ppermute | solution.py:32
  80.5 1.9 %collective-permute-start.26 = (bf16[32,384]{1,0:T(8,128)(2,1)S(1)}, bf16[32,384]{1,0:T(8,128)(2,1)S(1)}, u32[]{:S(2)}, u32[]{:S(2)}) collective-permute-start(bf16[32,384]{1,0:T(8,128)(2,1)S(1)} %shard_map.56), channel_id=1, source_target_pairs={{0,1},{1,2},{2,3},{4,13},{5,38},{6,15},{8,9},{9,10},{10,11},{12,21... | collective-permute-start | bytes 73736 | tf_op jit(solution)/shard_map/ppermute | solution.py:32
  82.4 2.3 %collective-permute-done.27.r1 = bf16[32,384]{1,0:T(8,128)(2,1)S(1)} collective-permute-done((bf16[32,384]{1,0:T(8,128)(2,1)S(1)}, bf16[32,384]{1,0:T(8,128)(2,1)S(1)}, u32[]{:S(2)}, u32[]{:S(2)}) %collective-permute-start.27) | collective-permute-done | bytes 24608 | tf_op jit(solution)/shard_map/ppermute | solution.py:32
  84.7 1.5 %collective-permute-done.26.r0 = bf16[32,384]{1,0:T(8,128)(2,1)S(1)} collective-permute-done((bf16[32,384]{1,0:T(8,128)(2,1)S(1)}, bf16[32,384]{1,0:T(8,128)(2,1)S(1)}, u32[]{:S(2)}, u32[]{:S(2)}) %collective-permute-start.26) | collective-permute-done | bytes 24608 | tf_op jit(solution)/shard_map/ppermute | solution.py:32
  86.4 1.2 %collective-permute-done.28.peer = f32[32,384]{1,0:T(8,128)S(1)} collective-permute-done((f32[32,384]{1,0:T(8,128)S(1)}, f32[32,384]{1,0:T(8,128)S(1)}, u32[]{:S(2)}, u32[]{:S(2)}) %collective-permute-start.28) | collective-permute-done | bytes 49184 | tf_op jit(solution)/shard_map/ppermute | solution.py:32
  88.9 3.1 %collective-permute-start.30 = (f32[64,48]{1,0:T(8,128)S(1)}, f32[64,48]{1,0:T(8,128)S(1)}, u32[]{:S(2)}, u32[]{:S(2)}) collective-permute-start(f32[64,48]{1,0:T(8,128)S(1)} %get-tuple-element.41), channel_id=1, source_target_pairs={{0,16},{1,65},{2,18},{3,67},{4,20},{5,69},{6,22},{7,71},{8,24},{9,... | collective-permute-start | bytes 36872 | tf_op jit(solution)/shard_map/ppermute | solution.py:32
  92.2 2.1 %collective-permute-done.30 = f32[64,48]{1,0:T(8,128)S(1)} collective-permute-done((f32[64,48]{1,0:T(8,128)S(1)}, f32[64,48]{1,0:T(8,128)S(1)}, u32[]{:S(2)}, u32[]{:S(2)}) %collective-permute-start.30) | collective-permute-done | bytes 12320 | tf_op jit(solution)/shard_map/ppermute | solution.py:32
  94.3 1.6 %collective-permute-done.31 = f32[64,48]{1,0:T(8,128)S(1)} collective-permute-done((f32[64,48]{1,0:T(8,128)S(1)}, f32[64,48]{1,0:T(8,128)S(1)}, u32[]{:S(2)}, u32[]{:S(2)}) %collective-permute-start.31) | collective-permute-done | bytes 12320 | tf_op jit(solution)/shard_map/ppermute | solution.py:32
  (54 shorter events, 14.2 us)
Async XLA Ops:
  0.0 1.8 %collective-permute-start.1 = (bf16[2,48,1536]{2,1,0:T(8,128)(2,1)}, bf16[2,48,1536]{2,1,0:T(8,128)(2,1)S(1)}, u32[]{:S(2)}, u32[]{:S(2)}) collective-permute-start(bf16[2,48,1536]{2,1,0:T(8,128)(2,1)} %own.3), channel_id=1, source_target_pairs={{0,4},{1,5},{2,6},{3,7},{4,0},{5,1},{6,2},{7,3},{8,12},{9,13},{10,... | collective-permute-start | bytes 884744 | tf_op jit(solution)/shard_map/ppermute | solution.py:32
  0.0 6.9 %collective-permute-start = (bf16[2,48,1536]{2,1,0:T(8,128)(2,1)}, bf16[2,48,1536]{2,1,0:T(8,128)(2,1)S(1)}, u32[]{:S(2)}, u32[]{:S(2)}) collective-permute-start(bf16[2,48,1536]{2,1,0:T(8,128)(2,1)} %own.2), channel_id=1, source_target_pairs={{0,4},{1,5},{2,6},{3,7},{4,0},{5,1},{6,2},{7,3},{8,12},{9,13},{10,... | collective-permute-start | bytes 884744 | tf_op jit(solution)/shard_map/ppermute | solution.py:32
  1.9 6.5 %collective-permute-start.2 = (bf16[96,384]{1,0:T(8,128)(2,1)S(1)}, bf16[96,384]{1,0:T(8,128)(2,1)S(1)}, u32[]{:S(2)}, u32[]{:S(2)}) collective-permute-start(bf16[96,384]{1,0:T(8,128)(2,1)S(1)} %get-tuple-element.25), channel_id=1, source_target_pairs={{0,8},{1,33},{2,10},{3,35},{4,12},{5,37},{6,14},{7,39},{8,16},{9,4... | collective-permute-start | bytes 221192 | tf_op jit(solution)/shard_map/ppermute | solution.py:32
  3.5 6.4 %collective-permute-start.3 = (bf16[96,384]{1,0:T(8,128)(2,1)S(1)}, bf16[96,384]{1,0:T(8,128)(2,1)S(1)}, u32[]{:S(2)}, u32[]{:S(2)}) collective-permute-start(bf16[96,384]{1,0:T(8,128)(2,1)S(1)} %get-tuple-element.26), channel_id=1, source_target_pairs={{0,16},{1,65},{2,18},{3,67},{4,20},{5,69},{6,22},{7,71},{8,24},{9,... | collective-permute-start | bytes 221192 | tf_op jit(solution)/shard_map/ppermute | solution.py:32
  4.5 5.5 %collective-permute-start.4 = (bf16[96,384]{1,0:T(8,128)(2,1)S(1)}, bf16[96,384]{1,0:T(8,128)(2,1)S(1)}, u32[]{:S(2)}, u32[]{:S(2)}) collective-permute-start(bf16[96,384]{1,0:T(8,128)(2,1)S(1)} %get-tuple-element.27), channel_id=1, source_target_pairs={{0,24},{1,97},{2,26},{3,99},{4,28},{5,101},{6,30},{7,103},{8,0},{9... | collective-permute-start | bytes 221192 | tf_op jit(solution)/shard_map/ppermute | solution.py:32
  6.9 3.1 %collective-permute-start.5 = (bf16[2,32,48]{2,1,0:T(8,128)(2,1)}, bf16[2,32,48]{2,1,0:T(8,128)(2,1)S(1)}, u32[]{:S(2)}, u32[]{:S(2)}) collective-permute-start(bf16[2,32,48]{2,1,0:T(8,128)(2,1)} %bitcast.5), channel_id=1, source_target_pairs={{0,4},{1,5},{2,6},{3,7},{4,0},{5,1},{6,2},{7,3},{8,12},{9,13},{10,... | collective-permute-start | bytes 18440 | tf_op jit(solution)/shard_map/ppermute | solution.py:32
  6.9 3.1 %collective-permute-start.6 = (f32[32,48]{1,0:T(8,128)}, f32[32,48]{1,0:T(8,128)S(1)}, u32[]{:S(2)}, u32[]{:S(2)}) collective-permute-start(f32[32,48]{1,0:T(8,128)} %bitcast.7), channel_id=1, source_target_pairs={{0,4},{1,5},{2,6},{3,7},{4,0},{5,1},{6,2},{7,3},{8,12},{9,13},{10,... | collective-permute-start | bytes 18440 | tf_op jit(solution)/shard_map/ppermute | solution.py:32
  10.1 8.1 %collective-permute-start.9 = (bf16[96,1536]{1,0:T(8,128)(2,1)S(1)}, bf16[96,1536]{1,0:T(8,128)(2,1)S(1)}, u32[]{:S(2)}, u32[]{:S(2)}) collective-permute-start(bf16[96,1536]{1,0:T(8,128)(2,1)S(1)} %shard_map.46.a0), channel_id=1, source_target_pairs={{0,24},{1,97},{2,26},{3,99},{4,28},{5,101},{6,30},{7,103},{8,0},{9... | collective-permute-start | bytes 884744 | tf_op jit(solution)/shard_map/ppermute | solution.py:32
  11.5 18.6 %collective-permute-start.12 = (bf16[416,384]{1,0:T(8,128)(2,1)S(1)}, bf16[416,384]{1,0:T(8,128)(2,1)S(1)}, u32[]{:S(2)}, u32[]{:S(2)}) collective-permute-start(bf16[416,384]{1,0:T(8,128)(2,1)S(1)} %shard_map.49.l0), channel_id=1, source_target_pairs={{0,96},{1,25},{2,98},{3,27},{4,100},{5,29},{6,102},{7,31},{8,104},... | collective-permute-start | bytes 958472 | tf_op jit(solution)/shard_map/ppermute | solution.py:32
  14.2 15.8 %collective-permute-start.11 = (bf16[416,384]{1,0:T(8,128)(2,1)S(1)}, bf16[416,384]{1,0:T(8,128)(2,1)S(1)}, u32[]{:S(2)}, u32[]{:S(2)}) collective-permute-start(bf16[416,384]{1,0:T(8,128)(2,1)S(1)} %shard_map.49.l0), channel_id=1, source_target_pairs={{0,64},{1,17},{2,66},{3,19},{4,68},{5,21},{6,70},{7,23},{8,72},{9,... | collective-permute-start | bytes 958472 | tf_op jit(solution)/shard_map/ppermute | solution.py:32
  15.0 15.3 %collective-permute-start.10 = (bf16[416,384]{1,0:T(8,128)(2,1)S(1)}, bf16[416,384]{1,0:T(8,128)(2,1)S(1)}, u32[]{:S(2)}, u32[]{:S(2)}) collective-permute-start(bf16[416,384]{1,0:T(8,128)(2,1)S(1)} %shard_map.49.l0), channel_id=1, source_target_pairs={{0,32},{1,9},{2,34},{3,11},{4,36},{5,13},{6,38},{7,15},{8,40},{9,1... | collective-permute-start | bytes 958472 | tf_op jit(solution)/shard_map/ppermute | solution.py:32
  15.9 9.2 %collective-permute-start.8 = (bf16[96,1536]{1,0:T(8,128)(2,1)S(1)}, bf16[96,1536]{1,0:T(8,128)(2,1)S(1)}, u32[]{:S(2)}, u32[]{:S(2)}) collective-permute-start(bf16[96,1536]{1,0:T(8,128)(2,1)S(1)} %shard_map.46.a0), channel_id=1, source_target_pairs={{0,16},{1,65},{2,18},{3,67},{4,20},{5,69},{6,22},{7,71},{8,24},{9,... | collective-permute-start | bytes 884744 | tf_op jit(solution)/shard_map/ppermute | solution.py:32
  18.2 11.8 %collective-permute-start.7 = (bf16[96,1536]{1,0:T(8,128)(2,1)S(1)}, bf16[96,1536]{1,0:T(8,128)(2,1)S(1)}, u32[]{:S(2)}, u32[]{:S(2)}) collective-permute-start(bf16[96,1536]{1,0:T(8,128)(2,1)S(1)} %shard_map.46.a0), channel_id=1, source_target_pairs={{0,8},{1,33},{2,10},{3,35},{4,12},{5,37},{6,14},{7,39},{8,16},{9,4... | collective-permute-start | bytes 884744 | tf_op jit(solution)/shard_map/ppermute | solution.py:32
  31.8 11.1 %collective-permute-start.15 = (bf16[448,384]{1,0:T(8,128)(2,1)S(1)}, bf16[448,384]{1,0:T(8,128)(2,1)S(1)}, u32[]{:S(2)}, u32[]{:S(2)}) collective-permute-start(bf16[448,384]{1,0:T(8,128)(2,1)S(1)} %shard_map.51.o0.message), channel_id=1, source_target_pairs={{0,96},{1,25},{2,98},{3,27},{4,28},{5,101},{6,30},{7,103},{8,104},... | collective-permute-start | bytes 1032200 | tf_op jit(solution)/shard_map/ppermute | solution.py:32
  34.4 8.9 %collective-permute-start.14 = (bf16[448,384]{1,0:T(8,128)(2,1)S(1)}, bf16[448,384]{1,0:T(8,128)(2,1)S(1)}, u32[]{:S(2)}, u32[]{:S(2)}) collective-permute-start(bf16[448,384]{1,0:T(8,128)(2,1)S(1)} %shard_map.51.o0.message), channel_id=1, source_target_pairs={{0,64},{1,17},{2,66},{3,19},{4,20},{5,69},{6,22},{7,71},{8,72},{9,... | collective-permute-start | bytes 1032200 | tf_op jit(solution)/shard_map/ppermute | solution.py:32
  35.2 11.6 %collective-permute-start.13 = (bf16[448,384]{1,0:T(8,128)(2,1)S(1)}, bf16[448,384]{1,0:T(8,128)(2,1)S(1)}, u32[]{:S(2)}, u32[]{:S(2)}) collective-permute-start(bf16[448,384]{1,0:T(8,128)(2,1)S(1)} %shard_map.51.o0.message), channel_id=1, source_target_pairs={{0,32},{1,9},{2,34},{3,11},{4,12},{5,37},{6,14},{7,39},{8,40},{9,1... | collective-permute-start | bytes 1032200 | tf_op jit(solution)/shard_map/ppermute | solution.py:32
  36.1 10.8 %collective-permute-start.16 = (bf16[448,384]{1,0:T(8,128)(2,1)S(1)}, bf16[448,384]{1,0:T(8,128)(2,1)S(1)}, u32[]{:S(2)}, u32[]{:S(2)}) collective-permute-start(bf16[448,384]{1,0:T(8,128)(2,1)S(1)} %shard_map.51.o0.message), channel_id=1, source_target_pairs={{0,4},{1,5},{2,6},{3,7},{4,0},{5,1},{6,2},{7,3},{8,12},{9,13},{10,... | collective-permute-start | bytes 1032200 | tf_op jit(solution)/shard_map/ppermute | solution.py:32
  42.9 4.0 %collective-permute-start.19 = (bf16[448,384]{1,0:T(8,128)(2,1)S(1)}, bf16[448,384]{1,0:T(8,128)(2,1)S(1)}, u32[]{:S(2)}, u32[]{:S(2)}) collective-permute-start(bf16[448,384]{1,0:T(8,128)(2,1)S(1)} %collective-permute-done.15.o3), channel_id=1, source_target_pairs={{0,4},{1,5},{2,6},{3,7},{4,0},{5,1},{6,2},{7,3},{8,12},{9,13},{10,... | collective-permute-start | bytes 1032200 | tf_op jit(solution)/shard_map/ppermute | solution.py:32
  43.3 3.6 %collective-permute-start.18 = (bf16[448,384]{1,0:T(8,128)(2,1)S(1)}, bf16[448,384]{1,0:T(8,128)(2,1)S(1)}, u32[]{:S(2)}, u32[]{:S(2)}) collective-permute-start(bf16[448,384]{1,0:T(8,128)(2,1)S(1)} %collective-permute-done.14.o2), channel_id=1, source_target_pairs={{0,4},{1,5},{2,6},{3,7},{4,0},{5,1},{6,2},{7,3},{8,12},{9,13},{10,... | collective-permute-start | bytes 1032200 | tf_op jit(solution)/shard_map/ppermute | solution.py:32
  46.8 1.7 %collective-permute-start.17 = (bf16[448,384]{1,0:T(8,128)(2,1)S(1)}, bf16[448,384]{1,0:T(8,128)(2,1)S(1)}, u32[]{:S(2)}, u32[]{:S(2)}) collective-permute-start(bf16[448,384]{1,0:T(8,128)(2,1)S(1)} %collective-permute-done.13.o1), channel_id=1, source_target_pairs={{0,4},{1,5},{2,6},{3,7},{4,0},{5,1},{6,2},{7,3},{8,12},{9,13},{10,... | collective-permute-start | bytes 1032200 | tf_op jit(solution)/shard_map/ppermute | solution.py:32
  49.9 8.7 %collective-permute-start.21 = (bf16[32,384]{1,0:T(8,128)(2,1)S(1)}, bf16[32,384]{1,0:T(8,128)(2,1)S(1)}, u32[]{:S(2)}, u32[]{:S(2)}) collective-permute-start(bf16[32,384]{1,0:T(8,128)(2,1)S(1)} %get-tuple-element.35), channel_id=1, source_target_pairs={{0,17},{1,66},{2,19},{4,29},{5,102},{6,31},{8,25},{9,74},{10,27},{... | collective-permute-start | bytes 73736 | tf_op jit(solution)/shard_map/ppermute | solution.py:32
  56.7 5.7 %collective-permute-start.20 = (bf16[32,384]{1,0:T(8,128)(2,1)S(1)}, bf16[32,384]{1,0:T(8,128)(2,1)S(1)}, u32[]{:S(2)}, u32[]{:S(2)}) collective-permute-start(bf16[32,384]{1,0:T(8,128)(2,1)S(1)} %get-tuple-element.35), channel_id=1, source_target_pairs={{0,1},{1,2},{2,3},{4,13},{5,38},{6,15},{8,9},{9,10},{10,11},{12,21... | collective-permute-start | bytes 73736 | tf_op jit(solution)/shard_map/ppermute | solution.py:32
  62.4 2.3 %collective-permute-start.22 = (f32[32,384]{1,0:T(8,128)S(1)}, f32[32,384]{1,0:T(8,128)S(1)}, u32[]{:S(2)}, u32[]{:S(2)}) collective-permute-start(f32[32,384]{1,0:T(8,128)S(1)} %shard_map.53.own), channel_id=1, source_target_pairs={{0,4},{1,5},{2,6},{3,7},{4,0},{5,1},{6,2},{7,3},{8,12},{9,13},{10,... | collective-permute-start | bytes 147464 | tf_op jit(solution)/shard_map/ppermute | solution.py:32
  65.1 8.1 %collective-permute-start.24 = (bf16[32,384]{1,0:T(8,128)(2,1)S(1)}, bf16[32,384]{1,0:T(8,128)(2,1)S(1)}, u32[]{:S(2)}, u32[]{:S(2)}) collective-permute-start(bf16[32,384]{1,0:T(8,128)(2,1)S(1)} %shard_map.54), channel_id=1, source_target_pairs={{0,17},{1,66},{2,19},{4,29},{5,102},{6,31},{8,25},{9,74},{10,27},{... | collective-permute-start | bytes 73736 | tf_op jit(solution)/shard_map/ppermute | solution.py:32
  68.9 5.7 %collective-permute-start.23 = (bf16[32,384]{1,0:T(8,128)(2,1)S(1)}, bf16[32,384]{1,0:T(8,128)(2,1)S(1)}, u32[]{:S(2)}, u32[]{:S(2)}) collective-permute-start(bf16[32,384]{1,0:T(8,128)(2,1)S(1)} %shard_map.54), channel_id=1, source_target_pairs={{0,1},{1,2},{2,3},{4,13},{5,38},{6,15},{8,9},{9,10},{10,11},{12,21... | collective-permute-start | bytes 73736 | tf_op jit(solution)/shard_map/ppermute | solution.py:32
  74.7 1.5 %collective-permute-start.25 = (f32[32,384]{1,0:T(8,128)S(1)}, f32[32,384]{1,0:T(8,128)S(1)}, u32[]{:S(2)}, u32[]{:S(2)}) collective-permute-start(f32[32,384]{1,0:T(8,128)S(1)} %shard_map.55.own), channel_id=1, source_target_pairs={{0,4},{1,5},{2,6},{3,7},{4,0},{5,1},{6,2},{7,3},{8,12},{9,13},{10,... | collective-permute-start | bytes 147464 | tf_op jit(solution)/shard_map/ppermute | solution.py:32
  76.5 8.1 %collective-permute-start.27 = (bf16[32,384]{1,0:T(8,128)(2,1)S(1)}, bf16[32,384]{1,0:T(8,128)(2,1)S(1)}, u32[]{:S(2)}, u32[]{:S(2)}) collective-permute-start(bf16[32,384]{1,0:T(8,128)(2,1)S(1)} %shard_map.56), channel_id=1, source_target_pairs={{0,17},{1,66},{2,19},{4,29},{5,102},{6,31},{8,25},{9,74},{10,27},{... | collective-permute-start | bytes 73736 | tf_op jit(solution)/shard_map/ppermute | solution.py:32
  80.5 5.7 %collective-permute-start.26 = (bf16[32,384]{1,0:T(8,128)(2,1)S(1)}, bf16[32,384]{1,0:T(8,128)(2,1)S(1)}, u32[]{:S(2)}, u32[]{:S(2)}) collective-permute-start(bf16[32,384]{1,0:T(8,128)(2,1)S(1)} %shard_map.56), channel_id=1, source_target_pairs={{0,1},{1,2},{2,3},{4,13},{5,38},{6,15},{8,9},{9,10},{10,11},{12,21... | collective-permute-start | bytes 73736 | tf_op jit(solution)/shard_map/ppermute | solution.py:32
  86.2 1.3 %collective-permute-start.28 = (f32[32,384]{1,0:T(8,128)S(1)}, f32[32,384]{1,0:T(8,128)S(1)}, u32[]{:S(2)}, u32[]{:S(2)}) collective-permute-start(f32[32,384]{1,0:T(8,128)S(1)} %shard_map.57.own), channel_id=1, source_target_pairs={{0,4},{1,5},{2,6},{3,7},{4,0},{5,1},{6,2},{7,3},{8,12},{9,13},{10,... | collective-permute-start | bytes 147464 | tf_op jit(solution)/shard_map/ppermute | solution.py:32
  88.2 4.0 %collective-permute-start.29 = (f32[64,48]{1,0:T(8,128)S(1)}, f32[64,48]{1,0:T(8,128)S(1)}, u32[]{:S(2)}, u32[]{:S(2)}) collective-permute-start(f32[64,48]{1,0:T(8,128)S(1)} %get-tuple-element.40), channel_id=1, source_target_pairs={{0,8},{1,33},{2,10},{3,35},{4,12},{5,37},{6,14},{7,39},{8,16},{9,4... | collective-permute-start | bytes 36872 | tf_op jit(solution)/shard_map/ppermute | solution.py:32
  88.9 5.4 %collective-permute-start.30 = (f32[64,48]{1,0:T(8,128)S(1)}, f32[64,48]{1,0:T(8,128)S(1)}, u32[]{:S(2)}, u32[]{:S(2)}) collective-permute-start(f32[64,48]{1,0:T(8,128)S(1)} %get-tuple-element.41), channel_id=1, source_target_pairs={{0,16},{1,65},{2,18},{3,67},{4,20},{5,69},{6,22},{7,71},{8,24},{9,... | collective-permute-start | bytes 36872 | tf_op jit(solution)/shard_map/ppermute | solution.py:32
  92.0 3.9 %collective-permute-start.31 = (f32[64,48]{1,0:T(8,128)S(1)}, f32[64,48]{1,0:T(8,128)S(1)}, u32[]{:S(2)}, u32[]{:S(2)}) collective-permute-start(f32[64,48]{1,0:T(8,128)S(1)} %get-tuple-element.42), channel_id=1, source_target_pairs={{0,24},{1,97},{2,26},{3,99},{4,28},{5,101},{6,30},{7,103},{8,0},{9... | collective-permute-start | bytes 36872 | tf_op jit(solution)/shard_map/ppermute | solution.py:32
  (4 other events, 18.9 us)

commit v6 on v5

--- a/solution.py
+++ b/solution.py
@@ -13,6 +13,7 @@
 N = BLOCK * Y
 R = 32
 LANES = 128
+ORDER = (0, 3, 1, 2)
 F32, BF16 = jnp.float32, jnp.bfloat16
 
 
@@ -32,6 +33,10 @@
     return lax.ppermute(value, AXES, pairs)
 
 
+def around(value, along):
+    return [value] + [send(value, along(d)) for d in ORDER[1:]]
+
+
 def to_peer(value):
     return send(value, lambda y, x, c, z: (y, x, 1 - c, z))
 
@@ -151,7 +156,7 @@
 def coupling_block(panel, l0, l1, l2, l3, out, lower, sides, entry):
     u, v, c, z = place()
     sides[...] = jnp.zeros_like(sides)
-    for d, piece in enumerate((l0, l1, l2, l3)):
+    for d, piece in zip(ORDER, (l0, l1, l2, l3)):
         from_u = behind(u, d)
         for j in range(4):
             lower[rows_at(chunk(from_u, j, z), CHIP), :] = piece[j * CHIP:(j + 1) * CHIP, :]
@@ -176,9 +181,9 @@
     u, v, c, _ = place()
 
     def run(firsts, seconds):
-        for d, piece in enumerate(seconds):
+        for d, piece in zip(ORDER, seconds):
             second[:, lanes_at(behind(v, d) * BLOCK, BLOCK)] = piece[:BLOCK, :]
-        for d, piece in enumerate(firsts):
+        for d, piece in zip(ORDER, firsts):
             from_u = behind(u, d)
             side = piece[BLOCK:, :].astype(F32)
             side = jnp.concatenate([side, jnp.zeros((LANES - 2 * R, BLOCK), F32)], axis=0).T.astype(BF16)
@@ -260,15 +265,17 @@
     low = [low[0]] + [send(low[d], along_v(d)) for d in range(1, 4)]
     forcing_peer = to_peer(forcing)
     inflow_peer = to_peer(inflow)
-    inv_own, low = lax.optimization_barrier((inv_own, low))
+    inv_own, low[1] = lax.optimization_barrier((inv_own, low[1]))
+    inv_2 = send(inv_own, along_v(2))
     own = call(
         lower_block, shape((BLOCK + R, BLOCK)), *low, forcing, forcing_peer, inflow, inflow_peer,
         scratch=[pltpu.VMEM((CHIP, LANES), F32)],
     )
     inv_own, own = lax.optimization_barrier((inv_own, own))
-    inv = [inv_own] + [send(inv_own, along_v(d)) for d in range(1, 4)]
+    inv_3, inv_1 = send(inv_own, along_v(3)), send(inv_own, along_v(1))
+    inv = [inv_own, inv_1, inv_2, inv_3]
     inv_panel = call(inverse_panel, shape((BLOCK, N)), *inv)
-    panel = [own] + [send(own, along_u(d)) for d in range(1, 4)]
+    panel = around(own, along_u)
 
     message = call(
         coupling_block, shape((BLOCK + 2 * R, BLOCK)), inv_panel, *panel,
@@ -277,7 +284,7 @@
         ],
         flops=2 * BLOCK * BLOCK * N,
     )
-    turn = [message] + [send(message, across(d)) for d in range(1, 4)]
+    turn = around(message, across)
     turn_peer = [to_peer(value) for value in turn]
     p_high, p_low, base, out = call(
         product_block,

time: 96.8 us -> 94.2 us (0.973)
  the two profiles are of different devices: /device:TPU:40 before, /device:TPU:56 now
where the time goes in v6:
time: 94.2 us; the launch traced here: 93.9 us
  waiting for transfers between devices  44 us (47%)
  starting transfers between devices  42.5 us (45%)
  Pallas kernels  4.75 us (5%)
  local copies, waits for them, and re-layouts  1.93 us (2%)
    ppermute x32, waiting for transfers between devices, send(): return lax.ppermute(value, AXES, pairs)  44 us
    ppermute x32, starting transfers between devices, send(): return lax.ppermute(value, AXES, pairs)  42.5 us
    pallas_call x13, Pallas kernels, call(): pl.pallas_call(kernel, out_shape=out, in_specs=[pl.BlockSpec(memory_space...  4.75 us
    unnamed x8, local copies, waits for them, and re-layouts  1.93 us
  transfers between devices with their start and end apart: 32, of which 20 were waited for; matrix products, arithmetic and copies ran while one was open for 0% of the time, Pallas kernels for 0%

profile of v6, /device:TPU:56, one launch (start us, length us, event | category | flops | bytes accessed | tf_op | source)
XLA Modules:
  0.0 93.9 jit_solution(5182146338091359037)
XLA Ops:
  0.5 1.0 %copy-done.1 = bf16[2,48,1536]{2,1,0:T(8,128)(2,1)S(1)} copy-done((bf16[2,48,1536]{2,1,0:T(8,128)(2,1)S(1)}, bf16[2,48,1536]{2,1,0:T(8,128)(2,1)}, u32[]{:S(2)}) %copy-start.1) | copy-done | bytes 294936
  2.2 2.6 %collective-permute-start.3 = (bf16[96,384]{1,0:T(8,128)(2,1)S(1)}, bf16[96,384]{1,0:T(8,128)(2,1)S(1)}, u32[]{:S(2)}, u32[]{:S(2)}) collective-permute-start(bf16[96,384]{1,0:T(8,128)(2,1)S(1)} %get-tuple-element.25), channel_id=1, source_target_pairs={{0,16},{1,65},{2,18},{3,67},{4,20},{5,69},{6,22},{7,71},{8,24},{9,... | collective-permute-start | bytes 221192 | tf_op jit(solution)/shard_map/ppermute | solution.py:33
  5.3 1.0 %copy-done = bf16[2,48,1536]{2,1,0:T(8,128)(2,1)S(1)} copy-done((bf16[2,48,1536]{2,1,0:T(8,128)(2,1)S(1)}, bf16[2,48,1536]{2,1,0:T(8,128)(2,1)}, u32[]{:S(2)}) %copy-start) | copy-done | bytes 294936
  7.1 1.0 %collective-permute-done.3.p2 = bf16[96,384]{1,0:T(8,128)(2,1)S(1)} collective-permute-done((bf16[96,384]{1,0:T(8,128)(2,1)S(1)}, bf16[96,384]{1,0:T(8,128)(2,1)S(1)}, u32[]{:S(2)}, u32[]{:S(2)}) %collective-permute-start.3) | collective-permute-done | bytes 73760 | tf_op jit(solution)/shard_map/ppermute | solution.py:33
  8.0 2.3 %collective-permute-done.4.p3 = bf16[96,384]{1,0:T(8,128)(2,1)S(1)} collective-permute-done((bf16[96,384]{1,0:T(8,128)(2,1)S(1)}, bf16[96,384]{1,0:T(8,128)(2,1)S(1)}, u32[]{:S(2)}, u32[]{:S(2)}) %collective-permute-start.4) | collective-permute-done | bytes 73760 | tf_op jit(solution)/shard_map/ppermute | solution.py:33
  10.6 3.1 %collective-permute-start.12 = (bf16[416,384]{1,0:T(8,128)(2,1)S(1)}, bf16[416,384]{1,0:T(8,128)(2,1)S(1)}, u32[]{:S(2)}, u32[]{:S(2)}) collective-permute-start(bf16[416,384]{1,0:T(8,128)(2,1)S(1)} %shard_map.49.l0), channel_id=1, source_target_pairs={{0,64},{1,17},{2,66},{3,19},{4,68},{5,21},{6,70},{7,23},{8,72},{9,... | collective-permute-start | bytes 958472 | tf_op jit(solution)/shard_map/ppermute | solution.py:33
  14.2 2.6 %collective-permute-start.10 = (bf16[416,384]{1,0:T(8,128)(2,1)S(1)}, bf16[416,384]{1,0:T(8,128)(2,1)S(1)}, u32[]{:S(2)}, u32[]{:S(2)}) collective-permute-start(bf16[416,384]{1,0:T(8,128)(2,1)S(1)} %shard_map.49.l0), channel_id=1, source_target_pairs={{0,96},{1,25},{2,98},{3,27},{4,100},{5,29},{6,102},{7,31},{8,104},... | collective-permute-start | bytes 958472 | tf_op jit(solution)/shard_map/ppermute | solution.py:33
  16.9 3.1 %collective-permute-start.7 = (bf16[96,1536]{1,0:T(8,128)(2,1)S(1)}, bf16[96,1536]{1,0:T(8,128)(2,1)S(1)}, u32[]{:S(2)}, u32[]{:S(2)}) collective-permute-start(bf16[96,1536]{1,0:T(8,128)(2,1)S(1)} %shard_map.46.a0), channel_id=1, source_target_pairs={{0,8},{1,33},{2,10},{3,35},{4,12},{5,37},{6,14},{7,39},{8,16},{9,4... | collective-permute-start | bytes 884744 | tf_op jit(solution)/shard_map/ppermute | solution.py:33
  20.0 10.1 %collective-permute-done.7.a1 = bf16[96,1536]{1,0:T(8,128)(2,1)S(1)} collective-permute-done((bf16[96,1536]{1,0:T(8,128)(2,1)S(1)}, bf16[96,1536]{1,0:T(8,128)(2,1)S(1)}, u32[]{:S(2)}, u32[]{:S(2)}) %collective-permute-start.7) | collective-permute-done | bytes 294944 | tf_op jit(solution)/shard_map/ppermute | solution.py:33
  30.3 1.5 %shard_map.51.o0.message = bf16[448,384]{1,0:T(8,128)(2,1)S(1)} custom-call(bf16[384,1536]{1,0:T(8,128)(2,1)S(1)} %shard_map.50.panel, bf16[416,384]{1,0:T(8,128)(2,1)S(1)} %shard_map.49.l0, bf16[416,384]{1,0:T(8,128)(2,1)S(1)} %collective-permute-done.10.l1, bf16[416,384]{1,0:T(8,128)(2,1)S(1)} %collective-permute-done.11.l2, ...), custom_call_target="tpu_custom_call" | custom-call | flops 452984832 | bytes 2457600 | tf_op jit(solution)/shard_map/pallas_call | solution.py:81
  32.1 0.9 collective-permute-start.14
  33.0 2.3 %collective-permute-start.13 = (bf16[448,384]{1,0:T(8,128)(2,1)S(1)}, bf16[448,384]{1,0:T(8,128)(2,1)S(1)}, u32[]{:S(2)}, u32[]{:S(2)}) collective-permute-start(bf16[448,384]{1,0:T(8,128)(2,1)S(1)} %shard_map.51.o0.message), channel_id=1, source_target_pairs={{0,96},{1,25},{2,98},{3,27},{4,28},{5,101},{6,30},{7,103},{8,104},... | collective-permute-start | bytes 1032200 | tf_op jit(solution)/shard_map/ppermute | solution.py:33
  35.3 5.4 %collective-permute-done.15.o3 = bf16[448,384]{1,0:T(8,128)(2,1)S(1)} collective-permute-done((bf16[448,384]{1,0:T(8,128)(2,1)S(1)}, bf16[448,384]{1,0:T(8,128)(2,1)S(1)}, u32[]{:S(2)}, u32[]{:S(2)}) %collective-permute-start.15) | collective-permute-done | bytes 344096 | tf_op jit(solution)/shard_map/ppermute | solution.py:33
  40.7 3.5 %collective-permute-done.14.o2 = bf16[448,384]{1,0:T(8,128)(2,1)S(1)} collective-permute-done((bf16[448,384]{1,0:T(8,128)(2,1)S(1)}, bf16[448,384]{1,0:T(8,128)(2,1)S(1)}, u32[]{:S(2)}, u32[]{:S(2)}) %collective-permute-start.14) | collective-permute-done | bytes 344096 | tf_op jit(solution)/shard_map/ppermute | solution.py:33
  44.7 1.1 %collective-permute-done.18.p2 = bf16[448,384]{1,0:T(8,128)(2,1)S(1)} collective-permute-done((bf16[448,384]{1,0:T(8,128)(2,1)S(1)}, bf16[448,384]{1,0:T(8,128)(2,1)S(1)}, u32[]{:S(2)}, u32[]{:S(2)}) %collective-permute-start.18) | collective-permute-done | bytes 344096 | tf_op jit(solution)/shard_map/ppermute | solution.py:33
  46.4 1.4 %shard_map.52 = (bf16[384,384]{1,0:T(8,128)(2,1)S(1)}, bf16[384,384]{1,0:T(8,128)(2,1)S(1)}, f32[32,384]{1,0:T(8,128)S(1)}, bf16[32,384]{1,0:T(8,128)(2,1)S(1)}) custom-call(bf16[448,384]{1,0:T(8,128)(2,1)S(1)} %shard_map.51.o0.message, bf16[448,384]{1,0:T(8,128)(2,1)S(1)} %collective-permute-done.13.o1, bf16[448,384]{1,0:T(8,128)(2,1)S(1)} %collective-permute-done.14.o2, ...), custom_call_target="tpu_custom_call" | custom-call | flops 452984832 | bytes 2752512 | tf_op jit(solution)/shard_map/pallas_call | solution.py:81
  47.8 5.6 %collective-permute-start.21 = (bf16[32,384]{1,0:T(8,128)(2,1)S(1)}, bf16[32,384]{1,0:T(8,128)(2,1)S(1)}, u32[]{:S(2)}, u32[]{:S(2)}) collective-permute-start(bf16[32,384]{1,0:T(8,128)(2,1)S(1)} %get-tuple-element.29), channel_id=1, source_target_pairs={{0,17},{1,66},{2,19},{4,29},{5,102},{6,31},{8,25},{9,74},{10,27},{... | collective-permute-start | bytes 73736 | tf_op jit(solution)/shard_map/ppermute | solution.py:33
  53.4 1.9 %collective-permute-start.20 = (bf16[32,384]{1,0:T(8,128)(2,1)S(1)}, bf16[32,384]{1,0:T(8,128)(2,1)S(1)}, u32[]{:S(2)}, u32[]{:S(2)}) collective-permute-start(bf16[32,384]{1,0:T(8,128)(2,1)S(1)} %get-tuple-element.29), channel_id=1, source_target_pairs={{0,1},{1,2},{2,3},{4,13},{5,38},{6,15},{8,9},{9,10},{10,11},{12,21... | collective-permute-start | bytes 73736 | tf_op jit(solution)/shard_map/ppermute | solution.py:33
  55.9 3.4 %collective-permute-done.20.r0 = bf16[32,384]{1,0:T(8,128)(2,1)S(1)} collective-permute-done((bf16[32,384]{1,0:T(8,128)(2,1)S(1)}, bf16[32,384]{1,0:T(8,128)(2,1)S(1)}, u32[]{:S(2)}, u32[]{:S(2)}) %collective-permute-start.20) | collective-permute-done | bytes 24608 | tf_op jit(solution)/shard_map/ppermute | solution.py:33
  59.4 1.2 %collective-permute-done.22.peer = f32[32,384]{1,0:T(8,128)S(1)} collective-permute-done((f32[32,384]{1,0:T(8,128)S(1)}, f32[32,384]{1,0:T(8,128)S(1)}, u32[]{:S(2)}, u32[]{:S(2)}) %collective-permute-start.22) | collective-permute-done | bytes 49184 | tf_op jit(solution)/shard_map/ppermute | solution.py:33
  61.0 3.7 %collective-permute-start.24 = (bf16[32,384]{1,0:T(8,128)(2,1)S(1)}, bf16[32,384]{1,0:T(8,128)(2,1)S(1)}, u32[]{:S(2)}, u32[]{:S(2)}) collective-permute-start(bf16[32,384]{1,0:T(8,128)(2,1)S(1)} %shard_map.54), channel_id=1, source_target_pairs={{0,17},{1,66},{2,19},{4,29},{5,102},{6,31},{8,25},{9,74},{10,27},{... | collective-permute-start | bytes 73736 | tf_op jit(solution)/shard_map/ppermute | solution.py:33
  64.8 2.2 %collective-permute-start.23 = (bf16[32,384]{1,0:T(8,128)(2,1)S(1)}, bf16[32,384]{1,0:T(8,128)(2,1)S(1)}, u32[]{:S(2)}, u32[]{:S(2)}) collective-permute-start(bf16[32,384]{1,0:T(8,128)(2,1)S(1)} %shard_map.54), channel_id=1, source_target_pairs={{0,1},{1,2},{2,3},{4,13},{5,38},{6,15},{8,9},{9,10},{10,11},{12,21... | collective-permute-start | bytes 73736 | tf_op jit(solution)/shard_map/ppermute | solution.py:33
  66.9 2.2 %collective-permute-done.24.r1 = bf16[32,384]{1,0:T(8,128)(2,1)S(1)} collective-permute-done((bf16[32,384]{1,0:T(8,128)(2,1)S(1)}, bf16[32,384]{1,0:T(8,128)(2,1)S(1)}, u32[]{:S(2)}, u32[]{:S(2)}) %collective-permute-start.24) | collective-permute-done | bytes 24608 | tf_op jit(solution)/shard_map/ppermute | solution.py:33
  69.2 1.3 %collective-permute-done.23.r0 = bf16[32,384]{1,0:T(8,128)(2,1)S(1)} collective-permute-done((bf16[32,384]{1,0:T(8,128)(2,1)S(1)}, bf16[32,384]{1,0:T(8,128)(2,1)S(1)}, u32[]{:S(2)}, u32[]{:S(2)}) %collective-permute-start.23) | collective-permute-done | bytes 24608 | tf_op jit(solution)/shard_map/ppermute | solution.py:33
  72.4 2.7 %collective-permute-start.27 = (bf16[32,384]{1,0:T(8,128)(2,1)S(1)}, bf16[32,384]{1,0:T(8,128)(2,1)S(1)}, u32[]{:S(2)}, u32[]{:S(2)}) collective-permute-start(bf16[32,384]{1,0:T(8,128)(2,1)S(1)} %shard_map.56), channel_id=1, source_target_pairs={{0,17},{1,66},{2,19},{4,29},{5,102},{6,31},{8,25},{9,74},{10,27},{... | collective-permute-start | bytes 73736 | tf_op jit(solution)/shard_map/ppermute | solution.py:33
  75.1 1.9 %collective-permute-start.26 = (bf16[32,384]{1,0:T(8,128)(2,1)S(1)}, bf16[32,384]{1,0:T(8,128)(2,1)S(1)}, u32[]{:S(2)}, u32[]{:S(2)}) collective-permute-start(bf16[32,384]{1,0:T(8,128)(2,1)S(1)} %shard_map.56), channel_id=1, source_target_pairs={{0,1},{1,2},{2,3},{4,13},{5,38},{6,15},{8,9},{9,10},{10,11},{12,21... | collective-permute-start | bytes 73736 | tf_op jit(solution)/shard_map/ppermute | solution.py:33
  77.1 3.5 %collective-permute-done.27.r1 = bf16[32,384]{1,0:T(8,128)(2,1)S(1)} collective-permute-done((bf16[32,384]{1,0:T(8,128)(2,1)S(1)}, bf16[32,384]{1,0:T(8,128)(2,1)S(1)}, u32[]{:S(2)}, u32[]{:S(2)}) %collective-permute-start.27) | collective-permute-done | bytes 24608 | tf_op jit(solution)/shard_map/ppermute | solution.py:33
  80.9 1.7 %collective-permute-start.28 = (f32[32,384]{1,0:T(8,128)S(1)}, f32[32,384]{1,0:T(8,128)S(1)}, u32[]{:S(2)}, u32[]{:S(2)}) collective-permute-start(f32[32,384]{1,0:T(8,128)S(1)} %shard_map.57.own), channel_id=1, source_target_pairs={{0,4},{1,5},{2,6},{3,7},{4,0},{5,1},{6,2},{7,3},{8,12},{9,13},{10,... | collective-permute-start | bytes 147464 | tf_op jit(solution)/shard_map/ppermute | solution.py:33
  84.2 2.3 %collective-permute-start.29 = (f32[64,48]{1,0:T(8,128)S(1)}, f32[64,48]{1,0:T(8,128)S(1)}, u32[]{:S(2)}, u32[]{:S(2)}) collective-permute-start(f32[64,48]{1,0:T(8,128)S(1)} %get-tuple-element.34), channel_id=1, source_target_pairs={{0,8},{1,33},{2,10},{3,35},{4,12},{5,37},{6,14},{7,39},{8,16},{9,4... | collective-permute-start | bytes 36872 | tf_op jit(solution)/shard_map/ppermute | solution.py:33
  86.4 1.7 %collective-permute-start.30 = (f32[64,48]{1,0:T(8,128)S(1)}, f32[64,48]{1,0:T(8,128)S(1)}, u32[]{:S(2)}, u32[]{:S(2)}) collective-permute-start(f32[64,48]{1,0:T(8,128)S(1)} %get-tuple-element.35), channel_id=1, source_target_pairs={{0,16},{1,65},{2,18},{3,67},{4,20},{5,69},{6,22},{7,71},{8,24},{9,... | collective-permute-start | bytes 36872 | tf_op jit(solution)/shard_map/ppermute | solution.py:33
  88.6 3.3 %collective-permute-done.30 = f32[64,48]{1,0:T(8,128)S(1)} collective-permute-done((f32[64,48]{1,0:T(8,128)S(1)}, f32[64,48]{1,0:T(8,128)S(1)}, u32[]{:S(2)}, u32[]{:S(2)}) %collective-permute-start.30) | collective-permute-done | bytes 12320 | tf_op jit(solution)/shard_map/ppermute | solution.py:33
  91.9 1.4 %collective-permute-done.31 = f32[64,48]{1,0:T(8,128)S(1)} collective-permute-done((f32[64,48]{1,0:T(8,128)S(1)}, f32[64,48]{1,0:T(8,128)S(1)}, u32[]{:S(2)}, u32[]{:S(2)}) %collective-permute-start.31) | collective-permute-done | bytes 12320 | tf_op jit(solution)/shard_map/ppermute | solution.py:33
  (54 shorter events, 10.7 us)
Async XLA Ops:
  0.0 1.8 %collective-permute-start.1 = (bf16[2,48,1536]{2,1,0:T(8,128)(2,1)}, bf16[2,48,1536]{2,1,0:T(8,128)(2,1)S(1)}, u32[]{:S(2)}, u32[]{:S(2)}) collective-permute-start(bf16[2,48,1536]{2,1,0:T(8,128)(2,1)} %own.3), channel_id=1, source_target_pairs={{0,4},{1,5},{2,6},{3,7},{4,0},{5,1},{6,2},{7,3},{8,12},{9,13},{10,... | collective-permute-start | bytes 884744 | tf_op jit(solution)/shard_map/ppermute | solution.py:33
  0.0 4.8 %collective-permute-start = (bf16[2,48,1536]{2,1,0:T(8,128)(2,1)}, bf16[2,48,1536]{2,1,0:T(8,128)(2,1)S(1)}, u32[]{:S(2)}, u32[]{:S(2)}) collective-permute-start(bf16[2,48,1536]{2,1,0:T(8,128)(2,1)} %own.2), channel_id=1, source_target_pairs={{0,4},{1,5},{2,6},{3,7},{4,0},{5,1},{6,2},{7,3},{8,12},{9,13},{10,... | collective-permute-start | bytes 884744 | tf_op jit(solution)/shard_map/ppermute | solution.py:33
  1.9 5.2 %collective-permute-start.2 = (bf16[96,384]{1,0:T(8,128)(2,1)S(1)}, bf16[96,384]{1,0:T(8,128)(2,1)S(1)}, u32[]{:S(2)}, u32[]{:S(2)}) collective-permute-start(bf16[96,384]{1,0:T(8,128)(2,1)S(1)} %get-tuple-element.21), channel_id=1, source_target_pairs={{0,8},{1,33},{2,10},{3,35},{4,12},{5,37},{6,14},{7,39},{8,16},{9,4... | collective-permute-start | bytes 221192 | tf_op jit(solution)/shard_map/ppermute | solution.py:33
  2.2 5.9 %collective-permute-start.3 = (bf16[96,384]{1,0:T(8,128)(2,1)S(1)}, bf16[96,384]{1,0:T(8,128)(2,1)S(1)}, u32[]{:S(2)}, u32[]{:S(2)}) collective-permute-start(bf16[96,384]{1,0:T(8,128)(2,1)S(1)} %get-tuple-element.25), channel_id=1, source_target_pairs={{0,16},{1,65},{2,18},{3,67},{4,20},{5,69},{6,22},{7,71},{8,24},{9,... | collective-permute-start | bytes 221192 | tf_op jit(solution)/shard_map/ppermute | solution.py:33
  4.8 5.6 %collective-permute-start.4 = (bf16[96,384]{1,0:T(8,128)(2,1)S(1)}, bf16[96,384]{1,0:T(8,128)(2,1)S(1)}, u32[]{:S(2)}, u32[]{:S(2)}) collective-permute-start(bf16[96,384]{1,0:T(8,128)(2,1)S(1)} %get-tuple-element.26), channel_id=1, source_target_pairs={{0,24},{1,97},{2,26},{3,99},{4,28},{5,101},{6,30},{7,103},{8,0},{9... | collective-permute-start | bytes 221192 | tf_op jit(solution)/shard_map/ppermute | solution.py:33
  4.8 2.3 %collective-permute-start.5 = (bf16[2,32,48]{2,1,0:T(8,128)(2,1)}, bf16[2,32,48]{2,1,0:T(8,128)(2,1)S(1)}, u32[]{:S(2)}, u32[]{:S(2)}) collective-permute-start(bf16[2,32,48]{2,1,0:T(8,128)(2,1)} %bitcast.5), channel_id=1, source_target_pairs={{0,4},{1,5},{2,6},{3,7},{4,0},{5,1},{6,2},{7,3},{8,12},{9,13},{10,... | collective-permute-start | bytes 18440 | tf_op jit(solution)/shard_map/ppermute | solution.py:33
  4.8 2.3 %collective-permute-start.6 = (f32[32,48]{1,0:T(8,128)}, f32[32,48]{1,0:T(8,128)S(1)}, u32[]{:S(2)}, u32[]{:S(2)}) collective-permute-start(f32[32,48]{1,0:T(8,128)} %bitcast.7), channel_id=1, source_target_pairs={{0,4},{1,5},{2,6},{3,7},{4,0},{5,1},{6,2},{7,3},{8,12},{9,13},{10,... | collective-permute-start | bytes 18440 | tf_op jit(solution)/shard_map/ppermute | solution.py:33
  10.5 9.6 %collective-permute-start.9 = (bf16[96,1536]{1,0:T(8,128)(2,1)S(1)}, bf16[96,1536]{1,0:T(8,128)(2,1)S(1)}, u32[]{:S(2)}, u32[]{:S(2)}) collective-permute-start(bf16[96,1536]{1,0:T(8,128)(2,1)S(1)} %shard_map.46.a0), channel_id=1, source_target_pairs={{0,24},{1,97},{2,26},{3,99},{4,28},{5,101},{6,30},{7,103},{8,0},{9... | collective-permute-start | bytes 884744 | tf_op jit(solution)/shard_map/ppermute | solution.py:33
  10.6 19.7 %collective-permute-start.12 = (bf16[416,384]{1,0:T(8,128)(2,1)S(1)}, bf16[416,384]{1,0:T(8,128)(2,1)S(1)}, u32[]{:S(2)}, u32[]{:S(2)}) collective-permute-start(bf16[416,384]{1,0:T(8,128)(2,1)S(1)} %shard_map.49.l0), channel_id=1, source_target_pairs={{0,64},{1,17},{2,66},{3,19},{4,68},{5,21},{6,70},{7,23},{8,72},{9,... | collective-permute-start | bytes 958472 | tf_op jit(solution)/shard_map/ppermute | solution.py:33
  13.7 16.6 %collective-permute-start.11 = (bf16[416,384]{1,0:T(8,128)(2,1)S(1)}, bf16[416,384]{1,0:T(8,128)(2,1)S(1)}, u32[]{:S(2)}, u32[]{:S(2)}) collective-permute-start(bf16[416,384]{1,0:T(8,128)(2,1)S(1)} %shard_map.49.l0), channel_id=1, source_target_pairs={{0,32},{1,9},{2,34},{3,11},{4,36},{5,13},{6,38},{7,15},{8,40},{9,1... | collective-permute-start | bytes 958472 | tf_op jit(solution)/shard_map/ppermute | solution.py:33
  14.2 16.0 %collective-permute-start.10 = (bf16[416,384]{1,0:T(8,128)(2,1)S(1)}, bf16[416,384]{1,0:T(8,128)(2,1)S(1)}, u32[]{:S(2)}, u32[]{:S(2)}) collective-permute-start(bf16[416,384]{1,0:T(8,128)(2,1)S(1)} %shard_map.49.l0), channel_id=1, source_target_pairs={{0,96},{1,25},{2,98},{3,27},{4,100},{5,29},{6,102},{7,31},{8,104},... | collective-permute-start | bytes 958472 | tf_op jit(solution)/shard_map/ppermute | solution.py:33
  16.9 13.2 %collective-permute-start.7 = (bf16[96,1536]{1,0:T(8,128)(2,1)S(1)}, bf16[96,1536]{1,0:T(8,128)(2,1)S(1)}, u32[]{:S(2)}, u32[]{:S(2)}) collective-permute-start(bf16[96,1536]{1,0:T(8,128)(2,1)S(1)} %shard_map.46.a0), channel_id=1, source_target_pairs={{0,8},{1,33},{2,10},{3,35},{4,12},{5,37},{6,14},{7,39},{8,16},{9,4... | collective-permute-start | bytes 884744 | tf_op jit(solution)/shard_map/ppermute | solution.py:33
  20.0 10.1 %collective-permute-start.8 = (bf16[96,1536]{1,0:T(8,128)(2,1)S(1)}, bf16[96,1536]{1,0:T(8,128)(2,1)S(1)}, u32[]{:S(2)}, u32[]{:S(2)}) collective-permute-start(bf16[96,1536]{1,0:T(8,128)(2,1)S(1)} %shard_map.46.a0), channel_id=1, source_target_pairs={{0,16},{1,65},{2,18},{3,67},{4,20},{5,69},{6,22},{7,71},{8,24},{9,... | collective-permute-start | bytes 884744 | tf_op jit(solution)/shard_map/ppermute | solution.py:33
  31.8 8.9 %collective-permute-start.15 = (bf16[448,384]{1,0:T(8,128)(2,1)S(1)}, bf16[448,384]{1,0:T(8,128)(2,1)S(1)}, u32[]{:S(2)}, u32[]{:S(2)}) collective-permute-start(bf16[448,384]{1,0:T(8,128)(2,1)S(1)} %shard_map.51.o0.message), channel_id=1, source_target_pairs={{0,64},{1,17},{2,66},{3,19},{4,20},{5,69},{6,22},{7,71},{8,72},{9,... | collective-permute-start | bytes 1032200 | tf_op jit(solution)/shard_map/ppermute | solution.py:33
  32.1 12.1 %collective-permute-start.14 = (bf16[448,384]{1,0:T(8,128)(2,1)S(1)}, bf16[448,384]{1,0:T(8,128)(2,1)S(1)}, u32[]{:S(2)}, u32[]{:S(2)}) collective-permute-start(bf16[448,384]{1,0:T(8,128)(2,1)S(1)} %shard_map.51.o0.message), channel_id=1, source_target_pairs={{0,32},{1,9},{2,34},{3,11},{4,12},{5,37},{6,14},{7,39},{8,40},{9,1... | collective-permute-start | bytes 1032200 | tf_op jit(solution)/shard_map/ppermute | solution.py:33
  33.0 11.2 %collective-permute-start.13 = (bf16[448,384]{1,0:T(8,128)(2,1)S(1)}, bf16[448,384]{1,0:T(8,128)(2,1)S(1)}, u32[]{:S(2)}, u32[]{:S(2)}) collective-permute-start(bf16[448,384]{1,0:T(8,128)(2,1)S(1)} %shard_map.51.o0.message), channel_id=1, source_target_pairs={{0,96},{1,25},{2,98},{3,27},{4,28},{5,101},{6,30},{7,103},{8,104},... | collective-permute-start | bytes 1032200 | tf_op jit(solution)/shard_map/ppermute | solution.py:33
  35.3 9.4 %collective-permute-start.16 = (bf16[448,384]{1,0:T(8,128)(2,1)S(1)}, bf16[448,384]{1,0:T(8,128)(2,1)S(1)}, u32[]{:S(2)}, u32[]{:S(2)}) collective-permute-start(bf16[448,384]{1,0:T(8,128)(2,1)S(1)} %shard_map.51.o0.message), channel_id=1, source_target_pairs={{0,4},{1,5},{2,6},{3,7},{4,0},{5,1},{6,2},{7,3},{8,12},{9,13},{10,... | collective-permute-start | bytes 1032200 | tf_op jit(solution)/shard_map/ppermute | solution.py:33
  40.7 4.0 %collective-permute-start.19 = (bf16[448,384]{1,0:T(8,128)(2,1)S(1)}, bf16[448,384]{1,0:T(8,128)(2,1)S(1)}, u32[]{:S(2)}, u32[]{:S(2)}) collective-permute-start(bf16[448,384]{1,0:T(8,128)(2,1)S(1)} %collective-permute-done.15.o3), channel_id=1, source_target_pairs={{0,4},{1,5},{2,6},{3,7},{4,0},{5,1},{6,2},{7,3},{8,12},{9,13},{10,... | collective-permute-start | bytes 1032200 | tf_op jit(solution)/shard_map/ppermute | solution.py:33
  44.2 1.7 %collective-permute-start.18 = (bf16[448,384]{1,0:T(8,128)(2,1)S(1)}, bf16[448,384]{1,0:T(8,128)(2,1)S(1)}, u32[]{:S(2)}, u32[]{:S(2)}) collective-permute-start(bf16[448,384]{1,0:T(8,128)(2,1)S(1)} %collective-permute-done.14.o2), channel_id=1, source_target_pairs={{0,4},{1,5},{2,6},{3,7},{4,0},{5,1},{6,2},{7,3},{8,12},{9,13},{10,... | collective-permute-start | bytes 1032200 | tf_op jit(solution)/shard_map/ppermute | solution.py:33
  44.2 2.1 %collective-permute-start.17 = (bf16[448,384]{1,0:T(8,128)(2,1)S(1)}, bf16[448,384]{1,0:T(8,128)(2,1)S(1)}, u32[]{:S(2)}, u32[]{:S(2)}) collective-permute-start(bf16[448,384]{1,0:T(8,128)(2,1)S(1)} %collective-permute-done.13.o1), channel_id=1, source_target_pairs={{0,4},{1,5},{2,6},{3,7},{4,0},{5,1},{6,2},{7,3},{8,12},{9,13},{10,... | collective-permute-start | bytes 1032200 | tf_op jit(solution)/shard_map/ppermute | solution.py:33
  47.8 8.1 %collective-permute-start.21 = (bf16[32,384]{1,0:T(8,128)(2,1)S(1)}, bf16[32,384]{1,0:T(8,128)(2,1)S(1)}, u32[]{:S(2)}, u32[]{:S(2)}) collective-permute-start(bf16[32,384]{1,0:T(8,128)(2,1)S(1)} %get-tuple-element.29), channel_id=1, source_target_pairs={{0,17},{1,66},{2,19},{4,29},{5,102},{6,31},{8,25},{9,74},{10,27},{... | collective-permute-start | bytes 73736 | tf_op jit(solution)/shard_map/ppermute | solution.py:33
  53.4 5.9 %collective-permute-start.20 = (bf16[32,384]{1,0:T(8,128)(2,1)S(1)}, bf16[32,384]{1,0:T(8,128)(2,1)S(1)}, u32[]{:S(2)}, u32[]{:S(2)}) collective-permute-start(bf16[32,384]{1,0:T(8,128)(2,1)S(1)} %get-tuple-element.29), channel_id=1, source_target_pairs={{0,1},{1,2},{2,3},{4,13},{5,38},{6,15},{8,9},{9,10},{10,11},{12,21... | collective-permute-start | bytes 73736 | tf_op jit(solution)/shard_map/ppermute | solution.py:33
  59.3 1.3 %collective-permute-start.22 = (f32[32,384]{1,0:T(8,128)S(1)}, f32[32,384]{1,0:T(8,128)S(1)}, u32[]{:S(2)}, u32[]{:S(2)}) collective-permute-start(f32[32,384]{1,0:T(8,128)S(1)} %shard_map.53.own), channel_id=1, source_target_pairs={{0,4},{1,5},{2,6},{3,7},{4,0},{5,1},{6,2},{7,3},{8,12},{9,13},{10,... | collective-permute-start | bytes 147464 | tf_op jit(solution)/shard_map/ppermute | solution.py:33
  61.0 8.1 %collective-permute-start.24 = (bf16[32,384]{1,0:T(8,128)(2,1)S(1)}, bf16[32,384]{1,0:T(8,128)(2,1)S(1)}, u32[]{:S(2)}, u32[]{:S(2)}) collective-permute-start(bf16[32,384]{1,0:T(8,128)(2,1)S(1)} %shard_map.54), channel_id=1, source_target_pairs={{0,17},{1,66},{2,19},{4,29},{5,102},{6,31},{8,25},{9,74},{10,27},{... | collective-permute-start | bytes 73736 | tf_op jit(solution)/shard_map/ppermute | solution.py:33
  64.8 5.7 %collective-permute-start.23 = (bf16[32,384]{1,0:T(8,128)(2,1)S(1)}, bf16[32,384]{1,0:T(8,128)(2,1)S(1)}, u32[]{:S(2)}, u32[]{:S(2)}) collective-permute-start(bf16[32,384]{1,0:T(8,128)(2,1)S(1)} %shard_map.54), channel_id=1, source_target_pairs={{0,1},{1,2},{2,3},{4,13},{5,38},{6,15},{8,9},{9,10},{10,11},{12,21... | collective-permute-start | bytes 73736 | tf_op jit(solution)/shard_map/ppermute | solution.py:33
  70.5 1.5 %collective-permute-start.25 = (f32[32,384]{1,0:T(8,128)S(1)}, f32[32,384]{1,0:T(8,128)S(1)}, u32[]{:S(2)}, u32[]{:S(2)}) collective-permute-start(f32[32,384]{1,0:T(8,128)S(1)} %shard_map.55.own), channel_id=1, source_target_pairs={{0,4},{1,5},{2,6},{3,7},{4,0},{5,1},{6,2},{7,3},{8,12},{9,13},{10,... | collective-permute-start | bytes 147464 | tf_op jit(solution)/shard_map/ppermute | solution.py:33
  72.4 8.1 %collective-permute-start.27 = (bf16[32,384]{1,0:T(8,128)(2,1)S(1)}, bf16[32,384]{1,0:T(8,128)(2,1)S(1)}, u32[]{:S(2)}, u32[]{:S(2)}) collective-permute-start(bf16[32,384]{1,0:T(8,128)(2,1)S(1)} %shard_map.56), channel_id=1, source_target_pairs={{0,17},{1,66},{2,19},{4,29},{5,102},{6,31},{8,25},{9,74},{10,27},{... | collective-permute-start | bytes 73736 | tf_op jit(solution)/shard_map/ppermute | solution.py:33
  75.1 5.7 %collective-permute-start.26 = (bf16[32,384]{1,0:T(8,128)(2,1)S(1)}, bf16[32,384]{1,0:T(8,128)(2,1)S(1)}, u32[]{:S(2)}, u32[]{:S(2)}) collective-permute-start(bf16[32,384]{1,0:T(8,128)(2,1)S(1)} %shard_map.56), channel_id=1, source_target_pairs={{0,1},{1,2},{2,3},{4,13},{5,38},{6,15},{8,9},{9,10},{10,11},{12,21... | collective-permute-start | bytes 73736 | tf_op jit(solution)/shard_map/ppermute | solution.py:33
  80.9 2.6 %collective-permute-start.28 = (f32[32,384]{1,0:T(8,128)S(1)}, f32[32,384]{1,0:T(8,128)S(1)}, u32[]{:S(2)}, u32[]{:S(2)}) collective-permute-start(f32[32,384]{1,0:T(8,128)S(1)} %shard_map.57.own), channel_id=1, source_target_pairs={{0,4},{1,5},{2,6},{3,7},{4,0},{5,1},{6,2},{7,3},{8,12},{9,13},{10,... | collective-permute-start | bytes 147464 | tf_op jit(solution)/shard_map/ppermute | solution.py:33
  84.2 4.4 %collective-permute-start.29 = (f32[64,48]{1,0:T(8,128)S(1)}, f32[64,48]{1,0:T(8,128)S(1)}, u32[]{:S(2)}, u32[]{:S(2)}) collective-permute-start(f32[64,48]{1,0:T(8,128)S(1)} %get-tuple-element.34), channel_id=1, source_target_pairs={{0,8},{1,33},{2,10},{3,35},{4,12},{5,37},{6,14},{7,39},{8,16},{9,4... | collective-permute-start | bytes 36872 | tf_op jit(solution)/shard_map/ppermute | solution.py:33
  86.4 5.4 %collective-permute-start.30 = (f32[64,48]{1,0:T(8,128)S(1)}, f32[64,48]{1,0:T(8,128)S(1)}, u32[]{:S(2)}, u32[]{:S(2)}) collective-permute-start(f32[64,48]{1,0:T(8,128)S(1)} %get-tuple-element.35), channel_id=1, source_target_pairs={{0,16},{1,65},{2,18},{3,67},{4,20},{5,69},{6,22},{7,71},{8,24},{9,... | collective-permute-start | bytes 36872 | tf_op jit(solution)/shard_map/ppermute | solution.py:33
  88.1 5.1 %collective-permute-start.31 = (f32[64,48]{1,0:T(8,128)S(1)}, f32[64,48]{1,0:T(8,128)S(1)}, u32[]{:S(2)}, u32[]{:S(2)}) collective-permute-start(f32[64,48]{1,0:T(8,128)S(1)} %get-tuple-element.36), channel_id=1, source_target_pairs={{0,24},{1,97},{2,26},{3,99},{4,28},{5,101},{6,30},{7,103},{8,0},{9... | collective-permute-start | bytes 36872 | tf_op jit(solution)/shard_map/ppermute | solution.py:33
  (4 other events, 19.6 us)

commit v7 on v6

--- a/solution.py
+++ b/solution.py
@@ -177,25 +177,28 @@
     out[BLOCK + R:, :] = low
 
 
-def product_block(o0, o1, o2, o3, p0, p1, p2, p3, high_out, low_out, base_out, start_out, second, first, shares):
-    u, v, c, _ = place()
-
-    def run(firsts, seconds):
-        for d, piece in zip(ORDER, seconds):
-            second[:, lanes_at(behind(v, d) * BLOCK, BLOCK)] = piece[:BLOCK, :]
-        for d, piece in zip(ORDER, firsts):
-            from_u = behind(u, d)
+def panels(u, v, firsts, seconds, second, first=None, shares=None):
+    for d, piece in zip(ORDER, seconds):
+        second[:, lanes_at(behind(v, d) * BLOCK, BLOCK)] = piece[:BLOCK, :]
+    for d, piece in zip(ORDER, firsts):
+        from_u = behind(u, d)
+        if shares is not None:
             side = piece[BLOCK:, :].astype(F32)
             side = jnp.concatenate([side, jnp.zeros((LANES - 2 * R, BLOCK), F32)], axis=0).T.astype(BF16)
-            for j in range(4):
-                at = rows_at(j * BLOCK + from_u * CHIP, CHIP)
+        for j in range(4):
+            at = rows_at(j * BLOCK + from_u * CHIP, CHIP)
+            if first is not None:
                 first[at, :] = piece[j * CHIP:(j + 1) * CHIP, :]
+            if shares is not None:
                 shares[at, :] = side[j * CHIP:(j + 1) * CHIP, :]
-        total = jnp.dot(second[...], first[...], preferred_element_type=F32)
-        taken = jnp.dot(second[...], shares[...], preferred_element_type=F32).T
-        high, low = halves(total)
-        high_out[...] = high
-        low_out[...] = low
+
+
+def base_block(o0, o1, o2, o3, p0, p1, p2, p3, second_out, base_out, start_out, shares):
+    u, v, c, _ = place()
+
+    def run(firsts, seconds):
+        panels(u, v, firsts, seconds, second_out, shares=shares)
+        taken = jnp.dot(second_out[...], shares[...], preferred_element_type=F32).T
         own = seconds[0][BLOCK:BLOCK + R, :].astype(F32) + seconds[0][BLOCK + R:, :].astype(F32)
         base = own - (taken[:R] + taken[R:2 * R])
         base_out[...] = base
@@ -212,6 +215,24 @@
         run(peer, own)
 
 
+def product_block(o0, o1, o2, o3, p0, p1, p2, p3, second, high_out, low_out, first):
+    u, v, c, _ = place()
+    own, peer = (o0, o1, o2, o3), (p0, p1, p2, p3)
+
+    @pl.when(c == 0)
+    def _():
+        panels(u, v, own, (), second, first=first)
+
+    @pl.when(c != 0)
+    def _():
+        panels(u, v, peer, (), second, first=first)
+
+    total = jnp.dot(second[...], first[...], preferred_element_type=F32)
+    high, low = halves(total)
+    high_out[...] = high
+    low_out[...] = low
+
+
 def pair_sum(r0, r1, out):
     out[...] = r0[...].astype(F32) + r1[...].astype(F32)
 
@@ -225,9 +246,10 @@
     out[...] = onward(own[...] + peer[...], p_high[...], p_low[...], base[...]).astype(BF16)
 
 
-def final_block(own, peer, p_high, p_low, base, message, message_peer, *outs):
+def final_block(*refs):
+    entries, (p_high, p_low, base, message, message_peer), outs = refs[:6], refs[6:11], refs[11:]
     _, v, c, _ = place()
-    entry = own[...] + peer[...]
+    entry = sum(e[...] for e in entries)
     high, low = halves(entry)
     second = onward(entry, p_high[...], p_low[...], base[...])
     first_block = jnp.where(c == 0, message[...], message_peer[...])
@@ -239,15 +261,16 @@
         outs[d][...] = pltpu.roll(states, lax.rem(BLOCK - at, BLOCK), 1)[:, :ROWS]
 
 
-def hop(out):
+def hop(out, plane, *beside):
     arrived = []
     for j in range(2):
         def target(y, x, c, z, j=j):
             y, x, c, _ = along_v(2 * j + c)(y, x, c, z)
-            return (y, x, c, z + 1) if z + 1 < Z else None
+            return (y, x, c, z + 1) if z + 1 == plane else None
         arrived.append(send(out, target))
+    arrived, beside = lax.optimization_barrier((arrived, beside))
     own = call(pair_sum, shape((R, BLOCK), F32), *arrived)
-    return own, to_peer(own)
+    return (own, to_peer(own)), beside
 
 
 def local(inverses, lower, forcing, inflow):
@@ -286,20 +309,23 @@
     )
     turn = around(message, across)
     turn_peer = [to_peer(value) for value in turn]
-    p_high, p_low, base, out = call(
-        product_block,
-        [shape((BLOCK, BLOCK)), shape((BLOCK, BLOCK)), shape((R, BLOCK), F32), shape((R, BLOCK))],
-        *turn, *turn_peer,
-        scratch=[pltpu.VMEM((BLOCK, N), BF16), pltpu.VMEM((N, BLOCK), BF16), pltpu.VMEM((N, LANES), BF16)],
-        flops=2 * BLOCK * BLOCK * N,
-    )
-
-    for step in range(Z - 1):
-        entry = hop(out)
-        if step + 1 < Z - 1:
+    second, base, out = call(
+        base_block, [shape((BLOCK, N)), shape((R, BLOCK), F32), shape((R, BLOCK))], *turn, *turn_peer,
+        scratch=[pltpu.VMEM((N, LANES), BF16)],
+    )
+    p_high, p_low = call(
+        product_block, [shape((BLOCK, BLOCK)), shape((BLOCK, BLOCK))], *turn, *turn_peer, second,
+        scratch=[pltpu.VMEM((N, BLOCK), BF16)], flops=2 * BLOCK * BLOCK * N,
+    )
+
+    entries = []
+    for plane in range(1, Z):
+        entry, (p_high, p_low) = hop(out, plane, p_high, p_low)
+        entries += entry
+        if plane + 1 < Z:
             out = call(hop_block, shape((R, BLOCK)), *entry, p_high, p_low, base)
     finals = call(
-        final_block, [shape((2 * R, ROWS), F32)] * 4, *entry, p_high, p_low, base, turn[0], turn_peer[0]
+        final_block, [shape((2 * R, ROWS), F32)] * 4, *entries, p_high, p_low, base, turn[0], turn_peer[0]
     )
     total = finals[0]
     for d in range(1, 4):

time: 94.2 us -> 81 us (0.86)
  the two profiles are of different devices: /device:TPU:56 before, /device:TPU:96 now
where the time goes in v7:
time: 81 us; the launch traced here: 80.6 us
  waiting for transfers between devices  41.4 us (51%)
  starting transfers between devices  31.4 us (39%)
  Pallas kernels  5.07 us (6%)
  local copies, waits for them, and re-layouts  1.93 us (2%)
    ppermute x32, waiting for transfers between devices, send(): return lax.ppermute(value, AXES, pairs)  41.4 us
    ppermute x32, starting transfers between devices, send(): return lax.ppermute(value, AXES, pairs)  31.4 us
    pallas_call x14, Pallas kernels, call(): pl.pallas_call(kernel, out_shape=out, in_specs=[pl.BlockSpec(memory_space...  5.07 us
    unnamed x8, local copies, waits for them, and re-layouts  1.93 us
  transfers between devices with their start and end apart: 32, of which 16 were waited for; matrix products, arithmetic and copies ran while one was open for 0% of the time, Pallas kernels for 1%

profile of v7, /device:TPU:96, one launch (start us, length us, event | category | flops | bytes accessed | tf_op | source)
XLA Modules:
  0.0 80.6 jit_solution(11588100546226628621)
XLA Ops:
  0.5 1.0 %copy-done.1 = bf16[2,48,1536]{2,1,0:T(8,128)(2,1)S(1)} copy-done((bf16[2,48,1536]{2,1,0:T(8,128)(2,1)S(1)}, bf16[2,48,1536]{2,1,0:T(8,128)(2,1)}, u32[]{:S(2)}) %copy-start.1) | copy-done | bytes 294936
  1.9 1.6 %collective-permute-start.2 = (bf16[96,384]{1,0:T(8,128)(2,1)S(1)}, bf16[96,384]{1,0:T(8,128)(2,1)S(1)}, u32[]{:S(2)}, u32[]{:S(2)}) collective-permute-start(bf16[96,384]{1,0:T(8,128)(2,1)S(1)} %get-tuple-element.34), channel_id=1, source_target_pairs={{0,8},{1,33},{2,10},{3,35},{4,12},{5,37},{6,14},{7,39},{8,16},{9,4... | collective-permute-start | bytes 221192 | tf_op jit(solution)/shard_map/ppermute | solution.py:33
  3.5 2.9 %collective-permute-start.3 = (bf16[96,384]{1,0:T(8,128)(2,1)S(1)}, bf16[96,384]{1,0:T(8,128)(2,1)S(1)}, u32[]{:S(2)}, u32[]{:S(2)}) collective-permute-start(bf16[96,384]{1,0:T(8,128)(2,1)S(1)} %get-tuple-element.38), channel_id=1, source_target_pairs={{0,16},{1,65},{2,18},{3,67},{4,20},{5,69},{6,22},{7,71},{8,24},{9,... | collective-permute-start | bytes 221192 | tf_op jit(solution)/shard_map/ppermute | solution.py:33
  6.4 1.3 %collective-permute-start.4 = (bf16[96,384]{1,0:T(8,128)(2,1)S(1)}, bf16[96,384]{1,0:T(8,128)(2,1)S(1)}, u32[]{:S(2)}, u32[]{:S(2)}) collective-permute-start(bf16[96,384]{1,0:T(8,128)(2,1)S(1)} %get-tuple-element.39), channel_id=1, source_target_pairs={{0,24},{1,97},{2,26},{3,99},{4,28},{5,101},{6,30},{7,103},{8,0},{9... | collective-permute-start | bytes 221192 | tf_op jit(solution)/shard_map/ppermute | solution.py:33
  8.3 1.0 %copy-done = bf16[2,48,1536]{2,1,0:T(8,128)(2,1)S(1)} copy-done((bf16[2,48,1536]{2,1,0:T(8,128)(2,1)S(1)}, bf16[2,48,1536]{2,1,0:T(8,128)(2,1)}, u32[]{:S(2)}) %copy-start) | copy-done | bytes 294936
  9.3 0.9 %collective-permute-done.3.p2 = bf16[96,384]{1,0:T(8,128)(2,1)S(1)} collective-permute-done((bf16[96,384]{1,0:T(8,128)(2,1)S(1)}, bf16[96,384]{1,0:T(8,128)(2,1)S(1)}, u32[]{:S(2)}, u32[]{:S(2)}) %collective-permute-start.3) | collective-permute-done | bytes 73760 | tf_op jit(solution)/shard_map/ppermute | solution.py:33
  10.9 2.6 %collective-permute-start.9 = (bf16[96,1536]{1,0:T(8,128)(2,1)S(1)}, bf16[96,1536]{1,0:T(8,128)(2,1)S(1)}, u32[]{:S(2)}, u32[]{:S(2)}) collective-permute-start(bf16[96,1536]{1,0:T(8,128)(2,1)S(1)} %shard_map.46.a0), channel_id=1, source_target_pairs={{0,24},{1,97},{2,26},{3,99},{4,28},{5,101},{6,30},{7,103},{8,0},{9... | collective-permute-start | bytes 884744 | tf_op jit(solution)/shard_map/ppermute | solution.py:33
  13.5 3.0 %collective-permute-start.12 = (bf16[416,384]{1,0:T(8,128)(2,1)S(1)}, bf16[416,384]{1,0:T(8,128)(2,1)S(1)}, u32[]{:S(2)}, u32[]{:S(2)}) collective-permute-start(bf16[416,384]{1,0:T(8,128)(2,1)S(1)} %shard_map.49.l0), channel_id=1, source_target_pairs={{0,64},{1,17},{2,66},{3,19},{4,68},{5,21},{6,70},{7,23},{8,72},{9,... | collective-permute-start | bytes 958472 | tf_op jit(solution)/shard_map/ppermute | solution.py:33
  17.2 2.6 %collective-permute-start.10 = (bf16[416,384]{1,0:T(8,128)(2,1)S(1)}, bf16[416,384]{1,0:T(8,128)(2,1)S(1)}, u32[]{:S(2)}, u32[]{:S(2)}) collective-permute-start(bf16[416,384]{1,0:T(8,128)(2,1)S(1)} %shard_map.49.l0), channel_id=1, source_target_pairs={{0,96},{1,25},{2,98},{3,27},{4,100},{5,29},{6,102},{7,31},{8,104},... | collective-permute-start | bytes 958472 | tf_op jit(solution)/shard_map/ppermute | solution.py:33
  19.8 1.6 %collective-permute-start.8 = (bf16[96,1536]{1,0:T(8,128)(2,1)S(1)}, bf16[96,1536]{1,0:T(8,128)(2,1)S(1)}, u32[]{:S(2)}, u32[]{:S(2)}) collective-permute-start(bf16[96,1536]{1,0:T(8,128)(2,1)S(1)} %shard_map.46.a0), channel_id=1, source_target_pairs={{0,16},{1,65},{2,18},{3,67},{4,20},{5,69},{6,22},{7,71},{8,24},{9,... | collective-permute-start | bytes 884744 | tf_op jit(solution)/shard_map/ppermute | solution.py:33
  21.4 12.2 %collective-permute-done.7.a1 = bf16[96,1536]{1,0:T(8,128)(2,1)S(1)} collective-permute-done((bf16[96,1536]{1,0:T(8,128)(2,1)S(1)}, bf16[96,1536]{1,0:T(8,128)(2,1)S(1)}, u32[]{:S(2)}, u32[]{:S(2)}) %collective-permute-start.7) | collective-permute-done | bytes 294944 | tf_op jit(solution)/shard_map/ppermute | solution.py:33
  33.7 1.5 %shard_map.51.o0.refs_9_ = bf16[448,384]{1,0:T(8,128)(2,1)S(1)} custom-call(bf16[384,1536]{1,0:T(8,128)(2,1)S(1)} %shard_map.50.panel, bf16[416,384]{1,0:T(8,128)(2,1)S(1)} %shard_map.49.l0, bf16[416,384]{1,0:T(8,128)(2,1)S(1)} %collective-permute-done.10.l1, bf16[416,384]{1,0:T(8,128)(2,1)S(1)} %collective-permute-done.11.l2, ...), custom_call_target="tpu_custom_call" | custom-call | flops 452984832 | bytes 2457600 | tf_op jit(solution)/shard_map/pallas_call | solution.py:81
  35.3 1.1 %collective-permute-start.14 = (bf16[448,384]{1,0:T(8,128)(2,1)S(1)}, bf16[448,384]{1,0:T(8,128)(2,1)S(1)}, u32[]{:S(2)}, u32[]{:S(2)}) collective-permute-start(bf16[448,384]{1,0:T(8,128)(2,1)S(1)} %shard_map.51.o0.refs_9_), channel_id=1, source_target_pairs={{0,32},{1,9},{2,34},{3,11},{4,12},{5,37},{6,14},{7,39},{8,40},{9,1... | collective-permute-start | bytes 1032200 | tf_op jit(solution)/shard_map/ppermute | solution.py:33
  36.4 2.2 %collective-permute-start.13 = (bf16[448,384]{1,0:T(8,128)(2,1)S(1)}, bf16[448,384]{1,0:T(8,128)(2,1)S(1)}, u32[]{:S(2)}, u32[]{:S(2)}) collective-permute-start(bf16[448,384]{1,0:T(8,128)(2,1)S(1)} %shard_map.51.o0.refs_9_), channel_id=1, source_target_pairs={{0,96},{1,25},{2,98},{3,27},{4,28},{5,101},{6,30},{7,103},{8,104},... | collective-permute-start | bytes 1032200 | tf_op jit(solution)/shard_map/ppermute | solution.py:33
  38.6 5.5 %collective-permute-done.15.o3 = bf16[448,384]{1,0:T(8,128)(2,1)S(1)} collective-permute-done((bf16[448,384]{1,0:T(8,128)(2,1)S(1)}, bf16[448,384]{1,0:T(8,128)(2,1)S(1)}, u32[]{:S(2)}, u32[]{:S(2)}) %collective-permute-start.15) | collective-permute-done | bytes 344096 | tf_op jit(solution)/shard_map/ppermute | solution.py:33
  44.2 3.4 %collective-permute-done.14.o2 = bf16[448,384]{1,0:T(8,128)(2,1)S(1)} collective-permute-done((bf16[448,384]{1,0:T(8,128)(2,1)S(1)}, bf16[448,384]{1,0:T(8,128)(2,1)S(1)}, u32[]{:S(2)}, u32[]{:S(2)}) %collective-permute-start.14) | collective-permute-done | bytes 344096 | tf_op jit(solution)/shard_map/ppermute | solution.py:33
  48.0 1.1 %collective-permute-done.18.p2 = bf16[448,384]{1,0:T(8,128)(2,1)S(1)} collective-permute-done((bf16[448,384]{1,0:T(8,128)(2,1)S(1)}, bf16[448,384]{1,0:T(8,128)(2,1)S(1)}, u32[]{:S(2)}, u32[]{:S(2)}) %collective-permute-start.18) | collective-permute-done | bytes 344096 | tf_op jit(solution)/shard_map/ppermute | solution.py:33
  49.7 0.8 %shard_map.52 = (bf16[384,1536]{1,0:T(8,128)(2,1)S(1)}, f32[32,384]{1,0:T(8,128)S(1)}, bf16[32,384]{1,0:T(8,128)(2,1)S(1)}) custom-call(bf16[448,384]{1,0:T(8,128)(2,1)S(1)} %shard_map.51.o0.refs_9_, bf16[448,384]{1,0:T(8,128)(2,1)S(1)} %collective-permute-done.13.o1, bf16[448,384]{1,0:T(8,128)(2,1)S(1)} %collective-permute-done.14.o2, ...), custom_call_target="tpu_custom_call" | custom-call | bytes 2752512 | tf_op jit(solution)/shard_map/pallas_call | solution.py:81
  50.5 0.7 collective-permute-start.21
  51.8 0.9 %shard_map.53 = (bf16[384,384]{1,0:T(8,128)(2,1)S(1)}, bf16[384,384]{1,0:T(8,128)(2,1)S(1)}) custom-call(bf16[448,384]{1,0:T(8,128)(2,1)S(1)} %shard_map.51.o0.refs_9_, bf16[448,384]{1,0:T(8,128)(2,1)S(1)} %collective-permute-done.13.o1, bf16[448,384]{1,0:T(8,128)(2,1)S(1)} %collective-permute-done.14.o2, bf16[448,384]{1,0:T(8,128)(2,1)S(1)} %collective-permute-done.15.o3, ...), custom_call_target="tpu_custom_call" | custom-call | flops 452984832 | bytes 3932160 | tf_op jit(solution)/shard_map/pallas_call | solution.py:81
  53.0 1.1 %collective-permute-done.22.peer.refs_1_ = f32[32,384]{1,0:T(8,128)S(1)} collective-permute-done((f32[32,384]{1,0:T(8,128)S(1)}, f32[32,384]{1,0:T(8,128)S(1)}, u32[]{:S(2)}, u32[]{:S(2)}) %collective-permute-start.22) | collective-permute-done | bytes 49184 | tf_op jit(solution)/shard_map/ppermute | solution.py:33
  54.5 0.7 collective-permute-start.24
  56.1 1.1 %collective-permute-done.25.peer.refs_3_ = f32[32,384]{1,0:T(8,128)S(1)} collective-permute-done((f32[32,384]{1,0:T(8,128)S(1)}, f32[32,384]{1,0:T(8,128)S(1)}, u32[]{:S(2)}, u32[]{:S(2)}) %collective-permute-start.25) | collective-permute-done | bytes 49184 | tf_op jit(solution)/shard_map/ppermute | solution.py:33
  57.6 1.3 %collective-permute-start.27 = (bf16[32,384]{1,0:T(8,128)(2,1)S(1)}, bf16[32,384]{1,0:T(8,128)(2,1)S(1)}, u32[]{:S(2)}, u32[]{:S(2)}) collective-permute-start(bf16[32,384]{1,0:T(8,128)(2,1)S(1)} %shard_map.57), channel_id=1, source_target_pairs={{2,19},{6,31},{10,27},{14,7},{18,3},{22,15},{26,11},{30,23},{34,51... | collective-permute-start | bytes 73736 | tf_op jit(solution)/shard_map/ppermute | solution.py:33
  58.9 1.3 %collective-permute-start.26 = (bf16[32,384]{1,0:T(8,128)(2,1)S(1)}, bf16[32,384]{1,0:T(8,128)(2,1)S(1)}, u32[]{:S(2)}, u32[]{:S(2)}) collective-permute-start(bf16[32,384]{1,0:T(8,128)(2,1)S(1)} %shard_map.57), channel_id=1, source_target_pairs={{2,3},{6,15},{10,11},{14,23},{18,19},{22,31},{26,27},{30,7},{34,35... | collective-permute-start | bytes 73736 | tf_op jit(solution)/shard_map/ppermute | solution.py:33
  60.2 11.2 %collective-permute-done.27.r1 = bf16[32,384]{1,0:T(8,128)(2,1)S(1)} collective-permute-done((bf16[32,384]{1,0:T(8,128)(2,1)S(1)}, bf16[32,384]{1,0:T(8,128)(2,1)S(1)}, u32[]{:S(2)}, u32[]{:S(2)}) %collective-permute-start.27) | collective-permute-done | bytes 24608 | tf_op jit(solution)/shard_map/ppermute | solution.py:33
  71.7 1.2 %collective-permute-done.28.refs_5_ = f32[32,384]{1,0:T(8,128)S(1)} collective-permute-done((f32[32,384]{1,0:T(8,128)S(1)}, f32[32,384]{1,0:T(8,128)S(1)}, u32[]{:S(2)}, u32[]{:S(2)}) %collective-permute-start.28) | collective-permute-done | bytes 49184 | tf_op jit(solution)/shard_map/ppermute | solution.py:33
  72.9 0.7 shard_map.59
  74.3 1.4 %collective-permute-start.30 = (f32[64,48]{1,0:T(8,128)S(1)}, f32[64,48]{1,0:T(8,128)S(1)}, u32[]{:S(2)}, u32[]{:S(2)}) collective-permute-start(f32[64,48]{1,0:T(8,128)S(1)} %get-tuple-element.61), channel_id=1, source_target_pairs={{0,16},{1,65},{2,18},{3,67},{4,20},{5,69},{6,22},{7,71},{8,24},{9,... | collective-permute-start | bytes 36872 | tf_op jit(solution)/shard_map/ppermute | solution.py:33
  75.6 2.3 %collective-permute-start.31 = (f32[64,48]{1,0:T(8,128)S(1)}, f32[64,48]{1,0:T(8,128)S(1)}, u32[]{:S(2)}, u32[]{:S(2)}) collective-permute-start(f32[64,48]{1,0:T(8,128)S(1)} %get-tuple-element.62), channel_id=1, source_target_pairs={{0,24},{1,97},{2,26},{3,99},{4,28},{5,101},{6,30},{7,103},{8,0},{9... | collective-permute-start | bytes 36872 | tf_op jit(solution)/shard_map/ppermute | solution.py:33
  78.0 1.0 %collective-permute-done.29 = f32[64,48]{1,0:T(8,128)S(1)} collective-permute-done((f32[64,48]{1,0:T(8,128)S(1)}, f32[64,48]{1,0:T(8,128)S(1)}, u32[]{:S(2)}, u32[]{:S(2)}) %collective-permute-start.29) | collective-permute-done | bytes 12320 | tf_op jit(solution)/shard_map/ppermute | solution.py:33
  78.9 0.7 collective-permute-done.30
  (55 shorter events, 8.5 us)
Async XLA Ops:
  0.0 1.8 %collective-permute-start.1 = (bf16[2,48,1536]{2,1,0:T(8,128)(2,1)}, bf16[2,48,1536]{2,1,0:T(8,128)(2,1)S(1)}, u32[]{:S(2)}, u32[]{:S(2)}) collective-permute-start(bf16[2,48,1536]{2,1,0:T(8,128)(2,1)} %own.3), channel_id=1, source_target_pairs={{0,4},{1,5},{2,6},{3,7},{4,0},{5,1},{6,2},{7,3},{8,12},{9,13},{10,... | collective-permute-start | bytes 884744 | tf_op jit(solution)/shard_map/ppermute | solution.py:33
  0.0 7.8 %collective-permute-start = (bf16[2,48,1536]{2,1,0:T(8,128)(2,1)}, bf16[2,48,1536]{2,1,0:T(8,128)(2,1)S(1)}, u32[]{:S(2)}, u32[]{:S(2)}) collective-permute-start(bf16[2,48,1536]{2,1,0:T(8,128)(2,1)} %own.2), channel_id=1, source_target_pairs={{0,4},{1,5},{2,6},{3,7},{4,0},{5,1},{6,2},{7,3},{8,12},{9,13},{10,... | collective-permute-start | bytes 884744 | tf_op jit(solution)/shard_map/ppermute | solution.py:33
  1.9 7.4 %collective-permute-start.2 = (bf16[96,384]{1,0:T(8,128)(2,1)S(1)}, bf16[96,384]{1,0:T(8,128)(2,1)S(1)}, u32[]{:S(2)}, u32[]{:S(2)}) collective-permute-start(bf16[96,384]{1,0:T(8,128)(2,1)S(1)} %get-tuple-element.34), channel_id=1, source_target_pairs={{0,8},{1,33},{2,10},{3,35},{4,12},{5,37},{6,14},{7,39},{8,16},{9,4... | collective-permute-start | bytes 221192 | tf_op jit(solution)/shard_map/ppermute | solution.py:33
  3.5 6.8 %collective-permute-start.3 = (bf16[96,384]{1,0:T(8,128)(2,1)S(1)}, bf16[96,384]{1,0:T(8,128)(2,1)S(1)}, u32[]{:S(2)}, u32[]{:S(2)}) collective-permute-start(bf16[96,384]{1,0:T(8,128)(2,1)S(1)} %get-tuple-element.38), channel_id=1, source_target_pairs={{0,16},{1,65},{2,18},{3,67},{4,20},{5,69},{6,22},{7,71},{8,24},{9,... | collective-permute-start | bytes 221192 | tf_op jit(solution)/shard_map/ppermute | solution.py:33
  6.4 4.4 %collective-permute-start.4 = (bf16[96,384]{1,0:T(8,128)(2,1)S(1)}, bf16[96,384]{1,0:T(8,128)(2,1)S(1)}, u32[]{:S(2)}, u32[]{:S(2)}) collective-permute-start(bf16[96,384]{1,0:T(8,128)(2,1)S(1)} %get-tuple-element.39), channel_id=1, source_target_pairs={{0,24},{1,97},{2,26},{3,99},{4,28},{5,101},{6,30},{7,103},{8,0},{9... | collective-permute-start | bytes 221192 | tf_op jit(solution)/shard_map/ppermute | solution.py:33
  7.8 1.5 %collective-permute-start.5 = (bf16[2,32,48]{2,1,0:T(8,128)(2,1)}, bf16[2,32,48]{2,1,0:T(8,128)(2,1)S(1)}, u32[]{:S(2)}, u32[]{:S(2)}) collective-permute-start(bf16[2,32,48]{2,1,0:T(8,128)(2,1)} %bitcast.5), channel_id=1, source_target_pairs={{0,4},{1,5},{2,6},{3,7},{4,0},{5,1},{6,2},{7,3},{8,12},{9,13},{10,... | collective-permute-start | bytes 18440 | tf_op jit(solution)/shard_map/ppermute | solution.py:33
  7.8 1.6 %collective-permute-start.6 = (f32[32,48]{1,0:T(8,128)}, f32[32,48]{1,0:T(8,128)S(1)}, u32[]{:S(2)}, u32[]{:S(2)}) collective-permute-start(f32[32,48]{1,0:T(8,128)} %bitcast.7), channel_id=1, source_target_pairs={{0,4},{1,5},{2,6},{3,7},{4,0},{5,1},{6,2},{7,3},{8,12},{9,13},{10,... | collective-permute-start | bytes 18440 | tf_op jit(solution)/shard_map/ppermute | solution.py:33
  10.9 8.9 %collective-permute-start.9 = (bf16[96,1536]{1,0:T(8,128)(2,1)S(1)}, bf16[96,1536]{1,0:T(8,128)(2,1)S(1)}, u32[]{:S(2)}, u32[]{:S(2)}) collective-permute-start(bf16[96,1536]{1,0:T(8,128)(2,1)S(1)} %shard_map.46.a0), channel_id=1, source_target_pairs={{0,24},{1,97},{2,26},{3,99},{4,28},{5,101},{6,30},{7,103},{8,0},{9... | collective-permute-start | bytes 884744 | tf_op jit(solution)/shard_map/ppermute | solution.py:33
  13.5 20.1 %collective-permute-start.12 = (bf16[416,384]{1,0:T(8,128)(2,1)S(1)}, bf16[416,384]{1,0:T(8,128)(2,1)S(1)}, u32[]{:S(2)}, u32[]{:S(2)}) collective-permute-start(bf16[416,384]{1,0:T(8,128)(2,1)S(1)} %shard_map.49.l0), channel_id=1, source_target_pairs={{0,64},{1,17},{2,66},{3,19},{4,68},{5,21},{6,70},{7,23},{8,72},{9,... | collective-permute-start | bytes 958472 | tf_op jit(solution)/shard_map/ppermute | solution.py:33
  16.6 17.1 %collective-permute-start.11 = (bf16[416,384]{1,0:T(8,128)(2,1)S(1)}, bf16[416,384]{1,0:T(8,128)(2,1)S(1)}, u32[]{:S(2)}, u32[]{:S(2)}) collective-permute-start(bf16[416,384]{1,0:T(8,128)(2,1)S(1)} %shard_map.49.l0), channel_id=1, source_target_pairs={{0,32},{1,9},{2,34},{3,11},{4,36},{5,13},{6,38},{7,15},{8,40},{9,1... | collective-permute-start | bytes 958472 | tf_op jit(solution)/shard_map/ppermute | solution.py:33
  17.2 16.5 %collective-permute-start.10 = (bf16[416,384]{1,0:T(8,128)(2,1)S(1)}, bf16[416,384]{1,0:T(8,128)(2,1)S(1)}, u32[]{:S(2)}, u32[]{:S(2)}) collective-permute-start(bf16[416,384]{1,0:T(8,128)(2,1)S(1)} %shard_map.49.l0), channel_id=1, source_target_pairs={{0,96},{1,25},{2,98},{3,27},{4,100},{5,29},{6,102},{7,31},{8,104},... | collective-permute-start | bytes 958472 | tf_op jit(solution)/shard_map/ppermute | solution.py:33
  19.8 13.8 %collective-permute-start.7 = (bf16[96,1536]{1,0:T(8,128)(2,1)S(1)}, bf16[96,1536]{1,0:T(8,128)(2,1)S(1)}, u32[]{:S(2)}, u32[]{:S(2)}) collective-permute-start(bf16[96,1536]{1,0:T(8,128)(2,1)S(1)} %shard_map.46.a0), channel_id=1, source_target_pairs={{0,8},{1,33},{2,10},{3,35},{4,12},{5,37},{6,14},{7,39},{8,16},{9,4... | collective-permute-start | bytes 884744 | tf_op jit(solution)/shard_map/ppermute | solution.py:33
  19.8 13.7 %collective-permute-start.8 = (bf16[96,1536]{1,0:T(8,128)(2,1)S(1)}, bf16[96,1536]{1,0:T(8,128)(2,1)S(1)}, u32[]{:S(2)}, u32[]{:S(2)}) collective-permute-start(bf16[96,1536]{1,0:T(8,128)(2,1)S(1)} %shard_map.46.a0), channel_id=1, source_target_pairs={{0,16},{1,65},{2,18},{3,67},{4,20},{5,69},{6,22},{7,71},{8,24},{9,... | collective-permute-start | bytes 884744 | tf_op jit(solution)/shard_map/ppermute | solution.py:33
  35.2 8.9 %collective-permute-start.15 = (bf16[448,384]{1,0:T(8,128)(2,1)S(1)}, bf16[448,384]{1,0:T(8,128)(2,1)S(1)}, u32[]{:S(2)}, u32[]{:S(2)}) collective-permute-start(bf16[448,384]{1,0:T(8,128)(2,1)S(1)} %shard_map.51.o0.refs_9_), channel_id=1, source_target_pairs={{0,64},{1,17},{2,66},{3,19},{4,20},{5,69},{6,22},{7,71},{8,72},{9,... | collective-permute-start | bytes 1032200 | tf_op jit(solution)/shard_map/ppermute | solution.py:33
  35.3 12.2 %collective-permute-start.14 = (bf16[448,384]{1,0:T(8,128)(2,1)S(1)}, bf16[448,384]{1,0:T(8,128)(2,1)S(1)}, u32[]{:S(2)}, u32[]{:S(2)}) collective-permute-start(bf16[448,384]{1,0:T(8,128)(2,1)S(1)} %shard_map.51.o0.refs_9_), channel_id=1, source_target_pairs={{0,32},{1,9},{2,34},{3,11},{4,12},{5,37},{6,14},{7,39},{8,40},{9,1... | collective-permute-start | bytes 1032200 | tf_op jit(solution)/shard_map/ppermute | solution.py:33
  36.4 11.1 %collective-permute-start.13 = (bf16[448,384]{1,0:T(8,128)(2,1)S(1)}, bf16[448,384]{1,0:T(8,128)(2,1)S(1)}, u32[]{:S(2)}, u32[]{:S(2)}) collective-permute-start(bf16[448,384]{1,0:T(8,128)(2,1)S(1)} %shard_map.51.o0.refs_9_), channel_id=1, source_target_pairs={{0,96},{1,25},{2,98},{3,27},{4,28},{5,101},{6,30},{7,103},{8,104},... | collective-permute-start | bytes 1032200 | tf_op jit(solution)/shard_map/ppermute | solution.py:33
  38.6 9.4 %collective-permute-start.16 = (bf16[448,384]{1,0:T(8,128)(2,1)S(1)}, bf16[448,384]{1,0:T(8,128)(2,1)S(1)}, u32[]{:S(2)}, u32[]{:S(2)}) collective-permute-start(bf16[448,384]{1,0:T(8,128)(2,1)S(1)} %shard_map.51.o0.refs_9_), channel_id=1, source_target_pairs={{0,4},{1,5},{2,6},{3,7},{4,0},{5,1},{6,2},{7,3},{8,12},{9,13},{10,... | collective-permute-start | bytes 1032200 | tf_op jit(solution)/shard_map/ppermute | solution.py:33
  44.1 3.9 %collective-permute-start.19 = (bf16[448,384]{1,0:T(8,128)(2,1)S(1)}, bf16[448,384]{1,0:T(8,128)(2,1)S(1)}, u32[]{:S(2)}, u32[]{:S(2)}) collective-permute-start(bf16[448,384]{1,0:T(8,128)(2,1)S(1)} %collective-permute-done.15.o3), channel_id=1, source_target_pairs={{0,4},{1,5},{2,6},{3,7},{4,0},{5,1},{6,2},{7,3},{8,12},{9,13},{10,... | collective-permute-start | bytes 1032200 | tf_op jit(solution)/shard_map/ppermute | solution.py:33
  47.5 1.7 %collective-permute-start.18 = (bf16[448,384]{1,0:T(8,128)(2,1)S(1)}, bf16[448,384]{1,0:T(8,128)(2,1)S(1)}, u32[]{:S(2)}, u32[]{:S(2)}) collective-permute-start(bf16[448,384]{1,0:T(8,128)(2,1)S(1)} %collective-permute-done.14.o2), channel_id=1, source_target_pairs={{0,4},{1,5},{2,6},{3,7},{4,0},{5,1},{6,2},{7,3},{8,12},{9,13},{10,... | collective-permute-start | bytes 1032200 | tf_op jit(solution)/shard_map/ppermute | solution.py:33
  47.5 2.1 %collective-permute-start.17 = (bf16[448,384]{1,0:T(8,128)(2,1)S(1)}, bf16[448,384]{1,0:T(8,128)(2,1)S(1)}, u32[]{:S(2)}, u32[]{:S(2)}) collective-permute-start(bf16[448,384]{1,0:T(8,128)(2,1)S(1)} %collective-permute-done.13.o1), channel_id=1, source_target_pairs={{0,4},{1,5},{2,6},{3,7},{4,0},{5,1},{6,2},{7,3},{8,12},{9,13},{10,... | collective-permute-start | bytes 1032200 | tf_op jit(solution)/shard_map/ppermute | solution.py:33
  50.5 2.3 %collective-permute-start.21 = (bf16[32,384]{1,0:T(8,128)(2,1)S(1)}, bf16[32,384]{1,0:T(8,128)(2,1)S(1)}, u32[]{:S(2)}, u32[]{:S(2)}) collective-permute-start(bf16[32,384]{1,0:T(8,128)(2,1)S(1)} %get-tuple-element.42), channel_id=1, source_target_pairs={{0,17},{4,29},{8,25},{12,5},{16,1},{20,13},{24,9},{28,21},{32,49},... | collective-permute-start | bytes 73736 | tf_op jit(solution)/shard_map/ppermute | solution.py:33
  51.2 1.6 %collective-permute-start.20 = (bf16[32,384]{1,0:T(8,128)(2,1)S(1)}, bf16[32,384]{1,0:T(8,128)(2,1)S(1)}, u32[]{:S(2)}, u32[]{:S(2)}) collective-permute-start(bf16[32,384]{1,0:T(8,128)(2,1)S(1)} %get-tuple-element.42), channel_id=1, source_target_pairs={{0,1},{4,13},{8,9},{12,21},{16,17},{20,29},{24,25},{28,5},{32,33},... | collective-permute-start | bytes 73736 | tf_op jit(solution)/shard_map/ppermute | solution.py:33
  52.8 1.3 %collective-permute-start.22 = (f32[32,384]{1,0:T(8,128)S(1)}, f32[32,384]{1,0:T(8,128)S(1)}, u32[]{:S(2)}, u32[]{:S(2)}) collective-permute-start(f32[32,384]{1,0:T(8,128)S(1)} %shard_map.54.own.refs_0_), channel_id=1, source_target_pairs={{0,4},{1,5},{2,6},{3,7},{4,0},{5,1},{6,2},{7,3},{8,12},{9,13},{10,... | collective-permute-start | bytes 147464 | tf_op jit(solution)/shard_map/ppermute | solution.py:33
  54.5 1.4 %collective-permute-start.24 = (bf16[32,384]{1,0:T(8,128)(2,1)S(1)}, bf16[32,384]{1,0:T(8,128)(2,1)S(1)}, u32[]{:S(2)}, u32[]{:S(2)}) collective-permute-start(bf16[32,384]{1,0:T(8,128)(2,1)S(1)} %shard_map.55), channel_id=1, source_target_pairs={{1,66},{5,102},{9,74},{13,110},{17,82},{21,118},{25,90},{29,126},{... | collective-permute-start | bytes 73736 | tf_op jit(solution)/shard_map/ppermute | solution.py:33
  55.2 0.7 collective-permute-start.23
  55.9 1.3 %collective-permute-start.25 = (f32[32,384]{1,0:T(8,128)S(1)}, f32[32,384]{1,0:T(8,128)S(1)}, u32[]{:S(2)}, u32[]{:S(2)}) collective-permute-start(f32[32,384]{1,0:T(8,128)S(1)} %shard_map.56.own.refs_2_), channel_id=1, source_target_pairs={{0,4},{1,5},{2,6},{3,7},{4,0},{5,1},{6,2},{7,3},{8,12},{9,13},{10,... | collective-permute-start | bytes 147464 | tf_op jit(solution)/shard_map/ppermute | solution.py:33
  57.6 13.8 %collective-permute-start.27 = (bf16[32,384]{1,0:T(8,128)(2,1)S(1)}, bf16[32,384]{1,0:T(8,128)(2,1)S(1)}, u32[]{:S(2)}, u32[]{:S(2)}) collective-permute-start(bf16[32,384]{1,0:T(8,128)(2,1)S(1)} %shard_map.57), channel_id=1, source_target_pairs={{2,19},{6,31},{10,27},{14,7},{18,3},{22,15},{26,11},{30,23},{34,51... | collective-permute-start | bytes 73736 | tf_op jit(solution)/shard_map/ppermute | solution.py:33
  58.9 12.7 %collective-permute-start.26 = (bf16[32,384]{1,0:T(8,128)(2,1)S(1)}, bf16[32,384]{1,0:T(8,128)(2,1)S(1)}, u32[]{:S(2)}, u32[]{:S(2)}) collective-permute-start(bf16[32,384]{1,0:T(8,128)(2,1)S(1)} %shard_map.57), channel_id=1, source_target_pairs={{2,3},{6,15},{10,11},{14,23},{18,19},{22,31},{26,27},{30,7},{34,35... | collective-permute-start | bytes 73736 | tf_op jit(solution)/shard_map/ppermute | solution.py:33
  71.6 1.3 %collective-permute-start.28 = (f32[32,384]{1,0:T(8,128)S(1)}, f32[32,384]{1,0:T(8,128)S(1)}, u32[]{:S(2)}, u32[]{:S(2)}) collective-permute-start(f32[32,384]{1,0:T(8,128)S(1)} %shard_map.58.refs_4_), channel_id=1, source_target_pairs={{0,4},{1,5},{2,6},{3,7},{4,0},{5,1},{6,2},{7,3},{8,12},{9,13},{10,... | collective-permute-start | bytes 147464 | tf_op jit(solution)/shard_map/ppermute | solution.py:33
  73.6 5.3 %collective-permute-start.29 = (f32[64,48]{1,0:T(8,128)S(1)}, f32[64,48]{1,0:T(8,128)S(1)}, u32[]{:S(2)}, u32[]{:S(2)}) collective-permute-start(f32[64,48]{1,0:T(8,128)S(1)} %get-tuple-element.60), channel_id=1, source_target_pairs={{0,8},{1,33},{2,10},{3,35},{4,12},{5,37},{6,14},{7,39},{8,16},{9,4... | collective-permute-start | bytes 36872 | tf_op jit(solution)/shard_map/ppermute | solution.py:33
  74.3 5.4 %collective-permute-start.30 = (f32[64,48]{1,0:T(8,128)S(1)}, f32[64,48]{1,0:T(8,128)S(1)}, u32[]{:S(2)}, u32[]{:S(2)}) collective-permute-start(f32[64,48]{1,0:T(8,128)S(1)} %get-tuple-element.61), channel_id=1, source_target_pairs={{0,16},{1,65},{2,18},{3,67},{4,20},{5,69},{6,22},{7,71},{8,24},{9,... | collective-permute-start | bytes 36872 | tf_op jit(solution)/shard_map/ppermute | solution.py:33
  75.6 4.4 %collective-permute-start.31 = (f32[64,48]{1,0:T(8,128)S(1)}, f32[64,48]{1,0:T(8,128)S(1)}, u32[]{:S(2)}, u32[]{:S(2)}) collective-permute-start(f32[64,48]{1,0:T(8,128)S(1)} %get-tuple-element.62), channel_id=1, source_target_pairs={{0,24},{1,97},{2,26},{3,99},{4,28},{5,101},{6,30},{7,103},{8,0},{9... | collective-permute-start | bytes 36872 | tf_op jit(solution)/shard_map/ppermute | solution.py:33
  (4 other events, 20.6 us)

commit v8 on v7

--- a/solution.py
+++ b/solution.py
@@ -13,7 +13,7 @@
 N = BLOCK * Y
 R = 32
 LANES = 128
-ORDER = (0, 3, 1, 2)
+ORDER = (0, 2, 1, 3)
 F32, BF16 = jnp.float32, jnp.bfloat16
 
 
@@ -134,7 +134,7 @@
     out[rows_at((1 - c) * ROWS, ROWS), :] = peer[c]
 
 
-def inverse_panel(a0, a1, a2, a3, out):
+def inverse_panel(a0, a3, a2, a1, out):
     v = place()[1]
     for d, piece in enumerate((a0, a1, a2, a3)):
         out[rows_at(behind(v, d) * CHIP, CHIP), :] = piece[...]
@@ -171,10 +171,8 @@
     known = known[:, R:2 * R] + known[:, 2 * R:3 * R]
     share = share - jnp.where((z == 0) & (c == 0), known, 0.0)
     share = jnp.concatenate([share, jnp.zeros((BLOCK, LANES - R), F32)], axis=1).T[:R]
-    high, low = halves(share)
     out[:BLOCK, :] = block
-    out[BLOCK:BLOCK + R, :] = high
-    out[BLOCK + R:, :] = low
+    out[BLOCK:, :] = share.astype(BF16)
 
 
 def panels(u, v, firsts, seconds, second, first=None, shares=None):
@@ -184,7 +182,7 @@
         from_u = behind(u, d)
         if shares is not None:
             side = piece[BLOCK:, :].astype(F32)
-            side = jnp.concatenate([side, jnp.zeros((LANES - 2 * R, BLOCK), F32)], axis=0).T.astype(BF16)
+            side = jnp.concatenate([side, jnp.zeros((LANES - R, BLOCK), F32)], axis=0).T.astype(BF16)
         for j in range(4):
             at = rows_at(j * BLOCK + from_u * CHIP, CHIP)
             if first is not None:
@@ -199,8 +197,7 @@
     def run(firsts, seconds):
         panels(u, v, firsts, seconds, second_out, shares=shares)
         taken = jnp.dot(second_out[...], shares[...], preferred_element_type=F32).T
-        own = seconds[0][BLOCK:BLOCK + R, :].astype(F32) + seconds[0][BLOCK + R:, :].astype(F32)
-        base = own - (taken[:R] + taken[R:2 * R])
+        base = seconds[0][BLOCK:, :].astype(F32) - taken[:R]
         base_out[...] = base
         start_out[...] = base.astype(BF16)
 
@@ -253,8 +250,7 @@
     high, low = halves(entry)
     second = onward(entry, p_high[...], p_low[...], base[...])
     first_block = jnp.where(c == 0, message[...], message_peer[...])
-    first = first_block[BLOCK:BLOCK + R, :].astype(F32) + first_block[BLOCK + R:, :].astype(F32)
-    first = first - (nt(high, first_block[:BLOCK, :]) + nt(low, first_block[:BLOCK, :]))
+    first = first_block[BLOCK:, :].astype(F32) - (nt(high, first_block[:BLOCK, :]) + nt(low, first_block[:BLOCK, :]))
     states = jnp.concatenate([first, second], axis=0)
     for d in range(4):
         at = lax.rem(v + d, 4) * CHIP + c * ROWS
@@ -296,12 +292,12 @@
     )
     inv_own, own = lax.optimization_barrier((inv_own, own))
     inv_3, inv_1 = send(inv_own, along_v(3)), send(inv_own, along_v(1))
-    inv = [inv_own, inv_1, inv_2, inv_3]
+    inv = [inv_own, inv_3, inv_2, inv_1]
     inv_panel = call(inverse_panel, shape((BLOCK, N)), *inv)
     panel = around(own, along_u)
 
     message = call(
-        coupling_block, shape((BLOCK + 2 * R, BLOCK)), inv_panel, *panel,
+        coupling_block, shape((BLOCK + R, BLOCK)), inv_panel, *panel,
         scratch=[
             pltpu.VMEM((N, BLOCK), BF16), pltpu.VMEM((N, LANES), BF16), pltpu.VMEM((BLOCK, LANES), BF16),
         ],

time: 81 us -> 80.4 us (level)
  starting transfers between devices: 31.4 us -> 29.8 us
  waiting for transfers between devices: 41.4 us -> 42.6 us
    ppermute x32, starting transfers between devices: 31.4 us -> 29.8 us  [send(): return lax.ppermute(value, AXES, pairs)]
    ppermute x32, waiting for transfers between devices: 41.4 us -> 42.6 us  [send(): return lax.ppermute(value, AXES, pairs)]
  transfers between devices with their start and end apart: 32 -> 32, of which waited for: 16 -> 18; matrix products, arithmetic and copies ran while one was open for 0% -> 0% of each run, Pallas kernels for 1% -> 1%
where the time goes in v8:
time: 80.4 us; the launch traced here: 80.2 us
  waiting for transfers between devices  42.6 us (53%)
  starting transfers between devices  29.8 us (37%)
  Pallas kernels  5.07 us (6%)
  local copies, waits for them, and re-layouts  1.93 us (2%)
    ppermute x32, waiting for transfers between devices, send(): return lax.ppermute(value, AXES, pairs)  42.6 us
    ppermute x32, starting transfers between devices, send(): return lax.ppermute(value, AXES, pairs)  29.8 us
    pallas_call x14, Pallas kernels, call(): pl.pallas_call(kernel, out_shape=out, in_specs=[pl.BlockSpec(memory_space...  5.07 us
    unnamed x8, local copies, waits for them, and re-layouts  1.93 us
  transfers between devices with their start and end apart: 32, of which 18 were waited for; matrix products, arithmetic and copies ran while one was open for 0% of the time, Pallas kernels for 1%

profile of v8, /device:TPU:96, one launch (start us, length us, event | category | flops | bytes accessed | tf_op | source)
XLA Modules:
  0.0 80.2 jit_solution(6194465221866377266)
XLA Ops:
  0.5 1.0 %copy-done.1 = bf16[2,48,1536]{2,1,0:T(8,128)(2,1)S(1)} copy-done((bf16[2,48,1536]{2,1,0:T(8,128)(2,1)S(1)}, bf16[2,48,1536]{2,1,0:T(8,128)(2,1)}, u32[]{:S(2)}) %copy-start.1) | copy-done | bytes 294936
  1.9 1.6 %collective-permute-start.2 = (bf16[96,384]{1,0:T(8,128)(2,1)S(1)}, bf16[96,384]{1,0:T(8,128)(2,1)S(1)}, u32[]{:S(2)}, u32[]{:S(2)}) collective-permute-start(bf16[96,384]{1,0:T(8,128)(2,1)S(1)} %get-tuple-element.34), channel_id=1, source_target_pairs={{0,8},{1,33},{2,10},{3,35},{4,12},{5,37},{6,14},{7,39},{8,16},{9,4... | collective-permute-start | bytes 221192 | tf_op jit(solution)/shard_map/ppermute | solution.py:33
  3.5 2.9 %collective-permute-start.3 = (bf16[96,384]{1,0:T(8,128)(2,1)S(1)}, bf16[96,384]{1,0:T(8,128)(2,1)S(1)}, u32[]{:S(2)}, u32[]{:S(2)}) collective-permute-start(bf16[96,384]{1,0:T(8,128)(2,1)S(1)} %get-tuple-element.38), channel_id=1, source_target_pairs={{0,16},{1,65},{2,18},{3,67},{4,20},{5,69},{6,22},{7,71},{8,24},{9,... | collective-permute-start | bytes 221192 | tf_op jit(solution)/shard_map/ppermute | solution.py:33
  6.4 1.3 %collective-permute-start.4 = (bf16[96,384]{1,0:T(8,128)(2,1)S(1)}, bf16[96,384]{1,0:T(8,128)(2,1)S(1)}, u32[]{:S(2)}, u32[]{:S(2)}) collective-permute-start(bf16[96,384]{1,0:T(8,128)(2,1)S(1)} %get-tuple-element.39), channel_id=1, source_target_pairs={{0,24},{1,97},{2,26},{3,99},{4,28},{5,101},{6,30},{7,103},{8,0},{9... | collective-permute-start | bytes 221192 | tf_op jit(solution)/shard_map/ppermute | solution.py:33
  8.3 1.0 %copy-done = bf16[2,48,1536]{2,1,0:T(8,128)(2,1)S(1)} copy-done((bf16[2,48,1536]{2,1,0:T(8,128)(2,1)S(1)}, bf16[2,48,1536]{2,1,0:T(8,128)(2,1)}, u32[]{:S(2)}) %copy-start) | copy-done | bytes 294936
  9.3 0.9 %collective-permute-done.3.p2 = bf16[96,384]{1,0:T(8,128)(2,1)S(1)} collective-permute-done((bf16[96,384]{1,0:T(8,128)(2,1)S(1)}, bf16[96,384]{1,0:T(8,128)(2,1)S(1)}, u32[]{:S(2)}, u32[]{:S(2)}) %collective-permute-start.3) | collective-permute-done | bytes 73760 | tf_op jit(solution)/shard_map/ppermute | solution.py:33
  10.9 0.8 %collective-permute-start.9 = (bf16[96,1536]{1,0:T(8,128)(2,1)S(1)}, bf16[96,1536]{1,0:T(8,128)(2,1)S(1)}, u32[]{:S(2)}, u32[]{:S(2)}) collective-permute-start(bf16[96,1536]{1,0:T(8,128)(2,1)S(1)} %shard_map.46.a0), channel_id=1, source_target_pairs={{0,8},{1,33},{2,10},{3,35},{4,12},{5,37},{6,14},{7,39},{8,16},{9,4... | collective-permute-start | bytes 884744 | tf_op jit(solution)/shard_map/ppermute | solution.py:33
  11.7 2.8 %collective-permute-start.12 = (bf16[416,384]{1,0:T(8,128)(2,1)S(1)}, bf16[416,384]{1,0:T(8,128)(2,1)S(1)}, u32[]{:S(2)}, u32[]{:S(2)}) collective-permute-start(bf16[416,384]{1,0:T(8,128)(2,1)S(1)} %shard_map.49.l0), channel_id=1, source_target_pairs={{0,96},{1,25},{2,98},{3,27},{4,100},{5,29},{6,102},{7,31},{8,104},... | collective-permute-start | bytes 958472 | tf_op jit(solution)/shard_map/ppermute | solution.py:33
  14.5 2.3 %collective-permute-start.10 = (bf16[416,384]{1,0:T(8,128)(2,1)S(1)}, bf16[416,384]{1,0:T(8,128)(2,1)S(1)}, u32[]{:S(2)}, u32[]{:S(2)}) collective-permute-start(bf16[416,384]{1,0:T(8,128)(2,1)S(1)} %shard_map.49.l0), channel_id=1, source_target_pairs={{0,64},{1,17},{2,66},{3,19},{4,68},{5,21},{6,70},{7,23},{8,72},{9,... | collective-permute-start | bytes 958472 | tf_op jit(solution)/shard_map/ppermute | solution.py:33
  16.8 2.5 %collective-permute-start.7 = (bf16[96,1536]{1,0:T(8,128)(2,1)S(1)}, bf16[96,1536]{1,0:T(8,128)(2,1)S(1)}, u32[]{:S(2)}, u32[]{:S(2)}) collective-permute-start(bf16[96,1536]{1,0:T(8,128)(2,1)S(1)} %shard_map.46.a0), channel_id=1, source_target_pairs={{0,24},{1,97},{2,26},{3,99},{4,28},{5,101},{6,30},{7,103},{8,0},{9... | collective-permute-start | bytes 884744 | tf_op jit(solution)/shard_map/ppermute | solution.py:33
  19.3 0.8 collective-permute-done.9.a1
  20.0 0.9 %collective-permute-start.8 = (bf16[96,1536]{1,0:T(8,128)(2,1)S(1)}, bf16[96,1536]{1,0:T(8,128)(2,1)S(1)}, u32[]{:S(2)}, u32[]{:S(2)}) collective-permute-start(bf16[96,1536]{1,0:T(8,128)(2,1)S(1)} %shard_map.46.a0), channel_id=1, source_target_pairs={{0,16},{1,65},{2,18},{3,67},{4,20},{5,69},{6,22},{7,71},{8,24},{9,... | collective-permute-start | bytes 884744 | tf_op jit(solution)/shard_map/ppermute | solution.py:33
  20.9 8.9 %collective-permute-done.7.a3 = bf16[96,1536]{1,0:T(8,128)(2,1)S(1)} collective-permute-done((bf16[96,1536]{1,0:T(8,128)(2,1)S(1)}, bf16[96,1536]{1,0:T(8,128)(2,1)S(1)}, u32[]{:S(2)}, u32[]{:S(2)}) %collective-permute-start.7) | collective-permute-done | bytes 294944 | tf_op jit(solution)/shard_map/ppermute | solution.py:33
  30.3 1.5 %shard_map.51.o0.refs_9_ = bf16[416,384]{1,0:T(8,128)(2,1)S(1)} custom-call(bf16[384,1536]{1,0:T(8,128)(2,1)S(1)} %shard_map.50.panel, bf16[416,384]{1,0:T(8,128)(2,1)S(1)} %shard_map.49.l0, bf16[416,384]{1,0:T(8,128)(2,1)S(1)} %collective-permute-done.10.l1, bf16[416,384]{1,0:T(8,128)(2,1)S(1)} %collective-permute-done.11.l2, ...), custom_call_target="tpu_custom_call" | custom-call | flops 452984832 | bytes 2457600 | tf_op jit(solution)/shard_map/pallas_call | solution.py:81
  31.8 1.1 %collective-permute-start.15 = (bf16[416,384]{1,0:T(8,128)(2,1)S(1)}, bf16[416,384]{1,0:T(8,128)(2,1)S(1)}, u32[]{:S(2)}, u32[]{:S(2)}) collective-permute-start(bf16[416,384]{1,0:T(8,128)(2,1)S(1)} %shard_map.51.o0.refs_9_), channel_id=1, source_target_pairs={{0,96},{1,25},{2,98},{3,27},{4,28},{5,101},{6,30},{7,103},{8,104},... | collective-permute-start | bytes 958472 | tf_op jit(solution)/shard_map/ppermute | solution.py:33
  32.9 1.0 %collective-permute-start.14 = (bf16[416,384]{1,0:T(8,128)(2,1)S(1)}, bf16[416,384]{1,0:T(8,128)(2,1)S(1)}, u32[]{:S(2)}, u32[]{:S(2)}) collective-permute-start(bf16[416,384]{1,0:T(8,128)(2,1)S(1)} %shard_map.51.o0.refs_9_), channel_id=1, source_target_pairs={{0,32},{1,9},{2,34},{3,11},{4,12},{5,37},{6,14},{7,39},{8,40},{9,1... | collective-permute-start | bytes 958472 | tf_op jit(solution)/shard_map/ppermute | solution.py:33
  33.9 1.6 %collective-permute-start.13 = (bf16[416,384]{1,0:T(8,128)(2,1)S(1)}, bf16[416,384]{1,0:T(8,128)(2,1)S(1)}, u32[]{:S(2)}, u32[]{:S(2)}) collective-permute-start(bf16[416,384]{1,0:T(8,128)(2,1)S(1)} %shard_map.51.o0.refs_9_), channel_id=1, source_target_pairs={{0,64},{1,17},{2,66},{3,19},{4,20},{5,69},{6,22},{7,71},{8,72},{9,... | collective-permute-start | bytes 958472 | tf_op jit(solution)/shard_map/ppermute | solution.py:33
  35.5 3.4 %collective-permute-done.15.o3 = bf16[416,384]{1,0:T(8,128)(2,1)S(1)} collective-permute-done((bf16[416,384]{1,0:T(8,128)(2,1)S(1)}, bf16[416,384]{1,0:T(8,128)(2,1)S(1)}, u32[]{:S(2)}, u32[]{:S(2)}) %collective-permute-start.15) | collective-permute-done | bytes 319520 | tf_op jit(solution)/shard_map/ppermute | solution.py:33
  38.8 5.7 %collective-permute-done.14.o2 = bf16[416,384]{1,0:T(8,128)(2,1)S(1)} collective-permute-done((bf16[416,384]{1,0:T(8,128)(2,1)S(1)}, bf16[416,384]{1,0:T(8,128)(2,1)S(1)}, u32[]{:S(2)}, u32[]{:S(2)}) %collective-permute-start.14) | collective-permute-done | bytes 319520 | tf_op jit(solution)/shard_map/ppermute | solution.py:33
  45.1 1.1 %collective-permute-done.18.p2 = bf16[416,384]{1,0:T(8,128)(2,1)S(1)} collective-permute-done((bf16[416,384]{1,0:T(8,128)(2,1)S(1)}, bf16[416,384]{1,0:T(8,128)(2,1)S(1)}, u32[]{:S(2)}, u32[]{:S(2)}) %collective-permute-start.18) | collective-permute-done | bytes 319520 | tf_op jit(solution)/shard_map/ppermute | solution.py:33
  46.6 0.8 %shard_map.52 = (bf16[384,1536]{1,0:T(8,128)(2,1)S(1)}, f32[32,384]{1,0:T(8,128)S(1)}, bf16[32,384]{1,0:T(8,128)(2,1)S(1)}) custom-call(bf16[416,384]{1,0:T(8,128)(2,1)S(1)} %shard_map.51.o0.refs_9_, bf16[416,384]{1,0:T(8,128)(2,1)S(1)} %collective-permute-done.13.o1, bf16[416,384]{1,0:T(8,128)(2,1)S(1)} %collective-permute-done.14.o2, ...), custom_call_target="tpu_custom_call" | custom-call | bytes 2555904 | tf_op jit(solution)/shard_map/pallas_call | solution.py:81
  48.8 0.9 %shard_map.53 = (bf16[384,384]{1,0:T(8,128)(2,1)S(1)}, bf16[384,384]{1,0:T(8,128)(2,1)S(1)}) custom-call(bf16[416,384]{1,0:T(8,128)(2,1)S(1)} %shard_map.51.o0.refs_9_, bf16[416,384]{1,0:T(8,128)(2,1)S(1)} %collective-permute-done.13.o1, bf16[416,384]{1,0:T(8,128)(2,1)S(1)} %collective-permute-done.14.o2, bf16[416,384]{1,0:T(8,128)(2,1)S(1)} %collective-permute-done.15.o3, ...), custom_call_target="tpu_custom_call" | custom-call | flops 452984832 | bytes 3735552 | tf_op jit(solution)/shard_map/pallas_call | solution.py:81
  50.0 1.1 %collective-permute-done.22.peer.refs_1_ = f32[32,384]{1,0:T(8,128)S(1)} collective-permute-done((f32[32,384]{1,0:T(8,128)S(1)}, f32[32,384]{1,0:T(8,128)S(1)}, u32[]{:S(2)}, u32[]{:S(2)}) %collective-permute-start.22) | collective-permute-done | bytes 49184 | tf_op jit(solution)/shard_map/ppermute | solution.py:33
  53.1 1.1 %collective-permute-done.25.peer.refs_3_ = f32[32,384]{1,0:T(8,128)S(1)} collective-permute-done((f32[32,384]{1,0:T(8,128)S(1)}, f32[32,384]{1,0:T(8,128)S(1)}, u32[]{:S(2)}, u32[]{:S(2)}) %collective-permute-start.25) | collective-permute-done | bytes 49184 | tf_op jit(solution)/shard_map/ppermute | solution.py:33
  54.5 1.3 %collective-permute-start.27 = (bf16[32,384]{1,0:T(8,128)(2,1)S(1)}, bf16[32,384]{1,0:T(8,128)(2,1)S(1)}, u32[]{:S(2)}, u32[]{:S(2)}) collective-permute-start(bf16[32,384]{1,0:T(8,128)(2,1)S(1)} %shard_map.57), channel_id=1, source_target_pairs={{2,19},{6,31},{10,27},{14,7},{18,3},{22,15},{26,11},{30,23},{34,51... | collective-permute-start | bytes 73736 | tf_op jit(solution)/shard_map/ppermute | solution.py:33
  55.9 1.3 %collective-permute-start.26 = (bf16[32,384]{1,0:T(8,128)(2,1)S(1)}, bf16[32,384]{1,0:T(8,128)(2,1)S(1)}, u32[]{:S(2)}, u32[]{:S(2)}) collective-permute-start(bf16[32,384]{1,0:T(8,128)(2,1)S(1)} %shard_map.57), channel_id=1, source_target_pairs={{2,3},{6,15},{10,11},{14,23},{18,19},{22,31},{26,27},{30,7},{34,35... | collective-permute-start | bytes 73736 | tf_op jit(solution)/shard_map/ppermute | solution.py:33
  57.2 13.1 %collective-permute-done.27.r1 = bf16[32,384]{1,0:T(8,128)(2,1)S(1)} collective-permute-done((bf16[32,384]{1,0:T(8,128)(2,1)S(1)}, bf16[32,384]{1,0:T(8,128)(2,1)S(1)}, u32[]{:S(2)}, u32[]{:S(2)}) %collective-permute-start.27) | collective-permute-done | bytes 24608 | tf_op jit(solution)/shard_map/ppermute | solution.py:33
  70.6 1.2 %collective-permute-done.28.refs_5_ = f32[32,384]{1,0:T(8,128)S(1)} collective-permute-done((f32[32,384]{1,0:T(8,128)S(1)}, f32[32,384]{1,0:T(8,128)S(1)}, u32[]{:S(2)}, u32[]{:S(2)}) %collective-permute-start.28) | collective-permute-done | bytes 49184 | tf_op jit(solution)/shard_map/ppermute | solution.py:33
  72.5 0.8 %collective-permute-start.29 = (f32[64,48]{1,0:T(8,128)S(1)}, f32[64,48]{1,0:T(8,128)S(1)}, u32[]{:S(2)}, u32[]{:S(2)}) collective-permute-start(f32[64,48]{1,0:T(8,128)S(1)} %get-tuple-element.60), channel_id=1, source_target_pairs={{0,8},{1,33},{2,10},{3,35},{4,12},{5,37},{6,14},{7,39},{8,16},{9,4... | collective-permute-start | bytes 36872 | tf_op jit(solution)/shard_map/ppermute | solution.py:33
  73.3 2.3 %collective-permute-start.30 = (f32[64,48]{1,0:T(8,128)S(1)}, f32[64,48]{1,0:T(8,128)S(1)}, u32[]{:S(2)}, u32[]{:S(2)}) collective-permute-start(f32[64,48]{1,0:T(8,128)S(1)} %get-tuple-element.61), channel_id=1, source_target_pairs={{0,16},{1,65},{2,18},{3,67},{4,20},{5,69},{6,22},{7,71},{8,24},{9,... | collective-permute-start | bytes 36872 | tf_op jit(solution)/shard_map/ppermute | solution.py:33
  76.1 1.9 %collective-permute-done.29 = f32[64,48]{1,0:T(8,128)S(1)} collective-permute-done((f32[64,48]{1,0:T(8,128)S(1)}, f32[64,48]{1,0:T(8,128)S(1)}, u32[]{:S(2)}, u32[]{:S(2)}) %collective-permute-start.29) | collective-permute-done | bytes 12320 | tf_op jit(solution)/shard_map/ppermute | solution.py:33
  78.7 0.8 %collective-permute-done.31 = f32[64,48]{1,0:T(8,128)S(1)} collective-permute-done((f32[64,48]{1,0:T(8,128)S(1)}, f32[64,48]{1,0:T(8,128)S(1)}, u32[]{:S(2)}, u32[]{:S(2)}) %collective-permute-start.31) | collective-permute-done | bytes 12320 | tf_op jit(solution)/shard_map/ppermute | solution.py:33
  (55 shorter events, 10.3 us)
Async XLA Ops:
  0.0 1.8 %collective-permute-start.1 = (bf16[2,48,1536]{2,1,0:T(8,128)(2,1)}, bf16[2,48,1536]{2,1,0:T(8,128)(2,1)S(1)}, u32[]{:S(2)}, u32[]{:S(2)}) collective-permute-start(bf16[2,48,1536]{2,1,0:T(8,128)(2,1)} %own.3), channel_id=1, source_target_pairs={{0,4},{1,5},{2,6},{3,7},{4,0},{5,1},{6,2},{7,3},{8,12},{9,13},{10,... | collective-permute-start | bytes 884744 | tf_op jit(solution)/shard_map/ppermute | solution.py:33
  0.0 7.8 %collective-permute-start = (bf16[2,48,1536]{2,1,0:T(8,128)(2,1)}, bf16[2,48,1536]{2,1,0:T(8,128)(2,1)S(1)}, u32[]{:S(2)}, u32[]{:S(2)}) collective-permute-start(bf16[2,48,1536]{2,1,0:T(8,128)(2,1)} %own.2), channel_id=1, source_target_pairs={{0,4},{1,5},{2,6},{3,7},{4,0},{5,1},{6,2},{7,3},{8,12},{9,13},{10,... | collective-permute-start | bytes 884744 | tf_op jit(solution)/shard_map/ppermute | solution.py:33
  1.9 7.4 %collective-permute-start.2 = (bf16[96,384]{1,0:T(8,128)(2,1)S(1)}, bf16[96,384]{1,0:T(8,128)(2,1)S(1)}, u32[]{:S(2)}, u32[]{:S(2)}) collective-permute-start(bf16[96,384]{1,0:T(8,128)(2,1)S(1)} %get-tuple-element.34), channel_id=1, source_target_pairs={{0,8},{1,33},{2,10},{3,35},{4,12},{5,37},{6,14},{7,39},{8,16},{9,4... | collective-permute-start | bytes 221192 | tf_op jit(solution)/shard_map/ppermute | solution.py:33
  3.5 6.8 %collective-permute-start.3 = (bf16[96,384]{1,0:T(8,128)(2,1)S(1)}, bf16[96,384]{1,0:T(8,128)(2,1)S(1)}, u32[]{:S(2)}, u32[]{:S(2)}) collective-permute-start(bf16[96,384]{1,0:T(8,128)(2,1)S(1)} %get-tuple-element.38), channel_id=1, source_target_pairs={{0,16},{1,65},{2,18},{3,67},{4,20},{5,69},{6,22},{7,71},{8,24},{9,... | collective-permute-start | bytes 221192 | tf_op jit(solution)/shard_map/ppermute | solution.py:33
  6.4 4.4 %collective-permute-start.4 = (bf16[96,384]{1,0:T(8,128)(2,1)S(1)}, bf16[96,384]{1,0:T(8,128)(2,1)S(1)}, u32[]{:S(2)}, u32[]{:S(2)}) collective-permute-start(bf16[96,384]{1,0:T(8,128)(2,1)S(1)} %get-tuple-element.39), channel_id=1, source_target_pairs={{0,24},{1,97},{2,26},{3,99},{4,28},{5,101},{6,30},{7,103},{8,0},{9... | collective-permute-start | bytes 221192 | tf_op jit(solution)/shard_map/ppermute | solution.py:33
  7.8 1.5 %collective-permute-start.5 = (bf16[2,32,48]{2,1,0:T(8,128)(2,1)}, bf16[2,32,48]{2,1,0:T(8,128)(2,1)S(1)}, u32[]{:S(2)}, u32[]{:S(2)}) collective-permute-start(bf16[2,32,48]{2,1,0:T(8,128)(2,1)} %bitcast.5), channel_id=1, source_target_pairs={{0,4},{1,5},{2,6},{3,7},{4,0},{5,1},{6,2},{7,3},{8,12},{9,13},{10,... | collective-permute-start | bytes 18440 | tf_op jit(solution)/shard_map/ppermute | solution.py:33
  7.8 1.6 %collective-permute-start.6 = (f32[32,48]{1,0:T(8,128)}, f32[32,48]{1,0:T(8,128)S(1)}, u32[]{:S(2)}, u32[]{:S(2)}) collective-permute-start(f32[32,48]{1,0:T(8,128)} %bitcast.7), channel_id=1, source_target_pairs={{0,4},{1,5},{2,6},{3,7},{4,0},{5,1},{6,2},{7,3},{8,12},{9,13},{10,... | collective-permute-start | bytes 18440 | tf_op jit(solution)/shard_map/ppermute | solution.py:33
  10.9 9.1 %collective-permute-start.9 = (bf16[96,1536]{1,0:T(8,128)(2,1)S(1)}, bf16[96,1536]{1,0:T(8,128)(2,1)S(1)}, u32[]{:S(2)}, u32[]{:S(2)}) collective-permute-start(bf16[96,1536]{1,0:T(8,128)(2,1)S(1)} %shard_map.46.a0), channel_id=1, source_target_pairs={{0,8},{1,33},{2,10},{3,35},{4,12},{5,37},{6,14},{7,39},{8,16},{9,4... | collective-permute-start | bytes 884744 | tf_op jit(solution)/shard_map/ppermute | solution.py:33
  11.7 18.3 %collective-permute-start.12 = (bf16[416,384]{1,0:T(8,128)(2,1)S(1)}, bf16[416,384]{1,0:T(8,128)(2,1)S(1)}, u32[]{:S(2)}, u32[]{:S(2)}) collective-permute-start(bf16[416,384]{1,0:T(8,128)(2,1)S(1)} %shard_map.49.l0), channel_id=1, source_target_pairs={{0,96},{1,25},{2,98},{3,27},{4,100},{5,29},{6,102},{7,31},{8,104},... | collective-permute-start | bytes 958472 | tf_op jit(solution)/shard_map/ppermute | solution.py:33
  14.5 15.8 %collective-permute-start.11 = (bf16[416,384]{1,0:T(8,128)(2,1)S(1)}, bf16[416,384]{1,0:T(8,128)(2,1)S(1)}, u32[]{:S(2)}, u32[]{:S(2)}) collective-permute-start(bf16[416,384]{1,0:T(8,128)(2,1)S(1)} %shard_map.49.l0), channel_id=1, source_target_pairs={{0,32},{1,9},{2,34},{3,11},{4,36},{5,13},{6,38},{7,15},{8,40},{9,1... | collective-permute-start | bytes 958472 | tf_op jit(solution)/shard_map/ppermute | solution.py:33
  14.5 15.8 %collective-permute-start.10 = (bf16[416,384]{1,0:T(8,128)(2,1)S(1)}, bf16[416,384]{1,0:T(8,128)(2,1)S(1)}, u32[]{:S(2)}, u32[]{:S(2)}) collective-permute-start(bf16[416,384]{1,0:T(8,128)(2,1)S(1)} %shard_map.49.l0), channel_id=1, source_target_pairs={{0,64},{1,17},{2,66},{3,19},{4,68},{5,21},{6,70},{7,23},{8,72},{9,... | collective-permute-start | bytes 958472 | tf_op jit(solution)/shard_map/ppermute | solution.py:33
  16.8 13.1 %collective-permute-start.7 = (bf16[96,1536]{1,0:T(8,128)(2,1)S(1)}, bf16[96,1536]{1,0:T(8,128)(2,1)S(1)}, u32[]{:S(2)}, u32[]{:S(2)}) collective-permute-start(bf16[96,1536]{1,0:T(8,128)(2,1)S(1)} %shard_map.46.a0), channel_id=1, source_target_pairs={{0,24},{1,97},{2,26},{3,99},{4,28},{5,101},{6,30},{7,103},{8,0},{9... | collective-permute-start | bytes 884744 | tf_op jit(solution)/shard_map/ppermute | solution.py:33
  20.0 9.8 %collective-permute-start.8 = (bf16[96,1536]{1,0:T(8,128)(2,1)S(1)}, bf16[96,1536]{1,0:T(8,128)(2,1)S(1)}, u32[]{:S(2)}, u32[]{:S(2)}) collective-permute-start(bf16[96,1536]{1,0:T(8,128)(2,1)S(1)} %shard_map.46.a0), channel_id=1, source_target_pairs={{0,16},{1,65},{2,18},{3,67},{4,20},{5,69},{6,22},{7,71},{8,24},{9,... | collective-permute-start | bytes 884744 | tf_op jit(solution)/shard_map/ppermute | solution.py:33
  31.8 7.1 %collective-permute-start.15 = (bf16[416,384]{1,0:T(8,128)(2,1)S(1)}, bf16[416,384]{1,0:T(8,128)(2,1)S(1)}, u32[]{:S(2)}, u32[]{:S(2)}) collective-permute-start(bf16[416,384]{1,0:T(8,128)(2,1)S(1)} %shard_map.51.o0.refs_9_), channel_id=1, source_target_pairs={{0,96},{1,25},{2,98},{3,27},{4,28},{5,101},{6,30},{7,103},{8,104},... | collective-permute-start | bytes 958472 | tf_op jit(solution)/shard_map/ppermute | solution.py:33
  32.9 11.6 %collective-permute-start.14 = (bf16[416,384]{1,0:T(8,128)(2,1)S(1)}, bf16[416,384]{1,0:T(8,128)(2,1)S(1)}, u32[]{:S(2)}, u32[]{:S(2)}) collective-permute-start(bf16[416,384]{1,0:T(8,128)(2,1)S(1)} %shard_map.51.o0.refs_9_), channel_id=1, source_target_pairs={{0,32},{1,9},{2,34},{3,11},{4,12},{5,37},{6,14},{7,39},{8,40},{9,1... | collective-permute-start | bytes 958472 | tf_op jit(solution)/shard_map/ppermute | solution.py:33
  33.9 10.7 %collective-permute-start.13 = (bf16[416,384]{1,0:T(8,128)(2,1)S(1)}, bf16[416,384]{1,0:T(8,128)(2,1)S(1)}, u32[]{:S(2)}, u32[]{:S(2)}) collective-permute-start(bf16[416,384]{1,0:T(8,128)(2,1)S(1)} %shard_map.51.o0.refs_9_), channel_id=1, source_target_pairs={{0,64},{1,17},{2,66},{3,19},{4,20},{5,69},{6,22},{7,71},{8,72},{9,... | collective-permute-start | bytes 958472 | tf_op jit(solution)/shard_map/ppermute | solution.py:33
  35.5 9.6 %collective-permute-start.16 = (bf16[416,384]{1,0:T(8,128)(2,1)S(1)}, bf16[416,384]{1,0:T(8,128)(2,1)S(1)}, u32[]{:S(2)}, u32[]{:S(2)}) collective-permute-start(bf16[416,384]{1,0:T(8,128)(2,1)S(1)} %shard_map.51.o0.refs_9_), channel_id=1, source_target_pairs={{0,4},{1,5},{2,6},{3,7},{4,0},{5,1},{6,2},{7,3},{8,12},{9,13},{10,... | collective-permute-start | bytes 958472 | tf_op jit(solution)/shard_map/ppermute | solution.py:33
  38.8 6.2 %collective-permute-start.19 = (bf16[416,384]{1,0:T(8,128)(2,1)S(1)}, bf16[416,384]{1,0:T(8,128)(2,1)S(1)}, u32[]{:S(2)}, u32[]{:S(2)}) collective-permute-start(bf16[416,384]{1,0:T(8,128)(2,1)S(1)} %collective-permute-done.15.o3), channel_id=1, source_target_pairs={{0,4},{1,5},{2,6},{3,7},{4,0},{5,1},{6,2},{7,3},{8,12},{9,13},{10,... | collective-permute-start | bytes 958472 | tf_op jit(solution)/shard_map/ppermute | solution.py:33
  44.5 1.6 %collective-permute-start.18 = (bf16[416,384]{1,0:T(8,128)(2,1)S(1)}, bf16[416,384]{1,0:T(8,128)(2,1)S(1)}, u32[]{:S(2)}, u32[]{:S(2)}) collective-permute-start(bf16[416,384]{1,0:T(8,128)(2,1)S(1)} %collective-permute-done.14.o2), channel_id=1, source_target_pairs={{0,4},{1,5},{2,6},{3,7},{4,0},{5,1},{6,2},{7,3},{8,12},{9,13},{10,... | collective-permute-start | bytes 958472 | tf_op jit(solution)/shard_map/ppermute | solution.py:33
  44.6 2.1 %collective-permute-start.17 = (bf16[416,384]{1,0:T(8,128)(2,1)S(1)}, bf16[416,384]{1,0:T(8,128)(2,1)S(1)}, u32[]{:S(2)}, u32[]{:S(2)}) collective-permute-start(bf16[416,384]{1,0:T(8,128)(2,1)S(1)} %collective-permute-done.13.o1), channel_id=1, source_target_pairs={{0,4},{1,5},{2,6},{3,7},{4,0},{5,1},{6,2},{7,3},{8,12},{9,13},{10,... | collective-permute-start | bytes 958472 | tf_op jit(solution)/shard_map/ppermute | solution.py:33
  47.5 2.3 %collective-permute-start.21 = (bf16[32,384]{1,0:T(8,128)(2,1)S(1)}, bf16[32,384]{1,0:T(8,128)(2,1)S(1)}, u32[]{:S(2)}, u32[]{:S(2)}) collective-permute-start(bf16[32,384]{1,0:T(8,128)(2,1)S(1)} %get-tuple-element.42), channel_id=1, source_target_pairs={{0,17},{4,29},{8,25},{12,5},{16,1},{20,13},{24,9},{28,21},{32,49},... | collective-permute-start | bytes 73736 | tf_op jit(solution)/shard_map/ppermute | solution.py:33
  48.1 1.6 %collective-permute-start.20 = (bf16[32,384]{1,0:T(8,128)(2,1)S(1)}, bf16[32,384]{1,0:T(8,128)(2,1)S(1)}, u32[]{:S(2)}, u32[]{:S(2)}) collective-permute-start(bf16[32,384]{1,0:T(8,128)(2,1)S(1)} %get-tuple-element.42), channel_id=1, source_target_pairs={{0,1},{4,13},{8,9},{12,21},{16,17},{20,29},{24,25},{28,5},{32,33},... | collective-permute-start | bytes 73736 | tf_op jit(solution)/shard_map/ppermute | solution.py:33
  49.8 1.3 %collective-permute-start.22 = (f32[32,384]{1,0:T(8,128)S(1)}, f32[32,384]{1,0:T(8,128)S(1)}, u32[]{:S(2)}, u32[]{:S(2)}) collective-permute-start(f32[32,384]{1,0:T(8,128)S(1)} %shard_map.54.own.refs_0_), channel_id=1, source_target_pairs={{0,4},{1,5},{2,6},{3,7},{4,0},{5,1},{6,2},{7,3},{8,12},{9,13},{10,... | collective-permute-start | bytes 147464 | tf_op jit(solution)/shard_map/ppermute | solution.py:33
  51.5 1.4 %collective-permute-start.24 = (bf16[32,384]{1,0:T(8,128)(2,1)S(1)}, bf16[32,384]{1,0:T(8,128)(2,1)S(1)}, u32[]{:S(2)}, u32[]{:S(2)}) collective-permute-start(bf16[32,384]{1,0:T(8,128)(2,1)S(1)} %shard_map.55), channel_id=1, source_target_pairs={{1,66},{5,102},{9,74},{13,110},{17,82},{21,118},{25,90},{29,126},{... | collective-permute-start | bytes 73736 | tf_op jit(solution)/shard_map/ppermute | solution.py:33
  52.1 0.7 collective-permute-start.23
  52.8 1.3 %collective-permute-start.25 = (f32[32,384]{1,0:T(8,128)S(1)}, f32[32,384]{1,0:T(8,128)S(1)}, u32[]{:S(2)}, u32[]{:S(2)}) collective-permute-start(f32[32,384]{1,0:T(8,128)S(1)} %shard_map.56.own.refs_2_), channel_id=1, source_target_pairs={{0,4},{1,5},{2,6},{3,7},{4,0},{5,1},{6,2},{7,3},{8,12},{9,13},{10,... | collective-permute-start | bytes 147464 | tf_op jit(solution)/shard_map/ppermute | solution.py:33
  54.5 15.7 %collective-permute-start.27 = (bf16[32,384]{1,0:T(8,128)(2,1)S(1)}, bf16[32,384]{1,0:T(8,128)(2,1)S(1)}, u32[]{:S(2)}, u32[]{:S(2)}) collective-permute-start(bf16[32,384]{1,0:T(8,128)(2,1)S(1)} %shard_map.57), channel_id=1, source_target_pairs={{2,19},{6,31},{10,27},{14,7},{18,3},{22,15},{26,11},{30,23},{34,51... | collective-permute-start | bytes 73736 | tf_op jit(solution)/shard_map/ppermute | solution.py:33
  55.9 14.6 %collective-permute-start.26 = (bf16[32,384]{1,0:T(8,128)(2,1)S(1)}, bf16[32,384]{1,0:T(8,128)(2,1)S(1)}, u32[]{:S(2)}, u32[]{:S(2)}) collective-permute-start(bf16[32,384]{1,0:T(8,128)(2,1)S(1)} %shard_map.57), channel_id=1, source_target_pairs={{2,3},{6,15},{10,11},{14,23},{18,19},{22,31},{26,27},{30,7},{34,35... | collective-permute-start | bytes 73736 | tf_op jit(solution)/shard_map/ppermute | solution.py:33
  70.5 1.3 %collective-permute-start.28 = (f32[32,384]{1,0:T(8,128)S(1)}, f32[32,384]{1,0:T(8,128)S(1)}, u32[]{:S(2)}, u32[]{:S(2)}) collective-permute-start(f32[32,384]{1,0:T(8,128)S(1)} %shard_map.58.refs_4_), channel_id=1, source_target_pairs={{0,4},{1,5},{2,6},{3,7},{4,0},{5,1},{6,2},{7,3},{8,12},{9,13},{10,... | collective-permute-start | bytes 147464 | tf_op jit(solution)/shard_map/ppermute | solution.py:33
  72.5 5.5 %collective-permute-start.29 = (f32[64,48]{1,0:T(8,128)S(1)}, f32[64,48]{1,0:T(8,128)S(1)}, u32[]{:S(2)}, u32[]{:S(2)}) collective-permute-start(f32[64,48]{1,0:T(8,128)S(1)} %get-tuple-element.60), channel_id=1, source_target_pairs={{0,8},{1,33},{2,10},{3,35},{4,12},{5,37},{6,14},{7,39},{8,16},{9,4... | collective-permute-start | bytes 36872 | tf_op jit(solution)/shard_map/ppermute | solution.py:33
  73.3 5.4 %collective-permute-start.30 = (f32[64,48]{1,0:T(8,128)S(1)}, f32[64,48]{1,0:T(8,128)S(1)}, u32[]{:S(2)}, u32[]{:S(2)}) collective-permute-start(f32[64,48]{1,0:T(8,128)S(1)} %get-tuple-element.61), channel_id=1, source_target_pairs={{0,16},{1,65},{2,18},{3,67},{4,20},{5,69},{6,22},{7,71},{8,24},{9,... | collective-permute-start | bytes 36872 | tf_op jit(solution)/shard_map/ppermute | solution.py:33
  75.6 3.9 %collective-permute-start.31 = (f32[64,48]{1,0:T(8,128)S(1)}, f32[64,48]{1,0:T(8,128)S(1)}, u32[]{:S(2)}, u32[]{:S(2)}) collective-permute-start(f32[64,48]{1,0:T(8,128)S(1)} %get-tuple-element.62), channel_id=1, source_target_pairs={{0,24},{1,97},{2,26},{3,99},{4,28},{5,101},{6,30},{7,103},{8,0},{9... | collective-permute-start | bytes 36872 | tf_op jit(solution)/shard_map/ppermute | solution.py:33
  (4 other events, 20.6 us)

commit v9 on v8

--- a/solution.py
+++ b/solution.py
@@ -13,7 +13,8 @@
 N = BLOCK * Y
 R = 32
 LANES = 128
-ORDER = (0, 2, 1, 3)
+LOWER_ORDER = (0, 2, 1, 3)
+TURN_ORDER = (0, 3, 1, 2)
 F32, BF16 = jnp.float32, jnp.bfloat16
 
 
@@ -33,8 +34,8 @@
     return lax.ppermute(value, AXES, pairs)
 
 
-def around(value, along):
-    return [value] + [send(value, along(d)) for d in ORDER[1:]]
+def around(value, along, order):
+    return [value] + [send(value, along(d)) for d in order[1:]]
 
 
 def to_peer(value):
@@ -134,12 +135,6 @@
     out[rows_at((1 - c) * ROWS, ROWS), :] = peer[c]
 
 
-def inverse_panel(a0, a3, a2, a1, out):
-    v = place()[1]
-    for d, piece in enumerate((a0, a1, a2, a3)):
-        out[rows_at(behind(v, d) * CHIP, CHIP), :] = piece[...]
-
-
 def lower_block(p0, p1, p2, p3, forcing, forcing_peer, inflow, inflow_peer, out, sides):
     _, v, c, _ = place()
     for d, piece in enumerate((p0, p1, p2, p3)):
@@ -153,20 +148,23 @@
         out[BLOCK:, g * LANES:(g + 1) * LANES] = sides[g * R:(g + 1) * R, :].astype(BF16)
 
 
-def coupling_block(panel, l0, l1, l2, l3, out, lower, sides, entry):
+def coupling_block(a0, a3, a2, a1, l0, l1, l2, l3, out, panel, lower, entry):
     u, v, c, z = place()
-    sides[...] = jnp.zeros_like(sides)
-    for d, piece in zip(ORDER, (l0, l1, l2, l3)):
+    lower[:, BLOCK:] = jnp.zeros((N, LANES), BF16)
+    for d, piece in enumerate((a0, a1, a2, a3)):
+        panel[rows_at(behind(v, d) * CHIP, CHIP), :] = piece[...]
+    for d, piece in zip(LOWER_ORDER, (l0, l1, l2, l3)):
         from_u = behind(u, d)
         for j in range(4):
-            lower[rows_at(chunk(from_u, j, z), CHIP), :] = piece[j * CHIP:(j + 1) * CHIP, :]
+            lower[rows_at(chunk(from_u, j, z), CHIP), :BLOCK] = piece[j * CHIP:(j + 1) * CHIP, :]
         at = chunk(from_u, v, z)
         for g in range(3):
             part = piece[BLOCK:, g * LANES:(g + 1) * LANES]
-            sides[rows_at(at + g * R, R), :] = part
+            lower[rows_at(at + g * R, R), BLOCK:] = part
             entry[rows_at(from_u * CHIP + g * R, R), :] = part
-    block = jnp.dot(panel[...], lower[...], preferred_element_type=F32).astype(BF16)
-    share = jnp.dot(panel[...], sides[...], preferred_element_type=F32)[:, :R]
+    both = jnp.dot(panel[...], lower[...], preferred_element_type=F32)
+    block = both[:, :BLOCK].astype(BF16)
+    share = both[:, BLOCK:BLOCK + R]
     known = jnp.dot(block, entry[...], preferred_element_type=F32)
     known = known[:, R:2 * R] + known[:, 2 * R:3 * R]
     share = share - jnp.where((z == 0) & (c == 0), known, 0.0)
@@ -176,9 +174,9 @@
 
 
 def panels(u, v, firsts, seconds, second, first=None, shares=None):
-    for d, piece in zip(ORDER, seconds):
+    for d, piece in zip(TURN_ORDER, seconds):
         second[:, lanes_at(behind(v, d) * BLOCK, BLOCK)] = piece[:BLOCK, :]
-    for d, piece in zip(ORDER, firsts):
+    for d, piece in zip(TURN_ORDER, firsts):
         from_u = behind(u, d)
         if shares is not None:
             side = piece[BLOCK:, :].astype(F32)
@@ -293,17 +291,16 @@
     inv_own, own = lax.optimization_barrier((inv_own, own))
     inv_3, inv_1 = send(inv_own, along_v(3)), send(inv_own, along_v(1))
     inv = [inv_own, inv_3, inv_2, inv_1]
-    inv_panel = call(inverse_panel, shape((BLOCK, N)), *inv)
-    panel = around(own, along_u)
+    panel = around(own, along_u, LOWER_ORDER)
 
     message = call(
-        coupling_block, shape((BLOCK + R, BLOCK)), inv_panel, *panel,
+        coupling_block, shape((BLOCK + R, BLOCK)), *inv, *panel,
         scratch=[
-            pltpu.VMEM((N, BLOCK), BF16), pltpu.VMEM((N, LANES), BF16), pltpu.VMEM((BLOCK, LANES), BF16),
+            pltpu.VMEM((BLOCK, N), BF16), pltpu.VMEM((N, BLOCK + LANES), BF16), pltpu.VMEM((BLOCK, LANES), BF16),
         ],
         flops=2 * BLOCK * BLOCK * N,
     )
-    turn = around(message, across)
+    turn = around(message, across, TURN_ORDER)
     turn_peer = [to_peer(value) for value in turn]
     second, base, out = call(
         base_block, [shape((BLOCK, N)), shape((R, BLOCK), F32), shape((R, BLOCK))], *turn, *turn_peer,

time: 80.4 us -> 79.7 us (level)
  waiting for transfers between devices: 42.6 us -> 40.4 us
  starting transfers between devices: 29.8 us -> 31.5 us
    ppermute x32, waiting for transfers between devices: 42.6 us -> 40.4 us  [send(): return lax.ppermute(value, AXES, pairs)]
    ppermute x32, starting transfers between devices: 29.8 us -> 31.5 us  [send(): return lax.ppermute(value, AXES, pairs)]
    pallas_call x14 -> x13, Pallas kernels: 5.07 us -> 4.79 us  [call(): pl.pallas_call(kernel, out_shape=out, in_specs=[pl.BlockSpec(memory_space...]
where the time goes in v9:
time: 79.7 us; the launch traced here: 79.4 us
  waiting for transfers between devices  40.4 us (51%)
  starting transfers between devices  31.5 us (40%)
  Pallas kernels  4.79 us (6%)
  local copies, waits for them, and re-layouts  1.93 us (2%)
    ppermute x32, waiting for transfers between devices, send(): return lax.ppermute(value, AXES, pairs)  40.4 us
    ppermute x32, starting transfers between devices, send(): return lax.ppermute(value, AXES, pairs)  31.5 us
    pallas_call x13, Pallas kernels, call(): pl.pallas_call(kernel, out_shape=out, in_specs=[pl.BlockSpec(memory_space...  4.79 us
    unnamed x8, local copies, waits for them, and re-layouts  1.93 us
  transfers between devices with their start and end apart: 32, of which 18 were waited for; matrix products, arithmetic and copies ran while one was open for 0% of the time, Pallas kernels for 1%

profile of v9, /device:TPU:96, one launch (start us, length us, event | category | flops | bytes accessed | tf_op | source)
XLA Modules:
  0.0 79.4 jit_solution(17824118487381410567)
XLA Ops:
  0.5 1.0 %copy-done.1 = bf16[2,48,1536]{2,1,0:T(8,128)(2,1)S(1)} copy-done((bf16[2,48,1536]{2,1,0:T(8,128)(2,1)S(1)}, bf16[2,48,1536]{2,1,0:T(8,128)(2,1)}, u32[]{:S(2)}) %copy-start.1) | copy-done | bytes 294936
  1.9 1.6 %collective-permute-start.2 = (bf16[96,384]{1,0:T(8,128)(2,1)S(1)}, bf16[96,384]{1,0:T(8,128)(2,1)S(1)}, u32[]{:S(2)}, u32[]{:S(2)}) collective-permute-start(bf16[96,384]{1,0:T(8,128)(2,1)S(1)} %get-tuple-element.34), channel_id=1, source_target_pairs={{0,8},{1,33},{2,10},{3,35},{4,12},{5,37},{6,14},{7,39},{8,16},{9,4... | collective-permute-start | bytes 221192 | tf_op jit(solution)/shard_map/ppermute | solution.py:34
  3.5 2.9 %collective-permute-start.3 = (bf16[96,384]{1,0:T(8,128)(2,1)S(1)}, bf16[96,384]{1,0:T(8,128)(2,1)S(1)}, u32[]{:S(2)}, u32[]{:S(2)}) collective-permute-start(bf16[96,384]{1,0:T(8,128)(2,1)S(1)} %get-tuple-element.38), channel_id=1, source_target_pairs={{0,16},{1,65},{2,18},{3,67},{4,20},{5,69},{6,22},{7,71},{8,24},{9,... | collective-permute-start | bytes 221192 | tf_op jit(solution)/shard_map/ppermute | solution.py:34
  6.4 1.3 %collective-permute-start.4 = (bf16[96,384]{1,0:T(8,128)(2,1)S(1)}, bf16[96,384]{1,0:T(8,128)(2,1)S(1)}, u32[]{:S(2)}, u32[]{:S(2)}) collective-permute-start(bf16[96,384]{1,0:T(8,128)(2,1)S(1)} %get-tuple-element.39), channel_id=1, source_target_pairs={{0,24},{1,97},{2,26},{3,99},{4,28},{5,101},{6,30},{7,103},{8,0},{9... | collective-permute-start | bytes 221192 | tf_op jit(solution)/shard_map/ppermute | solution.py:34
  8.3 1.0 %copy-done = bf16[2,48,1536]{2,1,0:T(8,128)(2,1)S(1)} copy-done((bf16[2,48,1536]{2,1,0:T(8,128)(2,1)S(1)}, bf16[2,48,1536]{2,1,0:T(8,128)(2,1)}, u32[]{:S(2)}) %copy-start) | copy-done | bytes 294936
  9.3 0.9 %collective-permute-done.3.p2 = bf16[96,384]{1,0:T(8,128)(2,1)S(1)} collective-permute-done((bf16[96,384]{1,0:T(8,128)(2,1)S(1)}, bf16[96,384]{1,0:T(8,128)(2,1)S(1)}, u32[]{:S(2)}, u32[]{:S(2)}) %collective-permute-start.3) | collective-permute-done | bytes 73760 | tf_op jit(solution)/shard_map/ppermute | solution.py:34
  10.9 0.8 %collective-permute-start.9 = (bf16[96,1536]{1,0:T(8,128)(2,1)S(1)}, bf16[96,1536]{1,0:T(8,128)(2,1)S(1)}, u32[]{:S(2)}, u32[]{:S(2)}) collective-permute-start(bf16[96,1536]{1,0:T(8,128)(2,1)S(1)} %shard_map.46.a0), channel_id=1, source_target_pairs={{0,8},{1,33},{2,10},{3,35},{4,12},{5,37},{6,14},{7,39},{8,16},{9,4... | collective-permute-start | bytes 884744 | tf_op jit(solution)/shard_map/ppermute | solution.py:34
  11.7 2.8 %collective-permute-start.12 = (bf16[416,384]{1,0:T(8,128)(2,1)S(1)}, bf16[416,384]{1,0:T(8,128)(2,1)S(1)}, u32[]{:S(2)}, u32[]{:S(2)}) collective-permute-start(bf16[416,384]{1,0:T(8,128)(2,1)S(1)} %shard_map.49.l0), channel_id=1, source_target_pairs={{0,96},{1,25},{2,98},{3,27},{4,100},{5,29},{6,102},{7,31},{8,104},... | collective-permute-start | bytes 958472 | tf_op jit(solution)/shard_map/ppermute | solution.py:34
  14.5 2.3 %collective-permute-start.10 = (bf16[416,384]{1,0:T(8,128)(2,1)S(1)}, bf16[416,384]{1,0:T(8,128)(2,1)S(1)}, u32[]{:S(2)}, u32[]{:S(2)}) collective-permute-start(bf16[416,384]{1,0:T(8,128)(2,1)S(1)} %shard_map.49.l0), channel_id=1, source_target_pairs={{0,64},{1,17},{2,66},{3,19},{4,68},{5,21},{6,70},{7,23},{8,72},{9,... | collective-permute-start | bytes 958472 | tf_op jit(solution)/shard_map/ppermute | solution.py:34
  16.8 2.5 %collective-permute-start.7 = (bf16[96,1536]{1,0:T(8,128)(2,1)S(1)}, bf16[96,1536]{1,0:T(8,128)(2,1)S(1)}, u32[]{:S(2)}, u32[]{:S(2)}) collective-permute-start(bf16[96,1536]{1,0:T(8,128)(2,1)S(1)} %shard_map.46.a0), channel_id=1, source_target_pairs={{0,24},{1,97},{2,26},{3,99},{4,28},{5,101},{6,30},{7,103},{8,0},{9... | collective-permute-start | bytes 884744 | tf_op jit(solution)/shard_map/ppermute | solution.py:34
  19.3 0.8 collective-permute-done.9.a1
  20.0 0.9 %collective-permute-start.8 = (bf16[96,1536]{1,0:T(8,128)(2,1)S(1)}, bf16[96,1536]{1,0:T(8,128)(2,1)S(1)}, u32[]{:S(2)}, u32[]{:S(2)}) collective-permute-start(bf16[96,1536]{1,0:T(8,128)(2,1)S(1)} %shard_map.46.a0), channel_id=1, source_target_pairs={{0,16},{1,65},{2,18},{3,67},{4,20},{5,69},{6,22},{7,71},{8,24},{9,... | collective-permute-start | bytes 884744 | tf_op jit(solution)/shard_map/ppermute | solution.py:34
  20.9 8.9 %collective-permute-done.7.a3 = bf16[96,1536]{1,0:T(8,128)(2,1)S(1)} collective-permute-done((bf16[96,1536]{1,0:T(8,128)(2,1)S(1)}, bf16[96,1536]{1,0:T(8,128)(2,1)S(1)}, u32[]{:S(2)}, u32[]{:S(2)}) %collective-permute-start.7) | collective-permute-done | bytes 294944 | tf_op jit(solution)/shard_map/ppermute | solution.py:34
  30.3 1.3 %shard_map.50.o0.refs_9_ = bf16[416,384]{1,0:T(8,128)(2,1)S(1)} custom-call(bf16[96,1536]{1,0:T(8,128)(2,1)S(1)} %shard_map.46.a0, bf16[96,1536]{1,0:T(8,128)(2,1)S(1)} %collective-permute-done.7.a3, bf16[96,1536]{1,0:T(8,128)(2,1)S(1)} %collective-permute-done.8.a2, bf16[96,1536]{1,0:T(8,128)(2,1)S(1)} %collective-permute-done.9.a1, ...), custom_call_target="tpu_custom_call" | custom-call | flops 452984832 | bytes 2457600 | tf_op jit(solution)/shard_map/pallas_call | solution.py:82
  31.6 1.3 %collective-permute-start.15 = (bf16[416,384]{1,0:T(8,128)(2,1)S(1)}, bf16[416,384]{1,0:T(8,128)(2,1)S(1)}, u32[]{:S(2)}, u32[]{:S(2)}) collective-permute-start(bf16[416,384]{1,0:T(8,128)(2,1)S(1)} %shard_map.50.o0.refs_9_), channel_id=1, source_target_pairs={{0,64},{1,17},{2,66},{3,19},{4,20},{5,69},{6,22},{7,71},{8,72},{9,... | collective-permute-start | bytes 958472 | tf_op jit(solution)/shard_map/ppermute | solution.py:34
  33.5 2.6 %collective-permute-start.13 = (bf16[416,384]{1,0:T(8,128)(2,1)S(1)}, bf16[416,384]{1,0:T(8,128)(2,1)S(1)}, u32[]{:S(2)}, u32[]{:S(2)}) collective-permute-start(bf16[416,384]{1,0:T(8,128)(2,1)S(1)} %shard_map.50.o0.refs_9_), channel_id=1, source_target_pairs={{0,96},{1,25},{2,98},{3,27},{4,28},{5,101},{6,30},{7,103},{8,104},... | collective-permute-start | bytes 958472 | tf_op jit(solution)/shard_map/ppermute | solution.py:34
  36.2 4.1 %collective-permute-done.15.o3 = bf16[416,384]{1,0:T(8,128)(2,1)S(1)} collective-permute-done((bf16[416,384]{1,0:T(8,128)(2,1)S(1)}, bf16[416,384]{1,0:T(8,128)(2,1)S(1)}, u32[]{:S(2)}, u32[]{:S(2)}) %collective-permute-start.15) | collective-permute-done | bytes 319520 | tf_op jit(solution)/shard_map/ppermute | solution.py:34
  40.3 3.3 %collective-permute-done.14.o2 = bf16[416,384]{1,0:T(8,128)(2,1)S(1)} collective-permute-done((bf16[416,384]{1,0:T(8,128)(2,1)S(1)}, bf16[416,384]{1,0:T(8,128)(2,1)S(1)}, u32[]{:S(2)}, u32[]{:S(2)}) %collective-permute-start.14) | collective-permute-done | bytes 319520 | tf_op jit(solution)/shard_map/ppermute | solution.py:34
  44.1 1.1 %collective-permute-done.18.p2 = bf16[416,384]{1,0:T(8,128)(2,1)S(1)} collective-permute-done((bf16[416,384]{1,0:T(8,128)(2,1)S(1)}, bf16[416,384]{1,0:T(8,128)(2,1)S(1)}, u32[]{:S(2)}, u32[]{:S(2)}) %collective-permute-start.18) | collective-permute-done | bytes 319520 | tf_op jit(solution)/shard_map/ppermute | solution.py:34
  45.7 0.8 %shard_map.51 = (bf16[384,1536]{1,0:T(8,128)(2,1)S(1)}, f32[32,384]{1,0:T(8,128)S(1)}, bf16[32,384]{1,0:T(8,128)(2,1)S(1)}) custom-call(bf16[416,384]{1,0:T(8,128)(2,1)S(1)} %shard_map.50.o0.refs_9_, bf16[416,384]{1,0:T(8,128)(2,1)S(1)} %collective-permute-done.13.o1, bf16[416,384]{1,0:T(8,128)(2,1)S(1)} %collective-permute-done.14.o2, ...), custom_call_target="tpu_custom_call" | custom-call | bytes 2555904 | tf_op jit(solution)/shard_map/pallas_call | solution.py:82
  47.9 0.9 %shard_map.52 = (bf16[384,384]{1,0:T(8,128)(2,1)S(1)}, bf16[384,384]{1,0:T(8,128)(2,1)S(1)}) custom-call(bf16[416,384]{1,0:T(8,128)(2,1)S(1)} %shard_map.50.o0.refs_9_, bf16[416,384]{1,0:T(8,128)(2,1)S(1)} %collective-permute-done.13.o1, bf16[416,384]{1,0:T(8,128)(2,1)S(1)} %collective-permute-done.14.o2, bf16[416,384]{1,0:T(8,128)(2,1)S(1)} %collective-permute-done.15.o3, ...), custom_call_target="tpu_custom_call" | custom-call | flops 452984832 | bytes 3735552 | tf_op jit(solution)/shard_map/pallas_call | solution.py:82
  49.0 1.1 %collective-permute-done.22.peer.refs_1_ = f32[32,384]{1,0:T(8,128)S(1)} collective-permute-done((f32[32,384]{1,0:T(8,128)S(1)}, f32[32,384]{1,0:T(8,128)S(1)}, u32[]{:S(2)}, u32[]{:S(2)}) %collective-permute-start.22) | collective-permute-done | bytes 49184 | tf_op jit(solution)/shard_map/ppermute | solution.py:34
  52.2 1.1 %collective-permute-done.25.peer.refs_3_ = f32[32,384]{1,0:T(8,128)S(1)} collective-permute-done((f32[32,384]{1,0:T(8,128)S(1)}, f32[32,384]{1,0:T(8,128)S(1)}, u32[]{:S(2)}, u32[]{:S(2)}) %collective-permute-start.25) | collective-permute-done | bytes 49184 | tf_op jit(solution)/shard_map/ppermute | solution.py:34
  53.6 1.3 %collective-permute-start.27 = (bf16[32,384]{1,0:T(8,128)(2,1)S(1)}, bf16[32,384]{1,0:T(8,128)(2,1)S(1)}, u32[]{:S(2)}, u32[]{:S(2)}) collective-permute-start(bf16[32,384]{1,0:T(8,128)(2,1)S(1)} %shard_map.56), channel_id=1, source_target_pairs={{2,19},{6,31},{10,27},{14,7},{18,3},{22,15},{26,11},{30,23},{34,51... | collective-permute-start | bytes 73736 | tf_op jit(solution)/shard_map/ppermute | solution.py:34
  54.9 1.3 %collective-permute-start.26 = (bf16[32,384]{1,0:T(8,128)(2,1)S(1)}, bf16[32,384]{1,0:T(8,128)(2,1)S(1)}, u32[]{:S(2)}, u32[]{:S(2)}) collective-permute-start(bf16[32,384]{1,0:T(8,128)(2,1)S(1)} %shard_map.56), channel_id=1, source_target_pairs={{2,3},{6,15},{10,11},{14,23},{18,19},{22,31},{26,27},{30,7},{34,35... | collective-permute-start | bytes 73736 | tf_op jit(solution)/shard_map/ppermute | solution.py:34
  56.2 13.0 %collective-permute-done.27.r1 = bf16[32,384]{1,0:T(8,128)(2,1)S(1)} collective-permute-done((bf16[32,384]{1,0:T(8,128)(2,1)S(1)}, bf16[32,384]{1,0:T(8,128)(2,1)S(1)}, u32[]{:S(2)}, u32[]{:S(2)}) %collective-permute-start.27) | collective-permute-done | bytes 24608 | tf_op jit(solution)/shard_map/ppermute | solution.py:34
  69.5 0.8 %collective-permute-start.28 = (f32[32,384]{1,0:T(8,128)S(1)}, f32[32,384]{1,0:T(8,128)S(1)}, u32[]{:S(2)}, u32[]{:S(2)}) collective-permute-start(f32[32,384]{1,0:T(8,128)S(1)} %shard_map.57.refs_4_), channel_id=1, source_target_pairs={{0,4},{1,5},{2,6},{3,7},{4,0},{5,1},{6,2},{7,3},{8,12},{9,13},{10,... | collective-permute-start | bytes 147464 | tf_op jit(solution)/shard_map/ppermute | solution.py:34
  70.4 0.9 %collective-permute-done.28.refs_5_ = f32[32,384]{1,0:T(8,128)S(1)} collective-permute-done((f32[32,384]{1,0:T(8,128)S(1)}, f32[32,384]{1,0:T(8,128)S(1)}, u32[]{:S(2)}, u32[]{:S(2)}) %collective-permute-start.28) | collective-permute-done | bytes 49184 | tf_op jit(solution)/shard_map/ppermute | solution.py:34
  72.4 2.5 %collective-permute-start.30 = (f32[64,48]{1,0:T(8,128)S(1)}, f32[64,48]{1,0:T(8,128)S(1)}, u32[]{:S(2)}, u32[]{:S(2)}) collective-permute-start(f32[64,48]{1,0:T(8,128)S(1)} %get-tuple-element.61), channel_id=1, source_target_pairs={{0,16},{1,65},{2,18},{3,67},{4,20},{5,69},{6,22},{7,71},{8,24},{9,... | collective-permute-start | bytes 36872 | tf_op jit(solution)/shard_map/ppermute | solution.py:34
  74.9 0.8 %collective-permute-start.31 = (f32[64,48]{1,0:T(8,128)S(1)}, f32[64,48]{1,0:T(8,128)S(1)}, u32[]{:S(2)}, u32[]{:S(2)}) collective-permute-start(f32[64,48]{1,0:T(8,128)S(1)} %get-tuple-element.62), channel_id=1, source_target_pairs={{0,24},{1,97},{2,26},{3,99},{4,28},{5,101},{6,30},{7,103},{8,0},{9... | collective-permute-start | bytes 36872 | tf_op jit(solution)/shard_map/ppermute | solution.py:34
  75.7 1.7 %collective-permute-done.29 = f32[64,48]{1,0:T(8,128)S(1)} collective-permute-done((f32[64,48]{1,0:T(8,128)S(1)}, f32[64,48]{1,0:T(8,128)S(1)}, u32[]{:S(2)}, u32[]{:S(2)}) %collective-permute-start.29) | collective-permute-done | bytes 12320 | tf_op jit(solution)/shard_map/ppermute | solution.py:34
  77.9 1.0 %collective-permute-done.31 = f32[64,48]{1,0:T(8,128)S(1)} collective-permute-done((f32[64,48]{1,0:T(8,128)S(1)}, f32[64,48]{1,0:T(8,128)S(1)}, u32[]{:S(2)}, u32[]{:S(2)}) %collective-permute-start.31) | collective-permute-done | bytes 12320 | tf_op jit(solution)/shard_map/ppermute | solution.py:34
  (54 shorter events, 10.6 us)
Async XLA Ops:
  0.0 1.8 %collective-permute-start.1 = (bf16[2,48,1536]{2,1,0:T(8,128)(2,1)}, bf16[2,48,1536]{2,1,0:T(8,128)(2,1)S(1)}, u32[]{:S(2)}, u32[]{:S(2)}) collective-permute-start(bf16[2,48,1536]{2,1,0:T(8,128)(2,1)} %own.3), channel_id=1, source_target_pairs={{0,4},{1,5},{2,6},{3,7},{4,0},{5,1},{6,2},{7,3},{8,12},{9,13},{10,... | collective-permute-start | bytes 884744 | tf_op jit(solution)/shard_map/ppermute | solution.py:34
  0.0 7.8 %collective-permute-start = (bf16[2,48,1536]{2,1,0:T(8,128)(2,1)}, bf16[2,48,1536]{2,1,0:T(8,128)(2,1)S(1)}, u32[]{:S(2)}, u32[]{:S(2)}) collective-permute-start(bf16[2,48,1536]{2,1,0:T(8,128)(2,1)} %own.2), channel_id=1, source_target_pairs={{0,4},{1,5},{2,6},{3,7},{4,0},{5,1},{6,2},{7,3},{8,12},{9,13},{10,... | collective-permute-start | bytes 884744 | tf_op jit(solution)/shard_map/ppermute | solution.py:34
  1.9 7.4 %collective-permute-start.2 = (bf16[96,384]{1,0:T(8,128)(2,1)S(1)}, bf16[96,384]{1,0:T(8,128)(2,1)S(1)}, u32[]{:S(2)}, u32[]{:S(2)}) collective-permute-start(bf16[96,384]{1,0:T(8,128)(2,1)S(1)} %get-tuple-element.34), channel_id=1, source_target_pairs={{0,8},{1,33},{2,10},{3,35},{4,12},{5,37},{6,14},{7,39},{8,16},{9,4... | collective-permute-start | bytes 221192 | tf_op jit(solution)/shard_map/ppermute | solution.py:34
  3.5 6.8 %collective-permute-start.3 = (bf16[96,384]{1,0:T(8,128)(2,1)S(1)}, bf16[96,384]{1,0:T(8,128)(2,1)S(1)}, u32[]{:S(2)}, u32[]{:S(2)}) collective-permute-start(bf16[96,384]{1,0:T(8,128)(2,1)S(1)} %get-tuple-element.38), channel_id=1, source_target_pairs={{0,16},{1,65},{2,18},{3,67},{4,20},{5,69},{6,22},{7,71},{8,24},{9,... | collective-permute-start | bytes 221192 | tf_op jit(solution)/shard_map/ppermute | solution.py:34
  6.4 4.4 %collective-permute-start.4 = (bf16[96,384]{1,0:T(8,128)(2,1)S(1)}, bf16[96,384]{1,0:T(8,128)(2,1)S(1)}, u32[]{:S(2)}, u32[]{:S(2)}) collective-permute-start(bf16[96,384]{1,0:T(8,128)(2,1)S(1)} %get-tuple-element.39), channel_id=1, source_target_pairs={{0,24},{1,97},{2,26},{3,99},{4,28},{5,101},{6,30},{7,103},{8,0},{9... | collective-permute-start | bytes 221192 | tf_op jit(solution)/shard_map/ppermute | solution.py:34
  7.8 1.5 %collective-permute-start.5 = (bf16[2,32,48]{2,1,0:T(8,128)(2,1)}, bf16[2,32,48]{2,1,0:T(8,128)(2,1)S(1)}, u32[]{:S(2)}, u32[]{:S(2)}) collective-permute-start(bf16[2,32,48]{2,1,0:T(8,128)(2,1)} %bitcast.5), channel_id=1, source_target_pairs={{0,4},{1,5},{2,6},{3,7},{4,0},{5,1},{6,2},{7,3},{8,12},{9,13},{10,... | collective-permute-start | bytes 18440 | tf_op jit(solution)/shard_map/ppermute | solution.py:34
  7.8 1.6 %collective-permute-start.6 = (f32[32,48]{1,0:T(8,128)}, f32[32,48]{1,0:T(8,128)S(1)}, u32[]{:S(2)}, u32[]{:S(2)}) collective-permute-start(f32[32,48]{1,0:T(8,128)} %bitcast.7), channel_id=1, source_target_pairs={{0,4},{1,5},{2,6},{3,7},{4,0},{5,1},{6,2},{7,3},{8,12},{9,13},{10,... | collective-permute-start | bytes 18440 | tf_op jit(solution)/shard_map/ppermute | solution.py:34
  10.9 9.1 %collective-permute-start.9 = (bf16[96,1536]{1,0:T(8,128)(2,1)S(1)}, bf16[96,1536]{1,0:T(8,128)(2,1)S(1)}, u32[]{:S(2)}, u32[]{:S(2)}) collective-permute-start(bf16[96,1536]{1,0:T(8,128)(2,1)S(1)} %shard_map.46.a0), channel_id=1, source_target_pairs={{0,8},{1,33},{2,10},{3,35},{4,12},{5,37},{6,14},{7,39},{8,16},{9,4... | collective-permute-start | bytes 884744 | tf_op jit(solution)/shard_map/ppermute | solution.py:34
  11.7 18.1 %collective-permute-start.12 = (bf16[416,384]{1,0:T(8,128)(2,1)S(1)}, bf16[416,384]{1,0:T(8,128)(2,1)S(1)}, u32[]{:S(2)}, u32[]{:S(2)}) collective-permute-start(bf16[416,384]{1,0:T(8,128)(2,1)S(1)} %shard_map.49.l0), channel_id=1, source_target_pairs={{0,96},{1,25},{2,98},{3,27},{4,100},{5,29},{6,102},{7,31},{8,104},... | collective-permute-start | bytes 958472 | tf_op jit(solution)/shard_map/ppermute | solution.py:34
  14.5 15.8 %collective-permute-start.11 = (bf16[416,384]{1,0:T(8,128)(2,1)S(1)}, bf16[416,384]{1,0:T(8,128)(2,1)S(1)}, u32[]{:S(2)}, u32[]{:S(2)}) collective-permute-start(bf16[416,384]{1,0:T(8,128)(2,1)S(1)} %shard_map.49.l0), channel_id=1, source_target_pairs={{0,32},{1,9},{2,34},{3,11},{4,36},{5,13},{6,38},{7,15},{8,40},{9,1... | collective-permute-start | bytes 958472 | tf_op jit(solution)/shard_map/ppermute | solution.py:34
  14.5 15.8 %collective-permute-start.10 = (bf16[416,384]{1,0:T(8,128)(2,1)S(1)}, bf16[416,384]{1,0:T(8,128)(2,1)S(1)}, u32[]{:S(2)}, u32[]{:S(2)}) collective-permute-start(bf16[416,384]{1,0:T(8,128)(2,1)S(1)} %shard_map.49.l0), channel_id=1, source_target_pairs={{0,64},{1,17},{2,66},{3,19},{4,68},{5,21},{6,70},{7,23},{8,72},{9,... | collective-permute-start | bytes 958472 | tf_op jit(solution)/shard_map/ppermute | solution.py:34
  16.8 13.1 %collective-permute-start.7 = (bf16[96,1536]{1,0:T(8,128)(2,1)S(1)}, bf16[96,1536]{1,0:T(8,128)(2,1)S(1)}, u32[]{:S(2)}, u32[]{:S(2)}) collective-permute-start(bf16[96,1536]{1,0:T(8,128)(2,1)S(1)} %shard_map.46.a0), channel_id=1, source_target_pairs={{0,24},{1,97},{2,26},{3,99},{4,28},{5,101},{6,30},{7,103},{8,0},{9... | collective-permute-start | bytes 884744 | tf_op jit(solution)/shard_map/ppermute | solution.py:34
  20.0 9.8 %collective-permute-start.8 = (bf16[96,1536]{1,0:T(8,128)(2,1)S(1)}, bf16[96,1536]{1,0:T(8,128)(2,1)S(1)}, u32[]{:S(2)}, u32[]{:S(2)}) collective-permute-start(bf16[96,1536]{1,0:T(8,128)(2,1)S(1)} %shard_map.46.a0), channel_id=1, source_target_pairs={{0,16},{1,65},{2,18},{3,67},{4,20},{5,69},{6,22},{7,71},{8,24},{9,... | collective-permute-start | bytes 884744 | tf_op jit(solution)/shard_map/ppermute | solution.py:34
  31.6 8.7 %collective-permute-start.15 = (bf16[416,384]{1,0:T(8,128)(2,1)S(1)}, bf16[416,384]{1,0:T(8,128)(2,1)S(1)}, u32[]{:S(2)}, u32[]{:S(2)}) collective-permute-start(bf16[416,384]{1,0:T(8,128)(2,1)S(1)} %shard_map.50.o0.refs_9_), channel_id=1, source_target_pairs={{0,64},{1,17},{2,66},{3,19},{4,20},{5,69},{6,22},{7,71},{8,72},{9,... | collective-permute-start | bytes 958472 | tf_op jit(solution)/shard_map/ppermute | solution.py:34
  32.9 10.7 %collective-permute-start.14 = (bf16[416,384]{1,0:T(8,128)(2,1)S(1)}, bf16[416,384]{1,0:T(8,128)(2,1)S(1)}, u32[]{:S(2)}, u32[]{:S(2)}) collective-permute-start(bf16[416,384]{1,0:T(8,128)(2,1)S(1)} %shard_map.50.o0.refs_9_), channel_id=1, source_target_pairs={{0,32},{1,9},{2,34},{3,11},{4,12},{5,37},{6,14},{7,39},{8,40},{9,1... | collective-permute-start | bytes 958472 | tf_op jit(solution)/shard_map/ppermute | solution.py:34
  33.5 10.1 %collective-permute-start.13 = (bf16[416,384]{1,0:T(8,128)(2,1)S(1)}, bf16[416,384]{1,0:T(8,128)(2,1)S(1)}, u32[]{:S(2)}, u32[]{:S(2)}) collective-permute-start(bf16[416,384]{1,0:T(8,128)(2,1)S(1)} %shard_map.50.o0.refs_9_), channel_id=1, source_target_pairs={{0,96},{1,25},{2,98},{3,27},{4,28},{5,101},{6,30},{7,103},{8,104},... | collective-permute-start | bytes 958472 | tf_op jit(solution)/shard_map/ppermute | solution.py:34
  36.1 8.0 %collective-permute-start.16 = (bf16[416,384]{1,0:T(8,128)(2,1)S(1)}, bf16[416,384]{1,0:T(8,128)(2,1)S(1)}, u32[]{:S(2)}, u32[]{:S(2)}) collective-permute-start(bf16[416,384]{1,0:T(8,128)(2,1)S(1)} %shard_map.50.o0.refs_9_), channel_id=1, source_target_pairs={{0,4},{1,5},{2,6},{3,7},{4,0},{5,1},{6,2},{7,3},{8,12},{9,13},{10,... | collective-permute-start | bytes 958472 | tf_op jit(solution)/shard_map/ppermute | solution.py:34
  40.3 3.8 %collective-permute-start.19 = (bf16[416,384]{1,0:T(8,128)(2,1)S(1)}, bf16[416,384]{1,0:T(8,128)(2,1)S(1)}, u32[]{:S(2)}, u32[]{:S(2)}) collective-permute-start(bf16[416,384]{1,0:T(8,128)(2,1)S(1)} %collective-permute-done.15.o3), channel_id=1, source_target_pairs={{0,4},{1,5},{2,6},{3,7},{4,0},{5,1},{6,2},{7,3},{8,12},{9,13},{10,... | collective-permute-start | bytes 958472 | tf_op jit(solution)/shard_map/ppermute | solution.py:34
  43.6 1.6 %collective-permute-start.18 = (bf16[416,384]{1,0:T(8,128)(2,1)S(1)}, bf16[416,384]{1,0:T(8,128)(2,1)S(1)}, u32[]{:S(2)}, u32[]{:S(2)}) collective-permute-start(bf16[416,384]{1,0:T(8,128)(2,1)S(1)} %collective-permute-done.14.o2), channel_id=1, source_target_pairs={{0,4},{1,5},{2,6},{3,7},{4,0},{5,1},{6,2},{7,3},{8,12},{9,13},{10,... | collective-permute-start | bytes 958472 | tf_op jit(solution)/shard_map/ppermute | solution.py:34
  43.6 2.1 %collective-permute-start.17 = (bf16[416,384]{1,0:T(8,128)(2,1)S(1)}, bf16[416,384]{1,0:T(8,128)(2,1)S(1)}, u32[]{:S(2)}, u32[]{:S(2)}) collective-permute-start(bf16[416,384]{1,0:T(8,128)(2,1)S(1)} %collective-permute-done.13.o1), channel_id=1, source_target_pairs={{0,4},{1,5},{2,6},{3,7},{4,0},{5,1},{6,2},{7,3},{8,12},{9,13},{10,... | collective-permute-start | bytes 958472 | tf_op jit(solution)/shard_map/ppermute | solution.py:34
  46.5 2.3 %collective-permute-start.21 = (bf16[32,384]{1,0:T(8,128)(2,1)S(1)}, bf16[32,384]{1,0:T(8,128)(2,1)S(1)}, u32[]{:S(2)}, u32[]{:S(2)}) collective-permute-start(bf16[32,384]{1,0:T(8,128)(2,1)S(1)} %get-tuple-element.42), channel_id=1, source_target_pairs={{0,17},{4,29},{8,25},{12,5},{16,1},{20,13},{24,9},{28,21},{32,49},... | collective-permute-start | bytes 73736 | tf_op jit(solution)/shard_map/ppermute | solution.py:34
  47.2 1.6 %collective-permute-start.20 = (bf16[32,384]{1,0:T(8,128)(2,1)S(1)}, bf16[32,384]{1,0:T(8,128)(2,1)S(1)}, u32[]{:S(2)}, u32[]{:S(2)}) collective-permute-start(bf16[32,384]{1,0:T(8,128)(2,1)S(1)} %get-tuple-element.42), channel_id=1, source_target_pairs={{0,1},{4,13},{8,9},{12,21},{16,17},{20,29},{24,25},{28,5},{32,33},... | collective-permute-start | bytes 73736 | tf_op jit(solution)/shard_map/ppermute | solution.py:34
  48.8 1.3 %collective-permute-start.22 = (f32[32,384]{1,0:T(8,128)S(1)}, f32[32,384]{1,0:T(8,128)S(1)}, u32[]{:S(2)}, u32[]{:S(2)}) collective-permute-start(f32[32,384]{1,0:T(8,128)S(1)} %shard_map.53.own.refs_0_), channel_id=1, source_target_pairs={{0,4},{1,5},{2,6},{3,7},{4,0},{5,1},{6,2},{7,3},{8,12},{9,13},{10,... | collective-permute-start | bytes 147464 | tf_op jit(solution)/shard_map/ppermute | solution.py:34
  50.5 1.4 %collective-permute-start.24 = (bf16[32,384]{1,0:T(8,128)(2,1)S(1)}, bf16[32,384]{1,0:T(8,128)(2,1)S(1)}, u32[]{:S(2)}, u32[]{:S(2)}) collective-permute-start(bf16[32,384]{1,0:T(8,128)(2,1)S(1)} %shard_map.54), channel_id=1, source_target_pairs={{1,66},{5,102},{9,74},{13,110},{17,82},{21,118},{25,90},{29,126},{... | collective-permute-start | bytes 73736 | tf_op jit(solution)/shard_map/ppermute | solution.py:34
  51.2 0.7 collective-permute-start.23
  51.9 1.3 %collective-permute-start.25 = (f32[32,384]{1,0:T(8,128)S(1)}, f32[32,384]{1,0:T(8,128)S(1)}, u32[]{:S(2)}, u32[]{:S(2)}) collective-permute-start(f32[32,384]{1,0:T(8,128)S(1)} %shard_map.55.own.refs_2_), channel_id=1, source_target_pairs={{0,4},{1,5},{2,6},{3,7},{4,0},{5,1},{6,2},{7,3},{8,12},{9,13},{10,... | collective-permute-start | bytes 147464 | tf_op jit(solution)/shard_map/ppermute | solution.py:34
  53.6 15.7 %collective-permute-start.27 = (bf16[32,384]{1,0:T(8,128)(2,1)S(1)}, bf16[32,384]{1,0:T(8,128)(2,1)S(1)}, u32[]{:S(2)}, u32[]{:S(2)}) collective-permute-start(bf16[32,384]{1,0:T(8,128)(2,1)S(1)} %shard_map.56), channel_id=1, source_target_pairs={{2,19},{6,31},{10,27},{14,7},{18,3},{22,15},{26,11},{30,23},{34,51... | collective-permute-start | bytes 73736 | tf_op jit(solution)/shard_map/ppermute | solution.py:34
  54.9 14.6 %collective-permute-start.26 = (bf16[32,384]{1,0:T(8,128)(2,1)S(1)}, bf16[32,384]{1,0:T(8,128)(2,1)S(1)}, u32[]{:S(2)}, u32[]{:S(2)}) collective-permute-start(bf16[32,384]{1,0:T(8,128)(2,1)S(1)} %shard_map.56), channel_id=1, source_target_pairs={{2,3},{6,15},{10,11},{14,23},{18,19},{22,31},{26,27},{30,7},{34,35... | collective-permute-start | bytes 73736 | tf_op jit(solution)/shard_map/ppermute | solution.py:34
  69.5 1.7 %collective-permute-start.28 = (f32[32,384]{1,0:T(8,128)S(1)}, f32[32,384]{1,0:T(8,128)S(1)}, u32[]{:S(2)}, u32[]{:S(2)}) collective-permute-start(f32[32,384]{1,0:T(8,128)S(1)} %shard_map.57.refs_4_), channel_id=1, source_target_pairs={{0,4},{1,5},{2,6},{3,7},{4,0},{5,1},{6,2},{7,3},{8,12},{9,13},{10,... | collective-permute-start | bytes 147464 | tf_op jit(solution)/shard_map/ppermute | solution.py:34
  71.9 5.5 %collective-permute-start.29 = (f32[64,48]{1,0:T(8,128)S(1)}, f32[64,48]{1,0:T(8,128)S(1)}, u32[]{:S(2)}, u32[]{:S(2)}) collective-permute-start(f32[64,48]{1,0:T(8,128)S(1)} %get-tuple-element.60), channel_id=1, source_target_pairs={{0,8},{1,33},{2,10},{3,35},{4,12},{5,37},{6,14},{7,39},{8,16},{9,4... | collective-permute-start | bytes 36872 | tf_op jit(solution)/shard_map/ppermute | solution.py:34
  72.4 5.4 %collective-permute-start.30 = (f32[64,48]{1,0:T(8,128)S(1)}, f32[64,48]{1,0:T(8,128)S(1)}, u32[]{:S(2)}, u32[]{:S(2)}) collective-permute-start(f32[64,48]{1,0:T(8,128)S(1)} %get-tuple-element.61), channel_id=1, source_target_pairs={{0,16},{1,65},{2,18},{3,67},{4,20},{5,69},{6,22},{7,71},{8,24},{9,... | collective-permute-start | bytes 36872 | tf_op jit(solution)/shard_map/ppermute | solution.py:34
  74.9 3.9 %collective-permute-start.31 = (f32[64,48]{1,0:T(8,128)S(1)}, f32[64,48]{1,0:T(8,128)S(1)}, u32[]{:S(2)}, u32[]{:S(2)}) collective-permute-start(f32[64,48]{1,0:T(8,128)S(1)} %get-tuple-element.62), channel_id=1, source_target_pairs={{0,24},{1,97},{2,26},{3,99},{4,28},{5,101},{6,30},{7,103},{8,0},{9... | collective-permute-start | bytes 36872 | tf_op jit(solution)/shard_map/ppermute | solution.py:34
  (4 other events, 20.6 us)

commit v10 on v9

--- a/solution.py
+++ b/solution.py
@@ -259,7 +259,7 @@
     arrived = []
     for j in range(2):
         def target(y, x, c, z, j=j):
-            y, x, c, _ = along_v(2 * j + c)(y, x, c, z)
+            y, x, c, _ = along_v(3 - j if c else j)(y, x, c, z)
             return (y, x, c, z + 1) if z + 1 == plane else None
         arrived.append(send(out, target))
     arrived, beside = lax.optimization_barrier((arrived, beside))

time: 79.7 us -> 79.2 us (level)
  no operation moved by 1% of the time
where the time goes in v10:
time: 79.2 us; the launch traced here: 79 us
  waiting for transfers between devices  39.7 us (50%)
  starting transfers between devices  31.8 us (40%)
  Pallas kernels  4.79 us (6%)
  local copies, waits for them, and re-layouts  1.93 us (2%)
    ppermute x32, waiting for transfers between devices, send(): return lax.ppermute(value, AXES, pairs)  39.7 us
    ppermute x32, starting transfers between devices, send(): return lax.ppermute(value, AXES, pairs)  31.8 us
    pallas_call x13, Pallas kernels, call(): pl.pallas_call(kernel, out_shape=out, in_specs=[pl.BlockSpec(memory_space...  4.79 us
    unnamed x8, local copies, waits for them, and re-layouts  1.93 us
  transfers between devices with their start and end apart: 32, of which 18 were waited for; matrix products, arithmetic and copies ran while one was open for 0% of the time, Pallas kernels for 1%

profile of v10, /device:TPU:96, one launch (start us, length us, event | category | flops | bytes accessed | tf_op | source)
XLA Modules:
  0.0 79.0 jit_solution(10114192670835126541)
XLA Ops:
  0.5 1.0 %copy-done.1 = bf16[2,48,1536]{2,1,0:T(8,128)(2,1)S(1)} copy-done((bf16[2,48,1536]{2,1,0:T(8,128)(2,1)S(1)}, bf16[2,48,1536]{2,1,0:T(8,128)(2,1)}, u32[]{:S(2)}) %copy-start.1) | copy-done | bytes 294936
  1.9 1.6 %collective-permute-start.2 = (bf16[96,384]{1,0:T(8,128)(2,1)S(1)}, bf16[96,384]{1,0:T(8,128)(2,1)S(1)}, u32[]{:S(2)}, u32[]{:S(2)}) collective-permute-start(bf16[96,384]{1,0:T(8,128)(2,1)S(1)} %get-tuple-element.34), channel_id=1, source_target_pairs={{0,8},{1,33},{2,10},{3,35},{4,12},{5,37},{6,14},{7,39},{8,16},{9,4... | collective-permute-start | bytes 221192 | tf_op jit(solution)/shard_map/ppermute | solution.py:34
  3.5 2.9 %collective-permute-start.3 = (bf16[96,384]{1,0:T(8,128)(2,1)S(1)}, bf16[96,384]{1,0:T(8,128)(2,1)S(1)}, u32[]{:S(2)}, u32[]{:S(2)}) collective-permute-start(bf16[96,384]{1,0:T(8,128)(2,1)S(1)} %get-tuple-element.38), channel_id=1, source_target_pairs={{0,16},{1,65},{2,18},{3,67},{4,20},{5,69},{6,22},{7,71},{8,24},{9,... | collective-permute-start | bytes 221192 | tf_op jit(solution)/shard_map/ppermute | solution.py:34
  6.4 1.3 %collective-permute-start.4 = (bf16[96,384]{1,0:T(8,128)(2,1)S(1)}, bf16[96,384]{1,0:T(8,128)(2,1)S(1)}, u32[]{:S(2)}, u32[]{:S(2)}) collective-permute-start(bf16[96,384]{1,0:T(8,128)(2,1)S(1)} %get-tuple-element.39), channel_id=1, source_target_pairs={{0,24},{1,97},{2,26},{3,99},{4,28},{5,101},{6,30},{7,103},{8,0},{9... | collective-permute-start | bytes 221192 | tf_op jit(solution)/shard_map/ppermute | solution.py:34
  8.3 1.0 %copy-done = bf16[2,48,1536]{2,1,0:T(8,128)(2,1)S(1)} copy-done((bf16[2,48,1536]{2,1,0:T(8,128)(2,1)S(1)}, bf16[2,48,1536]{2,1,0:T(8,128)(2,1)}, u32[]{:S(2)}) %copy-start) | copy-done | bytes 294936
  9.3 0.9 %collective-permute-done.3.p2 = bf16[96,384]{1,0:T(8,128)(2,1)S(1)} collective-permute-done((bf16[96,384]{1,0:T(8,128)(2,1)S(1)}, bf16[96,384]{1,0:T(8,128)(2,1)S(1)}, u32[]{:S(2)}, u32[]{:S(2)}) %collective-permute-start.3) | collective-permute-done | bytes 73760 | tf_op jit(solution)/shard_map/ppermute | solution.py:34
  10.9 0.8 %collective-permute-start.9 = (bf16[96,1536]{1,0:T(8,128)(2,1)S(1)}, bf16[96,1536]{1,0:T(8,128)(2,1)S(1)}, u32[]{:S(2)}, u32[]{:S(2)}) collective-permute-start(bf16[96,1536]{1,0:T(8,128)(2,1)S(1)} %shard_map.46.a0), channel_id=1, source_target_pairs={{0,8},{1,33},{2,10},{3,35},{4,12},{5,37},{6,14},{7,39},{8,16},{9,4... | collective-permute-start | bytes 884744 | tf_op jit(solution)/shard_map/ppermute | solution.py:34
  11.7 2.8 %collective-permute-start.12 = (bf16[416,384]{1,0:T(8,128)(2,1)S(1)}, bf16[416,384]{1,0:T(8,128)(2,1)S(1)}, u32[]{:S(2)}, u32[]{:S(2)}) collective-permute-start(bf16[416,384]{1,0:T(8,128)(2,1)S(1)} %shard_map.49.l0), channel_id=1, source_target_pairs={{0,96},{1,25},{2,98},{3,27},{4,100},{5,29},{6,102},{7,31},{8,104},... | collective-permute-start | bytes 958472 | tf_op jit(solution)/shard_map/ppermute | solution.py:34
  14.5 2.3 %collective-permute-start.10 = (bf16[416,384]{1,0:T(8,128)(2,1)S(1)}, bf16[416,384]{1,0:T(8,128)(2,1)S(1)}, u32[]{:S(2)}, u32[]{:S(2)}) collective-permute-start(bf16[416,384]{1,0:T(8,128)(2,1)S(1)} %shard_map.49.l0), channel_id=1, source_target_pairs={{0,64},{1,17},{2,66},{3,19},{4,68},{5,21},{6,70},{7,23},{8,72},{9,... | collective-permute-start | bytes 958472 | tf_op jit(solution)/shard_map/ppermute | solution.py:34
  16.8 2.5 %collective-permute-start.7 = (bf16[96,1536]{1,0:T(8,128)(2,1)S(1)}, bf16[96,1536]{1,0:T(8,128)(2,1)S(1)}, u32[]{:S(2)}, u32[]{:S(2)}) collective-permute-start(bf16[96,1536]{1,0:T(8,128)(2,1)S(1)} %shard_map.46.a0), channel_id=1, source_target_pairs={{0,24},{1,97},{2,26},{3,99},{4,28},{5,101},{6,30},{7,103},{8,0},{9... | collective-permute-start | bytes 884744 | tf_op jit(solution)/shard_map/ppermute | solution.py:34
  19.3 0.8 collective-permute-done.9.a1
  20.0 0.9 %collective-permute-start.8 = (bf16[96,1536]{1,0:T(8,128)(2,1)S(1)}, bf16[96,1536]{1,0:T(8,128)(2,1)S(1)}, u32[]{:S(2)}, u32[]{:S(2)}) collective-permute-start(bf16[96,1536]{1,0:T(8,128)(2,1)S(1)} %shard_map.46.a0), channel_id=1, source_target_pairs={{0,16},{1,65},{2,18},{3,67},{4,20},{5,69},{6,22},{7,71},{8,24},{9,... | collective-permute-start | bytes 884744 | tf_op jit(solution)/shard_map/ppermute | solution.py:34
  20.9 8.9 %collective-permute-done.7.a3 = bf16[96,1536]{1,0:T(8,128)(2,1)S(1)} collective-permute-done((bf16[96,1536]{1,0:T(8,128)(2,1)S(1)}, bf16[96,1536]{1,0:T(8,128)(2,1)S(1)}, u32[]{:S(2)}, u32[]{:S(2)}) %collective-permute-start.7) | collective-permute-done | bytes 294944 | tf_op jit(solution)/shard_map/ppermute | solution.py:34
  30.3 1.3 %shard_map.50.o0.refs_9_ = bf16[416,384]{1,0:T(8,128)(2,1)S(1)} custom-call(bf16[96,1536]{1,0:T(8,128)(2,1)S(1)} %shard_map.46.a0, bf16[96,1536]{1,0:T(8,128)(2,1)S(1)} %collective-permute-done.7.a3, bf16[96,1536]{1,0:T(8,128)(2,1)S(1)} %collective-permute-done.8.a2, bf16[96,1536]{1,0:T(8,128)(2,1)S(1)} %collective-permute-done.9.a1, ...), custom_call_target="tpu_custom_call" | custom-call | flops 452984832 | bytes 2457600 | tf_op jit(solution)/shard_map/pallas_call | solution.py:82
  31.6 1.3 %collective-permute-start.15 = (bf16[416,384]{1,0:T(8,128)(2,1)S(1)}, bf16[416,384]{1,0:T(8,128)(2,1)S(1)}, u32[]{:S(2)}, u32[]{:S(2)}) collective-permute-start(bf16[416,384]{1,0:T(8,128)(2,1)S(1)} %shard_map.50.o0.refs_9_), channel_id=1, source_target_pairs={{0,64},{1,17},{2,66},{3,19},{4,20},{5,69},{6,22},{7,71},{8,72},{9,... | collective-permute-start | bytes 958472 | tf_op jit(solution)/shard_map/ppermute | solution.py:34
  33.5 2.6 %collective-permute-start.13 = (bf16[416,384]{1,0:T(8,128)(2,1)S(1)}, bf16[416,384]{1,0:T(8,128)(2,1)S(1)}, u32[]{:S(2)}, u32[]{:S(2)}) collective-permute-start(bf16[416,384]{1,0:T(8,128)(2,1)S(1)} %shard_map.50.o0.refs_9_), channel_id=1, source_target_pairs={{0,96},{1,25},{2,98},{3,27},{4,28},{5,101},{6,30},{7,103},{8,104},... | collective-permute-start | bytes 958472 | tf_op jit(solution)/shard_map/ppermute | solution.py:34
  36.2 4.1 %collective-permute-done.15.o3 = bf16[416,384]{1,0:T(8,128)(2,1)S(1)} collective-permute-done((bf16[416,384]{1,0:T(8,128)(2,1)S(1)}, bf16[416,384]{1,0:T(8,128)(2,1)S(1)}, u32[]{:S(2)}, u32[]{:S(2)}) %collective-permute-start.15) | collective-permute-done | bytes 319520 | tf_op jit(solution)/shard_map/ppermute | solution.py:34
  40.3 3.3 %collective-permute-done.14.o2 = bf16[416,384]{1,0:T(8,128)(2,1)S(1)} collective-permute-done((bf16[416,384]{1,0:T(8,128)(2,1)S(1)}, bf16[416,384]{1,0:T(8,128)(2,1)S(1)}, u32[]{:S(2)}, u32[]{:S(2)}) %collective-permute-start.14) | collective-permute-done | bytes 319520 | tf_op jit(solution)/shard_map/ppermute | solution.py:34
  44.1 1.1 %collective-permute-done.18.p2 = bf16[416,384]{1,0:T(8,128)(2,1)S(1)} collective-permute-done((bf16[416,384]{1,0:T(8,128)(2,1)S(1)}, bf16[416,384]{1,0:T(8,128)(2,1)S(1)}, u32[]{:S(2)}, u32[]{:S(2)}) %collective-permute-start.18) | collective-permute-done | bytes 319520 | tf_op jit(solution)/shard_map/ppermute | solution.py:34
  45.7 0.8 %shard_map.51 = (bf16[384,1536]{1,0:T(8,128)(2,1)S(1)}, f32[32,384]{1,0:T(8,128)S(1)}, bf16[32,384]{1,0:T(8,128)(2,1)S(1)}) custom-call(bf16[416,384]{1,0:T(8,128)(2,1)S(1)} %shard_map.50.o0.refs_9_, bf16[416,384]{1,0:T(8,128)(2,1)S(1)} %collective-permute-done.13.o1, bf16[416,384]{1,0:T(8,128)(2,1)S(1)} %collective-permute-done.14.o2, ...), custom_call_target="tpu_custom_call" | custom-call | bytes 2555904 | tf_op jit(solution)/shard_map/pallas_call | solution.py:82
  47.9 0.9 %shard_map.52 = (bf16[384,384]{1,0:T(8,128)(2,1)S(1)}, bf16[384,384]{1,0:T(8,128)(2,1)S(1)}) custom-call(bf16[416,384]{1,0:T(8,128)(2,1)S(1)} %shard_map.50.o0.refs_9_, bf16[416,384]{1,0:T(8,128)(2,1)S(1)} %collective-permute-done.13.o1, bf16[416,384]{1,0:T(8,128)(2,1)S(1)} %collective-permute-done.14.o2, bf16[416,384]{1,0:T(8,128)(2,1)S(1)} %collective-permute-done.15.o3, ...), custom_call_target="tpu_custom_call" | custom-call | flops 452984832 | bytes 3735552 | tf_op jit(solution)/shard_map/pallas_call | solution.py:82
  49.0 1.1 %collective-permute-done.22.peer.refs_1_ = f32[32,384]{1,0:T(8,128)S(1)} collective-permute-done((f32[32,384]{1,0:T(8,128)S(1)}, f32[32,384]{1,0:T(8,128)S(1)}, u32[]{:S(2)}, u32[]{:S(2)}) %collective-permute-start.22) | collective-permute-done | bytes 49184 | tf_op jit(solution)/shard_map/ppermute | solution.py:34
  52.2 1.1 %collective-permute-done.25.peer.refs_3_ = f32[32,384]{1,0:T(8,128)S(1)} collective-permute-done((f32[32,384]{1,0:T(8,128)S(1)}, f32[32,384]{1,0:T(8,128)S(1)}, u32[]{:S(2)}, u32[]{:S(2)}) %collective-permute-start.25) | collective-permute-done | bytes 49184 | tf_op jit(solution)/shard_map/ppermute | solution.py:34
  53.6 1.3 %collective-permute-start.27 = (bf16[32,384]{1,0:T(8,128)(2,1)S(1)}, bf16[32,384]{1,0:T(8,128)(2,1)S(1)}, u32[]{:S(2)}, u32[]{:S(2)}) collective-permute-start(bf16[32,384]{1,0:T(8,128)(2,1)S(1)} %shard_map.56), channel_id=1, source_target_pairs={{2,11},{6,23},{10,19},{14,31},{18,27},{22,7},{26,3},{30,15},{34,43... | collective-permute-start | bytes 73736 | tf_op jit(solution)/shard_map/ppermute | solution.py:34
  54.9 1.3 %collective-permute-start.26 = (bf16[32,384]{1,0:T(8,128)(2,1)S(1)}, bf16[32,384]{1,0:T(8,128)(2,1)S(1)}, u32[]{:S(2)}, u32[]{:S(2)}) collective-permute-start(bf16[32,384]{1,0:T(8,128)(2,1)S(1)} %shard_map.56), channel_id=1, source_target_pairs={{2,3},{6,31},{10,11},{14,7},{18,19},{22,15},{26,27},{30,23},{34,35... | collective-permute-start | bytes 73736 | tf_op jit(solution)/shard_map/ppermute | solution.py:34
  56.2 12.6 %collective-permute-done.27.r1 = bf16[32,384]{1,0:T(8,128)(2,1)S(1)} collective-permute-done((bf16[32,384]{1,0:T(8,128)(2,1)S(1)}, bf16[32,384]{1,0:T(8,128)(2,1)S(1)}, u32[]{:S(2)}, u32[]{:S(2)}) %collective-permute-start.27) | collective-permute-done | bytes 24608 | tf_op jit(solution)/shard_map/ppermute | solution.py:34
  69.2 1.2 %collective-permute-done.28.refs_5_ = f32[32,384]{1,0:T(8,128)S(1)} collective-permute-done((f32[32,384]{1,0:T(8,128)S(1)}, f32[32,384]{1,0:T(8,128)S(1)}, u32[]{:S(2)}, u32[]{:S(2)}) %collective-permute-start.28) | collective-permute-done | bytes 49184 | tf_op jit(solution)/shard_map/ppermute | solution.py:34
  70.4 0.7 shard_map.58
  71.7 2.8 %collective-permute-start.30 = (f32[64,48]{1,0:T(8,128)S(1)}, f32[64,48]{1,0:T(8,128)S(1)}, u32[]{:S(2)}, u32[]{:S(2)}) collective-permute-start(f32[64,48]{1,0:T(8,128)S(1)} %get-tuple-element.61), channel_id=1, source_target_pairs={{0,16},{1,65},{2,18},{3,67},{4,20},{5,69},{6,22},{7,71},{8,24},{9,... | collective-permute-start | bytes 36872 | tf_op jit(solution)/shard_map/ppermute | solution.py:34
  74.5 1.4 %collective-permute-start.31 = (f32[64,48]{1,0:T(8,128)S(1)}, f32[64,48]{1,0:T(8,128)S(1)}, u32[]{:S(2)}, u32[]{:S(2)}) collective-permute-start(f32[64,48]{1,0:T(8,128)S(1)} %get-tuple-element.62), channel_id=1, source_target_pairs={{0,24},{1,97},{2,26},{3,99},{4,28},{5,101},{6,30},{7,103},{8,0},{9... | collective-permute-start | bytes 36872 | tf_op jit(solution)/shard_map/ppermute | solution.py:34
  76.3 0.7 collective-permute-done.30
  77.1 1.3 %collective-permute-done.31 = f32[64,48]{1,0:T(8,128)S(1)} collective-permute-done((f32[64,48]{1,0:T(8,128)S(1)}, f32[64,48]{1,0:T(8,128)S(1)}, u32[]{:S(2)}, u32[]{:S(2)}) %collective-permute-start.31) | collective-permute-done | bytes 12320 | tf_op jit(solution)/shard_map/ppermute | solution.py:34
  (54 shorter events, 10.1 us)
Async XLA Ops:
  0.0 1.8 %collective-permute-start.1 = (bf16[2,48,1536]{2,1,0:T(8,128)(2,1)}, bf16[2,48,1536]{2,1,0:T(8,128)(2,1)S(1)}, u32[]{:S(2)}, u32[]{:S(2)}) collective-permute-start(bf16[2,48,1536]{2,1,0:T(8,128)(2,1)} %own.3), channel_id=1, source_target_pairs={{0,4},{1,5},{2,6},{3,7},{4,0},{5,1},{6,2},{7,3},{8,12},{9,13},{10,... | collective-permute-start | bytes 884744 | tf_op jit(solution)/shard_map/ppermute | solution.py:34
  0.0 7.8 %collective-permute-start = (bf16[2,48,1536]{2,1,0:T(8,128)(2,1)}, bf16[2,48,1536]{2,1,0:T(8,128)(2,1)S(1)}, u32[]{:S(2)}, u32[]{:S(2)}) collective-permute-start(bf16[2,48,1536]{2,1,0:T(8,128)(2,1)} %own.2), channel_id=1, source_target_pairs={{0,4},{1,5},{2,6},{3,7},{4,0},{5,1},{6,2},{7,3},{8,12},{9,13},{10,... | collective-permute-start | bytes 884744 | tf_op jit(solution)/shard_map/ppermute | solution.py:34
  1.9 7.4 %collective-permute-start.2 = (bf16[96,384]{1,0:T(8,128)(2,1)S(1)}, bf16[96,384]{1,0:T(8,128)(2,1)S(1)}, u32[]{:S(2)}, u32[]{:S(2)}) collective-permute-start(bf16[96,384]{1,0:T(8,128)(2,1)S(1)} %get-tuple-element.34), channel_id=1, source_target_pairs={{0,8},{1,33},{2,10},{3,35},{4,12},{5,37},{6,14},{7,39},{8,16},{9,4... | collective-permute-start | bytes 221192 | tf_op jit(solution)/shard_map/ppermute | solution.py:34
  3.5 6.8 %collective-permute-start.3 = (bf16[96,384]{1,0:T(8,128)(2,1)S(1)}, bf16[96,384]{1,0:T(8,128)(2,1)S(1)}, u32[]{:S(2)}, u32[]{:S(2)}) collective-permute-start(bf16[96,384]{1,0:T(8,128)(2,1)S(1)} %get-tuple-element.38), channel_id=1, source_target_pairs={{0,16},{1,65},{2,18},{3,67},{4,20},{5,69},{6,22},{7,71},{8,24},{9,... | collective-permute-start | bytes 221192 | tf_op jit(solution)/shard_map/ppermute | solution.py:34
  6.4 4.4 %collective-permute-start.4 = (bf16[96,384]{1,0:T(8,128)(2,1)S(1)}, bf16[96,384]{1,0:T(8,128)(2,1)S(1)}, u32[]{:S(2)}, u32[]{:S(2)}) collective-permute-start(bf16[96,384]{1,0:T(8,128)(2,1)S(1)} %get-tuple-element.39), channel_id=1, source_target_pairs={{0,24},{1,97},{2,26},{3,99},{4,28},{5,101},{6,30},{7,103},{8,0},{9... | collective-permute-start | bytes 221192 | tf_op jit(solution)/shard_map/ppermute | solution.py:34
  7.8 1.5 %collective-permute-start.5 = (bf16[2,32,48]{2,1,0:T(8,128)(2,1)}, bf16[2,32,48]{2,1,0:T(8,128)(2,1)S(1)}, u32[]{:S(2)}, u32[]{:S(2)}) collective-permute-start(bf16[2,32,48]{2,1,0:T(8,128)(2,1)} %bitcast.5), channel_id=1, source_target_pairs={{0,4},{1,5},{2,6},{3,7},{4,0},{5,1},{6,2},{7,3},{8,12},{9,13},{10,... | collective-permute-start | bytes 18440 | tf_op jit(solution)/shard_map/ppermute | solution.py:34
  7.8 1.6 %collective-permute-start.6 = (f32[32,48]{1,0:T(8,128)}, f32[32,48]{1,0:T(8,128)S(1)}, u32[]{:S(2)}, u32[]{:S(2)}) collective-permute-start(f32[32,48]{1,0:T(8,128)} %bitcast.7), channel_id=1, source_target_pairs={{0,4},{1,5},{2,6},{3,7},{4,0},{5,1},{6,2},{7,3},{8,12},{9,13},{10,... | collective-permute-start | bytes 18440 | tf_op jit(solution)/shard_map/ppermute | solution.py:34
  10.9 9.1 %collective-permute-start.9 = (bf16[96,1536]{1,0:T(8,128)(2,1)S(1)}, bf16[96,1536]{1,0:T(8,128)(2,1)S(1)}, u32[]{:S(2)}, u32[]{:S(2)}) collective-permute-start(bf16[96,1536]{1,0:T(8,128)(2,1)S(1)} %shard_map.46.a0), channel_id=1, source_target_pairs={{0,8},{1,33},{2,10},{3,35},{4,12},{5,37},{6,14},{7,39},{8,16},{9,4... | collective-permute-start | bytes 884744 | tf_op jit(solution)/shard_map/ppermute | solution.py:34
  11.7 18.1 %collective-permute-start.12 = (bf16[416,384]{1,0:T(8,128)(2,1)S(1)}, bf16[416,384]{1,0:T(8,128)(2,1)S(1)}, u32[]{:S(2)}, u32[]{:S(2)}) collective-permute-start(bf16[416,384]{1,0:T(8,128)(2,1)S(1)} %shard_map.49.l0), channel_id=1, source_target_pairs={{0,96},{1,25},{2,98},{3,27},{4,100},{5,29},{6,102},{7,31},{8,104},... | collective-permute-start | bytes 958472 | tf_op jit(solution)/shard_map/ppermute | solution.py:34
  14.5 15.8 %collective-permute-start.11 = (bf16[416,384]{1,0:T(8,128)(2,1)S(1)}, bf16[416,384]{1,0:T(8,128)(2,1)S(1)}, u32[]{:S(2)}, u32[]{:S(2)}) collective-permute-start(bf16[416,384]{1,0:T(8,128)(2,1)S(1)} %shard_map.49.l0), channel_id=1, source_target_pairs={{0,32},{1,9},{2,34},{3,11},{4,36},{5,13},{6,38},{7,15},{8,40},{9,1... | collective-permute-start | bytes 958472 | tf_op jit(solution)/shard_map/ppermute | solution.py:34
  14.5 15.8 %collective-permute-start.10 = (bf16[416,384]{1,0:T(8,128)(2,1)S(1)}, bf16[416,384]{1,0:T(8,128)(2,1)S(1)}, u32[]{:S(2)}, u32[]{:S(2)}) collective-permute-start(bf16[416,384]{1,0:T(8,128)(2,1)S(1)} %shard_map.49.l0), channel_id=1, source_target_pairs={{0,64},{1,17},{2,66},{3,19},{4,68},{5,21},{6,70},{7,23},{8,72},{9,... | collective-permute-start | bytes 958472 | tf_op jit(solution)/shard_map/ppermute | solution.py:34
  16.8 13.1 %collective-permute-start.7 = (bf16[96,1536]{1,0:T(8,128)(2,1)S(1)}, bf16[96,1536]{1,0:T(8,128)(2,1)S(1)}, u32[]{:S(2)}, u32[]{:S(2)}) collective-permute-start(bf16[96,1536]{1,0:T(8,128)(2,1)S(1)} %shard_map.46.a0), channel_id=1, source_target_pairs={{0,24},{1,97},{2,26},{3,99},{4,28},{5,101},{6,30},{7,103},{8,0},{9... | collective-permute-start | bytes 884744 | tf_op jit(solution)/shard_map/ppermute | solution.py:34
  20.0 9.8 %collective-permute-start.8 = (bf16[96,1536]{1,0:T(8,128)(2,1)S(1)}, bf16[96,1536]{1,0:T(8,128)(2,1)S(1)}, u32[]{:S(2)}, u32[]{:S(2)}) collective-permute-start(bf16[96,1536]{1,0:T(8,128)(2,1)S(1)} %shard_map.46.a0), channel_id=1, source_target_pairs={{0,16},{1,65},{2,18},{3,67},{4,20},{5,69},{6,22},{7,71},{8,24},{9,... | collective-permute-start | bytes 884744 | tf_op jit(solution)/shard_map/ppermute | solution.py:34
  31.6 8.7 %collective-permute-start.15 = (bf16[416,384]{1,0:T(8,128)(2,1)S(1)}, bf16[416,384]{1,0:T(8,128)(2,1)S(1)}, u32[]{:S(2)}, u32[]{:S(2)}) collective-permute-start(bf16[416,384]{1,0:T(8,128)(2,1)S(1)} %shard_map.50.o0.refs_9_), channel_id=1, source_target_pairs={{0,64},{1,17},{2,66},{3,19},{4,20},{5,69},{6,22},{7,71},{8,72},{9,... | collective-permute-start | bytes 958472 | tf_op jit(solution)/shard_map/ppermute | solution.py:34
  32.9 10.7 %collective-permute-start.14 = (bf16[416,384]{1,0:T(8,128)(2,1)S(1)}, bf16[416,384]{1,0:T(8,128)(2,1)S(1)}, u32[]{:S(2)}, u32[]{:S(2)}) collective-permute-start(bf16[416,384]{1,0:T(8,128)(2,1)S(1)} %shard_map.50.o0.refs_9_), channel_id=1, source_target_pairs={{0,32},{1,9},{2,34},{3,11},{4,12},{5,37},{6,14},{7,39},{8,40},{9,1... | collective-permute-start | bytes 958472 | tf_op jit(solution)/shard_map/ppermute | solution.py:34
  33.5 10.1 %collective-permute-start.13 = (bf16[416,384]{1,0:T(8,128)(2,1)S(1)}, bf16[416,384]{1,0:T(8,128)(2,1)S(1)}, u32[]{:S(2)}, u32[]{:S(2)}) collective-permute-start(bf16[416,384]{1,0:T(8,128)(2,1)S(1)} %shard_map.50.o0.refs_9_), channel_id=1, source_target_pairs={{0,96},{1,25},{2,98},{3,27},{4,28},{5,101},{6,30},{7,103},{8,104},... | collective-permute-start | bytes 958472 | tf_op jit(solution)/shard_map/ppermute | solution.py:34
  36.1 8.0 %collective-permute-start.16 = (bf16[416,384]{1,0:T(8,128)(2,1)S(1)}, bf16[416,384]{1,0:T(8,128)(2,1)S(1)}, u32[]{:S(2)}, u32[]{:S(2)}) collective-permute-start(bf16[416,384]{1,0:T(8,128)(2,1)S(1)} %shard_map.50.o0.refs_9_), channel_id=1, source_target_pairs={{0,4},{1,5},{2,6},{3,7},{4,0},{5,1},{6,2},{7,3},{8,12},{9,13},{10,... | collective-permute-start | bytes 958472 | tf_op jit(solution)/shard_map/ppermute | solution.py:34
  40.3 3.8 %collective-permute-start.19 = (bf16[416,384]{1,0:T(8,128)(2,1)S(1)}, bf16[416,384]{1,0:T(8,128)(2,1)S(1)}, u32[]{:S(2)}, u32[]{:S(2)}) collective-permute-start(bf16[416,384]{1,0:T(8,128)(2,1)S(1)} %collective-permute-done.15.o3), channel_id=1, source_target_pairs={{0,4},{1,5},{2,6},{3,7},{4,0},{5,1},{6,2},{7,3},{8,12},{9,13},{10,... | collective-permute-start | bytes 958472 | tf_op jit(solution)/shard_map/ppermute | solution.py:34
  43.6 1.6 %collective-permute-start.18 = (bf16[416,384]{1,0:T(8,128)(2,1)S(1)}, bf16[416,384]{1,0:T(8,128)(2,1)S(1)}, u32[]{:S(2)}, u32[]{:S(2)}) collective-permute-start(bf16[416,384]{1,0:T(8,128)(2,1)S(1)} %collective-permute-done.14.o2), channel_id=1, source_target_pairs={{0,4},{1,5},{2,6},{3,7},{4,0},{5,1},{6,2},{7,3},{8,12},{9,13},{10,... | collective-permute-start | bytes 958472 | tf_op jit(solution)/shard_map/ppermute | solution.py:34
  43.6 2.1 %collective-permute-start.17 = (bf16[416,384]{1,0:T(8,128)(2,1)S(1)}, bf16[416,384]{1,0:T(8,128)(2,1)S(1)}, u32[]{:S(2)}, u32[]{:S(2)}) collective-permute-start(bf16[416,384]{1,0:T(8,128)(2,1)S(1)} %collective-permute-done.13.o1), channel_id=1, source_target_pairs={{0,4},{1,5},{2,6},{3,7},{4,0},{5,1},{6,2},{7,3},{8,12},{9,13},{10,... | collective-permute-start | bytes 958472 | tf_op jit(solution)/shard_map/ppermute | solution.py:34
  46.5 2.3 %collective-permute-start.21 = (bf16[32,384]{1,0:T(8,128)(2,1)S(1)}, bf16[32,384]{1,0:T(8,128)(2,1)S(1)}, u32[]{:S(2)}, u32[]{:S(2)}) collective-permute-start(bf16[32,384]{1,0:T(8,128)(2,1)S(1)} %get-tuple-element.42), channel_id=1, source_target_pairs={{0,9},{4,21},{8,17},{12,29},{16,25},{20,5},{24,1},{28,13},{32,41},... | collective-permute-start | bytes 73736 | tf_op jit(solution)/shard_map/ppermute | solution.py:34
  47.2 1.6 %collective-permute-start.20 = (bf16[32,384]{1,0:T(8,128)(2,1)S(1)}, bf16[32,384]{1,0:T(8,128)(2,1)S(1)}, u32[]{:S(2)}, u32[]{:S(2)}) collective-permute-start(bf16[32,384]{1,0:T(8,128)(2,1)S(1)} %get-tuple-element.42), channel_id=1, source_target_pairs={{0,1},{4,29},{8,9},{12,5},{16,17},{20,13},{24,25},{28,21},{32,33},... | collective-permute-start | bytes 73736 | tf_op jit(solution)/shard_map/ppermute | solution.py:34
  48.8 1.3 %collective-permute-start.22 = (f32[32,384]{1,0:T(8,128)S(1)}, f32[32,384]{1,0:T(8,128)S(1)}, u32[]{:S(2)}, u32[]{:S(2)}) collective-permute-start(f32[32,384]{1,0:T(8,128)S(1)} %shard_map.53.own.refs_0_), channel_id=1, source_target_pairs={{0,4},{1,5},{2,6},{3,7},{4,0},{5,1},{6,2},{7,3},{8,12},{9,13},{10,... | collective-permute-start | bytes 147464 | tf_op jit(solution)/shard_map/ppermute | solution.py:34
  50.5 1.4 %collective-permute-start.24 = (bf16[32,384]{1,0:T(8,128)(2,1)S(1)}, bf16[32,384]{1,0:T(8,128)(2,1)S(1)}, u32[]{:S(2)}, u32[]{:S(2)}) collective-permute-start(bf16[32,384]{1,0:T(8,128)(2,1)S(1)} %shard_map.54), channel_id=1, source_target_pairs={{1,34},{5,70},{9,42},{13,78},{17,50},{21,86},{25,58},{29,94},{33,6... | collective-permute-start | bytes 73736 | tf_op jit(solution)/shard_map/ppermute | solution.py:34
  51.2 0.7 collective-permute-start.23
  51.9 1.3 %collective-permute-start.25 = (f32[32,384]{1,0:T(8,128)S(1)}, f32[32,384]{1,0:T(8,128)S(1)}, u32[]{:S(2)}, u32[]{:S(2)}) collective-permute-start(f32[32,384]{1,0:T(8,128)S(1)} %shard_map.55.own.refs_2_), channel_id=1, source_target_pairs={{0,4},{1,5},{2,6},{3,7},{4,0},{5,1},{6,2},{7,3},{8,12},{9,13},{10,... | collective-permute-start | bytes 147464 | tf_op jit(solution)/shard_map/ppermute | solution.py:34
  53.6 15.2 %collective-permute-start.27 = (bf16[32,384]{1,0:T(8,128)(2,1)S(1)}, bf16[32,384]{1,0:T(8,128)(2,1)S(1)}, u32[]{:S(2)}, u32[]{:S(2)}) collective-permute-start(bf16[32,384]{1,0:T(8,128)(2,1)S(1)} %shard_map.56), channel_id=1, source_target_pairs={{2,11},{6,23},{10,19},{14,31},{18,27},{22,7},{26,3},{30,15},{34,43... | collective-permute-start | bytes 73736 | tf_op jit(solution)/shard_map/ppermute | solution.py:34
  54.9 14.1 %collective-permute-start.26 = (bf16[32,384]{1,0:T(8,128)(2,1)S(1)}, bf16[32,384]{1,0:T(8,128)(2,1)S(1)}, u32[]{:S(2)}, u32[]{:S(2)}) collective-permute-start(bf16[32,384]{1,0:T(8,128)(2,1)S(1)} %shard_map.56), channel_id=1, source_target_pairs={{2,3},{6,31},{10,11},{14,7},{18,19},{22,15},{26,27},{30,23},{34,35... | collective-permute-start | bytes 73736 | tf_op jit(solution)/shard_map/ppermute | solution.py:34
  69.1 1.3 %collective-permute-start.28 = (f32[32,384]{1,0:T(8,128)S(1)}, f32[32,384]{1,0:T(8,128)S(1)}, u32[]{:S(2)}, u32[]{:S(2)}) collective-permute-start(f32[32,384]{1,0:T(8,128)S(1)} %shard_map.57.refs_4_), channel_id=1, source_target_pairs={{0,4},{1,5},{2,6},{3,7},{4,0},{5,1},{6,2},{7,3},{8,12},{9,13},{10,... | collective-permute-start | bytes 147464 | tf_op jit(solution)/shard_map/ppermute | solution.py:34
  71.1 5.3 %collective-permute-start.29 = (f32[64,48]{1,0:T(8,128)S(1)}, f32[64,48]{1,0:T(8,128)S(1)}, u32[]{:S(2)}, u32[]{:S(2)}) collective-permute-start(f32[64,48]{1,0:T(8,128)S(1)} %get-tuple-element.60), channel_id=1, source_target_pairs={{0,8},{1,33},{2,10},{3,35},{4,12},{5,37},{6,14},{7,39},{8,16},{9,4... | collective-permute-start | bytes 36872 | tf_op jit(solution)/shard_map/ppermute | solution.py:34
  71.7 5.4 %collective-permute-start.30 = (f32[64,48]{1,0:T(8,128)S(1)}, f32[64,48]{1,0:T(8,128)S(1)}, u32[]{:S(2)}, u32[]{:S(2)}) collective-permute-start(f32[64,48]{1,0:T(8,128)S(1)} %get-tuple-element.61), channel_id=1, source_target_pairs={{0,16},{1,65},{2,18},{3,67},{4,20},{5,69},{6,22},{7,71},{8,24},{9,... | collective-permute-start | bytes 36872 | tf_op jit(solution)/shard_map/ppermute | solution.py:34
  74.5 3.9 %collective-permute-start.31 = (f32[64,48]{1,0:T(8,128)S(1)}, f32[64,48]{1,0:T(8,128)S(1)}, u32[]{:S(2)}, u32[]{:S(2)}) collective-permute-start(f32[64,48]{1,0:T(8,128)S(1)} %get-tuple-element.62), channel_id=1, source_target_pairs={{0,24},{1,97},{2,26},{3,99},{4,28},{5,101},{6,30},{7,103},{8,0},{9... | collective-permute-start | bytes 36872 | tf_op jit(solution)/shard_map/ppermute | solution.py:34
  (4 other events, 20.6 us)

commit v11 on v10

--- a/solution.py
+++ b/solution.py
@@ -13,7 +13,7 @@
 N = BLOCK * Y
 R = 32
 LANES = 128
-LOWER_ORDER = (0, 2, 1, 3)
+LOWER_ORDER = (0, 2, 3, 1)
 TURN_ORDER = (0, 3, 1, 2)
 F32, BF16 = jnp.float32, jnp.bfloat16
 

time: 79.2 us -> 78.9 us (level)
  transfers between devices with their start and end apart: 32 -> 32, of which waited for: 18 -> 17; matrix products, arithmetic and copies ran while one was open for 0% -> 0% of each run, Pallas kernels for 1% -> 1%
where the time goes in v11:
time: 78.9 us; the launch traced here: 78.7 us
  waiting for transfers between devices  39.2 us (50%)
  starting transfers between devices  31.9 us (40%)
  Pallas kernels  4.8 us (6%)
  local copies, waits for them, and re-layouts  1.93 us (2%)
    ppermute x32, waiting for transfers between devices, send(): return lax.ppermute(value, AXES, pairs)  39.2 us
    ppermute x32, starting transfers between devices, send(): return lax.ppermute(value, AXES, pairs)  31.9 us
    pallas_call x13, Pallas kernels, call(): pl.pallas_call(kernel, out_shape=out, in_specs=[pl.BlockSpec(memory_space...  4.8 us
    unnamed x8, local copies, waits for them, and re-layouts  1.93 us
  transfers between devices with their start and end apart: 32, of which 17 were waited for; matrix products, arithmetic and copies ran while one was open for 0% of the time, Pallas kernels for 1%

profile of v11, /device:TPU:96, one launch (start us, length us, event | category | flops | bytes accessed | tf_op | source)
XLA Modules:
  0.0 78.7 jit_solution(15969526782079141302)
XLA Ops:
  0.5 1.0 %copy-done.1 = bf16[2,48,1536]{2,1,0:T(8,128)(2,1)S(1)} copy-done((bf16[2,48,1536]{2,1,0:T(8,128)(2,1)S(1)}, bf16[2,48,1536]{2,1,0:T(8,128)(2,1)}, u32[]{:S(2)}) %copy-start.1) | copy-done | bytes 294936
  1.9 1.6 %collective-permute-start.2 = (bf16[96,384]{1,0:T(8,128)(2,1)S(1)}, bf16[96,384]{1,0:T(8,128)(2,1)S(1)}, u32[]{:S(2)}, u32[]{:S(2)}) collective-permute-start(bf16[96,384]{1,0:T(8,128)(2,1)S(1)} %get-tuple-element.34), channel_id=1, source_target_pairs={{0,8},{1,33},{2,10},{3,35},{4,12},{5,37},{6,14},{7,39},{8,16},{9,4... | collective-permute-start | bytes 221192 | tf_op jit(solution)/shard_map/ppermute | solution.py:34
  3.5 2.9 %collective-permute-start.3 = (bf16[96,384]{1,0:T(8,128)(2,1)S(1)}, bf16[96,384]{1,0:T(8,128)(2,1)S(1)}, u32[]{:S(2)}, u32[]{:S(2)}) collective-permute-start(bf16[96,384]{1,0:T(8,128)(2,1)S(1)} %get-tuple-element.38), channel_id=1, source_target_pairs={{0,16},{1,65},{2,18},{3,67},{4,20},{5,69},{6,22},{7,71},{8,24},{9,... | collective-permute-start | bytes 221192 | tf_op jit(solution)/shard_map/ppermute | solution.py:34
  6.4 1.3 %collective-permute-start.4 = (bf16[96,384]{1,0:T(8,128)(2,1)S(1)}, bf16[96,384]{1,0:T(8,128)(2,1)S(1)}, u32[]{:S(2)}, u32[]{:S(2)}) collective-permute-start(bf16[96,384]{1,0:T(8,128)(2,1)S(1)} %get-tuple-element.39), channel_id=1, source_target_pairs={{0,24},{1,97},{2,26},{3,99},{4,28},{5,101},{6,30},{7,103},{8,0},{9... | collective-permute-start | bytes 221192 | tf_op jit(solution)/shard_map/ppermute | solution.py:34
  8.3 1.0 %copy-done = bf16[2,48,1536]{2,1,0:T(8,128)(2,1)S(1)} copy-done((bf16[2,48,1536]{2,1,0:T(8,128)(2,1)S(1)}, bf16[2,48,1536]{2,1,0:T(8,128)(2,1)}, u32[]{:S(2)}) %copy-start) | copy-done | bytes 294936
  9.3 0.9 %collective-permute-done.3.p2 = bf16[96,384]{1,0:T(8,128)(2,1)S(1)} collective-permute-done((bf16[96,384]{1,0:T(8,128)(2,1)S(1)}, bf16[96,384]{1,0:T(8,128)(2,1)S(1)}, u32[]{:S(2)}, u32[]{:S(2)}) %collective-permute-start.3) | collective-permute-done | bytes 73760 | tf_op jit(solution)/shard_map/ppermute | solution.py:34
  10.9 0.8 %collective-permute-start.9 = (bf16[96,1536]{1,0:T(8,128)(2,1)S(1)}, bf16[96,1536]{1,0:T(8,128)(2,1)S(1)}, u32[]{:S(2)}, u32[]{:S(2)}) collective-permute-start(bf16[96,1536]{1,0:T(8,128)(2,1)S(1)} %shard_map.46.a0), channel_id=1, source_target_pairs={{0,8},{1,33},{2,10},{3,35},{4,12},{5,37},{6,14},{7,39},{8,16},{9,4... | collective-permute-start | bytes 884744 | tf_op jit(solution)/shard_map/ppermute | solution.py:34
  11.7 1.5 %collective-permute-start.12 = (bf16[416,384]{1,0:T(8,128)(2,1)S(1)}, bf16[416,384]{1,0:T(8,128)(2,1)S(1)}, u32[]{:S(2)}, u32[]{:S(2)}) collective-permute-start(bf16[416,384]{1,0:T(8,128)(2,1)S(1)} %shard_map.49.l0), channel_id=1, source_target_pairs={{0,32},{1,9},{2,34},{3,11},{4,36},{5,13},{6,38},{7,15},{8,40},{9,1... | collective-permute-start | bytes 958472 | tf_op jit(solution)/shard_map/ppermute | solution.py:34
  13.2 1.7 %collective-permute-start.11 = (bf16[416,384]{1,0:T(8,128)(2,1)S(1)}, bf16[416,384]{1,0:T(8,128)(2,1)S(1)}, u32[]{:S(2)}, u32[]{:S(2)}) collective-permute-start(bf16[416,384]{1,0:T(8,128)(2,1)S(1)} %shard_map.49.l0), channel_id=1, source_target_pairs={{0,96},{1,25},{2,98},{3,27},{4,100},{5,29},{6,102},{7,31},{8,104},... | collective-permute-start | bytes 958472 | tf_op jit(solution)/shard_map/ppermute | solution.py:34
  15.0 1.8 %collective-permute-start.10 = (bf16[416,384]{1,0:T(8,128)(2,1)S(1)}, bf16[416,384]{1,0:T(8,128)(2,1)S(1)}, u32[]{:S(2)}, u32[]{:S(2)}) collective-permute-start(bf16[416,384]{1,0:T(8,128)(2,1)S(1)} %shard_map.49.l0), channel_id=1, source_target_pairs={{0,64},{1,17},{2,66},{3,19},{4,68},{5,21},{6,70},{7,23},{8,72},{9,... | collective-permute-start | bytes 958472 | tf_op jit(solution)/shard_map/ppermute | solution.py:34
  16.8 2.5 %collective-permute-start.7 = (bf16[96,1536]{1,0:T(8,128)(2,1)S(1)}, bf16[96,1536]{1,0:T(8,128)(2,1)S(1)}, u32[]{:S(2)}, u32[]{:S(2)}) collective-permute-start(bf16[96,1536]{1,0:T(8,128)(2,1)S(1)} %shard_map.46.a0), channel_id=1, source_target_pairs={{0,24},{1,97},{2,26},{3,99},{4,28},{5,101},{6,30},{7,103},{8,0},{9... | collective-permute-start | bytes 884744 | tf_op jit(solution)/shard_map/ppermute | solution.py:34
  19.3 0.8 collective-permute-done.9.a1
  20.0 0.9 %collective-permute-start.8 = (bf16[96,1536]{1,0:T(8,128)(2,1)S(1)}, bf16[96,1536]{1,0:T(8,128)(2,1)S(1)}, u32[]{:S(2)}, u32[]{:S(2)}) collective-permute-start(bf16[96,1536]{1,0:T(8,128)(2,1)S(1)} %shard_map.46.a0), channel_id=1, source_target_pairs={{0,16},{1,65},{2,18},{3,67},{4,20},{5,69},{6,22},{7,71},{8,24},{9,... | collective-permute-start | bytes 884744 | tf_op jit(solution)/shard_map/ppermute | solution.py:34
  20.9 8.9 %collective-permute-done.7.a3 = bf16[96,1536]{1,0:T(8,128)(2,1)S(1)} collective-permute-done((bf16[96,1536]{1,0:T(8,128)(2,1)S(1)}, bf16[96,1536]{1,0:T(8,128)(2,1)S(1)}, u32[]{:S(2)}, u32[]{:S(2)}) %collective-permute-start.7) | collective-permute-done | bytes 294944 | tf_op jit(solution)/shard_map/ppermute | solution.py:34
  29.9 1.3 %shard_map.50.o0.refs_9_ = bf16[416,384]{1,0:T(8,128)(2,1)S(1)} custom-call(bf16[96,1536]{1,0:T(8,128)(2,1)S(1)} %shard_map.46.a0, bf16[96,1536]{1,0:T(8,128)(2,1)S(1)} %collective-permute-done.7.a3, bf16[96,1536]{1,0:T(8,128)(2,1)S(1)} %collective-permute-done.8.a2, bf16[96,1536]{1,0:T(8,128)(2,1)S(1)} %collective-permute-done.9.a1, ...), custom_call_target="tpu_custom_call" | custom-call | flops 452984832 | bytes 2457600 | tf_op jit(solution)/shard_map/pallas_call | solution.py:82
  31.2 1.8 %collective-permute-start.15 = (bf16[416,384]{1,0:T(8,128)(2,1)S(1)}, bf16[416,384]{1,0:T(8,128)(2,1)S(1)}, u32[]{:S(2)}, u32[]{:S(2)}) collective-permute-start(bf16[416,384]{1,0:T(8,128)(2,1)S(1)} %shard_map.50.o0.refs_9_), channel_id=1, source_target_pairs={{0,64},{1,17},{2,66},{3,19},{4,20},{5,69},{6,22},{7,71},{8,72},{9,... | collective-permute-start | bytes 958472 | tf_op jit(solution)/shard_map/ppermute | solution.py:34
  33.5 2.8 %collective-permute-start.13 = (bf16[416,384]{1,0:T(8,128)(2,1)S(1)}, bf16[416,384]{1,0:T(8,128)(2,1)S(1)}, u32[]{:S(2)}, u32[]{:S(2)}) collective-permute-start(bf16[416,384]{1,0:T(8,128)(2,1)S(1)} %shard_map.50.o0.refs_9_), channel_id=1, source_target_pairs={{0,96},{1,25},{2,98},{3,27},{4,28},{5,101},{6,30},{7,103},{8,104},... | collective-permute-start | bytes 958472 | tf_op jit(solution)/shard_map/ppermute | solution.py:34
  36.3 3.6 %collective-permute-done.15.o3 = bf16[416,384]{1,0:T(8,128)(2,1)S(1)} collective-permute-done((bf16[416,384]{1,0:T(8,128)(2,1)S(1)}, bf16[416,384]{1,0:T(8,128)(2,1)S(1)}, u32[]{:S(2)}, u32[]{:S(2)}) %collective-permute-start.15) | collective-permute-done | bytes 319520 | tf_op jit(solution)/shard_map/ppermute | solution.py:34
  39.9 3.3 %collective-permute-done.14.o2 = bf16[416,384]{1,0:T(8,128)(2,1)S(1)} collective-permute-done((bf16[416,384]{1,0:T(8,128)(2,1)S(1)}, bf16[416,384]{1,0:T(8,128)(2,1)S(1)}, u32[]{:S(2)}, u32[]{:S(2)}) %collective-permute-start.14) | collective-permute-done | bytes 319520 | tf_op jit(solution)/shard_map/ppermute | solution.py:34
  43.7 1.1 %collective-permute-done.18.p2 = bf16[416,384]{1,0:T(8,128)(2,1)S(1)} collective-permute-done((bf16[416,384]{1,0:T(8,128)(2,1)S(1)}, bf16[416,384]{1,0:T(8,128)(2,1)S(1)}, u32[]{:S(2)}, u32[]{:S(2)}) %collective-permute-start.18) | collective-permute-done | bytes 319520 | tf_op jit(solution)/shard_map/ppermute | solution.py:34
  45.3 0.8 %shard_map.51 = (bf16[384,1536]{1,0:T(8,128)(2,1)S(1)}, f32[32,384]{1,0:T(8,128)S(1)}, bf16[32,384]{1,0:T(8,128)(2,1)S(1)}) custom-call(bf16[416,384]{1,0:T(8,128)(2,1)S(1)} %shard_map.50.o0.refs_9_, bf16[416,384]{1,0:T(8,128)(2,1)S(1)} %collective-permute-done.13.o1, bf16[416,384]{1,0:T(8,128)(2,1)S(1)} %collective-permute-done.14.o2, ...), custom_call_target="tpu_custom_call" | custom-call | bytes 2555904 | tf_op jit(solution)/shard_map/pallas_call | solution.py:82
  47.5 0.9 %shard_map.52 = (bf16[384,384]{1,0:T(8,128)(2,1)S(1)}, bf16[384,384]{1,0:T(8,128)(2,1)S(1)}) custom-call(bf16[416,384]{1,0:T(8,128)(2,1)S(1)} %shard_map.50.o0.refs_9_, bf16[416,384]{1,0:T(8,128)(2,1)S(1)} %collective-permute-done.13.o1, bf16[416,384]{1,0:T(8,128)(2,1)S(1)} %collective-permute-done.14.o2, bf16[416,384]{1,0:T(8,128)(2,1)S(1)} %collective-permute-done.15.o3, ...), custom_call_target="tpu_custom_call" | custom-call | flops 452984832 | bytes 3735552 | tf_op jit(solution)/shard_map/pallas_call | solution.py:82
  48.6 1.1 %collective-permute-done.22.peer.refs_1_ = f32[32,384]{1,0:T(8,128)S(1)} collective-permute-done((f32[32,384]{1,0:T(8,128)S(1)}, f32[32,384]{1,0:T(8,128)S(1)}, u32[]{:S(2)}, u32[]{:S(2)}) %collective-permute-start.22) | collective-permute-done | bytes 49184 | tf_op jit(solution)/shard_map/ppermute | solution.py:34
  51.8 1.1 %collective-permute-done.25.peer.refs_3_ = f32[32,384]{1,0:T(8,128)S(1)} collective-permute-done((f32[32,384]{1,0:T(8,128)S(1)}, f32[32,384]{1,0:T(8,128)S(1)}, u32[]{:S(2)}, u32[]{:S(2)}) %collective-permute-start.25) | collective-permute-done | bytes 49184 | tf_op jit(solution)/shard_map/ppermute | solution.py:34
  53.2 1.3 %collective-permute-start.27 = (bf16[32,384]{1,0:T(8,128)(2,1)S(1)}, bf16[32,384]{1,0:T(8,128)(2,1)S(1)}, u32[]{:S(2)}, u32[]{:S(2)}) collective-permute-start(bf16[32,384]{1,0:T(8,128)(2,1)S(1)} %shard_map.56), channel_id=1, source_target_pairs={{2,11},{6,23},{10,19},{14,31},{18,27},{22,7},{26,3},{30,15},{34,43... | collective-permute-start | bytes 73736 | tf_op jit(solution)/shard_map/ppermute | solution.py:34
  54.5 1.3 %collective-permute-start.26 = (bf16[32,384]{1,0:T(8,128)(2,1)S(1)}, bf16[32,384]{1,0:T(8,128)(2,1)S(1)}, u32[]{:S(2)}, u32[]{:S(2)}) collective-permute-start(bf16[32,384]{1,0:T(8,128)(2,1)S(1)} %shard_map.56), channel_id=1, source_target_pairs={{2,3},{6,31},{10,11},{14,7},{18,19},{22,15},{26,27},{30,23},{34,35... | collective-permute-start | bytes 73736 | tf_op jit(solution)/shard_map/ppermute | solution.py:34
  55.8 12.7 %collective-permute-done.27.r1 = bf16[32,384]{1,0:T(8,128)(2,1)S(1)} collective-permute-done((bf16[32,384]{1,0:T(8,128)(2,1)S(1)}, bf16[32,384]{1,0:T(8,128)(2,1)S(1)}, u32[]{:S(2)}, u32[]{:S(2)}) %collective-permute-start.27) | collective-permute-done | bytes 24608 | tf_op jit(solution)/shard_map/ppermute | solution.py:34
  68.8 1.2 %collective-permute-done.28.refs_5_ = f32[32,384]{1,0:T(8,128)S(1)} collective-permute-done((f32[32,384]{1,0:T(8,128)S(1)}, f32[32,384]{1,0:T(8,128)S(1)}, u32[]{:S(2)}, u32[]{:S(2)}) %collective-permute-start.28) | collective-permute-done | bytes 49184 | tf_op jit(solution)/shard_map/ppermute | solution.py:34
  71.4 2.7 %collective-permute-start.30 = (f32[64,48]{1,0:T(8,128)S(1)}, f32[64,48]{1,0:T(8,128)S(1)}, u32[]{:S(2)}, u32[]{:S(2)}) collective-permute-start(f32[64,48]{1,0:T(8,128)S(1)} %get-tuple-element.61), channel_id=1, source_target_pairs={{0,16},{1,65},{2,18},{3,67},{4,20},{5,69},{6,22},{7,71},{8,24},{9,... | collective-permute-start | bytes 36872 | tf_op jit(solution)/shard_map/ppermute | solution.py:34
  74.1 1.0 %collective-permute-start.31 = (f32[64,48]{1,0:T(8,128)S(1)}, f32[64,48]{1,0:T(8,128)S(1)}, u32[]{:S(2)}, u32[]{:S(2)}) collective-permute-start(f32[64,48]{1,0:T(8,128)S(1)} %get-tuple-element.62), channel_id=1, source_target_pairs={{0,24},{1,97},{2,26},{3,99},{4,28},{5,101},{6,30},{7,103},{8,0},{9... | collective-permute-start | bytes 36872 | tf_op jit(solution)/shard_map/ppermute | solution.py:34
  75.1 0.9 %collective-permute-done.29 = f32[64,48]{1,0:T(8,128)S(1)} collective-permute-done((f32[64,48]{1,0:T(8,128)S(1)}, f32[64,48]{1,0:T(8,128)S(1)}, u32[]{:S(2)}, u32[]{:S(2)}) %collective-permute-start.29) | collective-permute-done | bytes 12320 | tf_op jit(solution)/shard_map/ppermute | solution.py:34
  76.8 1.2 %collective-permute-done.31 = f32[64,48]{1,0:T(8,128)S(1)} collective-permute-done((f32[64,48]{1,0:T(8,128)S(1)}, f32[64,48]{1,0:T(8,128)S(1)}, u32[]{:S(2)}, u32[]{:S(2)}) %collective-permute-start.31) | collective-permute-done | bytes 12320 | tf_op jit(solution)/shard_map/ppermute | solution.py:34
  (54 shorter events, 10.5 us)
Async XLA Ops:
  0.0 1.8 %collective-permute-start.1 = (bf16[2,48,1536]{2,1,0:T(8,128)(2,1)}, bf16[2,48,1536]{2,1,0:T(8,128)(2,1)S(1)}, u32[]{:S(2)}, u32[]{:S(2)}) collective-permute-start(bf16[2,48,1536]{2,1,0:T(8,128)(2,1)} %own.3), channel_id=1, source_target_pairs={{0,4},{1,5},{2,6},{3,7},{4,0},{5,1},{6,2},{7,3},{8,12},{9,13},{10,... | collective-permute-start | bytes 884744 | tf_op jit(solution)/shard_map/ppermute | solution.py:34
  0.0 7.8 %collective-permute-start = (bf16[2,48,1536]{2,1,0:T(8,128)(2,1)}, bf16[2,48,1536]{2,1,0:T(8,128)(2,1)S(1)}, u32[]{:S(2)}, u32[]{:S(2)}) collective-permute-start(bf16[2,48,1536]{2,1,0:T(8,128)(2,1)} %own.2), channel_id=1, source_target_pairs={{0,4},{1,5},{2,6},{3,7},{4,0},{5,1},{6,2},{7,3},{8,12},{9,13},{10,... | collective-permute-start | bytes 884744 | tf_op jit(solution)/shard_map/ppermute | solution.py:34
  1.9 7.4 %collective-permute-start.2 = (bf16[96,384]{1,0:T(8,128)(2,1)S(1)}, bf16[96,384]{1,0:T(8,128)(2,1)S(1)}, u32[]{:S(2)}, u32[]{:S(2)}) collective-permute-start(bf16[96,384]{1,0:T(8,128)(2,1)S(1)} %get-tuple-element.34), channel_id=1, source_target_pairs={{0,8},{1,33},{2,10},{3,35},{4,12},{5,37},{6,14},{7,39},{8,16},{9,4... | collective-permute-start | bytes 221192 | tf_op jit(solution)/shard_map/ppermute | solution.py:34
  3.5 6.8 %collective-permute-start.3 = (bf16[96,384]{1,0:T(8,128)(2,1)S(1)}, bf16[96,384]{1,0:T(8,128)(2,1)S(1)}, u32[]{:S(2)}, u32[]{:S(2)}) collective-permute-start(bf16[96,384]{1,0:T(8,128)(2,1)S(1)} %get-tuple-element.38), channel_id=1, source_target_pairs={{0,16},{1,65},{2,18},{3,67},{4,20},{5,69},{6,22},{7,71},{8,24},{9,... | collective-permute-start | bytes 221192 | tf_op jit(solution)/shard_map/ppermute | solution.py:34
  6.4 4.4 %collective-permute-start.4 = (bf16[96,384]{1,0:T(8,128)(2,1)S(1)}, bf16[96,384]{1,0:T(8,128)(2,1)S(1)}, u32[]{:S(2)}, u32[]{:S(2)}) collective-permute-start(bf16[96,384]{1,0:T(8,128)(2,1)S(1)} %get-tuple-element.39), channel_id=1, source_target_pairs={{0,24},{1,97},{2,26},{3,99},{4,28},{5,101},{6,30},{7,103},{8,0},{9... | collective-permute-start | bytes 221192 | tf_op jit(solution)/shard_map/ppermute | solution.py:34
  7.8 1.5 %collective-permute-start.5 = (bf16[2,32,48]{2,1,0:T(8,128)(2,1)}, bf16[2,32,48]{2,1,0:T(8,128)(2,1)S(1)}, u32[]{:S(2)}, u32[]{:S(2)}) collective-permute-start(bf16[2,32,48]{2,1,0:T(8,128)(2,1)} %bitcast.5), channel_id=1, source_target_pairs={{0,4},{1,5},{2,6},{3,7},{4,0},{5,1},{6,2},{7,3},{8,12},{9,13},{10,... | collective-permute-start | bytes 18440 | tf_op jit(solution)/shard_map/ppermute | solution.py:34
  7.8 1.6 %collective-permute-start.6 = (f32[32,48]{1,0:T(8,128)}, f32[32,48]{1,0:T(8,128)S(1)}, u32[]{:S(2)}, u32[]{:S(2)}) collective-permute-start(f32[32,48]{1,0:T(8,128)} %bitcast.7), channel_id=1, source_target_pairs={{0,4},{1,5},{2,6},{3,7},{4,0},{5,1},{6,2},{7,3},{8,12},{9,13},{10,... | collective-permute-start | bytes 18440 | tf_op jit(solution)/shard_map/ppermute | solution.py:34
  10.9 9.1 %collective-permute-start.9 = (bf16[96,1536]{1,0:T(8,128)(2,1)S(1)}, bf16[96,1536]{1,0:T(8,128)(2,1)S(1)}, u32[]{:S(2)}, u32[]{:S(2)}) collective-permute-start(bf16[96,1536]{1,0:T(8,128)(2,1)S(1)} %shard_map.46.a0), channel_id=1, source_target_pairs={{0,8},{1,33},{2,10},{3,35},{4,12},{5,37},{6,14},{7,39},{8,16},{9,4... | collective-permute-start | bytes 884744 | tf_op jit(solution)/shard_map/ppermute | solution.py:34
  11.7 18.1 %collective-permute-start.12 = (bf16[416,384]{1,0:T(8,128)(2,1)S(1)}, bf16[416,384]{1,0:T(8,128)(2,1)S(1)}, u32[]{:S(2)}, u32[]{:S(2)}) collective-permute-start(bf16[416,384]{1,0:T(8,128)(2,1)S(1)} %shard_map.49.l0), channel_id=1, source_target_pairs={{0,32},{1,9},{2,34},{3,11},{4,36},{5,13},{6,38},{7,15},{8,40},{9,1... | collective-permute-start | bytes 958472 | tf_op jit(solution)/shard_map/ppermute | solution.py:34
  13.2 16.7 %collective-permute-start.11 = (bf16[416,384]{1,0:T(8,128)(2,1)S(1)}, bf16[416,384]{1,0:T(8,128)(2,1)S(1)}, u32[]{:S(2)}, u32[]{:S(2)}) collective-permute-start(bf16[416,384]{1,0:T(8,128)(2,1)S(1)} %shard_map.49.l0), channel_id=1, source_target_pairs={{0,96},{1,25},{2,98},{3,27},{4,100},{5,29},{6,102},{7,31},{8,104},... | collective-permute-start | bytes 958472 | tf_op jit(solution)/shard_map/ppermute | solution.py:34
  15.0 14.9 %collective-permute-start.10 = (bf16[416,384]{1,0:T(8,128)(2,1)S(1)}, bf16[416,384]{1,0:T(8,128)(2,1)S(1)}, u32[]{:S(2)}, u32[]{:S(2)}) collective-permute-start(bf16[416,384]{1,0:T(8,128)(2,1)S(1)} %shard_map.49.l0), channel_id=1, source_target_pairs={{0,64},{1,17},{2,66},{3,19},{4,68},{5,21},{6,70},{7,23},{8,72},{9,... | collective-permute-start | bytes 958472 | tf_op jit(solution)/shard_map/ppermute | solution.py:34
  16.8 13.1 %collective-permute-start.7 = (bf16[96,1536]{1,0:T(8,128)(2,1)S(1)}, bf16[96,1536]{1,0:T(8,128)(2,1)S(1)}, u32[]{:S(2)}, u32[]{:S(2)}) collective-permute-start(bf16[96,1536]{1,0:T(8,128)(2,1)S(1)} %shard_map.46.a0), channel_id=1, source_target_pairs={{0,24},{1,97},{2,26},{3,99},{4,28},{5,101},{6,30},{7,103},{8,0},{9... | collective-permute-start | bytes 884744 | tf_op jit(solution)/shard_map/ppermute | solution.py:34
  20.0 9.8 %collective-permute-start.8 = (bf16[96,1536]{1,0:T(8,128)(2,1)S(1)}, bf16[96,1536]{1,0:T(8,128)(2,1)S(1)}, u32[]{:S(2)}, u32[]{:S(2)}) collective-permute-start(bf16[96,1536]{1,0:T(8,128)(2,1)S(1)} %shard_map.46.a0), channel_id=1, source_target_pairs={{0,16},{1,65},{2,18},{3,67},{4,20},{5,69},{6,22},{7,71},{8,24},{9,... | collective-permute-start | bytes 884744 | tf_op jit(solution)/shard_map/ppermute | solution.py:34
  31.2 8.7 %collective-permute-start.15 = (bf16[416,384]{1,0:T(8,128)(2,1)S(1)}, bf16[416,384]{1,0:T(8,128)(2,1)S(1)}, u32[]{:S(2)}, u32[]{:S(2)}) collective-permute-start(bf16[416,384]{1,0:T(8,128)(2,1)S(1)} %shard_map.50.o0.refs_9_), channel_id=1, source_target_pairs={{0,64},{1,17},{2,66},{3,19},{4,20},{5,69},{6,22},{7,71},{8,72},{9,... | collective-permute-start | bytes 958472 | tf_op jit(solution)/shard_map/ppermute | solution.py:34
  33.0 10.2 %collective-permute-start.14 = (bf16[416,384]{1,0:T(8,128)(2,1)S(1)}, bf16[416,384]{1,0:T(8,128)(2,1)S(1)}, u32[]{:S(2)}, u32[]{:S(2)}) collective-permute-start(bf16[416,384]{1,0:T(8,128)(2,1)S(1)} %shard_map.50.o0.refs_9_), channel_id=1, source_target_pairs={{0,32},{1,9},{2,34},{3,11},{4,12},{5,37},{6,14},{7,39},{8,40},{9,1... | collective-permute-start | bytes 958472 | tf_op jit(solution)/shard_map/ppermute | solution.py:34
  33.5 9.7 %collective-permute-start.13 = (bf16[416,384]{1,0:T(8,128)(2,1)S(1)}, bf16[416,384]{1,0:T(8,128)(2,1)S(1)}, u32[]{:S(2)}, u32[]{:S(2)}) collective-permute-start(bf16[416,384]{1,0:T(8,128)(2,1)S(1)} %shard_map.50.o0.refs_9_), channel_id=1, source_target_pairs={{0,96},{1,25},{2,98},{3,27},{4,28},{5,101},{6,30},{7,103},{8,104},... | collective-permute-start | bytes 958472 | tf_op jit(solution)/shard_map/ppermute | solution.py:34
  36.3 7.5 %collective-permute-start.16 = (bf16[416,384]{1,0:T(8,128)(2,1)S(1)}, bf16[416,384]{1,0:T(8,128)(2,1)S(1)}, u32[]{:S(2)}, u32[]{:S(2)}) collective-permute-start(bf16[416,384]{1,0:T(8,128)(2,1)S(1)} %shard_map.50.o0.refs_9_), channel_id=1, source_target_pairs={{0,4},{1,5},{2,6},{3,7},{4,0},{5,1},{6,2},{7,3},{8,12},{9,13},{10,... | collective-permute-start | bytes 958472 | tf_op jit(solution)/shard_map/ppermute | solution.py:34
  39.9 3.8 %collective-permute-start.19 = (bf16[416,384]{1,0:T(8,128)(2,1)S(1)}, bf16[416,384]{1,0:T(8,128)(2,1)S(1)}, u32[]{:S(2)}, u32[]{:S(2)}) collective-permute-start(bf16[416,384]{1,0:T(8,128)(2,1)S(1)} %collective-permute-done.15.o3), channel_id=1, source_target_pairs={{0,4},{1,5},{2,6},{3,7},{4,0},{5,1},{6,2},{7,3},{8,12},{9,13},{10,... | collective-permute-start | bytes 958472 | tf_op jit(solution)/shard_map/ppermute | solution.py:34
  43.2 1.6 %collective-permute-start.18 = (bf16[416,384]{1,0:T(8,128)(2,1)S(1)}, bf16[416,384]{1,0:T(8,128)(2,1)S(1)}, u32[]{:S(2)}, u32[]{:S(2)}) collective-permute-start(bf16[416,384]{1,0:T(8,128)(2,1)S(1)} %collective-permute-done.14.o2), channel_id=1, source_target_pairs={{0,4},{1,5},{2,6},{3,7},{4,0},{5,1},{6,2},{7,3},{8,12},{9,13},{10,... | collective-permute-start | bytes 958472 | tf_op jit(solution)/shard_map/ppermute | solution.py:34
  43.2 2.1 %collective-permute-start.17 = (bf16[416,384]{1,0:T(8,128)(2,1)S(1)}, bf16[416,384]{1,0:T(8,128)(2,1)S(1)}, u32[]{:S(2)}, u32[]{:S(2)}) collective-permute-start(bf16[416,384]{1,0:T(8,128)(2,1)S(1)} %collective-permute-done.13.o1), channel_id=1, source_target_pairs={{0,4},{1,5},{2,6},{3,7},{4,0},{5,1},{6,2},{7,3},{8,12},{9,13},{10,... | collective-permute-start | bytes 958472 | tf_op jit(solution)/shard_map/ppermute | solution.py:34
  46.1 2.3 %collective-permute-start.21 = (bf16[32,384]{1,0:T(8,128)(2,1)S(1)}, bf16[32,384]{1,0:T(8,128)(2,1)S(1)}, u32[]{:S(2)}, u32[]{:S(2)}) collective-permute-start(bf16[32,384]{1,0:T(8,128)(2,1)S(1)} %get-tuple-element.42), channel_id=1, source_target_pairs={{0,9},{4,21},{8,17},{12,29},{16,25},{20,5},{24,1},{28,13},{32,41},... | collective-permute-start | bytes 73736 | tf_op jit(solution)/shard_map/ppermute | solution.py:34
  46.8 1.6 %collective-permute-start.20 = (bf16[32,384]{1,0:T(8,128)(2,1)S(1)}, bf16[32,384]{1,0:T(8,128)(2,1)S(1)}, u32[]{:S(2)}, u32[]{:S(2)}) collective-permute-start(bf16[32,384]{1,0:T(8,128)(2,1)S(1)} %get-tuple-element.42), channel_id=1, source_target_pairs={{0,1},{4,29},{8,9},{12,5},{16,17},{20,13},{24,25},{28,21},{32,33},... | collective-permute-start | bytes 73736 | tf_op jit(solution)/shard_map/ppermute | solution.py:34
  48.4 1.3 %collective-permute-start.22 = (f32[32,384]{1,0:T(8,128)S(1)}, f32[32,384]{1,0:T(8,128)S(1)}, u32[]{:S(2)}, u32[]{:S(2)}) collective-permute-start(f32[32,384]{1,0:T(8,128)S(1)} %shard_map.53.own.refs_0_), channel_id=1, source_target_pairs={{0,4},{1,5},{2,6},{3,7},{4,0},{5,1},{6,2},{7,3},{8,12},{9,13},{10,... | collective-permute-start | bytes 147464 | tf_op jit(solution)/shard_map/ppermute | solution.py:34
  50.1 1.4 %collective-permute-start.24 = (bf16[32,384]{1,0:T(8,128)(2,1)S(1)}, bf16[32,384]{1,0:T(8,128)(2,1)S(1)}, u32[]{:S(2)}, u32[]{:S(2)}) collective-permute-start(bf16[32,384]{1,0:T(8,128)(2,1)S(1)} %shard_map.54), channel_id=1, source_target_pairs={{1,34},{5,70},{9,42},{13,78},{17,50},{21,86},{25,58},{29,94},{33,6... | collective-permute-start | bytes 73736 | tf_op jit(solution)/shard_map/ppermute | solution.py:34
  50.8 0.7 collective-permute-start.23
  51.5 1.3 %collective-permute-start.25 = (f32[32,384]{1,0:T(8,128)S(1)}, f32[32,384]{1,0:T(8,128)S(1)}, u32[]{:S(2)}, u32[]{:S(2)}) collective-permute-start(f32[32,384]{1,0:T(8,128)S(1)} %shard_map.55.own.refs_2_), channel_id=1, source_target_pairs={{0,4},{1,5},{2,6},{3,7},{4,0},{5,1},{6,2},{7,3},{8,12},{9,13},{10,... | collective-permute-start | bytes 147464 | tf_op jit(solution)/shard_map/ppermute | solution.py:34
  53.2 15.3 %collective-permute-start.27 = (bf16[32,384]{1,0:T(8,128)(2,1)S(1)}, bf16[32,384]{1,0:T(8,128)(2,1)S(1)}, u32[]{:S(2)}, u32[]{:S(2)}) collective-permute-start(bf16[32,384]{1,0:T(8,128)(2,1)S(1)} %shard_map.56), channel_id=1, source_target_pairs={{2,11},{6,23},{10,19},{14,31},{18,27},{22,7},{26,3},{30,15},{34,43... | collective-permute-start | bytes 73736 | tf_op jit(solution)/shard_map/ppermute | solution.py:34
  54.5 14.2 %collective-permute-start.26 = (bf16[32,384]{1,0:T(8,128)(2,1)S(1)}, bf16[32,384]{1,0:T(8,128)(2,1)S(1)}, u32[]{:S(2)}, u32[]{:S(2)}) collective-permute-start(bf16[32,384]{1,0:T(8,128)(2,1)S(1)} %shard_map.56), channel_id=1, source_target_pairs={{2,3},{6,31},{10,11},{14,7},{18,19},{22,15},{26,27},{30,23},{34,35... | collective-permute-start | bytes 73736 | tf_op jit(solution)/shard_map/ppermute | solution.py:34
  68.7 1.3 %collective-permute-start.28 = (f32[32,384]{1,0:T(8,128)S(1)}, f32[32,384]{1,0:T(8,128)S(1)}, u32[]{:S(2)}, u32[]{:S(2)}) collective-permute-start(f32[32,384]{1,0:T(8,128)S(1)} %shard_map.57.refs_4_), channel_id=1, source_target_pairs={{0,4},{1,5},{2,6},{3,7},{4,0},{5,1},{6,2},{7,3},{8,12},{9,13},{10,... | collective-permute-start | bytes 147464 | tf_op jit(solution)/shard_map/ppermute | solution.py:34
  70.8 5.3 %collective-permute-start.29 = (f32[64,48]{1,0:T(8,128)S(1)}, f32[64,48]{1,0:T(8,128)S(1)}, u32[]{:S(2)}, u32[]{:S(2)}) collective-permute-start(f32[64,48]{1,0:T(8,128)S(1)} %get-tuple-element.60), channel_id=1, source_target_pairs={{0,8},{1,33},{2,10},{3,35},{4,12},{5,37},{6,14},{7,39},{8,16},{9,4... | collective-permute-start | bytes 36872 | tf_op jit(solution)/shard_map/ppermute | solution.py:34
  71.4 5.4 %collective-permute-start.30 = (f32[64,48]{1,0:T(8,128)S(1)}, f32[64,48]{1,0:T(8,128)S(1)}, u32[]{:S(2)}, u32[]{:S(2)}) collective-permute-start(f32[64,48]{1,0:T(8,128)S(1)} %get-tuple-element.61), channel_id=1, source_target_pairs={{0,16},{1,65},{2,18},{3,67},{4,20},{5,69},{6,22},{7,71},{8,24},{9,... | collective-permute-start | bytes 36872 | tf_op jit(solution)/shard_map/ppermute | solution.py:34
  74.1 3.9 %collective-permute-start.31 = (f32[64,48]{1,0:T(8,128)S(1)}, f32[64,48]{1,0:T(8,128)S(1)}, u32[]{:S(2)}, u32[]{:S(2)}) collective-permute-start(f32[64,48]{1,0:T(8,128)S(1)} %get-tuple-element.62), channel_id=1, source_target_pairs={{0,24},{1,97},{2,26},{3,99},{4,28},{5,101},{6,30},{7,103},{8,0},{9... | collective-permute-start | bytes 36872 | tf_op jit(solution)/shard_map/ppermute | solution.py:34
  (4 other events, 20.6 us)

commit v12 on v11

--- a/solution.py
+++ b/solution.py
@@ -228,8 +228,10 @@
     low_out[...] = low
 
 
-def pair_sum(r0, r1, out):
-    out[...] = r0[...].astype(F32) + r1[...].astype(F32)
+def pair_sum(r0, r1, out, sent):
+    total = r0[...].astype(F32) + r1[...].astype(F32)
+    out[...] = total
+    sent[...] = total.astype(BF16)
 
 
 def onward(entry, p_high, p_low, base):
@@ -263,8 +265,8 @@
             return (y, x, c, z + 1) if z + 1 == plane else None
         arrived.append(send(out, target))
     arrived, beside = lax.optimization_barrier((arrived, beside))
-    own = call(pair_sum, shape((R, BLOCK), F32), *arrived)
-    return (own, to_peer(own)), beside
+    own, sent = call(pair_sum, [shape((R, BLOCK), F32), shape((R, BLOCK))], *arrived)
+    return (own, to_peer(sent)), beside
 
 
 def local(inverses, lower, forcing, inflow):

time: 78.9 us -> 78.8 us (level)
  no operation moved by 1% of the time
where the time goes in v12:
time: 78.8 us; the launch traced here: 78.6 us
  waiting for transfers between devices  39.1 us (50%)
  starting transfers between devices  31.9 us (40%)
  Pallas kernels  4.82 us (6%)
  local copies, waits for them, and re-layouts  1.93 us (2%)
    ppermute x32, waiting for transfers between devices, send(): return lax.ppermute(value, AXES, pairs)  39.1 us
    ppermute x32, starting transfers between devices, send(): return lax.ppermute(value, AXES, pairs)  31.9 us
    pallas_call x13, Pallas kernels, call(): pl.pallas_call(kernel, out_shape=out, in_specs=[pl.BlockSpec(memory_space...  4.82 us
    unnamed x8, local copies, waits for them, and re-layouts  1.93 us
  transfers between devices with their start and end apart: 32, of which 17 were waited for; matrix products, arithmetic and copies ran while one was open for 0% of the time, Pallas kernels for 1%

profile of v12, /device:TPU:96, one launch (start us, length us, event | category | flops | bytes accessed | tf_op | source)
XLA Modules:
  0.0 78.6 jit_solution(2088043012450398231)
XLA Ops:
  0.5 1.0 %copy-done.1 = bf16[2,48,1536]{2,1,0:T(8,128)(2,1)S(1)} copy-done((bf16[2,48,1536]{2,1,0:T(8,128)(2,1)S(1)}, bf16[2,48,1536]{2,1,0:T(8,128)(2,1)}, u32[]{:S(2)}) %copy-start.1) | copy-done | bytes 294936
  1.9 1.6 %collective-permute-start.2 = (bf16[96,384]{1,0:T(8,128)(2,1)S(1)}, bf16[96,384]{1,0:T(8,128)(2,1)S(1)}, u32[]{:S(2)}, u32[]{:S(2)}) collective-permute-start(bf16[96,384]{1,0:T(8,128)(2,1)S(1)} %get-tuple-element.40), channel_id=1, source_target_pairs={{0,8},{1,33},{2,10},{3,35},{4,12},{5,37},{6,14},{7,39},{8,16},{9,4... | collective-permute-start | bytes 221192 | tf_op jit(solution)/shard_map/ppermute | solution.py:34
  3.5 2.9 %collective-permute-start.3 = (bf16[96,384]{1,0:T(8,128)(2,1)S(1)}, bf16[96,384]{1,0:T(8,128)(2,1)S(1)}, u32[]{:S(2)}, u32[]{:S(2)}) collective-permute-start(bf16[96,384]{1,0:T(8,128)(2,1)S(1)} %get-tuple-element.44), channel_id=1, source_target_pairs={{0,16},{1,65},{2,18},{3,67},{4,20},{5,69},{6,22},{7,71},{8,24},{9,... | collective-permute-start | bytes 221192 | tf_op jit(solution)/shard_map/ppermute | solution.py:34
  6.4 1.3 %collective-permute-start.4 = (bf16[96,384]{1,0:T(8,128)(2,1)S(1)}, bf16[96,384]{1,0:T(8,128)(2,1)S(1)}, u32[]{:S(2)}, u32[]{:S(2)}) collective-permute-start(bf16[96,384]{1,0:T(8,128)(2,1)S(1)} %get-tuple-element.45), channel_id=1, source_target_pairs={{0,24},{1,97},{2,26},{3,99},{4,28},{5,101},{6,30},{7,103},{8,0},{9... | collective-permute-start | bytes 221192 | tf_op jit(solution)/shard_map/ppermute | solution.py:34
  8.3 1.0 %copy-done = bf16[2,48,1536]{2,1,0:T(8,128)(2,1)S(1)} copy-done((bf16[2,48,1536]{2,1,0:T(8,128)(2,1)S(1)}, bf16[2,48,1536]{2,1,0:T(8,128)(2,1)}, u32[]{:S(2)}) %copy-start) | copy-done | bytes 294936
  9.3 0.9 %collective-permute-done.3.p2 = bf16[96,384]{1,0:T(8,128)(2,1)S(1)} collective-permute-done((bf16[96,384]{1,0:T(8,128)(2,1)S(1)}, bf16[96,384]{1,0:T(8,128)(2,1)S(1)}, u32[]{:S(2)}, u32[]{:S(2)}) %collective-permute-start.3) | collective-permute-done | bytes 73760 | tf_op jit(solution)/shard_map/ppermute | solution.py:34
  10.9 0.8 %collective-permute-start.9 = (bf16[96,1536]{1,0:T(8,128)(2,1)S(1)}, bf16[96,1536]{1,0:T(8,128)(2,1)S(1)}, u32[]{:S(2)}, u32[]{:S(2)}) collective-permute-start(bf16[96,1536]{1,0:T(8,128)(2,1)S(1)} %shard_map.46.a0), channel_id=1, source_target_pairs={{0,8},{1,33},{2,10},{3,35},{4,12},{5,37},{6,14},{7,39},{8,16},{9,4... | collective-permute-start | bytes 884744 | tf_op jit(solution)/shard_map/ppermute | solution.py:34
  11.7 1.5 %collective-permute-start.12 = (bf16[416,384]{1,0:T(8,128)(2,1)S(1)}, bf16[416,384]{1,0:T(8,128)(2,1)S(1)}, u32[]{:S(2)}, u32[]{:S(2)}) collective-permute-start(bf16[416,384]{1,0:T(8,128)(2,1)S(1)} %shard_map.49.l0), channel_id=1, source_target_pairs={{0,32},{1,9},{2,34},{3,11},{4,36},{5,13},{6,38},{7,15},{8,40},{9,1... | collective-permute-start | bytes 958472 | tf_op jit(solution)/shard_map/ppermute | solution.py:34
  13.2 1.7 %collective-permute-start.11 = (bf16[416,384]{1,0:T(8,128)(2,1)S(1)}, bf16[416,384]{1,0:T(8,128)(2,1)S(1)}, u32[]{:S(2)}, u32[]{:S(2)}) collective-permute-start(bf16[416,384]{1,0:T(8,128)(2,1)S(1)} %shard_map.49.l0), channel_id=1, source_target_pairs={{0,96},{1,25},{2,98},{3,27},{4,100},{5,29},{6,102},{7,31},{8,104},... | collective-permute-start | bytes 958472 | tf_op jit(solution)/shard_map/ppermute | solution.py:34
  15.0 1.8 %collective-permute-start.10 = (bf16[416,384]{1,0:T(8,128)(2,1)S(1)}, bf16[416,384]{1,0:T(8,128)(2,1)S(1)}, u32[]{:S(2)}, u32[]{:S(2)}) collective-permute-start(bf16[416,384]{1,0:T(8,128)(2,1)S(1)} %shard_map.49.l0), channel_id=1, source_target_pairs={{0,64},{1,17},{2,66},{3,19},{4,68},{5,21},{6,70},{7,23},{8,72},{9,... | collective-permute-start | bytes 958472 | tf_op jit(solution)/shard_map/ppermute | solution.py:34
  16.8 2.5 %collective-permute-start.7 = (bf16[96,1536]{1,0:T(8,128)(2,1)S(1)}, bf16[96,1536]{1,0:T(8,128)(2,1)S(1)}, u32[]{:S(2)}, u32[]{:S(2)}) collective-permute-start(bf16[96,1536]{1,0:T(8,128)(2,1)S(1)} %shard_map.46.a0), channel_id=1, source_target_pairs={{0,24},{1,97},{2,26},{3,99},{4,28},{5,101},{6,30},{7,103},{8,0},{9... | collective-permute-start | bytes 884744 | tf_op jit(solution)/shard_map/ppermute | solution.py:34
  19.3 0.8 collective-permute-done.9.a1
  20.0 0.9 %collective-permute-start.8 = (bf16[96,1536]{1,0:T(8,128)(2,1)S(1)}, bf16[96,1536]{1,0:T(8,128)(2,1)S(1)}, u32[]{:S(2)}, u32[]{:S(2)}) collective-permute-start(bf16[96,1536]{1,0:T(8,128)(2,1)S(1)} %shard_map.46.a0), channel_id=1, source_target_pairs={{0,16},{1,65},{2,18},{3,67},{4,20},{5,69},{6,22},{7,71},{8,24},{9,... | collective-permute-start | bytes 884744 | tf_op jit(solution)/shard_map/ppermute | solution.py:34
  20.9 8.9 %collective-permute-done.7.a3 = bf16[96,1536]{1,0:T(8,128)(2,1)S(1)} collective-permute-done((bf16[96,1536]{1,0:T(8,128)(2,1)S(1)}, bf16[96,1536]{1,0:T(8,128)(2,1)S(1)}, u32[]{:S(2)}, u32[]{:S(2)}) %collective-permute-start.7) | collective-permute-done | bytes 294944 | tf_op jit(solution)/shard_map/ppermute | solution.py:34
  29.9 1.3 %shard_map.50.o0.refs_9_ = bf16[416,384]{1,0:T(8,128)(2,1)S(1)} custom-call(bf16[96,1536]{1,0:T(8,128)(2,1)S(1)} %shard_map.46.a0, bf16[96,1536]{1,0:T(8,128)(2,1)S(1)} %collective-permute-done.7.a3, bf16[96,1536]{1,0:T(8,128)(2,1)S(1)} %collective-permute-done.8.a2, bf16[96,1536]{1,0:T(8,128)(2,1)S(1)} %collective-permute-done.9.a1, ...), custom_call_target="tpu_custom_call" | custom-call | flops 452984832 | bytes 2457600 | tf_op jit(solution)/shard_map/pallas_call | solution.py:82
  31.2 1.8 %collective-permute-start.15 = (bf16[416,384]{1,0:T(8,128)(2,1)S(1)}, bf16[416,384]{1,0:T(8,128)(2,1)S(1)}, u32[]{:S(2)}, u32[]{:S(2)}) collective-permute-start(bf16[416,384]{1,0:T(8,128)(2,1)S(1)} %shard_map.50.o0.refs_9_), channel_id=1, source_target_pairs={{0,64},{1,17},{2,66},{3,19},{4,20},{5,69},{6,22},{7,71},{8,72},{9,... | collective-permute-start | bytes 958472 | tf_op jit(solution)/shard_map/ppermute | solution.py:34
  33.5 2.8 %collective-permute-start.13 = (bf16[416,384]{1,0:T(8,128)(2,1)S(1)}, bf16[416,384]{1,0:T(8,128)(2,1)S(1)}, u32[]{:S(2)}, u32[]{:S(2)}) collective-permute-start(bf16[416,384]{1,0:T(8,128)(2,1)S(1)} %shard_map.50.o0.refs_9_), channel_id=1, source_target_pairs={{0,96},{1,25},{2,98},{3,27},{4,28},{5,101},{6,30},{7,103},{8,104},... | collective-permute-start | bytes 958472 | tf_op jit(solution)/shard_map/ppermute | solution.py:34
  36.3 3.6 %collective-permute-done.15.o3 = bf16[416,384]{1,0:T(8,128)(2,1)S(1)} collective-permute-done((bf16[416,384]{1,0:T(8,128)(2,1)S(1)}, bf16[416,384]{1,0:T(8,128)(2,1)S(1)}, u32[]{:S(2)}, u32[]{:S(2)}) %collective-permute-start.15) | collective-permute-done | bytes 319520 | tf_op jit(solution)/shard_map/ppermute | solution.py:34
  39.9 3.3 %collective-permute-done.14.o2 = bf16[416,384]{1,0:T(8,128)(2,1)S(1)} collective-permute-done((bf16[416,384]{1,0:T(8,128)(2,1)S(1)}, bf16[416,384]{1,0:T(8,128)(2,1)S(1)}, u32[]{:S(2)}, u32[]{:S(2)}) %collective-permute-start.14) | collective-permute-done | bytes 319520 | tf_op jit(solution)/shard_map/ppermute | solution.py:34
  43.7 1.1 %collective-permute-done.18.p2 = bf16[416,384]{1,0:T(8,128)(2,1)S(1)} collective-permute-done((bf16[416,384]{1,0:T(8,128)(2,1)S(1)}, bf16[416,384]{1,0:T(8,128)(2,1)S(1)}, u32[]{:S(2)}, u32[]{:S(2)}) %collective-permute-start.18) | collective-permute-done | bytes 319520 | tf_op jit(solution)/shard_map/ppermute | solution.py:34
  45.3 0.8 %shard_map.51 = (bf16[384,1536]{1,0:T(8,128)(2,1)S(1)}, f32[32,384]{1,0:T(8,128)S(1)}, bf16[32,384]{1,0:T(8,128)(2,1)S(1)}) custom-call(bf16[416,384]{1,0:T(8,128)(2,1)S(1)} %shard_map.50.o0.refs_9_, bf16[416,384]{1,0:T(8,128)(2,1)S(1)} %collective-permute-done.13.o1, bf16[416,384]{1,0:T(8,128)(2,1)S(1)} %collective-permute-done.14.o2, ...), custom_call_target="tpu_custom_call" | custom-call | bytes 2555904 | tf_op jit(solution)/shard_map/pallas_call | solution.py:82
  47.5 0.9 %shard_map.52 = (bf16[384,384]{1,0:T(8,128)(2,1)S(1)}, bf16[384,384]{1,0:T(8,128)(2,1)S(1)}) custom-call(bf16[416,384]{1,0:T(8,128)(2,1)S(1)} %shard_map.50.o0.refs_9_, bf16[416,384]{1,0:T(8,128)(2,1)S(1)} %collective-permute-done.13.o1, bf16[416,384]{1,0:T(8,128)(2,1)S(1)} %collective-permute-done.14.o2, bf16[416,384]{1,0:T(8,128)(2,1)S(1)} %collective-permute-done.15.o3, ...), custom_call_target="tpu_custom_call" | custom-call | flops 452984832 | bytes 3735552 | tf_op jit(solution)/shard_map/pallas_call | solution.py:82
  48.6 1.1 %collective-permute-done.22.peer.refs_1_ = bf16[32,384]{1,0:T(8,128)(2,1)S(1)} collective-permute-done((bf16[32,384]{1,0:T(8,128)(2,1)S(1)}, bf16[32,384]{1,0:T(8,128)(2,1)S(1)}, u32[]{:S(2)}, u32[]{:S(2)}) %collective-permute-start.22) | collective-permute-done | bytes 24608 | tf_op jit(solution)/shard_map/ppermute | solution.py:34
  51.7 1.0 %collective-permute-done.25.peer.refs_3_ = bf16[32,384]{1,0:T(8,128)(2,1)S(1)} collective-permute-done((bf16[32,384]{1,0:T(8,128)(2,1)S(1)}, bf16[32,384]{1,0:T(8,128)(2,1)S(1)}, u32[]{:S(2)}, u32[]{:S(2)}) %collective-permute-start.25) | collective-permute-done | bytes 24608 | tf_op jit(solution)/shard_map/ppermute | solution.py:34
  53.2 1.3 %collective-permute-start.27 = (bf16[32,384]{1,0:T(8,128)(2,1)S(1)}, bf16[32,384]{1,0:T(8,128)(2,1)S(1)}, u32[]{:S(2)}, u32[]{:S(2)}) collective-permute-start(bf16[32,384]{1,0:T(8,128)(2,1)S(1)} %shard_map.56), channel_id=1, source_target_pairs={{2,11},{6,23},{10,19},{14,31},{18,27},{22,7},{26,3},{30,15},{34,43... | collective-permute-start | bytes 73736 | tf_op jit(solution)/shard_map/ppermute | solution.py:34
  54.5 1.3 %collective-permute-start.26 = (bf16[32,384]{1,0:T(8,128)(2,1)S(1)}, bf16[32,384]{1,0:T(8,128)(2,1)S(1)}, u32[]{:S(2)}, u32[]{:S(2)}) collective-permute-start(bf16[32,384]{1,0:T(8,128)(2,1)S(1)} %shard_map.56), channel_id=1, source_target_pairs={{2,3},{6,31},{10,11},{14,7},{18,19},{22,15},{26,27},{30,23},{34,35... | collective-permute-start | bytes 73736 | tf_op jit(solution)/shard_map/ppermute | solution.py:34
  55.8 12.7 %collective-permute-done.27.r1 = bf16[32,384]{1,0:T(8,128)(2,1)S(1)} collective-permute-done((bf16[32,384]{1,0:T(8,128)(2,1)S(1)}, bf16[32,384]{1,0:T(8,128)(2,1)S(1)}, u32[]{:S(2)}, u32[]{:S(2)}) %collective-permute-start.27) | collective-permute-done | bytes 24608 | tf_op jit(solution)/shard_map/ppermute | solution.py:34
  68.8 1.2 %collective-permute-done.28.refs_5_ = bf16[32,384]{1,0:T(8,128)(2,1)S(1)} collective-permute-done((bf16[32,384]{1,0:T(8,128)(2,1)S(1)}, bf16[32,384]{1,0:T(8,128)(2,1)S(1)}, u32[]{:S(2)}, u32[]{:S(2)}) %collective-permute-start.28) | collective-permute-done | bytes 24608 | tf_op jit(solution)/shard_map/ppermute | solution.py:34
  71.3 2.7 %collective-permute-start.30 = (f32[64,48]{1,0:T(8,128)S(1)}, f32[64,48]{1,0:T(8,128)S(1)}, u32[]{:S(2)}, u32[]{:S(2)}) collective-permute-start(f32[64,48]{1,0:T(8,128)S(1)} %get-tuple-element.73), channel_id=1, source_target_pairs={{0,16},{1,65},{2,18},{3,67},{4,20},{5,69},{6,22},{7,71},{8,24},{9,... | collective-permute-start | bytes 36872 | tf_op jit(solution)/shard_map/ppermute | solution.py:34
  74.0 1.0 %collective-permute-start.31 = (f32[64,48]{1,0:T(8,128)S(1)}, f32[64,48]{1,0:T(8,128)S(1)}, u32[]{:S(2)}, u32[]{:S(2)}) collective-permute-start(f32[64,48]{1,0:T(8,128)S(1)} %get-tuple-element.74), channel_id=1, source_target_pairs={{0,24},{1,97},{2,26},{3,99},{4,28},{5,101},{6,30},{7,103},{8,0},{9... | collective-permute-start | bytes 36872 | tf_op jit(solution)/shard_map/ppermute | solution.py:34
  75.1 0.9 %collective-permute-done.29 = f32[64,48]{1,0:T(8,128)S(1)} collective-permute-done((f32[64,48]{1,0:T(8,128)S(1)}, f32[64,48]{1,0:T(8,128)S(1)}, u32[]{:S(2)}, u32[]{:S(2)}) %collective-permute-start.29) | collective-permute-done | bytes 12320 | tf_op jit(solution)/shard_map/ppermute | solution.py:34
  76.7 1.2 %collective-permute-done.31 = f32[64,48]{1,0:T(8,128)S(1)} collective-permute-done((f32[64,48]{1,0:T(8,128)S(1)}, f32[64,48]{1,0:T(8,128)S(1)}, u32[]{:S(2)}, u32[]{:S(2)}) %collective-permute-start.31) | collective-permute-done | bytes 12320 | tf_op jit(solution)/shard_map/ppermute | solution.py:34
  (54 shorter events, 10.6 us)
Async XLA Ops:
  0.0 1.8 %collective-permute-start.1 = (bf16[2,48,1536]{2,1,0:T(8,128)(2,1)}, bf16[2,48,1536]{2,1,0:T(8,128)(2,1)S(1)}, u32[]{:S(2)}, u32[]{:S(2)}) collective-permute-start(bf16[2,48,1536]{2,1,0:T(8,128)(2,1)} %own.3), channel_id=1, source_target_pairs={{0,4},{1,5},{2,6},{3,7},{4,0},{5,1},{6,2},{7,3},{8,12},{9,13},{10,... | collective-permute-start | bytes 884744 | tf_op jit(solution)/shard_map/ppermute | solution.py:34
  0.0 7.8 %collective-permute-start = (bf16[2,48,1536]{2,1,0:T(8,128)(2,1)}, bf16[2,48,1536]{2,1,0:T(8,128)(2,1)S(1)}, u32[]{:S(2)}, u32[]{:S(2)}) collective-permute-start(bf16[2,48,1536]{2,1,0:T(8,128)(2,1)} %own.2), channel_id=1, source_target_pairs={{0,4},{1,5},{2,6},{3,7},{4,0},{5,1},{6,2},{7,3},{8,12},{9,13},{10,... | collective-permute-start | bytes 884744 | tf_op jit(solution)/shard_map/ppermute | solution.py:34
  1.9 7.4 %collective-permute-start.2 = (bf16[96,384]{1,0:T(8,128)(2,1)S(1)}, bf16[96,384]{1,0:T(8,128)(2,1)S(1)}, u32[]{:S(2)}, u32[]{:S(2)}) collective-permute-start(bf16[96,384]{1,0:T(8,128)(2,1)S(1)} %get-tuple-element.40), channel_id=1, source_target_pairs={{0,8},{1,33},{2,10},{3,35},{4,12},{5,37},{6,14},{7,39},{8,16},{9,4... | collective-permute-start | bytes 221192 | tf_op jit(solution)/shard_map/ppermute | solution.py:34
  3.5 6.8 %collective-permute-start.3 = (bf16[96,384]{1,0:T(8,128)(2,1)S(1)}, bf16[96,384]{1,0:T(8,128)(2,1)S(1)}, u32[]{:S(2)}, u32[]{:S(2)}) collective-permute-start(bf16[96,384]{1,0:T(8,128)(2,1)S(1)} %get-tuple-element.44), channel_id=1, source_target_pairs={{0,16},{1,65},{2,18},{3,67},{4,20},{5,69},{6,22},{7,71},{8,24},{9,... | collective-permute-start | bytes 221192 | tf_op jit(solution)/shard_map/ppermute | solution.py:34
  6.4 4.4 %collective-permute-start.4 = (bf16[96,384]{1,0:T(8,128)(2,1)S(1)}, bf16[96,384]{1,0:T(8,128)(2,1)S(1)}, u32[]{:S(2)}, u32[]{:S(2)}) collective-permute-start(bf16[96,384]{1,0:T(8,128)(2,1)S(1)} %get-tuple-element.45), channel_id=1, source_target_pairs={{0,24},{1,97},{2,26},{3,99},{4,28},{5,101},{6,30},{7,103},{8,0},{9... | collective-permute-start | bytes 221192 | tf_op jit(solution)/shard_map/ppermute | solution.py:34
  7.8 1.5 %collective-permute-start.5 = (bf16[2,32,48]{2,1,0:T(8,128)(2,1)}, bf16[2,32,48]{2,1,0:T(8,128)(2,1)S(1)}, u32[]{:S(2)}, u32[]{:S(2)}) collective-permute-start(bf16[2,32,48]{2,1,0:T(8,128)(2,1)} %bitcast.5), channel_id=1, source_target_pairs={{0,4},{1,5},{2,6},{3,7},{4,0},{5,1},{6,2},{7,3},{8,12},{9,13},{10,... | collective-permute-start | bytes 18440 | tf_op jit(solution)/shard_map/ppermute | solution.py:34
  7.8 1.6 %collective-permute-start.6 = (f32[32,48]{1,0:T(8,128)}, f32[32,48]{1,0:T(8,128)S(1)}, u32[]{:S(2)}, u32[]{:S(2)}) collective-permute-start(f32[32,48]{1,0:T(8,128)} %bitcast.7), channel_id=1, source_target_pairs={{0,4},{1,5},{2,6},{3,7},{4,0},{5,1},{6,2},{7,3},{8,12},{9,13},{10,... | collective-permute-start | bytes 18440 | tf_op jit(solution)/shard_map/ppermute | solution.py:34
  10.9 9.1 %collective-permute-start.9 = (bf16[96,1536]{1,0:T(8,128)(2,1)S(1)}, bf16[96,1536]{1,0:T(8,128)(2,1)S(1)}, u32[]{:S(2)}, u32[]{:S(2)}) collective-permute-start(bf16[96,1536]{1,0:T(8,128)(2,1)S(1)} %shard_map.46.a0), channel_id=1, source_target_pairs={{0,8},{1,33},{2,10},{3,35},{4,12},{5,37},{6,14},{7,39},{8,16},{9,4... | collective-permute-start | bytes 884744 | tf_op jit(solution)/shard_map/ppermute | solution.py:34
  11.7 18.1 %collective-permute-start.12 = (bf16[416,384]{1,0:T(8,128)(2,1)S(1)}, bf16[416,384]{1,0:T(8,128)(2,1)S(1)}, u32[]{:S(2)}, u32[]{:S(2)}) collective-permute-start(bf16[416,384]{1,0:T(8,128)(2,1)S(1)} %shard_map.49.l0), channel_id=1, source_target_pairs={{0,32},{1,9},{2,34},{3,11},{4,36},{5,13},{6,38},{7,15},{8,40},{9,1... | collective-permute-start | bytes 958472 | tf_op jit(solution)/shard_map/ppermute | solution.py:34
  13.2 16.7 %collective-permute-start.11 = (bf16[416,384]{1,0:T(8,128)(2,1)S(1)}, bf16[416,384]{1,0:T(8,128)(2,1)S(1)}, u32[]{:S(2)}, u32[]{:S(2)}) collective-permute-start(bf16[416,384]{1,0:T(8,128)(2,1)S(1)} %shard_map.49.l0), channel_id=1, source_target_pairs={{0,96},{1,25},{2,98},{3,27},{4,100},{5,29},{6,102},{7,31},{8,104},... | collective-permute-start | bytes 958472 | tf_op jit(solution)/shard_map/ppermute | solution.py:34
  15.0 14.9 %collective-permute-start.10 = (bf16[416,384]{1,0:T(8,128)(2,1)S(1)}, bf16[416,384]{1,0:T(8,128)(2,1)S(1)}, u32[]{:S(2)}, u32[]{:S(2)}) collective-permute-start(bf16[416,384]{1,0:T(8,128)(2,1)S(1)} %shard_map.49.l0), channel_id=1, source_target_pairs={{0,64},{1,17},{2,66},{3,19},{4,68},{5,21},{6,70},{7,23},{8,72},{9,... | collective-permute-start | bytes 958472 | tf_op jit(solution)/shard_map/ppermute | solution.py:34
  16.8 13.1 %collective-permute-start.7 = (bf16[96,1536]{1,0:T(8,128)(2,1)S(1)}, bf16[96,1536]{1,0:T(8,128)(2,1)S(1)}, u32[]{:S(2)}, u32[]{:S(2)}) collective-permute-start(bf16[96,1536]{1,0:T(8,128)(2,1)S(1)} %shard_map.46.a0), channel_id=1, source_target_pairs={{0,24},{1,97},{2,26},{3,99},{4,28},{5,101},{6,30},{7,103},{8,0},{9... | collective-permute-start | bytes 884744 | tf_op jit(solution)/shard_map/ppermute | solution.py:34
  20.0 9.8 %collective-permute-start.8 = (bf16[96,1536]{1,0:T(8,128)(2,1)S(1)}, bf16[96,1536]{1,0:T(8,128)(2,1)S(1)}, u32[]{:S(2)}, u32[]{:S(2)}) collective-permute-start(bf16[96,1536]{1,0:T(8,128)(2,1)S(1)} %shard_map.46.a0), channel_id=1, source_target_pairs={{0,16},{1,65},{2,18},{3,67},{4,20},{5,69},{6,22},{7,71},{8,24},{9,... | collective-permute-start | bytes 884744 | tf_op jit(solution)/shard_map/ppermute | solution.py:34
  31.2 8.7 %collective-permute-start.15 = (bf16[416,384]{1,0:T(8,128)(2,1)S(1)}, bf16[416,384]{1,0:T(8,128)(2,1)S(1)}, u32[]{:S(2)}, u32[]{:S(2)}) collective-permute-start(bf16[416,384]{1,0:T(8,128)(2,1)S(1)} %shard_map.50.o0.refs_9_), channel_id=1, source_target_pairs={{0,64},{1,17},{2,66},{3,19},{4,20},{5,69},{6,22},{7,71},{8,72},{9,... | collective-permute-start | bytes 958472 | tf_op jit(solution)/shard_map/ppermute | solution.py:34
  33.0 10.2 %collective-permute-start.14 = (bf16[416,384]{1,0:T(8,128)(2,1)S(1)}, bf16[416,384]{1,0:T(8,128)(2,1)S(1)}, u32[]{:S(2)}, u32[]{:S(2)}) collective-permute-start(bf16[416,384]{1,0:T(8,128)(2,1)S(1)} %shard_map.50.o0.refs_9_), channel_id=1, source_target_pairs={{0,32},{1,9},{2,34},{3,11},{4,12},{5,37},{6,14},{7,39},{8,40},{9,1... | collective-permute-start | bytes 958472 | tf_op jit(solution)/shard_map/ppermute | solution.py:34
  33.5 9.7 %collective-permute-start.13 = (bf16[416,384]{1,0:T(8,128)(2,1)S(1)}, bf16[416,384]{1,0:T(8,128)(2,1)S(1)}, u32[]{:S(2)}, u32[]{:S(2)}) collective-permute-start(bf16[416,384]{1,0:T(8,128)(2,1)S(1)} %shard_map.50.o0.refs_9_), channel_id=1, source_target_pairs={{0,96},{1,25},{2,98},{3,27},{4,28},{5,101},{6,30},{7,103},{8,104},... | collective-permute-start | bytes 958472 | tf_op jit(solution)/shard_map/ppermute | solution.py:34
  36.3 7.5 %collective-permute-start.16 = (bf16[416,384]{1,0:T(8,128)(2,1)S(1)}, bf16[416,384]{1,0:T(8,128)(2,1)S(1)}, u32[]{:S(2)}, u32[]{:S(2)}) collective-permute-start(bf16[416,384]{1,0:T(8,128)(2,1)S(1)} %shard_map.50.o0.refs_9_), channel_id=1, source_target_pairs={{0,4},{1,5},{2,6},{3,7},{4,0},{5,1},{6,2},{7,3},{8,12},{9,13},{10,... | collective-permute-start | bytes 958472 | tf_op jit(solution)/shard_map/ppermute | solution.py:34
  39.9 3.8 %collective-permute-start.19 = (bf16[416,384]{1,0:T(8,128)(2,1)S(1)}, bf16[416,384]{1,0:T(8,128)(2,1)S(1)}, u32[]{:S(2)}, u32[]{:S(2)}) collective-permute-start(bf16[416,384]{1,0:T(8,128)(2,1)S(1)} %collective-permute-done.15.o3), channel_id=1, source_target_pairs={{0,4},{1,5},{2,6},{3,7},{4,0},{5,1},{6,2},{7,3},{8,12},{9,13},{10,... | collective-permute-start | bytes 958472 | tf_op jit(solution)/shard_map/ppermute | solution.py:34
  43.2 1.6 %collective-permute-start.18 = (bf16[416,384]{1,0:T(8,128)(2,1)S(1)}, bf16[416,384]{1,0:T(8,128)(2,1)S(1)}, u32[]{:S(2)}, u32[]{:S(2)}) collective-permute-start(bf16[416,384]{1,0:T(8,128)(2,1)S(1)} %collective-permute-done.14.o2), channel_id=1, source_target_pairs={{0,4},{1,5},{2,6},{3,7},{4,0},{5,1},{6,2},{7,3},{8,12},{9,13},{10,... | collective-permute-start | bytes 958472 | tf_op jit(solution)/shard_map/ppermute | solution.py:34
  43.2 2.1 %collective-permute-start.17 = (bf16[416,384]{1,0:T(8,128)(2,1)S(1)}, bf16[416,384]{1,0:T(8,128)(2,1)S(1)}, u32[]{:S(2)}, u32[]{:S(2)}) collective-permute-start(bf16[416,384]{1,0:T(8,128)(2,1)S(1)} %collective-permute-done.13.o1), channel_id=1, source_target_pairs={{0,4},{1,5},{2,6},{3,7},{4,0},{5,1},{6,2},{7,3},{8,12},{9,13},{10,... | collective-permute-start | bytes 958472 | tf_op jit(solution)/shard_map/ppermute | solution.py:34
  46.1 2.3 %collective-permute-start.21 = (bf16[32,384]{1,0:T(8,128)(2,1)S(1)}, bf16[32,384]{1,0:T(8,128)(2,1)S(1)}, u32[]{:S(2)}, u32[]{:S(2)}) collective-permute-start(bf16[32,384]{1,0:T(8,128)(2,1)S(1)} %get-tuple-element.48), channel_id=1, source_target_pairs={{0,9},{4,21},{8,17},{12,29},{16,25},{20,5},{24,1},{28,13},{32,41},... | collective-permute-start | bytes 73736 | tf_op jit(solution)/shard_map/ppermute | solution.py:34
  46.8 1.6 %collective-permute-start.20 = (bf16[32,384]{1,0:T(8,128)(2,1)S(1)}, bf16[32,384]{1,0:T(8,128)(2,1)S(1)}, u32[]{:S(2)}, u32[]{:S(2)}) collective-permute-start(bf16[32,384]{1,0:T(8,128)(2,1)S(1)} %get-tuple-element.48), channel_id=1, source_target_pairs={{0,1},{4,29},{8,9},{12,5},{16,17},{20,13},{24,25},{28,21},{32,33},... | collective-permute-start | bytes 73736 | tf_op jit(solution)/shard_map/ppermute | solution.py:34
  48.4 1.3 %collective-permute-start.22 = (bf16[32,384]{1,0:T(8,128)(2,1)S(1)}, bf16[32,384]{1,0:T(8,128)(2,1)S(1)}, u32[]{:S(2)}, u32[]{:S(2)}) collective-permute-start(bf16[32,384]{1,0:T(8,128)(2,1)S(1)} %get-tuple-element.55), channel_id=1, source_target_pairs={{0,4},{1,5},{2,6},{3,7},{4,0},{5,1},{6,2},{7,3},{8,12},{9,13},{10,... | collective-permute-start | bytes 73736 | tf_op jit(solution)/shard_map/ppermute | solution.py:34
  50.1 1.4 %collective-permute-start.24 = (bf16[32,384]{1,0:T(8,128)(2,1)S(1)}, bf16[32,384]{1,0:T(8,128)(2,1)S(1)}, u32[]{:S(2)}, u32[]{:S(2)}) collective-permute-start(bf16[32,384]{1,0:T(8,128)(2,1)S(1)} %shard_map.54), channel_id=1, source_target_pairs={{1,34},{5,70},{9,42},{13,78},{17,50},{21,86},{25,58},{29,94},{33,6... | collective-permute-start | bytes 73736 | tf_op jit(solution)/shard_map/ppermute | solution.py:34
  50.8 0.7 collective-permute-start.23
  51.5 1.3 %collective-permute-start.25 = (bf16[32,384]{1,0:T(8,128)(2,1)S(1)}, bf16[32,384]{1,0:T(8,128)(2,1)S(1)}, u32[]{:S(2)}, u32[]{:S(2)}) collective-permute-start(bf16[32,384]{1,0:T(8,128)(2,1)S(1)} %get-tuple-element.62), channel_id=1, source_target_pairs={{0,4},{1,5},{2,6},{3,7},{4,0},{5,1},{6,2},{7,3},{8,12},{9,13},{10,... | collective-permute-start | bytes 73736 | tf_op jit(solution)/shard_map/ppermute | solution.py:34
  53.2 15.3 %collective-permute-start.27 = (bf16[32,384]{1,0:T(8,128)(2,1)S(1)}, bf16[32,384]{1,0:T(8,128)(2,1)S(1)}, u32[]{:S(2)}, u32[]{:S(2)}) collective-permute-start(bf16[32,384]{1,0:T(8,128)(2,1)S(1)} %shard_map.56), channel_id=1, source_target_pairs={{2,11},{6,23},{10,19},{14,31},{18,27},{22,7},{26,3},{30,15},{34,43... | collective-permute-start | bytes 73736 | tf_op jit(solution)/shard_map/ppermute | solution.py:34
  54.5 14.2 %collective-permute-start.26 = (bf16[32,384]{1,0:T(8,128)(2,1)S(1)}, bf16[32,384]{1,0:T(8,128)(2,1)S(1)}, u32[]{:S(2)}, u32[]{:S(2)}) collective-permute-start(bf16[32,384]{1,0:T(8,128)(2,1)S(1)} %shard_map.56), channel_id=1, source_target_pairs={{2,3},{6,31},{10,11},{14,7},{18,19},{22,15},{26,27},{30,23},{34,35... | collective-permute-start | bytes 73736 | tf_op jit(solution)/shard_map/ppermute | solution.py:34
  68.7 1.3 %collective-permute-start.28 = (bf16[32,384]{1,0:T(8,128)(2,1)S(1)}, bf16[32,384]{1,0:T(8,128)(2,1)S(1)}, u32[]{:S(2)}, u32[]{:S(2)}) collective-permute-start(bf16[32,384]{1,0:T(8,128)(2,1)S(1)} %get-tuple-element.68), channel_id=1, source_target_pairs={{0,4},{1,5},{2,6},{3,7},{4,0},{5,1},{6,2},{7,3},{8,12},{9,13},{10,... | collective-permute-start | bytes 73736 | tf_op jit(solution)/shard_map/ppermute | solution.py:34
  70.7 5.3 %collective-permute-start.29 = (f32[64,48]{1,0:T(8,128)S(1)}, f32[64,48]{1,0:T(8,128)S(1)}, u32[]{:S(2)}, u32[]{:S(2)}) collective-permute-start(f32[64,48]{1,0:T(8,128)S(1)} %get-tuple-element.72), channel_id=1, source_target_pairs={{0,8},{1,33},{2,10},{3,35},{4,12},{5,37},{6,14},{7,39},{8,16},{9,4... | collective-permute-start | bytes 36872 | tf_op jit(solution)/shard_map/ppermute | solution.py:34
  71.3 5.4 %collective-permute-start.30 = (f32[64,48]{1,0:T(8,128)S(1)}, f32[64,48]{1,0:T(8,128)S(1)}, u32[]{:S(2)}, u32[]{:S(2)}) collective-permute-start(f32[64,48]{1,0:T(8,128)S(1)} %get-tuple-element.73), channel_id=1, source_target_pairs={{0,16},{1,65},{2,18},{3,67},{4,20},{5,69},{6,22},{7,71},{8,24},{9,... | collective-permute-start | bytes 36872 | tf_op jit(solution)/shard_map/ppermute | solution.py:34
  74.0 3.9 %collective-permute-start.31 = (f32[64,48]{1,0:T(8,128)S(1)}, f32[64,48]{1,0:T(8,128)S(1)}, u32[]{:S(2)}, u32[]{:S(2)}) collective-permute-start(f32[64,48]{1,0:T(8,128)S(1)} %get-tuple-element.74), channel_id=1, source_target_pairs={{0,24},{1,97},{2,26},{3,99},{4,28},{5,101},{6,30},{7,103},{8,0},{9... | collective-permute-start | bytes 36872 | tf_op jit(solution)/shard_map/ppermute | solution.py:34
  (4 other events, 20.6 us)
